TPU v7x, 32 devices: a whole 2x2x4 slice. The times are simulated.
32 devices in a mesh: drift: 8 (over y, x, core), wire: 4 (over z).
Axes of the slice: x: 2, y: 2, z: 4, core: 2. Of those that a mesh axis runs over, the one named last changes fastest.
Arguments:
- features: bfloat16 [8, 4, 576, 128], P('drift', 'wire'), may hold values from -6 to 6
- first_weight: bfloat16 [27, 128, 128], replicated, may hold values from -0.109375 to 0.109375
- second_weight: bfloat16 [27, 128, 128], replicated, may hold values from -0.109375 to 0.109375
- cotangent: bfloat16 [8, 4, 576, 128], P('drift', 'wire'), may hold values from -6 to 6
- counts: int32 [8, 4], P('drift', 'wire'), may hold values from 1 to 9, as said below
- kernel_map: int32 [8, 4, 27, 9], P('drift', 'wire'), may hold values from 0 to 25, as said below
- send_lists: int32 [8, 4, 16], P('drift', 'wire'), may hold values from 0 to 9, as said below
Outputs:
- output: bfloat16 [8, 4, 576, 128], P('drift', 'wire')
- grad_features: bfloat16 [8, 4, 576, 128], P('drift', 'wire')
- grad_first: float32 [27, 128, 128], replicated
- grad_second: float32 [27, 128, 128], replicated
Inputs may be any that keep to these rules, and one draw needn't show every extreme that they name: Slots below counts[i, j] hold the region's active blocks in order of position; some region has all 9 positions active and some region exactly one. kernel_map[i, j, k, s] is the block_table row of the active block at block offset k of slot s: a slot below 9 for a block of the same region, 10 + a segment position for a block of a neighbouring region (listed there in that region's send list), and 9 where that block is inactive, outside the volume, or s is an empty slot. `send_lists`: each segment lists, in order of position, the positions of the region's face, edge or corner next to that neighbour: the slot of an active block there, else 9.
All inputs are finite; a program needn't handle non-finite values.
Results may differ from a plain program's by a relative error of at most 0.0031.
Values may be sent and summed in bfloat16 or wider, within the bound.
No kernel may reach another device: no remote copies, remote signals or barrier semaphores. Data moves between devices by JAX's collectives and lax.ppermute only.
A program may use at most 128 MiB of HBM per device.

v0:
```python
import functools
import math

import jax
import jax.numpy as jnp
from jax import lax
from jax.experimental import pallas as pl
from jax.experimental.pallas import tpu as pltpu
from jax.sharding import PartitionSpec as P

BX = 3
BW = 3
NX = 4 * BX
NY = 4 * BW
J = 16
PLANE = NX * J
WIDE = (NX + 2) * J
ROWS = 4 * PLANE
FACE = 4 * NX
SLAB = 4 * J
VMEM = pl.BlockSpec(memory_space=pltpu.VMEM)
SMEM = pl.BlockSpec(memory_space=pltpu.SMEM)
LISTED = {0: 0, 1: 1, 2: 2, 3: 7, 5: 10, 6: 3, 7: 4, 8: 5}


def call(kernel, out_shape, n_smem, n_vmem, scratch=(), flops=0, bytes_accessed=0):
    return pl.pallas_call(
        kernel,
        out_shape=out_shape,
        in_specs=[SMEM] * n_smem + [VMEM] * n_vmem,
        out_specs=jax.tree.map(lambda _: VMEM, out_shape),
        scratch_shapes=list(scratch),
        compiler_params=pltpu.CompilerParams(vmem_limit_bytes=40 * 1024 * 1024),
        cost_estimate=pl.CostEstimate(flops=flops, bytes_accessed=bytes_accessed, transcendentals=0),
    )


def bf16(*shape):
    return jax.ShapeDtypeStruct(shape, jnp.bfloat16)


def f32(*shape):
    return jax.ShapeDtypeStruct(shape, jnp.float32)


def iota(shape, dim):
    return lax.broadcasted_iota(jnp.int32, shape, dim)


def position_slots(geo):
    slots = {p: geo[i] for p, i in LISTED.items()}
    present = {p: (s < 9).astype(jnp.int32) for p, s in slots.items()}
    before = present[0] + present[1] + present[2] + present[3]
    others = before + present[5] + present[6] + present[7] + present[8]
    slots[4] = jnp.where(geo[16] > others, before, 9)
    return slots


def slot_rows(slots, z, x, y, valid):
    position = (x >> 2) * BW + (y >> 2)
    slot = jnp.full(position.shape, 9, jnp.int32)
    for p, s in slots.items():
        slot = jnp.where(position == p, s, slot)
    row = slot * 64 + (x & 3) * 16 + (y & 3) * 4 + z
    return jnp.where(valid & (slot < 9), row, -1)


def one_hot(rows, width):
    lane = iota(rows.shape, 1)
    parts = [jnp.where(rows == lane + 128 * c, 1.0, 0.0).astype(jnp.bfloat16) for c in range(width // 128)]
    return jnp.concatenate(parts, axis=1)


def dot(a, b):
    return jnp.dot(a, b, preferred_element_type=jnp.float32)


def grid_indices():
    shape = (4, NX, J, 128)
    z, x, j = (iota(shape, d).reshape(ROWS, 128) for d in range(3))
    return z, x, j


def faces_kernel(geo, f, g, low, high, both):
    both[...] = jnp.zeros_like(both)
    both[0 : f.shape[0], 0:128] = f[...]
    both[0 : f.shape[0], 128:256] = g[...]
    slots = position_slots(geo)
    shape = (4, NX // 4, 4, 128)
    r = iota((FACE, 128), 0)
    z = (r >= NX).astype(jnp.int32) + (r >= 2 * NX) + (r >= 3 * NX)
    x = r - NX * z
    for y, out in ((0, low), (NY - 1, high)):
        rows = slot_rows(slots, z, x, jnp.full_like(x, y), x >= 0)
        out[...] = dot(one_hot(rows, 640), both[...]).astype(jnp.bfloat16)


def place_kernel(geo, f, g, out, live, both):
    both[...] = jnp.zeros_like(both)
    both[0 : f.shape[0], 0:128] = f[...]
    both[0 : f.shape[0], 128:256] = g[...]
    z, x, j = grid_indices()
    rows = slot_rows(position_slots(geo), z, x, j - 1, (j >= 1) & (j <= NY))
    live[...] = (rows >= 0).astype(jnp.bfloat16)
    out[...] = dot(one_hot(rows, 640), both[...]).astype(jnp.bfloat16)


def insert_kernel(placed, from_low, from_high, out, slab_low, slab_high, faces):
    faces[...] = jnp.zeros_like(faces)
    faces[0:FACE, :] = from_low[...]
    faces[FACE : 2 * FACE, :] = from_high[...]
    z, x, j = grid_indices()
    rows = z * NX + x
    rows = jnp.where(j == 0, rows, jnp.where(j == NY + 1, rows + FACE, -1))
    full = (placed[...].astype(jnp.float32) + dot(one_hot(rows, 128), faces[...])).astype(jnp.bfloat16)
    out[...] = full
    for z in range(4):
        slab_low[z * J : (z + 1) * J, :] = full[z * PLANE : z * PLANE + J, :]
        slab_high[z * J : (z + 1) * J, :] = full[(z + 1) * PLANE - J : (z + 1) * PLANE, :]


def build_window(window, base, plane_of):
    for zi in range(4):
        plane = plane_of(zi)
        wide = plane.astype(jnp.float32)
        before = pltpu.roll(wide, 1, 0).astype(jnp.bfloat16)
        after = pltpu.roll(wide, WIDE - 1, 0).astype(jnp.bfloat16)
        for oy, shifted in enumerate((before, plane, after)):
            for z in range(max(0, zi - 1), min(3, zi + 1) + 1):
                lane = 128 * (3 * oy + zi - z + 1)
                window[base + z, :, lane : lane + 128] = shifted
    empty = jnp.zeros((WIDE, 128), jnp.bfloat16)
    for oy in range(3):
        window[base, :, 384 * oy : 384 * oy + 128] = empty
        window[base + 3, :, 384 * oy + 256 : 384 * oy + 384] = empty


def wide_plane(full, low, high, z, lanes):
    return jnp.concatenate(
        [
            low[z * J : (z + 1) * J, lanes],
            full[z * PLANE : (z + 1) * PLANE, lanes],
            high[z * J : (z + 1) * J, lanes],
        ],
        axis=0,
    )


def conv(window, weight):
    total = None
    for ox in range(3):
        rows = window[:, ox * J : ox * J + PLANE, :].reshape(ROWS, 1152)
        term = dot(rows, weight[1152 * ox : 1152 * (ox + 1), :])
        total = term if total is None else total + term
    return total


def first_kernel(place, full, low, high, live, w1, w2f, hb, face_low, face_high, keep, send, window):
    core = place[0]
    f_lanes, g_lanes = slice(0, 128), slice(128, 256)
    alive = live[...].astype(jnp.float32)
    build_window(window, 0, lambda z: wide_plane(full, low, high, z, f_lanes))
    first_pre = conv(window, w1)
    gate = jax.nn.sigmoid(first_pre)
    hidden = (alive * (first_pre * gate)).astype(jnp.bfloat16)
    slope = alive * (gate * (1.0 + first_pre * (1.0 - gate)))
    build_window(window, 0, lambda z: wide_plane(full, low, high, z, g_lanes))
    back = (conv(window, w2f) * slope).astype(jnp.bfloat16)
    both = jnp.concatenate([hidden, back], axis=1)
    hb[...] = both
    r = iota((FACE, 128), 0)
    z = (r >= NX).astype(jnp.int32) + (r >= 2 * NX) + (r >= 3 * NX)
    rows = z * PLANE + (r - NX * z) * J
    face_low[...] = dot(one_hot(rows + 1, ROWS), both).astype(jnp.bfloat16)
    face_high[...] = dot(one_hot(rows + NY, ROWS), both).astype(jnp.bfloat16)

    def write(to, values, lanes):
        to[0:ROWS, :] = values
        for z in range(4):
            start = ROWS + z * WIDE
            to[start : start + WIDE, :] = wide_plane(full, low, high, z, lanes)

    @pl.when(core == 0)
    def _():
        write(keep, hidden, g_lanes)
        write(send, back, f_lanes)

    @pl.when(core != 0)
    def _():
        write(keep, back, f_lanes)
        write(send, hidden, g_lanes)


def terms_kernel(chunk, place, mine, theirs, *refs):
    *sends, own, window, total = refs
    for base, part in ((0, mine), (4, theirs)):
        build_window(
            window, base, lambda z: part[ROWS + z * WIDE : ROWS + (z + 1) * WIDE, :]
        )
    left = jnp.concatenate([mine[0:ROWS, :], theirs[0:ROWS, :]], axis=0)
    left = left.astype(jnp.float32).T.astype(jnp.bfloat16)
    if total.shape[0] > 3456:
        total[3456:, :] = jnp.zeros((total.shape[0] - 3456, 128), jnp.float32)
    for ox in range(3):
        rows = window[:, ox * J : ox * J + PLANE, :].reshape(2 * ROWS, 1152)
        product = dot(left, rows)
        for k in range(9):
            start = 128 * (9 * ox + k)
            total[start : start + 128, :] = product[:, 128 * k : 128 * (k + 1)]
    me = place[1]
    own[...] = total[pl.ds(pl.multiple_of(me * chunk, 8), chunk), :]
    for step, out in enumerate(sends):
        start = pl.multiple_of((me ^ (step + 1)) * chunk, 8)
        out[...] = total[pl.ds(start, chunk), :].astype(jnp.bfloat16)


def split_kernel(unit, count, place, own, *refs):
    received, (*sends, rest, total) = refs[:count], refs[count:]
    summed = own[...]
    for part in received:
        summed = summed + part[...].astype(jnp.float32)
    total[...] = summed
    me = place[2]
    rest[...] = total[pl.ds(pl.multiple_of(me * unit, 8), unit), :]
    for step, out in enumerate(sends):
        start = pl.multiple_of((me ^ (step + 1)) * unit, 8)
        out[...] = total[pl.ds(start, unit), :].astype(jnp.bfloat16)


def joined_kernel(unit, place, *refs):
    *parts, out, total = refs
    me = place[2]
    for step, part in enumerate(parts):
        start = pl.multiple_of((me ^ step) * unit, 8)
        total[pl.ds(start, unit), :] = part[...].astype(jnp.float32)
    out[...] = total[...].astype(jnp.bfloat16)


def final_kernel(chunk, count, place, *refs):
    mine, theirs = refs[:count], refs[count : 2 * count]
    first, second, total = refs[2 * count :]
    core, me = place[0], place[1]
    for step in range(count):
        start = pl.multiple_of((me ^ step) * chunk, 8)
        total[core, pl.ds(start, chunk), :] = mine[step][...].astype(jnp.float32)
        total[1 - core, pl.ds(start, chunk), :] = theirs[step][...].astype(jnp.float32)
    for k in range(27):
        second[26 - k] = total[0, 128 * k : 128 * (k + 1), :]
        first[k] = total[1, 128 * k : 128 * (k + 1), :].T


def second_kernel(geo, hb, low, high, base, live, w2, w1f, output, grad, window):
    alive = live[...].astype(jnp.float32)
    results = []
    for lanes, weight in ((slice(0, 128), w2), (slice(128, 256), w1f)):
        build_window(window, 0, lambda z: wide_plane(hb, low, high, z, lanes))
        value = conv(window, weight)
        results.append((alive * (base[:, lanes].astype(jnp.float32) + value)).astype(jnp.bfloat16))
    both = jnp.concatenate(results, axis=1)
    slots = position_slots(geo)
    pieces = []
    row = iota((576, 128), 0)
    for c in range(ROWS // 128):
        col = iota((8, 128), 1) + 128 * c
        z = (col >= PLANE).astype(jnp.int32) + (col >= 2 * PLANE) + (col >= 3 * PLANE)
        rest = col - PLANE * z
        x, j = rest >> 4, rest & 15
        source = slot_rows(slots, z, x, j - 1, (j >= 1) & (j <= NY))
        source = jnp.broadcast_to(source[0:1, :], (576, 128))
        pieces.append(jnp.where(row == source, 1.0, 0.0).astype(jnp.bfloat16))
    by_slot = dot(jnp.concatenate(pieces, axis=1), both).astype(jnp.bfloat16)
    output[...] = by_slot[:, 0:128]
    grad[...] = by_slot[:, 128:256]


def shift(value, axis, steps):
    count = lax.axis_size(axis)
    return lax.ppermute(value, axis, [(i, i + steps) for i in range(count) if 0 <= i + steps < count])


def on_device(features, first_weight, second_weight, cotangent, counts, kernel_map, send_lists):
    drift, wire = lax.axis_size("drift"), lax.axis_size("wire")
    chips = drift // 2
    rows = 27 * 128
    unit = -(-rows // (chips * wire * 8)) * 8
    chunk = unit * wire
    f, g = features[0, 0], cotangent[0, 0]
    slots = f.shape[0]
    geo = jnp.concatenate([send_lists.reshape(16), counts.reshape(1)])
    d, w = lax.axis_index("drift"), lax.axis_index("wire")
    place = jnp.stack([d % 2, d // 2, w]).astype(jnp.int32)
    w1, w2 = first_weight.reshape(rows, 128), second_weight.reshape(rows, 128)
    w1f = jnp.transpose(first_weight[::-1], (0, 2, 1)).reshape(rows, 128)
    w2f = jnp.transpose(second_weight[::-1], (0, 2, 1)).reshape(rows, 128)
    both = pltpu.VMEM((640, 256), jnp.bfloat16)
    window = pltpu.VMEM((4, WIDE, 1152), jnp.bfloat16)

    def halo(placed, face_low, face_high):
        from_high = shift(face_low, "wire", -1)
        from_low = shift(face_high, "wire", 1)
        full, slab_low, slab_high = call(
            insert_kernel,
            (bf16(ROWS, 256), bf16(SLAB, 256), bf16(SLAB, 256)),
            0,
            3,
            [pltpu.VMEM((128, 256), jnp.bfloat16)],
        )(placed, from_low, from_high)
        high = shift(slab_low, "drift", -1)
        low = shift(slab_high, "drift", 1)
        return full, low, high

    face_low, face_high = call(faces_kernel, (bf16(FACE, 256), bf16(FACE, 256)), 1, 2, [both])(geo, f, g)
    placed, live = call(place_kernel, (bf16(ROWS, 256), bf16(ROWS, 128)), 1, 2, [both])(geo, f, g)
    full, low, high = halo(placed, face_low, face_high)
    message = bf16(ROWS + 4 * WIDE, 128)
    hb, hb_low, hb_high, keep, send = call(
        first_kernel,
        (bf16(ROWS, 256), bf16(FACE, 256), bf16(FACE, 256), message, message),
        1,
        6,
        [window],
    )(place, full, low, high, live, w1, w2f)

    def swap_core(value):
        return lax.ppermute(value, "drift", [(i, i ^ 1) for i in range(drift)])

    def to_chip(value, step):
        return lax.ppermute(value, "drift", [(i, i ^ (2 * step)) for i in range(drift)])

    def to_wire(value, step):
        return lax.ppermute(value, "wire", [(i, i ^ step) for i in range(wire)])

    got = swap_core(send)
    *sends, own = call(
        functools.partial(terms_kernel, chunk),
        tuple([bf16(chunk, 128)] * (chips - 1) + [f32(chunk, 128)]),
        1,
        2,
        [pltpu.VMEM((8, WIDE, 1152), jnp.bfloat16), pltpu.VMEM((chunk * chips, 128), jnp.float32)],
    )(place, keep, got)
    parts = [to_chip(s, k + 1) for k, s in enumerate(sends)]
    *sends, own = call(
        functools.partial(split_kernel, unit, chips - 1),
        tuple([bf16(unit, 128)] * (wire - 1) + [f32(unit, 128)]),
        1,
        chips,
        [pltpu.VMEM((chunk, 128), jnp.float32)],
    )(place, own, *parts)
    summed = own
    for k, s in enumerate(sends):
        summed = summed + to_wire(s, k + 1).astype(jnp.float32)
    summed = (summed / math.sqrt(float(drift * wire * slots))).astype(jnp.bfloat16)
    pieces = [summed] + [to_wire(summed, k) for k in range(1, wire)]
    mine = call(
        functools.partial(joined_kernel, unit), bf16(chunk, 128), 1, wire, [pltpu.VMEM((chunk, 128), jnp.float32)]
    )(place, *pieces)
    mine = [mine] + [to_chip(mine, k) for k in range(1, chips)]
    theirs = [swap_core(m) for m in mine]
    grad_first, grad_second = call(
        functools.partial(final_kernel, chunk, chips),
        (f32(27, 128, 128), f32(27, 128, 128)),
        1,
        2 * chips,
        [pltpu.VMEM((2, chunk * chips, 128), jnp.float32)],
    )(place, *mine, *theirs)

    hb_full, hb_low, hb_high = halo(hb, hb_low, hb_high)
    output, grad_features = call(
        second_kernel, (bf16(slots, 128), bf16(slots, 128)), 1, 7, [window]
    )(geo, hb_full, hb_low, hb_high, full, live, w2, w1f)
    return output[None, None], grad_features[None, None], grad_first, grad_second


def solution(mesh):
    placed = (
        P("drift", "wire", None, None),
        P(),
        P(),
        P("drift", "wire", None, None),
        P("drift", "wire"),
        P("drift", "wire", None, None),
        P("drift", "wire", None),
    )
    return jax.shard_map(
        on_device,
        mesh=mesh,
        in_specs=placed,
        out_specs=(P("drift", "wire", None, None), P("drift", "wire", None, None), P(), P()),
        check_vma=False,
    )
```

profile of v0, /device:TPU:13, one launch (start us, length us, event | category | flops | bytes accessed | tf_op | source)
XLA Modules:
  0.0 105.1 jit_solution(16325946961632716587)
XLA Ops:
  4.6 3.2 %collective-permute-start = (bf16[48,256]{1,0:T(8,128)(2,1)S(1)}, bf16[48,256]{1,0:T(8,128)(2,1)S(1)}, u32[]{:S(2)}, u32[]{:S(2)}) collective-permute-start(bf16[48,256]{1,0:T(8,128)(2,1)S(1)} %get-tuple-element.32), channel_id=1, source_target_pairs={{0,1},{1,2},{2,3},{4,5},{5,6},{6,7},{8,9},{9,10},{10,11},{12,13},{... | collective-permute-start | bytes 73736 | tf_op jit(solution)/shard_map/ppermute | solution.py:278
  7.9 2.2 %collective-permute-start.1 = (bf16[48,256]{1,0:T(8,128)(2,1)S(1)}, bf16[48,256]{1,0:T(8,128)(2,1)S(1)}, u32[]{:S(2)}, u32[]{:S(2)}) collective-permute-start(bf16[48,256]{1,0:T(8,128)(2,1)S(1)} %get-tuple-element.33), channel_id=1, source_target_pairs={{1,0},{2,1},{3,2},{5,4},{6,5},{7,6},{9,8},{10,9},{11,10},{13,12},{... | collective-permute-start | bytes 73736 | tf_op jit(solution)/shard_map/ppermute | solution.py:278
  10.1 1.2 %reverse_bitcast_fusion.1 = bf16[27,128,128]{1,2,0:T(8,128)(2,1)S(1)} fusion(bf16[27,128,128]{2,1,0:T(8,128)(2,1)} %param.9), kind=kLoop, calls=%fused_computation.1 | loop fusion | bytes 1769472 | tf_op jit(solution)/shard_map/transpose | solution.py:294
  12.8 5.1 %collective-permute-start.2 = (bf16[64,256]{1,0:T(8,128)(2,1)S(1)}, bf16[64,256]{1,0:T(8,128)(2,1)S(1)}, u32[]{:S(2)}, u32[]{:S(2)}) collective-permute-start(bf16[64,256]{1,0:T(8,128)(2,1)S(1)} %get-tuple-element.35), channel_id=1, source_target_pairs={{0,4},{4,8},{8,12},{12,16},{16,20},{20,24},{24,28},{1,5},{5,9},{9,... | collective-permute-start | bytes 98312 | tf_op jit(solution)/shard_map/ppermute | solution.py:278
  17.9 1.9 %collective-permute-start.3 = (bf16[64,256]{1,0:T(8,128)(2,1)S(1)}, bf16[64,256]{1,0:T(8,128)(2,1)S(1)}, u32[]{:S(2)}, u32[]{:S(2)}) collective-permute-start(bf16[64,256]{1,0:T(8,128)(2,1)S(1)} %get-tuple-element.36), channel_id=1, source_target_pairs={{4,0},{8,4},{12,8},{16,12},{20,16},{24,20},{28,24},{5,1},{9,5},{13... | collective-permute-start | bytes 98312 | tf_op jit(solution)/shard_map/ppermute | solution.py:278
  19.9 1.3 %copy.10 = bf16[27,128,128]{2,1,0:T(8,128)(2,1)S(1)} copy(bf16[27,128,128]{1,2,0:T(8,128)(2,1)S(1)} %reverse_bitcast_fusion.1) | data formatting | bytes 1769472 | tf_op jit(solution)/shard_map/transpose | solution.py:294
  21.3 1.9 %collective-permute-done.3.high = bf16[64,256]{1,0:T(8,128)(2,1)S(1)} collective-permute-done((bf16[64,256]{1,0:T(8,128)(2,1)S(1)}, bf16[64,256]{1,0:T(8,128)(2,1)S(1)}, u32[]{:S(2)}, u32[]{:S(2)}) %collective-permute-start.3) | collective-permute-done | bytes 32800 | tf_op jit(solution)/shard_map/ppermute | solution.py:278
  23.2 4.0 %shard_map.96 = (bf16[768,256]{1,0:T(8,128)(2,1)S(1)}, bf16[48,256]{1,0:T(8,128)(2,1)S(1)}, bf16[48,256]{1,0:T(8,128)(2,1)S(1)}, bf16[1664,128]{1,0:T(8,128)(2,1)S(1)}, bf16[1664,128]{1,0:T(8,128)(2,1)S(1)}) custom-call(s32[3]{0:T(128)S(1)} %pad_add_fusion.1.place, bf16[768,256]{1,0:T(8,128)(2,1)S(1)} %get-tuple-element.34.full.base, ...), custom_call_target="tpu_custom_call" | custom-call | tf_op jit(solution)/shard_map/pallas_call | solution.py:316
  27.2 1.8 %collective-permute-done.8.theirs = bf16[1664,128]{1,0:T(8,128)(2,1)S(1)} collective-permute-done((bf16[1664,128]{1,0:T(8,128)(2,1)S(1)}, bf16[1664,128]{1,0:T(8,128)(2,1)S(1)}, u32[]{:S(2)}, u32[]{:S(2)}) %collective-permute-start.8) | collective-permute-done | bytes 426016 | tf_op jit(solution)/shard_map/ppermute | solution.py:325
  29.0 2.7 %shard_map.99 = (bf16[864,128]{1,0:T(8,128)(2,1)S(1)}, bf16[864,128]{1,0:T(8,128)(2,1)S(1)}, bf16[864,128]{1,0:T(8,128)(2,1)S(1)}, f32[864,128]{1,0:T(8,128)S(1)}) custom-call(s32[3]{0:T(128)S(1)} %pad_add_fusion.1.place, bf16[1664,128]{1,0:T(8,128)(2,1)S(1)} %get-tuple-element.46.mine, bf16[1664,128]{1,0:T(8,128)(2,1)S(1)} %collective-permute-done.8.theirs), custom_call_target="tpu_custom_call" | custom-call | tf_op jit(solution)/shard_map/pallas_call | solution.py:334
  31.8 2.3 %collective-permute-start.10 = (bf16[864,128]{1,0:T(8,128)(2,1)S(1)}, bf16[864,128]{1,0:T(8,128)(2,1)S(1)}, u32[]{:S(2)}, u32[]{:S(2)}) collective-permute-start(bf16[864,128]{1,0:T(8,128)(2,1)S(1)} %get-tuple-element.50), channel_id=1, source_target_pairs={{0,16},{4,20},{8,24},{12,28},{16,0},{20,4},{24,8},{28,12},{1,17},{... | collective-permute-start | bytes 663560 | tf_op jit(solution)/shard_map/ppermute | solution.py:328
  34.4 4.2 %collective-permute-done.9.refs_0_ = bf16[864,128]{1,0:T(8,128)(2,1)S(1)} collective-permute-done((bf16[864,128]{1,0:T(8,128)(2,1)S(1)}, bf16[864,128]{1,0:T(8,128)(2,1)S(1)}, u32[]{:S(2)}, u32[]{:S(2)}) %collective-permute-start.9) | collective-permute-done | bytes 221216 | tf_op jit(solution)/shard_map/ppermute | solution.py:328
  39.6 4.7 %collective-permute-done.11.refs_2_ = bf16[864,128]{1,0:T(8,128)(2,1)S(1)} collective-permute-done((bf16[864,128]{1,0:T(8,128)(2,1)S(1)}, bf16[864,128]{1,0:T(8,128)(2,1)S(1)}, u32[]{:S(2)}, u32[]{:S(2)}) %collective-permute-start.11) | collective-permute-done | bytes 221216 | tf_op jit(solution)/shard_map/ppermute | solution.py:328
  45.2 2.3 %collective-permute-start.13 = (bf16[216,128]{1,0:T(8,128)(2,1)S(1)}, bf16[216,128]{1,0:T(8,128)(2,1)S(1)}, u32[]{:S(2)}, u32[]{:S(2)}) collective-permute-start(bf16[216,128]{1,0:T(8,128)(2,1)S(1)} %get-tuple-element.54), channel_id=1, source_target_pairs={{0,2},{1,3},{2,0},{3,1},{4,6},{5,7},{6,4},{7,5},{8,10},{9,11},{10,... | collective-permute-start | bytes 165896 | tf_op jit(solution)/shard_map/ppermute | solution.py:331
  48.1 1.7 %collective-permute-done.13 = bf16[216,128]{1,0:T(8,128)(2,1)S(1)} collective-permute-done((bf16[216,128]{1,0:T(8,128)(2,1)S(1)}, bf16[216,128]{1,0:T(8,128)(2,1)S(1)}, u32[]{:S(2)}, u32[]{:S(2)}) %collective-permute-start.13) | collective-permute-done | bytes 55328 | tf_op jit(solution)/shard_map/ppermute | solution.py:331
  49.8 2.2 %collective-permute-done.14 = bf16[216,128]{1,0:T(8,128)(2,1)S(1)} collective-permute-done((bf16[216,128]{1,0:T(8,128)(2,1)S(1)}, bf16[216,128]{1,0:T(8,128)(2,1)S(1)}, u32[]{:S(2)}, u32[]{:S(2)}) %collective-permute-start.14) | collective-permute-done | bytes 55328 | tf_op jit(solution)/shard_map/ppermute | solution.py:331
  52.0 2.0 %collective-permute-start.17 = (bf16[216,128]{1,0:T(8,128)(2,1)S(1)}, bf16[216,128]{1,0:T(8,128)(2,1)S(1)}, u32[]{:S(2)}, u32[]{:S(2)}) collective-permute-start(bf16[216,128]{1,0:T(8,128)(2,1)S(1)} %multiply_convert_fusion.refs_0_), channel_id=1, source_target_pairs={{0,3},{1,2},{2,1},{3,0},{4,7},{5,6},{6,5},{7,4},{8,11},{9,10},{10,... | collective-permute-start | bytes 165896 | tf_op jit(solution)/shard_map/ppermute | solution.py:331
  54.0 1.1 %collective-permute-start.16 = (bf16[216,128]{1,0:T(8,128)(2,1)S(1)}, bf16[216,128]{1,0:T(8,128)(2,1)S(1)}, u32[]{:S(2)}, u32[]{:S(2)}) collective-permute-start(bf16[216,128]{1,0:T(8,128)(2,1)S(1)} %multiply_convert_fusion.refs_0_), channel_id=1, source_target_pairs={{0,2},{1,3},{2,0},{3,1},{4,6},{5,7},{6,4},{7,5},{8,10},{9,11},{10,... | collective-permute-start | bytes 165896 | tf_op jit(solution)/shard_map/ppermute | solution.py:331
  55.6 2.5 %collective-permute-done.16.refs_2_ = bf16[216,128]{1,0:T(8,128)(2,1)S(1)} collective-permute-done((bf16[216,128]{1,0:T(8,128)(2,1)S(1)}, bf16[216,128]{1,0:T(8,128)(2,1)S(1)}, u32[]{:S(2)}, u32[]{:S(2)}) %collective-permute-start.16) | collective-permute-done | bytes 55328 | tf_op jit(solution)/shard_map/ppermute | solution.py:331
  59.1 1.3 %collective-permute-start.20 = (bf16[864,128]{1,0:T(8,128)(2,1)S(1)}, bf16[864,128]{1,0:T(8,128)(2,1)S(1)}, u32[]{:S(2)}, u32[]{:S(2)}) collective-permute-start(bf16[864,128]{1,0:T(8,128)(2,1)S(1)} %shard_map.101.refs_0_), channel_id=1, source_target_pairs={{0,24},{4,28},{8,16},{12,20},{16,8},{20,12},{24,0},{28,4},{1,25},{... | collective-permute-start | bytes 663560 | tf_op jit(solution)/shard_map/ppermute | solution.py:328
  61.8 4.6 %collective-permute-start.21 = (bf16[864,128]{1,0:T(8,128)(2,1)S(1)}, bf16[864,128]{1,0:T(8,128)(2,1)}, u32[]{:S(2)}, u32[]{:S(2)}) collective-permute-start(bf16[864,128]{1,0:T(8,128)(2,1)S(1)} %shard_map.101.refs_0_), channel_id=1, source_target_pairs={{0,4},{4,0},{8,12},{12,8},{16,20},{20,16},{24,28},{28,24},{1,5},{5... | collective-permute-start | bytes 663560 | tf_op jit(solution)/shard_map/ppermute | solution.py:325
  66.4 3.9 %collective-permute-start.24 = (bf16[864,128]{1,0:T(8,128)(2,1)S(1)}, bf16[864,128]{1,0:T(8,128)(2,1)}, u32[]{:S(2)}, u32[]{:S(2)}) collective-permute-start(bf16[864,128]{1,0:T(8,128)(2,1)S(1)} %collective-permute-done.20.refs_3_), channel_id=1, source_target_pairs={{0,4},{4,0},{8,12},{12,8},{16,20},{20,16},{24,28},{28,24},{1,5},{5... | collective-permute-start | bytes 663560 | tf_op jit(solution)/shard_map/ppermute | solution.py:325
  70.4 2.2 %collective-permute-start.23 = (bf16[864,128]{1,0:T(8,128)(2,1)S(1)}, bf16[864,128]{1,0:T(8,128)(2,1)}, u32[]{:S(2)}, u32[]{:S(2)}) collective-permute-start(bf16[864,128]{1,0:T(8,128)(2,1)S(1)} %collective-permute-done.19.refs_2_), channel_id=1, source_target_pairs={{0,4},{4,0},{8,12},{12,8},{16,20},{20,16},{24,28},{28,24},{1,5},{5... | collective-permute-start | bytes 663560 | tf_op jit(solution)/shard_map/ppermute | solution.py:325
  73.1 2.0 %collective-permute-start.4 = (bf16[48,256]{1,0:T(8,128)(2,1)S(1)}, bf16[48,256]{1,0:T(8,128)(2,1)S(1)}, u32[]{:S(2)}, u32[]{:S(2)}) collective-permute-start(bf16[48,256]{1,0:T(8,128)(2,1)S(1)} %get-tuple-element.39), channel_id=1, source_target_pairs={{0,1},{1,2},{2,3},{4,5},{5,6},{6,7},{8,9},{9,10},{10,11},{12,13},{... | collective-permute-start | bytes 73736 | tf_op jit(solution)/shard_map/ppermute | solution.py:278
  75.2 2.5 %collective-permute-done.4.from_low = bf16[48,256]{1,0:T(8,128)(2,1)S(1)} collective-permute-done((bf16[48,256]{1,0:T(8,128)(2,1)S(1)}, bf16[48,256]{1,0:T(8,128)(2,1)S(1)}, u32[]{:S(2)}, u32[]{:S(2)}) %collective-permute-start.4) | collective-permute-done | bytes 24608 | tf_op jit(solution)/shard_map/ppermute | solution.py:278
  77.7 1.9 %collective-permute-start.5 = (bf16[48,256]{1,0:T(8,128)(2,1)S(1)}, bf16[48,256]{1,0:T(8,128)(2,1)S(1)}, u32[]{:S(2)}, u32[]{:S(2)}) collective-permute-start(bf16[48,256]{1,0:T(8,128)(2,1)S(1)} %get-tuple-element.40), channel_id=1, source_target_pairs={{1,0},{2,1},{3,2},{5,4},{6,5},{7,6},{9,8},{10,9},{11,10},{13,12},{... | collective-permute-start | bytes 73736 | tf_op jit(solution)/shard_map/ppermute | solution.py:278
  79.6 2.6 %collective-permute-done.5.from_high = bf16[48,256]{1,0:T(8,128)(2,1)S(1)} collective-permute-done((bf16[48,256]{1,0:T(8,128)(2,1)S(1)}, bf16[48,256]{1,0:T(8,128)(2,1)S(1)}, u32[]{:S(2)}, u32[]{:S(2)}) %collective-permute-start.5) | collective-permute-done | bytes 24608 | tf_op jit(solution)/shard_map/ppermute | solution.py:278
  82.5 5.3 %collective-permute-start.6 = (bf16[64,256]{1,0:T(8,128)(2,1)S(1)}, bf16[64,256]{1,0:T(8,128)(2,1)S(1)}, u32[]{:S(2)}, u32[]{:S(2)}) collective-permute-start(bf16[64,256]{1,0:T(8,128)(2,1)S(1)} %get-tuple-element.42), channel_id=1, source_target_pairs={{0,4},{4,8},{8,12},{12,16},{16,20},{20,24},{24,28},{1,5},{5,9},{9,... | collective-permute-start | bytes 98312 | tf_op jit(solution)/shard_map/ppermute | solution.py:278
  88.8 4.4 %collective-permute-start.7 = (bf16[64,256]{1,0:T(8,128)(2,1)S(1)}, bf16[64,256]{1,0:T(8,128)(2,1)S(1)}, u32[]{:S(2)}, u32[]{:S(2)}) collective-permute-start(bf16[64,256]{1,0:T(8,128)(2,1)S(1)} %get-tuple-element.43), channel_id=1, source_target_pairs={{4,0},{8,4},{12,8},{16,12},{20,16},{24,20},{28,24},{5,1},{9,5},{13... | collective-permute-start | bytes 98312 | tf_op jit(solution)/shard_map/ppermute | solution.py:278
  94.1 1.9 %copy.11 = bf16[27,128,128]{2,1,0:T(8,128)(2,1)S(1)} copy(bf16[27,128,128]{1,2,0:T(8,128)(2,1)} %reverse_bitcast_fusion) | data formatting | bytes 1769472 | tf_op jit(solution)/shard_map/transpose | solution.py:293
  96.0 5.1 %shard_map.98 = (bf16[576,128]{1,0:T(8,128)(2,1)}, bf16[576,128]{1,0:T(8,128)(2,1)}) custom-call(s32[17]{0:T(128)S(1)} %pad_add_fusion.geo, bf16[768,256]{1,0:T(8,128)(2,1)S(1)} %get-tuple-element.41.hb, bf16[64,256]{1,0:T(8,128)(2,1)S(1)} %collective-permute-done.6.low, bf16[64,256]{1,0:T(8,128)(2,1)S(1)} %collective-permute-done.7.high, ...), custom_call_target="tpu_custom_call" | custom-call | tf_op jit(solution)/shard_map/pallas_call | solution.py:368
  101.2 3.9 %shard_map.102 = (f32[27,128,128]{2,1,0:T(8,128)}, f32[27,128,128]{2,1,0:T(8,128)}) custom-call(s32[3]{0:T(128)S(1)} %pad_add_fusion.1.place, bf16[864,128]{1,0:T(8,128)(2,1)S(1)} %shard_map.101.refs_0_, bf16[864,128]{1,0:T(8,128)(2,1)} %collective-permute-done.18.refs_1_, bf16[864,128]{1,0:T(8,128)(2,1)S(1)} %collective-permute-done.19.refs_2_, ...), custom_call_target="tpu_custom_call" | custom-call | tf_op jit(solution)/shard_map/pallas_call | solution.py:359
  (47 shorter events, 13.4 us)
Async XLA Ops:
  2.0 0.9 copy-start.2
  2.9 0.9 copy-start.4
  3.8 7.5 %copy-start.3 = (bf16[1,1,576,128]{3,2,1,0:T(8,128)(2,1)S(1)}, bf16[1,1,576,128]{3,2,1,0:T(8,128)(2,1)}, u32[]{:S(2)}) copy-start(bf16[1,1,576,128]{3,2,1,0:T(8,128)(2,1)} %param.7) | copy-start | bytes 442372
  3.8 7.5 %copy-start.5 = (bf16[1,1,576,128]{3,2,1,0:T(8,128)(2,1)S(1)}, bf16[1,1,576,128]{3,2,1,0:T(8,128)(2,1)}, u32[]{:S(2)}) copy-start(bf16[1,1,576,128]{3,2,1,0:T(8,128)(2,1)} %param.10) | copy-start | bytes 442372
  4.6 7.8 %collective-permute-start = (bf16[48,256]{1,0:T(8,128)(2,1)S(1)}, bf16[48,256]{1,0:T(8,128)(2,1)S(1)}, u32[]{:S(2)}, u32[]{:S(2)}) collective-permute-start(bf16[48,256]{1,0:T(8,128)(2,1)S(1)} %get-tuple-element.32), channel_id=1, source_target_pairs={{0,1},{1,2},{2,3},{4,5},{5,6},{6,7},{8,9},{9,10},{10,11},{12,13},{... | collective-permute-start | bytes 73736 | tf_op jit(solution)/shard_map/ppermute | solution.py:278
  7.8 15.3 %copy-start.1 = (bf16[27,128,128]{2,1,0:T(8,128)(2,1)S(1)}, bf16[27,128,128]{2,1,0:T(8,128)(2,1)}, u32[]{:S(2)}) copy-start(bf16[27,128,128]{2,1,0:T(8,128)(2,1)} %param.8) | copy-start | bytes 2654212
  7.9 4.7 %collective-permute-start.1 = (bf16[48,256]{1,0:T(8,128)(2,1)S(1)}, bf16[48,256]{1,0:T(8,128)(2,1)S(1)}, u32[]{:S(2)}, u32[]{:S(2)}) collective-permute-start(bf16[48,256]{1,0:T(8,128)(2,1)S(1)} %get-tuple-element.33), channel_id=1, source_target_pairs={{1,0},{2,1},{3,2},{5,4},{6,5},{7,6},{9,8},{10,9},{11,10},{13,12},{... | collective-permute-start | bytes 73736 | tf_op jit(solution)/shard_map/ppermute | solution.py:278
  12.8 8.4 %collective-permute-start.2 = (bf16[64,256]{1,0:T(8,128)(2,1)S(1)}, bf16[64,256]{1,0:T(8,128)(2,1)S(1)}, u32[]{:S(2)}, u32[]{:S(2)}) collective-permute-start(bf16[64,256]{1,0:T(8,128)(2,1)S(1)} %get-tuple-element.35), channel_id=1, source_target_pairs={{0,4},{4,8},{8,12},{12,16},{16,20},{20,24},{24,28},{1,5},{5,9},{9,... | collective-permute-start | bytes 98312 | tf_op jit(solution)/shard_map/ppermute | solution.py:278
  17.9 5.2 %collective-permute-start.3 = (bf16[64,256]{1,0:T(8,128)(2,1)S(1)}, bf16[64,256]{1,0:T(8,128)(2,1)S(1)}, u32[]{:S(2)}, u32[]{:S(2)}) collective-permute-start(bf16[64,256]{1,0:T(8,128)(2,1)S(1)} %get-tuple-element.36), channel_id=1, source_target_pairs={{4,0},{8,4},{12,8},{16,12},{20,16},{24,20},{28,24},{5,1},{9,5},{13... | collective-permute-start | bytes 98312 | tf_op jit(solution)/shard_map/ppermute | solution.py:278
  27.2 1.8 %collective-permute-start.8 = (bf16[1664,128]{1,0:T(8,128)(2,1)S(1)}, bf16[1664,128]{1,0:T(8,128)(2,1)S(1)}, u32[]{:S(2)}, u32[]{:S(2)}) collective-permute-start(bf16[1664,128]{1,0:T(8,128)(2,1)S(1)} %get-tuple-element.47), channel_id=1, source_target_pairs={{0,4},{4,0},{8,12},{12,8},{16,20},{20,16},{24,28},{28,24},{1,5},{5... | collective-permute-start | bytes 1277960 | tf_op jit(solution)/shard_map/ppermute | solution.py:325
  31.7 7.0 %collective-permute-start.9 = (bf16[864,128]{1,0:T(8,128)(2,1)S(1)}, bf16[864,128]{1,0:T(8,128)(2,1)S(1)}, u32[]{:S(2)}, u32[]{:S(2)}) collective-permute-start(bf16[864,128]{1,0:T(8,128)(2,1)S(1)} %get-tuple-element.49), channel_id=1, source_target_pairs={{0,8},{4,12},{8,0},{12,4},{16,24},{20,28},{24,16},{28,20},{1,9},{5... | collective-permute-start | bytes 663560 | tf_op jit(solution)/shard_map/ppermute | solution.py:328
  31.8 7.8 %collective-permute-start.10 = (bf16[864,128]{1,0:T(8,128)(2,1)S(1)}, bf16[864,128]{1,0:T(8,128)(2,1)S(1)}, u32[]{:S(2)}, u32[]{:S(2)}) collective-permute-start(bf16[864,128]{1,0:T(8,128)(2,1)S(1)} %get-tuple-element.50), channel_id=1, source_target_pairs={{0,16},{4,20},{8,24},{12,28},{16,0},{20,4},{24,8},{28,12},{1,17},{... | collective-permute-start | bytes 663560 | tf_op jit(solution)/shard_map/ppermute | solution.py:328
  34.1 10.2 %collective-permute-start.11 = (bf16[864,128]{1,0:T(8,128)(2,1)S(1)}, bf16[864,128]{1,0:T(8,128)(2,1)S(1)}, u32[]{:S(2)}, u32[]{:S(2)}) collective-permute-start(bf16[864,128]{1,0:T(8,128)(2,1)S(1)} %get-tuple-element.51), channel_id=1, source_target_pairs={{0,24},{4,28},{8,16},{12,20},{16,8},{20,12},{24,0},{28,4},{1,25},{... | collective-permute-start | bytes 663560 | tf_op jit(solution)/shard_map/ppermute | solution.py:328
  45.0 3.1 %collective-permute-start.12 = (bf16[216,128]{1,0:T(8,128)(2,1)S(1)}, bf16[216,128]{1,0:T(8,128)(2,1)S(1)}, u32[]{:S(2)}, u32[]{:S(2)}) collective-permute-start(bf16[216,128]{1,0:T(8,128)(2,1)S(1)} %get-tuple-element.53), channel_id=1, source_target_pairs={{0,1},{1,0},{2,3},{3,2},{4,5},{5,4},{6,7},{7,6},{8,9},{9,8},{10,11... | collective-permute-start | bytes 165896 | tf_op jit(solution)/shard_map/ppermute | solution.py:331
  45.2 4.5 %collective-permute-start.13 = (bf16[216,128]{1,0:T(8,128)(2,1)S(1)}, bf16[216,128]{1,0:T(8,128)(2,1)S(1)}, u32[]{:S(2)}, u32[]{:S(2)}) collective-permute-start(bf16[216,128]{1,0:T(8,128)(2,1)S(1)} %get-tuple-element.54), channel_id=1, source_target_pairs={{0,2},{1,3},{2,0},{3,1},{4,6},{5,7},{6,4},{7,5},{8,10},{9,11},{10,... | collective-permute-start | bytes 165896 | tf_op jit(solution)/shard_map/ppermute | solution.py:331
  47.5 4.5 %collective-permute-start.14 = (bf16[216,128]{1,0:T(8,128)(2,1)S(1)}, bf16[216,128]{1,0:T(8,128)(2,1)S(1)}, u32[]{:S(2)}, u32[]{:S(2)}) collective-permute-start(bf16[216,128]{1,0:T(8,128)(2,1)S(1)} %get-tuple-element.55), channel_id=1, source_target_pairs={{0,3},{1,2},{2,1},{3,0},{4,7},{5,6},{6,5},{7,4},{8,11},{9,10},{10,... | collective-permute-start | bytes 165896 | tf_op jit(solution)/shard_map/ppermute | solution.py:331
  52.0 3.5 %collective-permute-start.17 = (bf16[216,128]{1,0:T(8,128)(2,1)S(1)}, bf16[216,128]{1,0:T(8,128)(2,1)S(1)}, u32[]{:S(2)}, u32[]{:S(2)}) collective-permute-start(bf16[216,128]{1,0:T(8,128)(2,1)S(1)} %multiply_convert_fusion.refs_0_), channel_id=1, source_target_pairs={{0,3},{1,2},{2,1},{3,0},{4,7},{5,6},{6,5},{7,4},{8,11},{9,10},{10,... | collective-permute-start | bytes 165896 | tf_op jit(solution)/shard_map/ppermute | solution.py:331
  54.0 4.0 %collective-permute-start.16 = (bf16[216,128]{1,0:T(8,128)(2,1)S(1)}, bf16[216,128]{1,0:T(8,128)(2,1)S(1)}, u32[]{:S(2)}, u32[]{:S(2)}) collective-permute-start(bf16[216,128]{1,0:T(8,128)(2,1)S(1)} %multiply_convert_fusion.refs_0_), channel_id=1, source_target_pairs={{0,2},{1,3},{2,0},{3,1},{4,6},{5,7},{6,4},{7,5},{8,10},{9,11},{10,... | collective-permute-start | bytes 165896 | tf_op jit(solution)/shard_map/ppermute | solution.py:331
  55.1 3.3 %collective-permute-start.15 = (bf16[216,128]{1,0:T(8,128)(2,1)S(1)}, bf16[216,128]{1,0:T(8,128)(2,1)S(1)}, u32[]{:S(2)}, u32[]{:S(2)}) collective-permute-start(bf16[216,128]{1,0:T(8,128)(2,1)S(1)} %multiply_convert_fusion.refs_0_), channel_id=1, source_target_pairs={{0,1},{1,0},{2,3},{3,2},{4,5},{5,4},{6,7},{7,6},{8,9},{9,8},{10,11... | collective-permute-start | bytes 165896 | tf_op jit(solution)/shard_map/ppermute | solution.py:331
  59.1 7.4 %collective-permute-start.20 = (bf16[864,128]{1,0:T(8,128)(2,1)S(1)}, bf16[864,128]{1,0:T(8,128)(2,1)S(1)}, u32[]{:S(2)}, u32[]{:S(2)}) collective-permute-start(bf16[864,128]{1,0:T(8,128)(2,1)S(1)} %shard_map.101.refs_0_), channel_id=1, source_target_pairs={{0,24},{4,28},{8,16},{12,20},{16,8},{20,12},{24,0},{28,4},{1,25},{... | collective-permute-start | bytes 663560 | tf_op jit(solution)/shard_map/ppermute | solution.py:328
  60.4 10.0 %collective-permute-start.19 = (bf16[864,128]{1,0:T(8,128)(2,1)S(1)}, bf16[864,128]{1,0:T(8,128)(2,1)S(1)}, u32[]{:S(2)}, u32[]{:S(2)}) collective-permute-start(bf16[864,128]{1,0:T(8,128)(2,1)S(1)} %shard_map.101.refs_0_), channel_id=1, source_target_pairs={{0,16},{4,20},{8,24},{12,28},{16,0},{20,4},{24,8},{28,12},{1,17},{... | collective-permute-start | bytes 663560 | tf_op jit(solution)/shard_map/ppermute | solution.py:328
  61.5 11.1 %collective-permute-start.18 = (bf16[864,128]{1,0:T(8,128)(2,1)S(1)}, bf16[864,128]{1,0:T(8,128)(2,1)}, u32[]{:S(2)}, u32[]{:S(2)}) collective-permute-start(bf16[864,128]{1,0:T(8,128)(2,1)S(1)} %shard_map.101.refs_0_), channel_id=1, source_target_pairs={{0,8},{4,12},{8,0},{12,4},{16,24},{20,28},{24,16},{28,20},{1,9},{5... | collective-permute-start | bytes 663560 | tf_op jit(solution)/shard_map/ppermute | solution.py:328
  61.8 39.3 %collective-permute-start.21 = (bf16[864,128]{1,0:T(8,128)(2,1)S(1)}, bf16[864,128]{1,0:T(8,128)(2,1)}, u32[]{:S(2)}, u32[]{:S(2)}) collective-permute-start(bf16[864,128]{1,0:T(8,128)(2,1)S(1)} %shard_map.101.refs_0_), channel_id=1, source_target_pairs={{0,4},{4,0},{8,12},{12,8},{16,20},{20,16},{24,28},{28,24},{1,5},{5... | collective-permute-start | bytes 663560 | tf_op jit(solution)/shard_map/ppermute | solution.py:325
  66.4 34.7 %collective-permute-start.24 = (bf16[864,128]{1,0:T(8,128)(2,1)S(1)}, bf16[864,128]{1,0:T(8,128)(2,1)}, u32[]{:S(2)}, u32[]{:S(2)}) collective-permute-start(bf16[864,128]{1,0:T(8,128)(2,1)S(1)} %collective-permute-done.20.refs_3_), channel_id=1, source_target_pairs={{0,4},{4,0},{8,12},{12,8},{16,20},{20,16},{24,28},{28,24},{1,5},{5... | collective-permute-start | bytes 663560 | tf_op jit(solution)/shard_map/ppermute | solution.py:325
  70.4 30.8 %collective-permute-start.23 = (bf16[864,128]{1,0:T(8,128)(2,1)S(1)}, bf16[864,128]{1,0:T(8,128)(2,1)}, u32[]{:S(2)}, u32[]{:S(2)}) collective-permute-start(bf16[864,128]{1,0:T(8,128)(2,1)S(1)} %collective-permute-done.19.refs_2_), channel_id=1, source_target_pairs={{0,4},{4,0},{8,12},{12,8},{16,20},{20,16},{24,28},{28,24},{1,5},{5... | collective-permute-start | bytes 663560 | tf_op jit(solution)/shard_map/ppermute | solution.py:325
  72.6 28.5 %collective-permute-start.22 = (bf16[864,128]{1,0:T(8,128)(2,1)}, bf16[864,128]{1,0:T(8,128)(2,1)}, u32[]{:S(2)}, u32[]{:S(2)}) collective-permute-start(bf16[864,128]{1,0:T(8,128)(2,1)} %collective-permute-done.18.refs_1_), channel_id=1, source_target_pairs={{0,4},{4,0},{8,12},{12,8},{16,20},{20,16},{24,28},{28,24},{1,5},{5... | collective-permute-start | bytes 663560 | tf_op jit(solution)/shard_map/ppermute | solution.py:325
  73.1 4.6 %collective-permute-start.4 = (bf16[48,256]{1,0:T(8,128)(2,1)S(1)}, bf16[48,256]{1,0:T(8,128)(2,1)S(1)}, u32[]{:S(2)}, u32[]{:S(2)}) collective-permute-start(bf16[48,256]{1,0:T(8,128)(2,1)S(1)} %get-tuple-element.39), channel_id=1, source_target_pairs={{0,1},{1,2},{2,3},{4,5},{5,6},{6,7},{8,9},{9,10},{10,11},{12,13},{... | collective-permute-start | bytes 73736 | tf_op jit(solution)/shard_map/ppermute | solution.py:278
  77.7 4.6 %collective-permute-start.5 = (bf16[48,256]{1,0:T(8,128)(2,1)S(1)}, bf16[48,256]{1,0:T(8,128)(2,1)S(1)}, u32[]{:S(2)}, u32[]{:S(2)}) collective-permute-start(bf16[48,256]{1,0:T(8,128)(2,1)S(1)} %get-tuple-element.40), channel_id=1, source_target_pairs={{1,0},{2,1},{3,2},{5,4},{6,5},{7,6},{9,8},{10,9},{11,10},{13,12},{... | collective-permute-start | bytes 73736 | tf_op jit(solution)/shard_map/ppermute | solution.py:278
  82.5 6.3 %collective-permute-start.6 = (bf16[64,256]{1,0:T(8,128)(2,1)S(1)}, bf16[64,256]{1,0:T(8,128)(2,1)S(1)}, u32[]{:S(2)}, u32[]{:S(2)}) collective-permute-start(bf16[64,256]{1,0:T(8,128)(2,1)S(1)} %get-tuple-element.42), channel_id=1, source_target_pairs={{0,4},{4,8},{8,12},{12,16},{16,20},{20,24},{24,28},{1,5},{5,9},{9,... | collective-permute-start | bytes 98312 | tf_op jit(solution)/shard_map/ppermute | solution.py:278
  88.8 7.3 %copy-start = (bf16[27,128,128]{2,1,0:T(8,128)(2,1)S(1)}, bf16[27,128,128]{2,1,0:T(8,128)(2,1)}, u32[]{:S(2)}) copy-start(bf16[27,128,128]{2,1,0:T(8,128)(2,1)} %param.9) | copy-start | bytes 2654212
  88.8 7.3 %collective-permute-start.7 = (bf16[64,256]{1,0:T(8,128)(2,1)S(1)}, bf16[64,256]{1,0:T(8,128)(2,1)S(1)}, u32[]{:S(2)}, u32[]{:S(2)}) collective-permute-start(bf16[64,256]{1,0:T(8,128)(2,1)S(1)} %get-tuple-element.43), channel_id=1, source_target_pairs={{4,0},{8,4},{12,8},{16,12},{20,16},{24,20},{28,24},{5,1},{9,5},{13... | collective-permute-start | bytes 98312 | tf_op jit(solution)/shard_map/ppermute | solution.py:278
where the time goes:
time: 106 us; the launch traced here: 105 us
  starting transfers between devices  48.8 us (46%)
  waiting for transfers between devices  27.3 us (26%)
  Pallas kernels  19.4 us (18%)
  local copies, waits for them, and re-layouts  7.21 us (7%)
  between operations  1.56 us (1%)
    ppermute x8, starting transfers between devices, shift(): lax.ppermute(value, axis, [(i, i + steps) for i in range(count) if 0 <= i...  26 us
    ppermute x5, starting transfers between devices, swap_core(): return lax.ppermute(value, 'drift', [(i, i ^ 1) for i in range(drift)])  11.4 us
    ppermute x6, waiting for transfers between devices, to_chip(): lax.ppermute(value, 'drift', [(i, i ^ 2 * step) for i in range(drift)])  9.87 us
    ppermute x8, waiting for transfers between devices, shift(): lax.ppermute(value, axis, [(i, i + steps) for i in range(count) if 0 <= i...  8.17 us
    ppermute x6, waiting for transfers between devices, to_wire(): return lax.ppermute(value, 'wire', [(i, i ^ step) for i in range(wire)])  7.45 us
    ppermute x6, starting transfers between devices, to_wire(): return lax.ppermute(value, 'wire', [(i, i ^ step) for i in range(wire)])  5.95 us
    ppermute x6, starting transfers between devices, to_chip(): lax.ppermute(value, 'drift', [(i, i ^ 2 * step) for i in range(drift)])  5.47 us
    pallas_call x1, Pallas kernels, on_device(): call(second_kernel, (bf16(slots, 128), bf16(slots, 128)), 1, 7, [window])  5.09 us
  transfers between devices with their start and end apart: 25, of which 15 were waited for; matrix products, arithmetic and copies ran while one was open for 5% of the time, Pallas kernels for 6%

commit v1 on v0

v1 whole, which is shorter than its diff:
```python
import functools
import math

import jax
import jax.numpy as jnp
from jax import lax
from jax.experimental import pallas as pl
from jax.experimental.pallas import tpu as pltpu
from jax.sharding import PartitionSpec as P

BX = 3
BW = 3
NX = 4 * BX
NY = 4 * BW
J = 16
PLANE = NX * J
WIDE = (NX + 2) * J
ROWS = 4 * PLANE
FACE = 4 * NX
SLAB = 4 * J
CHANNELS = 128
TAPS = 27
VMEM = pl.BlockSpec(memory_space=pltpu.VMEM)
HBM = pl.BlockSpec(memory_space=pltpu.HBM)
SMEM = pl.BlockSpec(memory_space=pltpu.SMEM)
LISTED = {0: 0, 1: 1, 2: 2, 3: 7, 5: 10, 6: 3, 7: 4, 8: 5}


def call(kernel, out_shape, in_specs, scratch=(), microseconds=0, out_spec=VMEM, aliases={}, vmem=40):
    return pl.pallas_call(
        kernel,
        out_shape=out_shape,
        in_specs=in_specs,
        out_specs=jax.tree.map(lambda _: out_spec, out_shape),
        scratch_shapes=list(scratch),
        input_output_aliases=aliases,
        compiler_params=pltpu.CompilerParams(vmem_limit_bytes=vmem * 1024 * 1024),
        cost_estimate=pl.CostEstimate(
            flops=0, bytes_accessed=int(microseconds * 3.0e6), transcendentals=0
        ),
    )


def bf16(*shape):
    return jax.ShapeDtypeStruct(shape, jnp.bfloat16)


def f32(*shape):
    return jax.ShapeDtypeStruct(shape, jnp.float32)


def iota(shape, dim):
    return lax.broadcasted_iota(jnp.int32, shape, dim)


def position_slots(lists, counts):
    slots = {p: lists[0, 0, i] for p, i in LISTED.items()}
    present = {p: (s < 9).astype(jnp.int32) for p, s in slots.items()}
    before = present[0] + present[1] + present[2] + present[3]
    others = before + present[5] + present[6] + present[7] + present[8]
    slots[4] = jnp.where(counts[0, 0] > others, before, 9)
    return slots


def slot_rows(slots, z, x, y, valid):
    position = (x >> 2) * BW + (y >> 2)
    slot = jnp.full(position.shape, 9, jnp.int32)
    for p, s in slots.items():
        slot = jnp.where(position == p, s, slot)
    row = slot * 64 + (x & 3) * 16 + (y & 3) * 4 + z
    return jnp.where(valid & (slot < 9), row, -1)


def one_hot(rows, width):
    lane = iota(rows.shape, 1)
    parts = [jnp.where(rows == lane + 128 * c, 1.0, 0.0).astype(jnp.bfloat16) for c in range(width // 128)]
    return jnp.concatenate(parts, axis=1)


def dot(a, b):
    return jnp.dot(a, b, preferred_element_type=jnp.float32)


def grid_indices():
    shape = (4, NX, J, 128)
    z, x, j = (iota(shape, d).reshape(ROWS, 128) for d in range(3))
    return z, x, j


def load_pair(lists, f, g, held_lists, both, sems):
    count = f.shape[0]
    copies = [
        pltpu.make_async_copy(lists, held_lists, sems.at[2]),
        pltpu.make_async_copy(f, both.at[pl.ds(0, count), pl.ds(0, 128)], sems.at[0]),
        pltpu.make_async_copy(g, both.at[pl.ds(0, count), pl.ds(128, 128)], sems.at[1]),
    ]
    for copy in copies:
        copy.start()
    both[count:, :] = jnp.zeros((both.shape[0] - count, 256), jnp.bfloat16)
    copies[0].wait()
    return copies[1:]


def face_indices():
    r = iota((FACE, 128), 0)
    z = (r >= NX).astype(jnp.int32) + (r >= 2 * NX) + (r >= 3 * NX)
    return z, r - NX * z


def write_by_parity(axis, low, high, first, second):
    even = lax.axis_index(axis) % 2 == 0
    first[...] = jnp.where(even, high, low)
    second[...] = jnp.where(even, low, high)


def read_by_parity(axis, first, second):
    me, count = lax.axis_index(axis), lax.axis_size(axis)
    even = me % 2 == 0
    a, b = first[...], second[...]
    nothing = jnp.zeros_like(a)
    low = jnp.where(me > 0, jnp.where(even, b, a), nothing)
    high = jnp.where(me < count - 1, jnp.where(even, a, b), nothing)
    return low, high


def faces_kernel(counts, lists, f, g, first, second, held_lists, both, sems):
    copies = load_pair(lists, f, g, held_lists, both, sems)
    slots = position_slots(held_lists, counts)
    z, x = face_indices()
    picks = [
        one_hot(slot_rows(slots, z, x, jnp.full_like(x, y), x >= 0), both.shape[0]) for y in (0, NY - 1)
    ]
    for copy in copies:
        copy.wait()
    low, high = (dot(pick, both[...]).astype(jnp.bfloat16) for pick in picks)
    write_by_parity("wire", low, high, first, second)


def place_kernel(counts, lists, f, g, out, live, held_lists, both, sems):
    copies = load_pair(lists, f, g, held_lists, both, sems)
    z, x, j = grid_indices()
    rows = slot_rows(position_slots(held_lists, counts), z, x, j - 1, (j >= 1) & (j <= NY))
    live[...] = (rows >= 0).astype(jnp.bfloat16)
    pick = one_hot(rows, both.shape[0])
    for copy in copies:
        copy.wait()
    out[...] = dot(pick, both[...]).astype(jnp.bfloat16)


def insert_faces(placed, got_first, got_second, out, slab_first, slab_second, faces):
    low, high = read_by_parity("wire", got_first, got_second)
    faces[0:FACE, :] = low
    faces[FACE : 2 * FACE, :] = high
    faces[2 * FACE :, :] = jnp.zeros((faces.shape[0] - 2 * FACE, 256), jnp.bfloat16)
    z, x, j = grid_indices()
    rows = z * NX + x
    rows = jnp.where(j == 0, rows, jnp.where(j == NY + 1, rows + FACE, -1))
    full = (placed[...].astype(jnp.float32) + dot(one_hot(rows, 128), faces[...])).astype(jnp.bfloat16)
    out[...] = full
    low = jnp.concatenate([full[z * PLANE : z * PLANE + J, :] for z in range(4)], axis=0)
    high = jnp.concatenate([full[(z + 1) * PLANE - J : (z + 1) * PLANE, :] for z in range(4)], axis=0)
    write_by_parity("drift", low, high, slab_first, slab_second)


def build_window(window, base, plane_of):
    for zi in range(4):
        plane = plane_of(zi)
        wide = plane.astype(jnp.float32)
        before = pltpu.roll(wide, 1, 0).astype(jnp.bfloat16)
        after = pltpu.roll(wide, WIDE - 1, 0).astype(jnp.bfloat16)
        for oy, shifted in enumerate((before, plane, after)):
            for z in range(max(0, zi - 1), min(3, zi + 1) + 1):
                lane = 128 * (3 * oy + zi - z + 1)
                window[base + z, :, lane : lane + 128] = shifted
    empty = jnp.zeros((WIDE, 128), jnp.bfloat16)
    for oy in range(3):
        window[base, :, 384 * oy : 384 * oy + 128] = empty
        window[base + 3, :, 384 * oy + 256 : 384 * oy + 384] = empty


def wide_plane(full, low, high, z, lanes):
    return jnp.concatenate(
        [
            low[z * J : (z + 1) * J, lanes],
            full[z * PLANE : (z + 1) * PLANE, lanes],
            high[z * J : (z + 1) * J, lanes],
        ],
        axis=0,
    )


def conv(window, weight):
    total = None
    for ox in range(3):
        rows = window[:, ox * J : ox * J + PLANE, :].reshape(ROWS, 1152)
        term = dot(rows, weight[9 * ox : 9 * (ox + 1)].reshape(1152, 128))
        total = term if total is None else total + term
    return total


def flip_blocks(weight, flipped):
    for k in range(TAPS):
        flipped[:, 128 * k : 128 * (k + 1)] = weight[TAPS - 1 - k]


def conv_flipped(window, flipped):
    total = None
    for ox in range(3):
        rows = window[:, ox * J : ox * J + PLANE, :].reshape(ROWS, 1152)
        term = lax.dot_general(
            rows,
            flipped[:, 1152 * ox : 1152 * (ox + 1)],
            (((1,), (1,)), ((), ())),
            preferred_element_type=jnp.float32,
        )
        total = term if total is None else total + term
    return total


def first_kernel(full, got_first, got_second, live, w1, w2, hb, keep, send, window, flipped):
    f_lanes, g_lanes = slice(0, 128), slice(128, 256)
    low, high = read_by_parity("drift", got_first, got_second)
    alive = live[...].astype(jnp.float32)
    flip_blocks(w2, flipped)
    build_window(window, 0, lambda z: wide_plane(full, low, high, z, f_lanes))
    first_pre = conv(window, w1)
    gate = jax.nn.sigmoid(first_pre)
    hidden = (alive * (first_pre * gate)).astype(jnp.bfloat16)
    slope = alive * (gate * (1.0 + first_pre * (1.0 - gate)))
    build_window(window, 0, lambda z: wide_plane(full, low, high, z, g_lanes))
    back = (conv_flipped(window, flipped) * slope).astype(jnp.bfloat16)
    hb[...] = jnp.concatenate([hidden, back], axis=1)
    core = lax.axis_index("drift") % 2

    def write(to, values, lanes):
        to[0:ROWS, :] = values
        for z in range(4):
            start = ROWS + z * WIDE
            to[start : start + WIDE, :] = wide_plane(full, low, high, z, lanes)

    @pl.when(core == 0)
    def _():
        write(keep, hidden, g_lanes)
        write(send, back, f_lanes)

    @pl.when(core != 0)
    def _():
        write(keep, back, f_lanes)
        write(send, hidden, g_lanes)


def terms_kernel(chunk, mine, theirs, hb, *refs):
    *sends, own, first, second, window, total = refs
    for base, part in ((0, mine), (4, theirs)):
        build_window(window, base, lambda z: part[ROWS + z * WIDE : ROWS + (z + 1) * WIDE, :])
    left = jnp.concatenate([mine[0:ROWS, :], theirs[0:ROWS, :]], axis=0)
    left = left.astype(jnp.float32).T.astype(jnp.bfloat16)
    rows = TAPS * CHANNELS
    if total.shape[0] > rows:
        total[rows:, :] = jnp.zeros((total.shape[0] - rows, 128), jnp.float32)
    for ox in range(3):
        shifted = window[:, ox * J : ox * J + PLANE, :].reshape(2 * ROWS, 1152)
        product = dot(left, shifted)
        for k in range(9):
            start = 128 * (9 * ox + k)
            total[start : start + 128, :] = product[:, 128 * k : 128 * (k + 1)]
    me = lax.axis_index("drift") // 2
    own[...] = total[pl.ds(pl.multiple_of(me * chunk, 16), chunk), :]
    for step, out in enumerate(sends):
        start = pl.multiple_of((me ^ (step + 1)) * chunk, 16)
        out[...] = total[pl.ds(start, chunk), :].astype(jnp.bfloat16)
    z, x = face_indices()
    start = z * PLANE + x * J
    low, high = (dot(one_hot(start + j, ROWS), hb[...]).astype(jnp.bfloat16) for j in (1, NY))
    write_by_parity("wire", low, high, first, second)


def split_kernel(unit, count, after_first, after_second, own, *refs):
    received, (*sends, rest, total) = refs[:count], refs[count:]
    summed = own[...]
    for part in received:
        summed = summed + part[...].astype(jnp.float32)
    total[...] = summed
    me = lax.axis_index("wire")
    rest[...] = total[pl.ds(pl.multiple_of(me * unit, 16), unit), :]
    for step, out in enumerate(sends):
        start = pl.multiple_of((me ^ (step + 1)) * unit, 16)
        out[...] = total[pl.ds(start, unit), :].astype(jnp.bfloat16)


def sum_kernel(scale, after, own, *refs):
    *received, out = refs
    summed = own[...]
    for part in received:
        summed = summed + part[...].astype(jnp.float32)
    out[...] = (summed * scale).astype(jnp.bfloat16)


def joined_kernel(unit, after, *refs):
    *parts, out = refs
    me = lax.axis_index("wire")
    for step, part in enumerate(parts):
        start = pl.multiple_of((me ^ step) * unit, 16)
        out[pl.ds(start, unit), :] = part[...]


def final_kernel(step, *refs):
    mine, theirs = refs[:2]
    first, second, staged, sems = refs[-4:]
    me = lax.axis_index("drift") // 2
    even = lax.axis_index("drift") % 2 == 0
    blocks = staged.shape[1]

    def copies(i):
        tap = (me ^ step) * blocks + i
        safe = jnp.minimum(tap, TAPS - 1)
        return tap < TAPS, (
            pltpu.make_async_copy(staged.at[0, i], second.at[TAPS - 1 - safe], sems.at[0, i]),
            pltpu.make_async_copy(staged.at[1, i], first.at[safe], sems.at[1, i]),
        )

    a, b = mine[...], theirs[...]
    for_second = jnp.where(even, a, b).astype(jnp.float32)
    for_first = jnp.where(even, b, a).astype(jnp.float32)
    for i in range(blocks):
        staged[0, i] = for_second[128 * i : 128 * (i + 1), :]
        staged[1, i] = for_first[128 * i : 128 * (i + 1), :].T
        used, pair = copies(i)

        @pl.when(used)
        def _():
            for copy in pair:
                copy.start()

    for i in range(blocks):
        used, pair = copies(i)

        @pl.when(used)
        def _():
            for copy in pair:
                copy.wait()


def second_kernel(field, flip, lists, counts, hb, got_first, got_second, base, live, weight, output, done, window, *flipped):
    low, high = read_by_parity("drift", got_first, got_second)
    lanes = slice(128 * field, 128 * (field + 1))
    build_window(window, 0, lambda z: wide_plane(hb, low, high, z, lanes))
    if flip:
        flip_blocks(weight, *flipped)
        value = conv_flipped(window, *flipped)
    else:
        value = conv(window, weight)
    result = (live[...].astype(jnp.float32) * (base[:, lanes].astype(jnp.float32) + value)).astype(jnp.bfloat16)
    slots = position_slots(lists, counts)
    count = output.shape[0]
    pieces = []
    row = iota((count, 128), 0)
    for c in range(ROWS // 128):
        col = iota((8, 128), 1) + 128 * c
        z = (col >= PLANE).astype(jnp.int32) + (col >= 2 * PLANE) + (col >= 3 * PLANE)
        rest = col - PLANE * z
        x, j = rest >> 4, rest & 15
        source = slot_rows(slots, z, x, j - 1, (j >= 1) & (j <= NY))
        source = jnp.broadcast_to(source[0:1, :], (count, 128))
        pieces.append(jnp.where(row == source, 1.0, 0.0).astype(jnp.bfloat16))
    output[...] = dot(jnp.concatenate(pieces, axis=1), result).astype(jnp.bfloat16)
    done[...] = jnp.zeros_like(done)


def pairs(value_first, value_second, axis, wrap):
    count = lax.axis_size(axis)
    first = [(i, i ^ 1) for i in range(count) if i ^ 1 < count]
    second = [(i, i + 1) for i in range(1, count - 1, 2)] + [(i + 1, i) for i in range(1, count - 1, 2)]
    if wrap and count % 2 == 0:
        second = second + [(0, count - 1), (count - 1, 0)]
    got_second = lax.ppermute(value_second, axis, second)
    got_first = lax.ppermute(value_first, axis, first)
    return got_first, got_second


def on_device(features, first_weight, second_weight, cotangent, counts, kernel_map, send_lists):
    drift, wire = lax.axis_size("drift"), lax.axis_size("wire")
    chips = drift // 2
    blocks = -(-TAPS // chips)
    chunk = blocks * CHANNELS
    unit = chunk // wire
    rows = TAPS * CHANNELS
    f, g = features[0, 0], cotangent[0, 0]
    slots = f.shape[0]
    padded = -(-slots // 128) * 128
    pair_scratch = [
        pltpu.SMEM((1, 1, 16), jnp.int32),
        pltpu.VMEM((padded, 256), jnp.bfloat16),
        pltpu.SemaphoreType.DMA((3,)),
    ]
    conv_scratch = [pltpu.VMEM((4, WIDE, 1152), jnp.bfloat16), pltpu.VMEM((128, rows), jnp.bfloat16)]
    faces_scratch = pltpu.VMEM((128, 256), jnp.bfloat16)
    face, slab, grid = bf16(FACE, 256), bf16(SLAB, 256), bf16(ROWS, 256)

    def swap_core(value):
        return lax.ppermute(value, "drift", [(i, i ^ 1) for i in range(drift)])

    def to_chip(value, step):
        return lax.ppermute(value, "drift", [(i, i ^ (2 * step)) for i in range(drift)])

    def to_wire(value, step):
        return lax.ppermute(value, "wire", [(i, i ^ step) for i in range(wire)])

    faces = call(faces_kernel, (face, face), [SMEM] + [HBM] * 3, pair_scratch, 20, vmem=60)(
        counts, send_lists, f, g
    )
    placed, live = call(place_kernel, (grid, bf16(ROWS, 128)), [SMEM] + [HBM] * 3, pair_scratch, 20)(
        counts, send_lists, f, g
    )
    faces = pairs(*faces, "wire", False)
    full, *slabs = call(insert_faces, (grid, slab, slab), [VMEM] * 3, [faces_scratch], 20)(placed, *faces)
    slabs = pairs(*slabs, "drift", True)
    message = bf16(ROWS + 4 * WIDE, 128)
    hb, keep, send = call(first_kernel, (grid, message, message), [VMEM] * 6, conv_scratch)(
        full, *slabs, live, first_weight, second_weight
    )
    got = swap_core(send)
    *sends, own, face_first, face_second = call(
        functools.partial(terms_kernel, chunk),
        tuple([bf16(chunk, 128)] * (chips - 1) + [f32(chunk, 128), face, face]),
        [VMEM] * 3,
        [pltpu.VMEM((8, WIDE, 1152), jnp.bfloat16), pltpu.VMEM((chunk * chips, 128), jnp.float32)],
    )(keep, got, hb)
    parts = [to_chip(s, k + 1) for k, s in enumerate(sends)]
    faces = pairs(face_first, face_second, "wire", False)
    hb_full, *hb_slabs = call(insert_faces, (grid, slab, slab), [VMEM] * 3, [faces_scratch])(hb, *faces)
    hb_slabs = pairs(*hb_slabs, "drift", True)
    *sends, own = call(
        functools.partial(split_kernel, unit, chips - 1),
        tuple([bf16(unit, 128)] * (wire - 1) + [f32(unit, 128)]),
        [HBM] * 2 + [VMEM] * chips,
        [pltpu.VMEM((chunk, 128), jnp.float32)],
    )(*hb_slabs, own, *parts)

    def second(field, weight, flip):
        return call(
            functools.partial(second_kernel, field, flip),
            (bf16(slots, 128), f32(8, 128)),
            [SMEM] * 2 + [VMEM] * 6,
            conv_scratch if flip else conv_scratch[:1],
            3,
        )(send_lists, counts, hb_full, *hb_slabs, full, live, weight)

    grad_features, done = second(1, first_weight, True)
    received = [to_wire(s, k + 1) for k, s in enumerate(sends)]
    scale = 1.0 / math.sqrt(float(drift * wire * slots))
    summed = call(functools.partial(sum_kernel, scale), bf16(unit, 128), [VMEM] * (1 + wire))(
        done, own, *received
    )
    pieces = [summed] + [to_wire(summed, k) for k in range(1, wire)]
    output, done = second(0, second_weight, False)
    mine = call(functools.partial(joined_kernel, unit), bf16(chunk, 128), [VMEM] * (1 + wire))(done, *pieces)
    mine = [mine] + [to_chip(mine, k) for k in range(1, chips)]
    grads = ()
    for step in range(chips):
        grads = call(
            functools.partial(final_kernel, step),
            (f32(TAPS, 128, 128), f32(TAPS, 128, 128)),
            [VMEM] * 2 + [HBM] * len(grads),
            [pltpu.VMEM((2, blocks, 128, 128), jnp.float32), pltpu.SemaphoreType.DMA((2, blocks))],
            10,
            HBM,
            {2: 0, 3: 1} if grads else {},
        )(mine[step], swap_core(mine[step]), *grads)
    grad_first, grad_second = grads
    return output[None, None], grad_features[None, None], grad_first, grad_second


def solution(mesh):
    placed = (
        P("drift", "wire", None, None),
        P(),
        P(),
        P("drift", "wire", None, None),
        P("drift", "wire"),
        P("drift", "wire", None, None),
        P("drift", "wire", None),
    )
    return jax.shard_map(
        on_device,
        mesh=mesh,
        in_specs=placed,
        out_specs=(P("drift", "wire", None, None), P("drift", "wire", None, None), P(), P()),
        check_vma=False,
    )
```

time: 106 us -> 79.8 us (0.75)
  the two profiles are of different devices: /device:TPU:13 before, /device:TPU:0 now
where the time goes in v1:
time: 79.8 us; the launch traced here: 79.5 us
  starting transfers between devices  33.3 us (42%)
  Pallas kernels  21.2 us (27%)
  waiting for transfers between devices  18.5 us (23%)
  local copies, waits for them, and re-layouts  4.82 us (6%)
  between operations  1.67 us (2%)
    ppermute x6, starting transfers between devices, to_wire(): return lax.ppermute(value, 'wire', [(i, i ^ step) for i in range(wire)])  11 us
    ppermute x6, waiting for transfers between devices, to_chip(): lax.ppermute(value, 'drift', [(i, i ^ 2 * step) for i in range(drift)])  9.78 us
    ppermute x4, starting transfers between devices, pairs(): got_first = lax.ppermute(value_first, axis, first)  7.62 us
    ppermute x6, starting transfers between devices, to_chip(): lax.ppermute(value, 'drift', [(i, i ^ 2 * step) for i in range(drift)])  7.5 us
    pallas_call x2, Pallas kernels, second(): call(functools.partial(second_kernel, field, flip), (bf16(slots, 128), f3...  7.07 us
    ppermute x4, starting transfers between devices, pairs(): got_second = lax.ppermute(value_second, axis, second)  6.64 us
    unnamed x16, local copies, waits for them, and re-layouts  4.82 us
    pallas_call x4, Pallas kernels, on_device(): call(functools.partial(final_kernel, step), (f32(TAPS, 128, 128), f32(TAP...  4.57 us
  transfers between devices with their start and end apart: 25, of which 8 were waited for; matrix products, arithmetic and copies ran while one was open for 0% of the time, Pallas kernels for 15%

profile of v1, /device:TPU:0, one launch (start us, length us, event | category | flops | bytes accessed | tf_op | source)
XLA Modules:
  0.0 79.5 jit_solution(4927943472985990946)
XLA Ops:
  1.3 1.9 %shard_map.94 = (bf16[48,256]{1,0:T(8,128)(2,1)}, bf16[48,256]{1,0:T(8,128)(2,1)}) custom-call(s32[1,1]{1,0:T(1,128)S(6)} %copy.22.counts, s32[1,1,16]{2,1,0:T(1,128)} %lists.7, bf16[576,128]{1,0:T(8,128)(2,1)} %bitcast.4, bf16[576,128]{1,0:T(8,128)(2,1)} %bitcast.6), custom_call_target="tpu_custom_call" | custom-call | bytes 60000000 | tf_op jit(solution)/shard_map/pallas_call | solution.py:409
  3.1 3.1 %collective-permute-start = (bf16[48,256]{1,0:T(8,128)(2,1)}, bf16[48,256]{1,0:T(8,128)(2,1)S(1)}, u32[]{:S(2)}, u32[]{:S(2)}) collective-permute-start(bf16[48,256]{1,0:T(8,128)(2,1)} %get-tuple-element.40), channel_id=1, source_target_pairs={{0,1},{1,0},{2,3},{3,2},{4,5},{5,4},{6,7},{7,6},{8,9},{9,8},{10,11... | collective-permute-start | bytes 73736 | tf_op jit(solution)/shard_map/ppermute | solution.py:377
  7.8 0.9 %copy-done.5 = bf16[1,1,576,128]{3,2,1,0:T(8,128)(2,1)S(1)} copy-done((bf16[1,1,576,128]{3,2,1,0:T(8,128)(2,1)S(1)}, bf16[1,1,576,128]{3,2,1,0:T(8,128)(2,1)}, u32[]{:S(2)}) %copy-start.5) | copy-done | bytes 147480
  9.4 1.4 %shard_map.93 = (bf16[768,256]{1,0:T(8,128)(2,1)S(1)}, bf16[768,128]{1,0:T(8,128)(2,1)S(1)}) custom-call(s32[1,1]{1,0:T(1,128)S(6)} %copy.22.counts, s32[1,1,16]{2,1,0:T(1,128)S(1)} %copy-done.6, bf16[576,128]{1,0:T(8,128)(2,1)S(1)} %bitcast.5, bf16[576,128]{1,0:T(8,128)(2,1)S(1)} %bitcast.7), custom_call_target="tpu_custom_call" | custom-call | bytes 60000000 | tf_op jit(solution)/shard_map/pallas_call | solution.py:412
  11.1 2.5 %collective-permute-start.3 = (bf16[64,256]{1,0:T(8,128)(2,1)S(1)}, bf16[64,256]{1,0:T(8,128)(2,1)S(1)}, u32[]{:S(2)}, u32[]{:S(2)}) collective-permute-start(bf16[64,256]{1,0:T(8,128)(2,1)S(1)} %get-tuple-element.44), channel_id=1, source_target_pairs={{4,8},{12,16},{20,24},{8,4},{16,12},{24,20},{0,28},{28,0},{5,9},{1... | collective-permute-start | bytes 98312 | tf_op jit(solution)/shard_map/ppermute | solution.py:376
  13.7 1.8 %collective-permute-done.3.got_second = bf16[64,256]{1,0:T(8,128)(2,1)S(1)} collective-permute-done((bf16[64,256]{1,0:T(8,128)(2,1)S(1)}, bf16[64,256]{1,0:T(8,128)(2,1)S(1)}, u32[]{:S(2)}, u32[]{:S(2)}) %collective-permute-start.3) | collective-permute-done | bytes 32800 | tf_op jit(solution)/shard_map/ppermute | solution.py:376
  15.4 1.2 %copy-done = bf16[27,128,128]{2,1,0:T(8,128)(2,1)S(1)} copy-done((bf16[27,128,128]{2,1,0:T(8,128)(2,1)S(1)}, bf16[27,128,128]{2,1,0:T(8,128)(2,1)}, u32[]{:S(2)}) %copy-start) | copy-done | bytes 884760
  16.6 1.2 %copy-done.2 = bf16[27,128,128]{2,1,0:T(8,128)(2,1)S(1)} copy-done((bf16[27,128,128]{2,1,0:T(8,128)(2,1)S(1)}, bf16[27,128,128]{2,1,0:T(8,128)(2,1)}, u32[]{:S(2)}) %copy-start.2) | copy-done | bytes 884760
  17.8 3.4 %shard_map.96 = (bf16[768,256]{1,0:T(8,128)(2,1)S(1)}, bf16[1664,128]{1,0:T(8,128)(2,1)S(1)}, bf16[1664,128]{1,0:T(8,128)(2,1)S(1)}) custom-call(bf16[768,256]{1,0:T(8,128)(2,1)S(1)} %get-tuple-element.42.full.base, bf16[64,256]{1,0:T(8,128)(2,1)S(1)} %collective-permute-done.2.got_first, bf16[64,256]{1,0:T(8,128)(2,1)S(1)} %collective-permute-done.3.got_second, ...), custom_call_target="tpu_custom_call" | custom-call | tf_op jit(solution)/shard_map/pallas_call | solution.py:419
  21.3 1.8 %collective-permute-done.4.theirs = bf16[1664,128]{1,0:T(8,128)(2,1)S(1)} collective-permute-done((bf16[1664,128]{1,0:T(8,128)(2,1)S(1)}, bf16[1664,128]{1,0:T(8,128)(2,1)S(1)}, u32[]{:S(2)}, u32[]{:S(2)}) %collective-permute-start.4) | collective-permute-done | bytes 426016 | tf_op jit(solution)/shard_map/ppermute | solution.py:401
  23.0 2.2 %shard_map.97 = (bf16[896,128]{1,0:T(8,128)(2,1)S(1)}, bf16[896,128]{1,0:T(8,128)(2,1)S(1)}, bf16[896,128]{1,0:T(8,128)(2,1)S(1)}, f32[896,128]{1,0:T(8,128)S(1)...) custom-call(bf16[1664,128]{1,0:T(8,128)(2,1)S(1)} %get-tuple-element.47.mine, ...), custom_call_target="tpu_custom_call" | custom-call | tf_op jit(solution)/shard_map/pallas_call | solution.py:423
  25.2 1.6 %collective-permute-start.10 = (bf16[896,128]{1,0:T(8,128)(2,1)S(1)}, bf16[896,128]{1,0:T(8,128)(2,1)S(1)}, u32[]{:S(2)}, u32[]{:S(2)}) collective-permute-start(bf16[896,128]{1,0:T(8,128)(2,1)S(1)} %get-tuple-element.60), channel_id=1, source_target_pairs={{0,16},{4,20},{8,24},{12,28},{16,0},{20,4},{24,8},{28,12},{1,17},{... | collective-permute-start | bytes 688136 | tf_op jit(solution)/shard_map/ppermute | solution.py:404
  26.8 1.5 %collective-permute-start.11 = (bf16[896,128]{1,0:T(8,128)(2,1)S(1)}, bf16[896,128]{1,0:T(8,128)(2,1)S(1)}, u32[]{:S(2)}, u32[]{:S(2)}) collective-permute-start(bf16[896,128]{1,0:T(8,128)(2,1)S(1)} %get-tuple-element.61), channel_id=1, source_target_pairs={{0,24},{4,28},{8,16},{12,20},{16,8},{20,12},{24,0},{28,4},{1,25},{... | collective-permute-start | bytes 688136 | tf_op jit(solution)/shard_map/ppermute | solution.py:404
  28.8 4.4 %collective-permute-start.5 = (bf16[48,256]{1,0:T(8,128)(2,1)S(1)}, bf16[48,256]{1,0:T(8,128)(2,1)S(1)}, u32[]{:S(2)}, u32[]{:S(2)}) collective-permute-start(bf16[48,256]{1,0:T(8,128)(2,1)S(1)} %get-tuple-element.49), channel_id=1, source_target_pairs={{0,1},{1,0},{2,3},{3,2},{4,5},{5,4},{6,7},{7,6},{8,9},{9,8},{10,11... | collective-permute-start | bytes 73736 | tf_op jit(solution)/shard_map/ppermute | solution.py:377
  34.0 1.0 %collective-permute-done.5.got_first = bf16[48,256]{1,0:T(8,128)(2,1)S(1)} collective-permute-done((bf16[48,256]{1,0:T(8,128)(2,1)S(1)}, bf16[48,256]{1,0:T(8,128)(2,1)S(1)}, u32[]{:S(2)}, u32[]{:S(2)}) %collective-permute-start.5) | collective-permute-done | bytes 24608 | tf_op jit(solution)/shard_map/ppermute | solution.py:377
  35.3 2.6 %collective-permute-start.8 = (bf16[64,256]{1,0:T(8,128)(2,1)S(1)}, bf16[64,256]{1,0:T(8,128)(2,1)S(1)}, u32[]{:S(2)}, u32[]{:S(2)}) collective-permute-start(bf16[64,256]{1,0:T(8,128)(2,1)S(1)} %get-tuple-element.53), channel_id=1, source_target_pairs={{4,8},{12,16},{20,24},{8,4},{16,12},{24,20},{0,28},{28,0},{5,9},{1... | collective-permute-start | bytes 98312 | tf_op jit(solution)/shard_map/ppermute | solution.py:376
  37.9 2.1 %collective-permute-done.8.got_second.after_second = bf16[64,256]{1,0:T(8,128)(2,1)S(1)} collective-permute-done((bf16[64,256]{1,0:T(8,128)(2,1)S(1)}, bf16[64,256]{1,0:T(8,128)(2,1)S(1)}, u32[]{:S(2)}, u32[]{:S(2)}) %collective-permute-start.8) | collective-permute-done | bytes 32800 | tf_op jit(solution)/shard_map/ppermute | solution.py:376
  40.2 4.1 %collective-permute-start.12 = (bf16[224,128]{1,0:T(8,128)(2,1)S(1)}, bf16[224,128]{1,0:T(8,128)(2,1)S(1)}, u32[]{:S(2)}, u32[]{:S(2)}) collective-permute-start(bf16[224,128]{1,0:T(8,128)(2,1)S(1)} %get-tuple-element.63), channel_id=1, source_target_pairs={{0,1},{1,0},{2,3},{3,2},{4,5},{5,4},{6,7},{7,6},{8,9},{9,8},{10,11... | collective-permute-start | bytes 172040 | tf_op jit(solution)/shard_map/ppermute | solution.py:407
  44.3 2.4 %collective-permute-start.14 = (bf16[224,128]{1,0:T(8,128)(2,1)S(1)}, bf16[224,128]{1,0:T(8,128)(2,1)S(1)}, u32[]{:S(2)}, u32[]{:S(2)}) collective-permute-start(bf16[224,128]{1,0:T(8,128)(2,1)S(1)} %get-tuple-element.65), channel_id=1, source_target_pairs={{0,3},{1,2},{2,1},{3,0},{4,7},{5,6},{6,5},{7,4},{8,11},{9,10},{10,... | collective-permute-start | bytes 172040 | tf_op jit(solution)/shard_map/ppermute | solution.py:407
  46.7 3.6 %shard_map.100 = (bf16[576,128]{1,0:T(8,128)(2,1)}, f32[8,128]{1,0:T(8,128)S(1)}) custom-call(s32[1,1,16]{2,1,0:T(1,128)S(1)} %copy-done.7, s32[1,1]{1,0:T(1,128)S(6)} %copy.22.counts, bf16[768,256]{1,0:T(8,128)(2,1)S(1)} %get-tuple-element.51.hb, bf16[64,256]{1,0:T(8,128)(2,1)S(1)} %collective-permute-done.7.got_first.after_first, ...), custom_call_target="tpu_custom_call" | custom-call | bytes 9000000 | tf_op jit(solution)/shard_map/pallas_call | solution.py:441
  50.3 1.0 %collective-permute-done.13.refs_1_ = bf16[224,128]{1,0:T(8,128)(2,1)S(1)} collective-permute-done((bf16[224,128]{1,0:T(8,128)(2,1)S(1)}, bf16[224,128]{1,0:T(8,128)(2,1)S(1)}, u32[]{:S(2)}, u32[]{:S(2)}) %collective-permute-start.13) | collective-permute-done | bytes 57376 | tf_op jit(solution)/shard_map/ppermute | solution.py:407
  51.4 1.7 %collective-permute-start.15 = (bf16[224,128]{1,0:T(8,128)(2,1)S(1)}, bf16[224,128]{1,0:T(8,128)(2,1)S(1)}, u32[]{:S(2)}, u32[]{:S(2)}) collective-permute-start(bf16[224,128]{1,0:T(8,128)(2,1)S(1)} %shard_map.102.refs_0_), channel_id=1, source_target_pairs={{0,1},{1,0},{2,3},{3,2},{4,5},{5,4},{6,7},{7,6},{8,9},{9,8},{10,11... | collective-permute-start | bytes 172040 | tf_op jit(solution)/shard_map/ppermute | solution.py:407
  53.6 2.2 %collective-permute-start.17 = (bf16[224,128]{1,0:T(8,128)(2,1)S(1)}, bf16[224,128]{1,0:T(8,128)(2,1)S(1)}, u32[]{:S(2)}, u32[]{:S(2)}) collective-permute-start(bf16[224,128]{1,0:T(8,128)(2,1)S(1)} %shard_map.102.refs_0_), channel_id=1, source_target_pairs={{0,3},{1,2},{2,1},{3,0},{4,7},{5,6},{6,5},{7,4},{8,11},{9,10},{10,... | collective-permute-start | bytes 172040 | tf_op jit(solution)/shard_map/ppermute | solution.py:407
  55.8 3.5 %shard_map.99 = (bf16[576,128]{1,0:T(8,128)(2,1)}, f32[8,128]{1,0:T(8,128)S(1)}) custom-call(s32[1,1,16]{2,1,0:T(1,128)S(1)} %copy-done.7, s32[1,1]{1,0:T(1,128)S(6)} %copy.22.counts, bf16[768,256]{1,0:T(8,128)(2,1)S(1)} %get-tuple-element.51.hb, bf16[64,256]{1,0:T(8,128)(2,1)S(1)} %collective-permute-done.7.got_first.after_first, ...), custom_call_target="tpu_custom_call" | custom-call | bytes 9000000 | tf_op jit(solution)/shard_map/pallas_call | solution.py:441
  59.3 1.1 %collective-permute-done.16.refs_2_ = bf16[224,128]{1,0:T(8,128)(2,1)S(1)} collective-permute-done((bf16[224,128]{1,0:T(8,128)(2,1)S(1)}, bf16[224,128]{1,0:T(8,128)(2,1)S(1)}, u32[]{:S(2)}, u32[]{:S(2)}) %collective-permute-start.16) | collective-permute-done | bytes 57376 | tf_op jit(solution)/shard_map/ppermute | solution.py:407
  60.5 2.4 %collective-permute-start.22 = (bf16[896,128]{1,0:T(8,128)(2,1)S(1)}, bf16[896,128]{1,0:T(8,128)(2,1)S(1)}, u32[]{:S(2)}, u32[]{:S(2)}) collective-permute-start(bf16[896,128]{1,0:T(8,128)(2,1)S(1)} %shard_map.103.refs_0_), channel_id=1, source_target_pairs={{0,8},{4,12},{8,0},{12,4},{16,24},{20,28},{24,16},{28,20},{1,9},{5... | collective-permute-start | bytes 688136 | tf_op jit(solution)/shard_map/ppermute | solution.py:404
  64.4 5.0 %collective-permute-done.22.refs_0_ = bf16[896,128]{1,0:T(8,128)(2,1)S(1)} collective-permute-done((bf16[896,128]{1,0:T(8,128)(2,1)S(1)}, bf16[896,128]{1,0:T(8,128)(2,1)S(1)}, u32[]{:S(2)}, u32[]{:S(2)}) %collective-permute-start.22) | collective-permute-done | bytes 229408 | tf_op jit(solution)/shard_map/ppermute | solution.py:404
  69.4 4.8 %collective-permute-done.20.refs_0_ = bf16[896,128]{1,0:T(8,128)(2,1)S(1)} collective-permute-done((bf16[896,128]{1,0:T(8,128)(2,1)S(1)}, bf16[896,128]{1,0:T(8,128)(2,1)S(1)}, u32[]{:S(2)}, u32[]{:S(2)}) %collective-permute-start.20) | collective-permute-done | bytes 229408 | tf_op jit(solution)/shard_map/ppermute | solution.py:404
  74.7 1.1 %shard_map.104 = (f32[27,128,128]{2,1,0:T(8,128)}, f32[27,128,128]{2,1,0:T(8,128)}) custom-call(bf16[896,128]{1,0:T(8,128)(2,1)S(1)} %shard_map.103.refs_0_, bf16[896,128]{1,0:T(8,128)(2,1)S(1)} %collective-permute-done.24.refs_1_), custom_call_target="tpu_custom_call" | custom-call | bytes 30000000 | tf_op jit(solution)/shard_map/pallas_call | solution.py:461
  75.9 1.2 %shard_map.105 = (f32[27,128,128]{2,1,0:T(8,128)}, f32[27,128,128]{2,1,0:T(8,128)}) custom-call(bf16[896,128]{1,0:T(8,128)(2,1)S(1)} %collective-permute-done.22.refs_0_, bf16[896,128]{1,0:T(8,128)(2,1)S(1)} %collective-permute-done.23.refs_1_, f32[27,128,128]{2,1,0:T(8,128)} %get-tuple-element.66.refs_2_, ...), custom_call_target="tpu_custom_call", output_to_operand_aliasing={{0}: (2, {}), {1}: (3, {})} | custom-call | bytes 30000000 | tf_op jit(solution)/shard_map/pallas_call | solution.py:461
  77.0 1.2 %shard_map.106 = (f32[27,128,128]{2,1,0:T(8,128)}, f32[27,128,128]{2,1,0:T(8,128)}) custom-call(bf16[896,128]{1,0:T(8,128)(2,1)S(1)} %collective-permute-done.20.refs_0_, bf16[896,128]{1,0:T(8,128)(2,1)S(1)} %collective-permute-done.21.refs_1_, f32[27,128,128]{2,1,0:T(8,128)} %get-tuple-element.68.refs_2_, ...), custom_call_target="tpu_custom_call", output_to_operand_aliasing={{0}: (2, {}), {1}: (3, {})} | custom-call | bytes 30000000 | tf_op jit(solution)/shard_map/pallas_call | solution.py:461
  78.2 1.1 %shard_map.107 = (f32[27,128,128]{2,1,0:T(8,128)}, f32[27,128,128]{2,1,0:T(8,128)}) custom-call(bf16[896,128]{1,0:T(8,128)(2,1)S(1)} %collective-permute-done.18.refs_0_, bf16[896,128]{1,0:T(8,128)(2,1)S(1)} %collective-permute-done.19.refs_1_, f32[27,128,128]{2,1,0:T(8,128)} %get-tuple-element.70.refs_2_, ...), custom_call_target="tpu_custom_call", output_to_operand_aliasing={{0}: (2, {}), {1}: (3, {})} | custom-call | bytes 30000000 | tf_op jit(solution)/shard_map/pallas_call | solution.py:461
  (49 shorter events, 7.2 us)
Async XLA Ops:
  3.1 7.6 %collective-permute-start = (bf16[48,256]{1,0:T(8,128)(2,1)}, bf16[48,256]{1,0:T(8,128)(2,1)S(1)}, u32[]{:S(2)}, u32[]{:S(2)}) collective-permute-start(bf16[48,256]{1,0:T(8,128)(2,1)} %get-tuple-element.40), channel_id=1, source_target_pairs={{0,1},{1,0},{2,3},{3,2},{4,5},{5,4},{6,7},{7,6},{8,9},{9,8},{10,11... | collective-permute-start | bytes 73736 | tf_op jit(solution)/shard_map/ppermute | solution.py:377
  6.2 4.5 %collective-permute-start.1 = (bf16[48,256]{1,0:T(8,128)(2,1)}, bf16[48,256]{1,0:T(8,128)(2,1)S(1)}, u32[]{:S(2)}, u32[]{:S(2)}) collective-permute-start(bf16[48,256]{1,0:T(8,128)(2,1)} %get-tuple-element.41), channel_id=1, source_target_pairs={{1,2},{2,1},{5,6},{6,5},{9,10},{10,9},{13,14},{14,13},{17,18},{18,... | collective-permute-start | bytes 73736 | tf_op jit(solution)/shard_map/ppermute | solution.py:376
  6.9 0.9 %copy-start.4 = (bf16[1,1,576,128]{3,2,1,0:T(8,128)(2,1)S(1)}, bf16[1,1,576,128]{3,2,1,0:T(8,128)(2,1)}, u32[]{:S(2)}) copy-start(bf16[1,1,576,128]{3,2,1,0:T(8,128)(2,1)} %param.7) | copy-start | bytes 442372
  7.8 0.9 %copy-start.5 = (bf16[1,1,576,128]{3,2,1,0:T(8,128)(2,1)S(1)}, bf16[1,1,576,128]{3,2,1,0:T(8,128)(2,1)}, u32[]{:S(2)}) copy-start(bf16[1,1,576,128]{3,2,1,0:T(8,128)(2,1)} %param.10) | copy-start | bytes 442372
  11.0 2.6 %collective-permute-start.2 = (bf16[64,256]{1,0:T(8,128)(2,1)S(1)}, bf16[64,256]{1,0:T(8,128)(2,1)S(1)}, u32[]{:S(2)}, u32[]{:S(2)}) collective-permute-start(bf16[64,256]{1,0:T(8,128)(2,1)S(1)} %get-tuple-element.43), channel_id=1, source_target_pairs={{0,4},{4,0},{8,12},{12,8},{16,20},{20,16},{24,28},{28,24},{1,5},{5... | collective-permute-start | bytes 98312 | tf_op jit(solution)/shard_map/ppermute | solution.py:377
  11.1 4.3 %collective-permute-start.3 = (bf16[64,256]{1,0:T(8,128)(2,1)S(1)}, bf16[64,256]{1,0:T(8,128)(2,1)S(1)}, u32[]{:S(2)}, u32[]{:S(2)}) collective-permute-start(bf16[64,256]{1,0:T(8,128)(2,1)S(1)} %get-tuple-element.44), channel_id=1, source_target_pairs={{4,8},{12,16},{20,24},{8,4},{16,12},{24,20},{0,28},{28,0},{5,9},{1... | collective-permute-start | bytes 98312 | tf_op jit(solution)/shard_map/ppermute | solution.py:376
  15.4 1.2 %copy-start = (bf16[27,128,128]{2,1,0:T(8,128)(2,1)S(1)}, bf16[27,128,128]{2,1,0:T(8,128)(2,1)}, u32[]{:S(2)}) copy-start(bf16[27,128,128]{2,1,0:T(8,128)(2,1)} %weight.3) | copy-start | bytes 2654212
  16.6 1.2 %copy-start.2 = (bf16[27,128,128]{2,1,0:T(8,128)(2,1)S(1)}, bf16[27,128,128]{2,1,0:T(8,128)(2,1)}, u32[]{:S(2)}) copy-start(bf16[27,128,128]{2,1,0:T(8,128)(2,1)} %weight.2) | copy-start | bytes 2654212
  21.2 25.6 %copy-start.1 = (bf16[27,128,128]{2,1,0:T(8,128)(2,1)S(1)}, bf16[27,128,128]{2,1,0:T(8,128)(2,1)}, u32[]{:S(2)}) copy-start(bf16[27,128,128]{2,1,0:T(8,128)(2,1)} %weight.3) | copy-start | bytes 2654212
  21.2 25.6 %copy-start.7 = (s32[1,1,16]{2,1,0:T(1,128)S(1)}, s32[1,1,16]{2,1,0:T(1,128)}, u32[]{:S(2)}) copy-start(s32[1,1,16]{2,1,0:T(1,128)} %lists.7) | copy-start | bytes 196
  21.2 1.8 %collective-permute-start.4 = (bf16[1664,128]{1,0:T(8,128)(2,1)S(1)}, bf16[1664,128]{1,0:T(8,128)(2,1)S(1)}, u32[]{:S(2)}, u32[]{:S(2)}) collective-permute-start(bf16[1664,128]{1,0:T(8,128)(2,1)S(1)} %get-tuple-element.48), channel_id=1, source_target_pairs={{0,4},{4,0},{8,12},{12,8},{16,20},{20,16},{24,28},{28,24},{1,5},{5... | collective-permute-start | bytes 1277960 | tf_op jit(solution)/shard_map/ppermute | solution.py:401
  25.2 14.8 %collective-permute-start.10 = (bf16[896,128]{1,0:T(8,128)(2,1)S(1)}, bf16[896,128]{1,0:T(8,128)(2,1)S(1)}, u32[]{:S(2)}, u32[]{:S(2)}) collective-permute-start(bf16[896,128]{1,0:T(8,128)(2,1)S(1)} %get-tuple-element.60), channel_id=1, source_target_pairs={{0,16},{4,20},{8,24},{12,28},{16,0},{20,4},{24,8},{28,12},{1,17},{... | collective-permute-start | bytes 688136 | tf_op jit(solution)/shard_map/ppermute | solution.py:404
  26.8 13.2 %collective-permute-start.11 = (bf16[896,128]{1,0:T(8,128)(2,1)S(1)}, bf16[896,128]{1,0:T(8,128)(2,1)S(1)}, u32[]{:S(2)}, u32[]{:S(2)}) collective-permute-start(bf16[896,128]{1,0:T(8,128)(2,1)S(1)} %get-tuple-element.61), channel_id=1, source_target_pairs={{0,24},{4,28},{8,16},{12,20},{16,8},{20,12},{24,0},{28,4},{1,25},{... | collective-permute-start | bytes 688136 | tf_op jit(solution)/shard_map/ppermute | solution.py:404
  28.3 11.7 %collective-permute-start.9 = (bf16[896,128]{1,0:T(8,128)(2,1)S(1)}, bf16[896,128]{1,0:T(8,128)(2,1)S(1)}, u32[]{:S(2)}, u32[]{:S(2)}) collective-permute-start(bf16[896,128]{1,0:T(8,128)(2,1)S(1)} %get-tuple-element.59), channel_id=1, source_target_pairs={{0,8},{4,12},{8,0},{12,4},{16,24},{20,28},{24,16},{28,20},{1,9},{5... | collective-permute-start | bytes 688136 | tf_op jit(solution)/shard_map/ppermute | solution.py:404
  28.8 6.2 %collective-permute-start.5 = (bf16[48,256]{1,0:T(8,128)(2,1)S(1)}, bf16[48,256]{1,0:T(8,128)(2,1)S(1)}, u32[]{:S(2)}, u32[]{:S(2)}) collective-permute-start(bf16[48,256]{1,0:T(8,128)(2,1)S(1)} %get-tuple-element.49), channel_id=1, source_target_pairs={{0,1},{1,0},{2,3},{3,2},{4,5},{5,4},{6,7},{7,6},{8,9},{9,8},{10,11... | collective-permute-start | bytes 73736 | tf_op jit(solution)/shard_map/ppermute | solution.py:377
  33.2 1.8 %collective-permute-start.6 = (bf16[48,256]{1,0:T(8,128)(2,1)S(1)}, bf16[48,256]{1,0:T(8,128)(2,1)S(1)}, u32[]{:S(2)}, u32[]{:S(2)}) collective-permute-start(bf16[48,256]{1,0:T(8,128)(2,1)S(1)} %get-tuple-element.50), channel_id=1, source_target_pairs={{1,2},{2,1},{5,6},{6,5},{9,10},{10,9},{13,14},{14,13},{17,18},{18,... | collective-permute-start | bytes 73736 | tf_op jit(solution)/shard_map/ppermute | solution.py:376
  35.2 20.6 %copy-start.3 = (bf16[27,128,128]{2,1,0:T(8,128)(2,1)S(1)}, bf16[27,128,128]{2,1,0:T(8,128)(2,1)}, u32[]{:S(2)}) copy-start(bf16[27,128,128]{2,1,0:T(8,128)(2,1)} %weight.2) | copy-start | bytes 2654212
  35.2 2.7 %collective-permute-start.7 = (bf16[64,256]{1,0:T(8,128)(2,1)S(1)}, bf16[64,256]{1,0:T(8,128)(2,1)S(1)}, u32[]{:S(2)}, u32[]{:S(2)}) collective-permute-start(bf16[64,256]{1,0:T(8,128)(2,1)S(1)} %get-tuple-element.52), channel_id=1, source_target_pairs={{0,4},{4,0},{8,12},{12,8},{16,20},{20,16},{24,28},{28,24},{1,5},{5... | collective-permute-start | bytes 98312 | tf_op jit(solution)/shard_map/ppermute | solution.py:377
  35.3 4.7 %collective-permute-start.8 = (bf16[64,256]{1,0:T(8,128)(2,1)S(1)}, bf16[64,256]{1,0:T(8,128)(2,1)S(1)}, u32[]{:S(2)}, u32[]{:S(2)}) collective-permute-start(bf16[64,256]{1,0:T(8,128)(2,1)S(1)} %get-tuple-element.53), channel_id=1, source_target_pairs={{4,8},{12,16},{20,24},{8,4},{16,12},{24,20},{0,28},{28,0},{5,9},{1... | collective-permute-start | bytes 98312 | tf_op jit(solution)/shard_map/ppermute | solution.py:376
  40.2 10.1 %collective-permute-start.12 = (bf16[224,128]{1,0:T(8,128)(2,1)S(1)}, bf16[224,128]{1,0:T(8,128)(2,1)S(1)}, u32[]{:S(2)}, u32[]{:S(2)}) collective-permute-start(bf16[224,128]{1,0:T(8,128)(2,1)S(1)} %get-tuple-element.63), channel_id=1, source_target_pairs={{0,1},{1,0},{2,3},{3,2},{4,5},{5,4},{6,7},{7,6},{8,9},{9,8},{10,11... | collective-permute-start | bytes 172040 | tf_op jit(solution)/shard_map/ppermute | solution.py:407
  44.3 7.0 %collective-permute-start.13 = (bf16[224,128]{1,0:T(8,128)(2,1)S(1)}, bf16[224,128]{1,0:T(8,128)(2,1)S(1)}, u32[]{:S(2)}, u32[]{:S(2)}) collective-permute-start(bf16[224,128]{1,0:T(8,128)(2,1)S(1)} %get-tuple-element.64), channel_id=1, source_target_pairs={{0,2},{1,3},{2,0},{3,1},{4,6},{5,7},{6,4},{7,5},{8,10},{9,11},{10,... | collective-permute-start | bytes 172040 | tf_op jit(solution)/shard_map/ppermute | solution.py:407
  44.3 7.0 %collective-permute-start.14 = (bf16[224,128]{1,0:T(8,128)(2,1)S(1)}, bf16[224,128]{1,0:T(8,128)(2,1)S(1)}, u32[]{:S(2)}, u32[]{:S(2)}) collective-permute-start(bf16[224,128]{1,0:T(8,128)(2,1)S(1)} %get-tuple-element.65), channel_id=1, source_target_pairs={{0,3},{1,2},{2,1},{3,0},{4,7},{5,6},{6,5},{7,4},{8,11},{9,10},{10,... | collective-permute-start | bytes 172040 | tf_op jit(solution)/shard_map/ppermute | solution.py:407
  51.4 7.9 %collective-permute-start.15 = (bf16[224,128]{1,0:T(8,128)(2,1)S(1)}, bf16[224,128]{1,0:T(8,128)(2,1)S(1)}, u32[]{:S(2)}, u32[]{:S(2)}) collective-permute-start(bf16[224,128]{1,0:T(8,128)(2,1)S(1)} %shard_map.102.refs_0_), channel_id=1, source_target_pairs={{0,1},{1,0},{2,3},{3,2},{4,5},{5,4},{6,7},{7,6},{8,9},{9,8},{10,11... | collective-permute-start | bytes 172040 | tf_op jit(solution)/shard_map/ppermute | solution.py:407
  53.1 7.3 %collective-permute-start.16 = (bf16[224,128]{1,0:T(8,128)(2,1)S(1)}, bf16[224,128]{1,0:T(8,128)(2,1)S(1)}, u32[]{:S(2)}, u32[]{:S(2)}) collective-permute-start(bf16[224,128]{1,0:T(8,128)(2,1)S(1)} %shard_map.102.refs_0_), channel_id=1, source_target_pairs={{0,2},{1,3},{2,0},{3,1},{4,6},{5,7},{6,4},{7,5},{8,10},{9,11},{10,... | collective-permute-start | bytes 172040 | tf_op jit(solution)/shard_map/ppermute | solution.py:407
  53.6 6.8 %collective-permute-start.17 = (bf16[224,128]{1,0:T(8,128)(2,1)S(1)}, bf16[224,128]{1,0:T(8,128)(2,1)S(1)}, u32[]{:S(2)}, u32[]{:S(2)}) collective-permute-start(bf16[224,128]{1,0:T(8,128)(2,1)S(1)} %shard_map.102.refs_0_), channel_id=1, source_target_pairs={{0,3},{1,2},{2,1},{3,0},{4,7},{5,6},{6,5},{7,4},{8,11},{9,10},{10,... | collective-permute-start | bytes 172040 | tf_op jit(solution)/shard_map/ppermute | solution.py:407
  60.5 8.9 %collective-permute-start.22 = (bf16[896,128]{1,0:T(8,128)(2,1)S(1)}, bf16[896,128]{1,0:T(8,128)(2,1)S(1)}, u32[]{:S(2)}, u32[]{:S(2)}) collective-permute-start(bf16[896,128]{1,0:T(8,128)(2,1)S(1)} %shard_map.103.refs_0_), channel_id=1, source_target_pairs={{0,8},{4,12},{8,0},{12,4},{16,24},{20,28},{24,16},{28,20},{1,9},{5... | collective-permute-start | bytes 688136 | tf_op jit(solution)/shard_map/ppermute | solution.py:404
  62.9 11.3 %collective-permute-start.20 = (bf16[896,128]{1,0:T(8,128)(2,1)S(1)}, bf16[896,128]{1,0:T(8,128)(2,1)S(1)}, u32[]{:S(2)}, u32[]{:S(2)}) collective-permute-start(bf16[896,128]{1,0:T(8,128)(2,1)S(1)} %shard_map.103.refs_0_), channel_id=1, source_target_pairs={{0,16},{4,20},{8,24},{12,28},{16,0},{20,4},{24,8},{28,12},{1,17},{... | collective-permute-start | bytes 688136 | tf_op jit(solution)/shard_map/ppermute | solution.py:404
  63.6 10.6 %collective-permute-start.18 = (bf16[896,128]{1,0:T(8,128)(2,1)S(1)}, bf16[896,128]{1,0:T(8,128)(2,1)S(1)}, u32[]{:S(2)}, u32[]{:S(2)}) collective-permute-start(bf16[896,128]{1,0:T(8,128)(2,1)S(1)} %shard_map.103.refs_0_), channel_id=1, source_target_pairs={{0,24},{4,28},{8,16},{12,20},{16,8},{20,12},{24,0},{28,4},{1,25},{... | collective-permute-start | bytes 688136 | tf_op jit(solution)/shard_map/ppermute | solution.py:404
  64.4 10.3 %collective-permute-start.24 = (bf16[896,128]{1,0:T(8,128)(2,1)S(1)}, bf16[896,128]{1,0:T(8,128)(2,1)S(1)}, u32[]{:S(2)}, u32[]{:S(2)}) collective-permute-start(bf16[896,128]{1,0:T(8,128)(2,1)S(1)} %shard_map.103.refs_0_), channel_id=1, source_target_pairs={{0,4},{4,0},{8,12},{12,8},{16,20},{20,16},{24,28},{28,24},{1,5},{5... | collective-permute-start | bytes 688136 | tf_op jit(solution)/shard_map/ppermute | solution.py:401
  69.4 6.5 %collective-permute-start.23 = (bf16[896,128]{1,0:T(8,128)(2,1)S(1)}, bf16[896,128]{1,0:T(8,128)(2,1)S(1)}, u32[]{:S(2)}, u32[]{:S(2)}) collective-permute-start(bf16[896,128]{1,0:T(8,128)(2,1)S(1)} %collective-permute-done.22.refs_0_), channel_id=1, source_target_pairs={{0,4},{4,0},{8,12},{12,8},{16,20},{20,16},{24,28},{28,24},{1,5},{5... | collective-permute-start | bytes 688136 | tf_op jit(solution)/shard_map/ppermute | solution.py:401
  74.2 2.9 %collective-permute-start.21 = (bf16[896,128]{1,0:T(8,128)(2,1)S(1)}, bf16[896,128]{1,0:T(8,128)(2,1)S(1)}, u32[]{:S(2)}, u32[]{:S(2)}) collective-permute-start(bf16[896,128]{1,0:T(8,128)(2,1)S(1)} %collective-permute-done.20.refs_0_), channel_id=1, source_target_pairs={{0,4},{4,0},{8,12},{12,8},{16,20},{20,16},{24,28},{28,24},{1,5},{5... | collective-permute-start | bytes 688136 | tf_op jit(solution)/shard_map/ppermute | solution.py:401
  74.2 4.0 %collective-permute-start.19 = (bf16[896,128]{1,0:T(8,128)(2,1)S(1)}, bf16[896,128]{1,0:T(8,128)(2,1)S(1)}, u32[]{:S(2)}, u32[]{:S(2)}) collective-permute-start(bf16[896,128]{1,0:T(8,128)(2,1)S(1)} %collective-permute-done.18.refs_0_), channel_id=1, source_target_pairs={{0,4},{4,0},{8,12},{12,8},{16,20},{20,16},{24,28},{28,24},{1,5},{5... | collective-permute-start | bytes 688136 | tf_op jit(solution)/shard_map/ppermute | solution.py:401
  (1 other events, 0.7 us)

commit v2 on v1

v2 whole, which is shorter than its diff:
```python
import functools
import math

import jax
import jax.numpy as jnp
from jax import lax
from jax.experimental import pallas as pl
from jax.experimental.pallas import tpu as pltpu
from jax.sharding import PartitionSpec as P

BX = 3
BW = 3
NX = 4 * BX
NY = 4 * BW
J = 16
PLANE = NX * J
WIDE = (NX + 2) * J
ROWS = 4 * PLANE
FACE = 4 * NX
SLAB = 4 * J
CHANNELS = 128
TAPS = 27
VMEM = pl.BlockSpec(memory_space=pltpu.VMEM)
HBM = pl.BlockSpec(memory_space=pltpu.HBM)
SMEM = pl.BlockSpec(memory_space=pltpu.SMEM)
LISTED = {0: 0, 1: 1, 2: 2, 3: 7, 5: 10, 6: 3, 7: 4, 8: 5}


def call(kernel, out_shape, in_specs, scratch=(), flops=0, out_spec=VMEM, aliases={}, vmem=40):
    return pl.pallas_call(
        kernel,
        out_shape=out_shape,
        in_specs=in_specs,
        out_specs=jax.tree.map(lambda _: out_spec, out_shape),
        scratch_shapes=list(scratch),
        input_output_aliases=aliases,
        compiler_params=pltpu.CompilerParams(vmem_limit_bytes=vmem * 1024 * 1024),
        cost_estimate=pl.CostEstimate(
            flops=flops, bytes_accessed=0, transcendentals=0
        ),
    )


def bf16(*shape):
    return jax.ShapeDtypeStruct(shape, jnp.bfloat16)


def f32(*shape):
    return jax.ShapeDtypeStruct(shape, jnp.float32)


def iota(shape, dim):
    return lax.broadcasted_iota(jnp.int32, shape, dim)


def position_slots(lists, counts):
    slots = {p: lists[0, 0, i] for p, i in LISTED.items()}
    present = {p: (s < 9).astype(jnp.int32) for p, s in slots.items()}
    before = present[0] + present[1] + present[2] + present[3]
    others = before + present[5] + present[6] + present[7] + present[8]
    slots[4] = jnp.where(counts[0, 0] > others, before, 9)
    return slots


def slot_rows(slots, z, x, y, valid):
    position = (x >> 2) * BW + (y >> 2)
    slot = jnp.full(position.shape, 9, jnp.int32)
    for p, s in slots.items():
        slot = jnp.where(position == p, s, slot)
    row = slot * 64 + (x & 3) * 16 + (y & 3) * 4 + z
    return jnp.where(valid & (slot < 9), row, -1)


def one_hot(rows, width):
    lane = iota(rows.shape, 1)
    parts = [jnp.where(rows == lane + 128 * c, 1.0, 0.0).astype(jnp.bfloat16) for c in range(width // 128)]
    return jnp.concatenate(parts, axis=1)


def dot(a, b):
    return jnp.dot(a, b, preferred_element_type=jnp.float32)


def grid_indices():
    shape = (4, NX, J, 128)
    z, x, j = (iota(shape, d).reshape(ROWS, 128) for d in range(3))
    return z, x, j


def face_indices():
    r = iota((FACE, 128), 0)
    z = (r >= NX).astype(jnp.int32) + (r >= 2 * NX) + (r >= 3 * NX)
    return z, r - NX * z


def write_by_parity(axis, low, high, first, second):
    even = lax.axis_index(axis) % 2 == 0
    first[...] = jnp.where(even, high, low)
    second[...] = jnp.where(even, low, high)


def read_by_parity(axis, first, second):
    me, count = lax.axis_index(axis), lax.axis_size(axis)
    even = me % 2 == 0
    a, b = first[...], second[...]
    nothing = jnp.zeros_like(a)
    low = jnp.where(me > 0, jnp.where(even, b, a), nothing)
    high = jnp.where(me < count - 1, jnp.where(even, a, b), nothing)
    return low, high


def place_kernel(counts, lists, pair, first, second, out, live, both):
    count = pair.shape[0]
    both[0:count, :] = pair[...]
    both[count:, :] = jnp.zeros((both.shape[0] - count, 256), jnp.bfloat16)
    slots = position_slots(lists, counts)
    z, x = face_indices()
    low, high = (
        dot(
            one_hot(slot_rows(slots, z, x, jnp.full_like(x, y), x >= 0), both.shape[0]), both[...]
        ).astype(jnp.bfloat16)
        for y in (0, NY - 1)
    )
    write_by_parity("wire", low, high, first, second)
    z, x, j = grid_indices()
    rows = slot_rows(slots, z, x, j - 1, (j >= 1) & (j <= NY))
    live[...] = (rows >= 0).astype(jnp.bfloat16)
    out[...] = dot(one_hot(rows, both.shape[0]), both[...]).astype(jnp.bfloat16)


def insert_faces(placed, got_first, got_second, out, slab_first, slab_second, faces):
    low, high = read_by_parity("wire", got_first, got_second)
    faces[0:FACE, :] = low
    faces[FACE : 2 * FACE, :] = high
    faces[2 * FACE :, :] = jnp.zeros((faces.shape[0] - 2 * FACE, 256), jnp.bfloat16)
    z, x, j = grid_indices()
    rows = z * NX + x
    rows = jnp.where(j == 0, rows, jnp.where(j == NY + 1, rows + FACE, -1))
    full = (placed[...].astype(jnp.float32) + dot(one_hot(rows, 128), faces[...])).astype(jnp.bfloat16)
    out[...] = full
    low = jnp.concatenate([full[z * PLANE : z * PLANE + J, :] for z in range(4)], axis=0)
    high = jnp.concatenate([full[(z + 1) * PLANE - J : (z + 1) * PLANE, :] for z in range(4)], axis=0)
    write_by_parity("drift", low, high, slab_first, slab_second)


def build_window(window, base, plane_of):
    for zi in range(4):
        plane = plane_of(zi)
        wide = plane.astype(jnp.float32)
        before = pltpu.roll(wide, 1, 0).astype(jnp.bfloat16)
        after = pltpu.roll(wide, plane.shape[0] - 1, 0).astype(jnp.bfloat16)
        for oy, shifted in enumerate((before, plane, after)):
            for z in range(max(0, zi - 1), min(3, zi + 1) + 1):
                lane = 128 * (3 * oy + zi - z + 1)
                window[base + z, :, lane : lane + 128] = shifted
    empty = jnp.zeros((plane.shape[0], 128), jnp.bfloat16)
    for oy in range(3):
        window[base, :, 384 * oy : 384 * oy + 128] = empty
        window[base + 3, :, 384 * oy + 256 : 384 * oy + 384] = empty


def wide_plane(full, low, high, z, lanes):
    return jnp.concatenate(
        [
            low[z * J : (z + 1) * J, lanes],
            full[z * PLANE : (z + 1) * PLANE, lanes],
            high[z * J : (z + 1) * J, lanes],
        ],
        axis=0,
    )


def conv(window, weights, base):
    total = None
    for ox in range(3):
        rows = window[:, ox * J : ox * J + PLANE, :].reshape(ROWS, 1152)
        term = dot(rows, weights[base + 9 * ox : base + 9 * (ox + 1)].reshape(1152, 128))
        total = term if total is None else total + term
    return total


def flip_blocks(weights, base, flipped):
    for k in range(TAPS):
        flipped[:, 128 * k : 128 * (k + 1)] = weights[base + TAPS - 1 - k]


def conv_flipped(window, flipped):
    total = None
    for ox in range(3):
        rows = window[:, ox * J : ox * J + PLANE, :].reshape(ROWS, 1152)
        term = lax.dot_general(
            rows,
            flipped[:, 1152 * ox : 1152 * (ox + 1)],
            (((1,), (1,)), ((), ())),
            preferred_element_type=jnp.float32,
        )
        total = term if total is None else total + term
    return total


def inner_kernel(full, weights, pre, window):
    edge = jnp.zeros((SLAB, 128), jnp.bfloat16)
    build_window(window, 0, lambda z: wide_plane(full, edge, edge, z, slice(0, 128)))
    pre[...] = conv(window, weights, 0)


def add_edges(pre, low, high, weights, edge_window):
    for ox, x, slab in ((0, 0, low), (2, NX - 1, high)):
        build_window(edge_window, 0, lambda z: slab[z * J : (z + 1) * J, :])
        taps = weights[9 * ox : 9 * (ox + 1)].reshape(1152, 128)
        term = dot(edge_window[...].reshape(SLAB, 1152), taps)
        for z in range(4):
            start = z * PLANE + x * J
            pre[start : start + J, :] += term[z * J : (z + 1) * J, :]


def first_kernel(full, got_first, got_second, live, weights, inner, hb, keep, send, window, flipped, edge_window, pre):
    f_lanes, g_lanes = slice(0, 128), slice(128, 256)
    low, high = read_by_parity("drift", got_first, got_second)
    alive = live[...].astype(jnp.float32)
    flip_blocks(weights, TAPS, flipped)
    pre[...] = inner[...]
    add_edges(pre, low[:, f_lanes], high[:, f_lanes], weights, edge_window)
    first_pre = pre[...]
    gate = jax.nn.sigmoid(first_pre)
    hidden = (alive * (first_pre * gate)).astype(jnp.bfloat16)
    slope = alive * (gate * (1.0 + first_pre * (1.0 - gate)))
    build_window(window, 0, lambda z: wide_plane(full, low, high, z, g_lanes))
    back = (conv_flipped(window, flipped) * slope).astype(jnp.bfloat16)
    hb[...] = jnp.concatenate([hidden, back], axis=1)
    core = lax.axis_index("drift") % 2

    def write(to, values, lanes):
        to[0:ROWS, :] = values
        for z in range(4):
            start = ROWS + z * WIDE
            to[start : start + WIDE, :] = wide_plane(full, low, high, z, lanes)

    @pl.when(core == 0)
    def _():
        write(keep, hidden, g_lanes)
        write(send, back, f_lanes)

    @pl.when(core != 0)
    def _():
        write(keep, back, f_lanes)
        write(send, hidden, g_lanes)


def add_terms(part, window, total, fresh):
    build_window(window, 0, lambda z: part[ROWS + z * WIDE : ROWS + (z + 1) * WIDE, :])
    left = part[0:ROWS, :].astype(jnp.float32).T.astype(jnp.bfloat16)
    for ox in range(3):
        shifted = window[:, ox * J : ox * J + PLANE, :].reshape(ROWS, 1152)
        product = dot(left, shifted)
        for k in range(9):
            start = 128 * (9 * ox + k)
            term = product[:, 128 * k : 128 * (k + 1)]
            total[start : start + 128, :] = term if fresh else total[start : start + 128, :] + term


def own_terms_kernel(mine, total, window):
    rows = TAPS * CHANNELS
    if total.shape[0] > rows:
        total[rows:, :] = jnp.zeros((total.shape[0] - rows, 128), jnp.float32)
    add_terms(mine, window, total, True)


def terms_kernel(chunk, mine, theirs, hb, *refs):
    *sends, own, first, second, window, total = refs
    total[...] = mine[...]
    add_terms(theirs, window, total, False)
    me = lax.axis_index("drift") // 2
    own[...] = total[pl.ds(pl.multiple_of(me * chunk, 16), chunk), :]
    for step, out in enumerate(sends):
        start = pl.multiple_of((me ^ (step + 1)) * chunk, 16)
        out[...] = total[pl.ds(start, chunk), :].astype(jnp.bfloat16)
    z, x = face_indices()
    start = z * PLANE + x * J
    low, high = (dot(one_hot(start + j, ROWS), hb[...]).astype(jnp.bfloat16) for j in (1, NY))
    write_by_parity("wire", low, high, first, second)


def split_kernel(unit, count, after, own, *refs):
    received, (*sends, rest, total) = refs[:count], refs[count:]
    summed = own[...]
    for part in received:
        summed = summed + part[...].astype(jnp.float32)
    total[...] = summed
    me = lax.axis_index("wire")
    rest[...] = total[pl.ds(pl.multiple_of(me * unit, 16), unit), :]
    for step, out in enumerate(sends):
        start = pl.multiple_of((me ^ (step + 1)) * unit, 16)
        out[...] = total[pl.ds(start, unit), :].astype(jnp.bfloat16)


def sum_kernel(scale, after_first, after_second, own, *refs):
    *received, out = refs
    summed = own[...]
    for part in received:
        summed = summed + part[...].astype(jnp.float32)
    out[...] = (summed * scale).astype(jnp.bfloat16)


def joined_kernel(unit, after, *refs):
    *parts, out = refs
    me = lax.axis_index("wire")
    for step, part in enumerate(parts):
        start = pl.multiple_of((me ^ step) * unit, 16)
        out[pl.ds(start, unit), :] = part[...]


def final_kernel(steps, blocks, after, *refs):
    mine, theirs = refs[: len(steps)], refs[len(steps) : 2 * len(steps)]
    first, second, staged, sems = refs[-4:]
    me = lax.axis_index("drift") // 2
    even = lax.axis_index("drift") % 2 == 0

    def copies(n, i):
        tap = (me ^ steps[n]) * blocks + i
        here = n * blocks + i
        safe = jnp.minimum(tap, TAPS - 1)
        return tap < TAPS, (
            pltpu.make_async_copy(staged.at[0, here], second.at[TAPS - 1 - safe], sems.at[0, here]),
            pltpu.make_async_copy(staged.at[1, here], first.at[safe], sems.at[1, here]),
        )

    for n in range(len(steps)):
        a, b = mine[n][...], theirs[n][...]
        for_second = jnp.where(even, a, b).astype(jnp.float32)
        for_first = jnp.where(even, b, a).astype(jnp.float32)
        for i in range(blocks):
            here = n * blocks + i
            staged[0, here] = for_second[128 * i : 128 * (i + 1), :]
            staged[1, here] = for_first[128 * i : 128 * (i + 1), :].T
            used, pair = copies(n, i)

            @pl.when(used)
            def _():
                for copy in pair:
                    copy.start()

    for n in range(len(steps)):
        for i in range(blocks):
            used, pair = copies(n, i)

            @pl.when(used)
            def _():
                for copy in pair:
                    copy.wait()


def second_kernel(field, flip, lists, counts, hb, got_first, got_second, base, live, weights, output, done, window, *flipped):
    low, high = read_by_parity("drift", got_first, got_second)
    lanes = slice(128 * field, 128 * (field + 1))
    build_window(window, 0, lambda z: wide_plane(hb, low, high, z, lanes))
    if flip:
        flip_blocks(weights, 0, *flipped)
        value = conv_flipped(window, *flipped)
    else:
        value = conv(window, weights, TAPS)
    result = (live[...].astype(jnp.float32) * (base[:, lanes].astype(jnp.float32) + value)).astype(jnp.bfloat16)
    slots = position_slots(lists, counts)
    count = output.shape[0]
    pieces = []
    row = iota((count, 128), 0)
    for c in range(ROWS // 128):
        col = iota((8, 128), 1) + 128 * c
        z = (col >= PLANE).astype(jnp.int32) + (col >= 2 * PLANE) + (col >= 3 * PLANE)
        rest = col - PLANE * z
        x, j = rest >> 4, rest & 15
        source = slot_rows(slots, z, x, j - 1, (j >= 1) & (j <= NY))
        source = jnp.broadcast_to(source[0:1, :], (count, 128))
        pieces.append(jnp.where(row == source, 1.0, 0.0).astype(jnp.bfloat16))
    output[...] = dot(jnp.concatenate(pieces, axis=1), result).astype(jnp.bfloat16)
    done[...] = jnp.zeros_like(done)


def pairs(value_first, value_second, axis):
    drift, wire = lax.axis_size("drift"), lax.axis_size("wire")
    count = lax.axis_size(axis)
    first = [(i, i ^ 1) for i in range(count) if i ^ 1 < count]
    second = {i: i + 1 if i % 2 else i - 1 for i in range(1, count - 1)}
    if axis == "drift":
        second.update({0: count - 1, count - 1: 0})
        got_second = lax.ppermute(value_second, axis, sorted(second.items()))
    else:
        moves = [
            (d * wire + w, d * wire + second[w] if w in second else (d ^ 1) * wire + w)
            for d in range(drift)
            for w in range(wire)
        ]
        got_second = lax.ppermute(value_second, ("drift", "wire"), moves)
    got_first = lax.ppermute(value_first, axis, first)
    return got_first, got_second


def on_device(features, first_weight, second_weight, cotangent, counts, kernel_map, send_lists):
    drift, wire = lax.axis_size("drift"), lax.axis_size("wire")
    chips = drift // 2
    blocks = -(-TAPS // chips)
    chunk = blocks * CHANNELS
    unit = chunk // wire
    rows = TAPS * CHANNELS
    f, g = features[0, 0], cotangent[0, 0]
    slots = f.shape[0]
    padded = -(-slots // 128) * 128
    conv_scratch = [pltpu.VMEM((4, WIDE, 1152), jnp.bfloat16), pltpu.VMEM((128, rows), jnp.bfloat16)]
    faces_scratch = pltpu.VMEM((128, 256), jnp.bfloat16)
    face, slab, grid = bf16(FACE, 256), bf16(SLAB, 256), bf16(ROWS, 256)

    def swap_core(value):
        return lax.ppermute(value, "drift", [(i, i ^ 1) for i in range(drift)])

    def to_chip(value, step):
        return lax.ppermute(value, "drift", [(i, i ^ (2 * step)) for i in range(drift)])

    def to_wire(value, step):
        return lax.ppermute(value, "wire", [(i, i ^ step) for i in range(wire)])

    pair = jnp.concatenate([f, g], axis=1)
    weights = jnp.concatenate([first_weight, second_weight], axis=0)
    *faces, placed, live = call(
        place_kernel,
        (face, face, grid, bf16(ROWS, 128)),
        [SMEM] * 2 + [VMEM],
        [pltpu.VMEM((padded, 256), jnp.bfloat16)],
    )(counts, send_lists, pair)
    faces = pairs(*faces, "wire")
    full, *slabs = call(insert_faces, (grid, slab, slab), [VMEM] * 3, [faces_scratch])(placed, *faces)
    slabs = pairs(*slabs, "drift")
    message = bf16(ROWS + 4 * WIDE, 128)
    inner = call(inner_kernel, f32(ROWS, 128), [VMEM] * 2, conv_scratch[:1])(full, weights)
    hb, keep, send = call(
        first_kernel,
        (grid, message, message),
        [VMEM] * 6,
        conv_scratch + [pltpu.VMEM((4, J, 1152), jnp.bfloat16), pltpu.VMEM((ROWS, 128), jnp.float32)],
    )(full, *slabs, live, weights, inner)
    got = swap_core(send)
    term_window = pltpu.VMEM((4, WIDE, 1152), jnp.bfloat16)
    terms = f32(chunk * chips, 128)
    own_terms = call(own_terms_kernel, terms, [VMEM], [term_window])(keep)
    *sends, own, face_first, face_second = call(
        functools.partial(terms_kernel, chunk),
        tuple([bf16(chunk, 128)] * (chips - 1) + [f32(chunk, 128), face, face]),
        [VMEM] * 3,
        [term_window, pltpu.VMEM(terms.shape, jnp.float32)],
    )(own_terms, got, hb)
    parts = [to_chip(s, k + 1) for k, s in enumerate(sends)]
    faces = pairs(face_first, face_second, "wire")
    hb_full, *hb_slabs = call(insert_faces, (grid, slab, slab), [VMEM] * 3, [faces_scratch])(hb, *faces)
    inserted = hb_slabs[0]
    hb_slabs = pairs(*hb_slabs, "drift")
    def second(field, flip):
        return call(
            functools.partial(second_kernel, field, flip),
            (bf16(slots, 128), f32(8, 128)),
            [SMEM] * 2 + [VMEM] * 6,
            conv_scratch if flip else conv_scratch[:1],
        )(send_lists, counts, hb_full, *hb_slabs, full, live, weights)

    grad_features, grad_done = second(1, True)
    output, output_done = second(0, False)
    *sends, own = call(
        functools.partial(split_kernel, unit, chips - 1),
        tuple([bf16(unit, 128)] * (wire - 1) + [f32(unit, 128)]),
        [VMEM] * (1 + chips),
        [pltpu.VMEM((chunk, 128), jnp.float32)],
    )(inserted, own, *parts)

    received = [to_wire(s, k + 1) for k, s in enumerate(sends)]
    scale = 1.0 / math.sqrt(float(drift * wire * slots))
    summed = call(functools.partial(sum_kernel, scale), bf16(unit, 128), [VMEM] * (2 + wire))(
        *hb_slabs, own, *received
    )
    pieces = [summed] + [to_wire(summed, k) for k in range(1, wire)]
    mine = call(functools.partial(joined_kernel, unit), bf16(chunk, 128), [VMEM] * (1 + wire))(grad_done, *pieces)
    mine = [mine] + [to_chip(mine, k) for k in range(1, chips)]
    grads = ()
    early = max(1, chips - 2)
    for steps in [tuple(range(early))] + [(k,) for k in range(early, chips)]:
        staged = blocks * len(steps)
        grads = call(
            functools.partial(final_kernel, steps, blocks),
            (f32(TAPS, 128, 128), f32(TAPS, 128, 128)),
            [VMEM] * (1 + 2 * len(steps)) + [HBM] * len(grads),
            [pltpu.VMEM((2, staged, 128, 128), jnp.float32), pltpu.SemaphoreType.DMA((2, staged))],
            50 * 10**9,
            HBM,
            {1 + 2 * len(steps): 0, 2 + 2 * len(steps): 1} if grads else {},
        )(output_done, *(mine[k] for k in steps), *(swap_core(mine[k]) for k in steps), *grads)
    grad_first, grad_second = grads
    return output[None, None], grad_features[None, None], grad_first, grad_second


def solution(mesh):
    placed = (
        P("drift", "wire", None, None),
        P(),
        P(),
        P("drift", "wire", None, None),
        P("drift", "wire"),
        P("drift", "wire", None, None),
        P("drift", "wire", None),
    )
    return jax.shard_map(
        on_device,
        mesh=mesh,
        in_specs=placed,
        out_specs=(P("drift", "wire", None, None), P("drift", "wire", None, None), P(), P()),
        check_vma=False,
    )
```

time: 79.8 us -> 70 us (0.88)
  starting transfers between devices: 33.3 us -> 29.5 us
  local copies, waits for them, and re-layouts: 4.82 us -> 2.02 us
  Pallas kernels: 21.2 us -> 18.9 us
  waiting for transfers between devices: 18.5 us -> 16.7 us
  other arithmetic: 0 us -> 1.02 us
    unnamed x16 -> x7, local copies, waits for them, and re-layouts: 4.82 us -> 1.91 us
    ppermute x4, waiting for transfers between devices: 3.86 us -> 1.6 us  [the longest x2 1.6 us: pairs(): got_second = lax.ppermute(value_second, axis, sorted(second.items()))]
    ppermute x4, starting transfers between devices: 7.62 us -> 5.87 us  [pairs(): got_first = lax.ppermute(value_first, axis, first)]
    pallas_call x9 -> x8, Pallas kernels: 11.5 us -> 9.93 us  [the longest x3 3.88 us: on_device(): call(functools.partial(final_kernel, steps, blocks), (f32(TAPS, 128, 128)...]
    ppermute x4, waiting for transfers between devices: 0.97 us -> 2.35 us  [pairs(): got_first = lax.ppermute(value_first, axis, first)]
    ppermute x6, waiting for transfers between devices: 9.78 us -> 11.1 us  [to_chip(): lax.ppermute(value, 'drift', [(i, i ^ 2 * step) for i in range(drift)])]
    ppermute x5, waiting for transfers between devices: 1.77 us -> 0.64 us  [swap_core(): return lax.ppermute(value, 'drift', [(i, i ^ 1) for i in range(drift)])]
    concatenate x0 -> x1, other arithmetic: none -> 1.02 us  [on_device(): pair = jnp.concatenate([f, g], axis=1)]
  transfers between devices with their start and end apart: 25 -> 25, of which waited for: 8 -> 10; matrix products, arithmetic and copies ran while one was open for 0% -> 2% of each run, Pallas kernels for 15% -> 18%
where the time goes in v2:
time: 70 us; the launch traced here: 69.8 us
  starting transfers between devices  29.5 us (42%)
  Pallas kernels  18.9 us (27%)
  waiting for transfers between devices  16.7 us (24%)
  local copies, waits for them, and re-layouts  2.02 us (3%)
  between operations  1.61 us (2%)
  other arithmetic  1.02 us (1%)
    ppermute x6, waiting for transfers between devices, to_chip(): lax.ppermute(value, 'drift', [(i, i ^ 2 * step) for i in range(drift)])  11.1 us
    ppermute x6, starting transfers between devices, to_wire(): return lax.ppermute(value, 'wire', [(i, i ^ step) for i in range(wire)])  10.1 us
    ppermute x6, starting transfers between devices, to_chip(): lax.ppermute(value, 'drift', [(i, i ^ 2 * step) for i in range(drift)])  7.11 us
    pallas_call x2, Pallas kernels, second(): call(functools.partial(second_kernel, field, flip), (bf16(slots, 128), f3...  7.08 us
    ppermute x4, starting transfers between devices, pairs(): got_first = lax.ppermute(value_first, axis, first)  5.87 us
    ppermute x2, starting transfers between devices, pairs(): got_second = lax.ppermute(value_second, axis, sorted(second.items()))  5.75 us
    pallas_call x3, Pallas kernels, on_device(): call(functools.partial(final_kernel, steps, blocks), (f32(TAPS, 128, 128)...  3.88 us
    ppermute x4, waiting for transfers between devices, pairs(): got_first = lax.ppermute(value_first, axis, first)  2.35 us
  transfers between devices with their start and end apart: 25, of which 10 were waited for; matrix products, arithmetic and copies ran while one was open for 2% of the time, Pallas kernels for 18%

profile of v2, /device:TPU:0, one launch (start us, length us, event | category | flops | bytes accessed | tf_op | source)
XLA Modules:
  0.0 69.8 jit_solution(1558093807700399837)
XLA Ops:
  1.3 1.0 %pad_maximum_fusion.pair = bf16[576,256]{1,0:T(8,128)(2,1)S(1)} fusion(bf16[576,128]{1,0:T(8,128)(2,1)} %bitcast.4, bf16[576,128]{1,0:T(8,128)(2,1)} %bitcast.5), kind=kLoop, calls=%fused_computation | loop fusion | flops 589824 | bytes 589824 | tf_op jit(solution)/shard_map/concatenate | solution.py:421
  3.0 1.1 %shard_map.93 = (bf16[48,256]{1,0:T(8,128)(2,1)S(1)}, bf16[48,256]{1,0:T(8,128)(2,1)S(1)}, bf16[768,256]{1,0:T(8,128)(2,1)S(1)}, bf16[768,128]{1,0:T(8,128)(2,1)S(1)}) custom-call(s32[1,1]{1,0:T(1,128)S(6)} %copy.19.counts, s32[1,1,16]{2,1,0:T(1,128)S(1)} %copy-done, bf16[576,256]{1,0:T(8,128)(2,1)S(1)} %pad_maximum_fusion.pair), custom_call_target="tpu_custom_call" | custom-call | tf_op jit(solution)/shard_map/pallas_call | solution.py:423
  4.1 3.1 %collective-permute-start = (bf16[48,256]{1,0:T(8,128)(2,1)S(1)}, bf16[48,256]{1,0:T(8,128)(2,1)S(1)}, u32[]{:S(2)}, u32[]{:S(2)}) collective-permute-start(bf16[48,256]{1,0:T(8,128)(2,1)S(1)} %get-tuple-element.38), channel_id=1, source_target_pairs={{0,1},{1,0},{2,3},{3,2},{4,5},{5,4},{6,7},{7,6},{8,9},{9,8},{10,11... | collective-permute-start | bytes 73736 | tf_op jit(solution)/shard_map/ppermute | solution.py:394
  7.2 1.2 %constant_dynamic-update-slice_fusion.1 = bf16[54,128,128]{2,1,0:T(8,128)(2,1)S(1)} fusion(bf16[27,128,128]{2,1,0:T(8,128)(2,1)} %param.8), kind=kLoop, calls=%fused_computation.2 | loop fusion | bytes 1769472
  9.3 3.0 %collective-permute-start.3 = (bf16[64,256]{1,0:T(8,128)(2,1)S(1)}, bf16[64,256]{1,0:T(8,128)(2,1)S(1)}, u32[]{:S(2)}, u32[]{:S(2)}) collective-permute-start(bf16[64,256]{1,0:T(8,128)(2,1)S(1)} %get-tuple-element.42), channel_id=1, source_target_pairs={{0,28},{4,8},{8,4},{12,16},{16,12},{20,24},{24,20},{28,0},{1,29},{... | collective-permute-start | bytes 98312 | tf_op jit(solution)/shard_map/ppermute | solution.py:386
  12.5 1.6 %shard_map.95.inner = f32[768,128]{1,0:T(8,128)S(1)} custom-call(bf16[768,256]{1,0:T(8,128)(2,1)S(1)} %get-tuple-element.40.full.base, bf16[54,128,128]{2,1,0:T(8,128)(2,1)S(1)} %constant_dynamic-update-slice_fusion.weights), custom_call_target="tpu_custom_call" | custom-call | tf_op jit(solution)/shard_map/pallas_call | solution.py:433
  14.1 2.1 %shard_map.96 = (bf16[768,256]{1,0:T(8,128)(2,1)S(1)}, bf16[1664,128]{1,0:T(8,128)(2,1)S(1)}, bf16[1664,128]{1,0:T(8,128)(2,1)S(1)}) custom-call(bf16[768,256]{1,0:T(8,128)(2,1)S(1)} %get-tuple-element.40.full.base, bf16[64,256]{1,0:T(8,128)(2,1)S(1)} %collective-permute-done.2.got_first, bf16[64,256]{1,0:T(8,128)(2,1)S(1)} %collective-permute-done.3.got_second, ...), custom_call_target="tpu_custom_call" | custom-call | tf_op jit(solution)/shard_map/pallas_call | solution.py:434
  16.3 1.1 %shard_map.97.mine = f32[3584,128]{1,0:T(8,128)S(1)} custom-call(bf16[1664,128]{1,0:T(8,128)(2,1)S(1)} %get-tuple-element.45.mine), custom_call_target="tpu_custom_call" | custom-call | tf_op jit(solution)/shard_map/pallas_call | solution.py:443
  18.1 1.2 %shard_map.98 = (bf16[896,128]{1,0:T(8,128)(2,1)S(1)}, bf16[896,128]{1,0:T(8,128)(2,1)S(1)}, bf16[896,128]{1,0:T(8,128)(2,1)S(1)}, f32[896,128]{1,0:T(8,128)S(1)...) custom-call(f32[3584,128]{1,0:T(8,128)S(1)} %shard_map.97.mine, ...), custom_call_target="tpu_custom_call" | custom-call | tf_op jit(solution)/shard_map/pallas_call | solution.py:444
  19.3 1.6 %collective-permute-start.10 = (bf16[896,128]{1,0:T(8,128)(2,1)S(1)}, bf16[896,128]{1,0:T(8,128)(2,1)S(1)}, u32[]{:S(2)}, u32[]{:S(2)}) collective-permute-start(bf16[896,128]{1,0:T(8,128)(2,1)S(1)} %get-tuple-element.58), channel_id=1, source_target_pairs={{0,16},{4,20},{8,24},{12,28},{16,0},{20,4},{24,8},{28,12},{1,17},{... | collective-permute-start | bytes 688136 | tf_op jit(solution)/shard_map/ppermute | solution.py:416
  20.9 1.5 %collective-permute-start.11 = (bf16[896,128]{1,0:T(8,128)(2,1)S(1)}, bf16[896,128]{1,0:T(8,128)(2,1)S(1)}, u32[]{:S(2)}, u32[]{:S(2)}) collective-permute-start(bf16[896,128]{1,0:T(8,128)(2,1)S(1)} %get-tuple-element.59), channel_id=1, source_target_pairs={{0,24},{4,28},{8,16},{12,20},{16,8},{20,12},{24,0},{28,4},{1,25},{... | collective-permute-start | bytes 688136 | tf_op jit(solution)/shard_map/ppermute | solution.py:416
  22.9 2.7 %collective-permute-start.5 = (bf16[48,256]{1,0:T(8,128)(2,1)S(1)}, bf16[48,256]{1,0:T(8,128)(2,1)S(1)}, u32[]{:S(2)}, u32[]{:S(2)}) collective-permute-start(bf16[48,256]{1,0:T(8,128)(2,1)S(1)} %get-tuple-element.47), channel_id=1, source_target_pairs={{0,1},{1,0},{2,3},{3,2},{4,5},{5,4},{6,7},{7,6},{8,9},{9,8},{10,11... | collective-permute-start | bytes 73736 | tf_op jit(solution)/shard_map/ppermute | solution.py:394
  25.6 1.8 %collective-permute-done.5.got_first = bf16[48,256]{1,0:T(8,128)(2,1)S(1)} collective-permute-done((bf16[48,256]{1,0:T(8,128)(2,1)S(1)}, bf16[48,256]{1,0:T(8,128)(2,1)S(1)}, u32[]{:S(2)}, u32[]{:S(2)}) %collective-permute-start.5) | collective-permute-done | bytes 24608 | tf_op jit(solution)/shard_map/ppermute | solution.py:394
  27.7 4.3 %collective-permute-done.10.refs_1_ = bf16[896,128]{1,0:T(8,128)(2,1)S(1)} collective-permute-done((bf16[896,128]{1,0:T(8,128)(2,1)S(1)}, bf16[896,128]{1,0:T(8,128)(2,1)S(1)}, u32[]{:S(2)}, u32[]{:S(2)}) %collective-permute-start.10) | collective-permute-done | bytes 229408 | tf_op jit(solution)/shard_map/ppermute | solution.py:416
  32.0 1.3 %collective-permute-done.9.refs_0_ = bf16[896,128]{1,0:T(8,128)(2,1)S(1)} collective-permute-done((bf16[896,128]{1,0:T(8,128)(2,1)S(1)}, bf16[896,128]{1,0:T(8,128)(2,1)S(1)}, u32[]{:S(2)}, u32[]{:S(2)}) %collective-permute-start.9) | collective-permute-done | bytes 229408 | tf_op jit(solution)/shard_map/ppermute | solution.py:416
  33.5 2.8 %collective-permute-start.12 = (bf16[224,128]{1,0:T(8,128)(2,1)S(1)}, bf16[224,128]{1,0:T(8,128)(2,1)S(1)}, u32[]{:S(2)}, u32[]{:S(2)}) collective-permute-start(bf16[224,128]{1,0:T(8,128)(2,1)S(1)} %get-tuple-element.61), channel_id=1, source_target_pairs={{0,1},{1,0},{2,3},{3,2},{4,5},{5,4},{6,7},{7,6},{8,9},{9,8},{10,11... | collective-permute-start | bytes 172040 | tf_op jit(solution)/shard_map/ppermute | solution.py:419
  36.2 1.5 %collective-permute-start.13 = (bf16[224,128]{1,0:T(8,128)(2,1)S(1)}, bf16[224,128]{1,0:T(8,128)(2,1)S(1)}, u32[]{:S(2)}, u32[]{:S(2)}) collective-permute-start(bf16[224,128]{1,0:T(8,128)(2,1)S(1)} %get-tuple-element.62), channel_id=1, source_target_pairs={{0,2},{1,3},{2,0},{3,1},{4,6},{5,7},{6,4},{7,5},{8,10},{9,11},{10,... | collective-permute-start | bytes 172040 | tf_op jit(solution)/shard_map/ppermute | solution.py:419
  37.8 1.4 %collective-permute-start.14 = (bf16[224,128]{1,0:T(8,128)(2,1)S(1)}, bf16[224,128]{1,0:T(8,128)(2,1)S(1)}, u32[]{:S(2)}, u32[]{:S(2)}) collective-permute-start(bf16[224,128]{1,0:T(8,128)(2,1)S(1)} %get-tuple-element.63), channel_id=1, source_target_pairs={{0,3},{1,2},{2,1},{3,0},{4,7},{5,6},{6,5},{7,4},{8,11},{9,10},{10,... | collective-permute-start | bytes 172040 | tf_op jit(solution)/shard_map/ppermute | solution.py:419
  39.2 2.8 %collective-permute-start.8 = (bf16[64,256]{1,0:T(8,128)(2,1)S(1)}, bf16[64,256]{1,0:T(8,128)(2,1)S(1)}, u32[]{:S(2)}, u32[]{:S(2)}) collective-permute-start(bf16[64,256]{1,0:T(8,128)(2,1)S(1)} %get-tuple-element.51), channel_id=1, source_target_pairs={{0,28},{4,8},{8,4},{12,16},{16,12},{20,24},{24,20},{28,0},{1,29},{... | collective-permute-start | bytes 98312 | tf_op jit(solution)/shard_map/ppermute | solution.py:386
  41.9 1.6 %collective-permute-done.8.got_second.after_second = bf16[64,256]{1,0:T(8,128)(2,1)S(1)} collective-permute-done((bf16[64,256]{1,0:T(8,128)(2,1)S(1)}, bf16[64,256]{1,0:T(8,128)(2,1)S(1)}, u32[]{:S(2)}, u32[]{:S(2)}) %collective-permute-start.8) | collective-permute-done | bytes 32800 | tf_op jit(solution)/shard_map/ppermute | solution.py:386
  43.9 0.8 %collective-permute-start.15 = (bf16[224,128]{1,0:T(8,128)(2,1)S(1)}, bf16[224,128]{1,0:T(8,128)(2,1)S(1)}, u32[]{:S(2)}, u32[]{:S(2)}) collective-permute-start(bf16[224,128]{1,0:T(8,128)(2,1)S(1)} %shard_map.103.refs_0_), channel_id=1, source_target_pairs={{0,1},{1,0},{2,3},{3,2},{4,5},{5,4},{6,7},{7,6},{8,9},{9,8},{10,11... | collective-permute-start | bytes 172040 | tf_op jit(solution)/shard_map/ppermute | solution.py:419
  44.7 1.9 %collective-permute-start.16 = (bf16[224,128]{1,0:T(8,128)(2,1)S(1)}, bf16[224,128]{1,0:T(8,128)(2,1)S(1)}, u32[]{:S(2)}, u32[]{:S(2)}) collective-permute-start(bf16[224,128]{1,0:T(8,128)(2,1)S(1)} %shard_map.103.refs_0_), channel_id=1, source_target_pairs={{0,2},{1,3},{2,0},{3,1},{4,6},{5,7},{6,4},{7,5},{8,10},{9,11},{10,... | collective-permute-start | bytes 172040 | tf_op jit(solution)/shard_map/ppermute | solution.py:419
  46.6 1.7 %collective-permute-start.17 = (bf16[224,128]{1,0:T(8,128)(2,1)S(1)}, bf16[224,128]{1,0:T(8,128)(2,1)S(1)}, u32[]{:S(2)}, u32[]{:S(2)}) collective-permute-start(bf16[224,128]{1,0:T(8,128)(2,1)S(1)} %shard_map.103.refs_0_), channel_id=1, source_target_pairs={{0,3},{1,2},{2,1},{3,0},{4,7},{5,6},{6,5},{7,4},{8,11},{9,10},{10,... | collective-permute-start | bytes 172040 | tf_op jit(solution)/shard_map/ppermute | solution.py:419
  48.3 3.6 %shard_map.101 = (bf16[576,128]{1,0:T(8,128)(2,1)}, f32[8,128]{1,0:T(8,128)S(1)}) custom-call(s32[1,1,16]{2,1,0:T(1,128)S(1)} %copy-done.1, s32[1,1]{1,0:T(1,128)S(6)} %copy.19.counts, bf16[768,256]{1,0:T(8,128)(2,1)S(1)} %get-tuple-element.49.hb, bf16[64,256]{1,0:T(8,128)(2,1)S(1)} %collective-permute-done.7.got_first.after_first, ...), custom_call_target="tpu_custom_call" | custom-call | tf_op jit(solution)/shard_map/pallas_call | solution.py:456
  52.0 0.8 %collective-permute-done.17.refs_3_ = bf16[224,128]{1,0:T(8,128)(2,1)S(1)} collective-permute-done((bf16[224,128]{1,0:T(8,128)(2,1)S(1)}, bf16[224,128]{1,0:T(8,128)(2,1)S(1)}, u32[]{:S(2)}, u32[]{:S(2)}) %collective-permute-start.17) | collective-permute-done | bytes 57376 | tf_op jit(solution)/shard_map/ppermute | solution.py:419
  52.7 1.7 %collective-permute-start.22 = (bf16[896,128]{1,0:T(8,128)(2,1)S(1)}, bf16[896,128]{1,0:T(8,128)(2,1)S(1)}, u32[]{:S(2)}, u32[]{:S(2)}) collective-permute-start(bf16[896,128]{1,0:T(8,128)(2,1)S(1)} %shard_map.104.refs_0_), channel_id=1, source_target_pairs={{0,8},{4,12},{8,0},{12,4},{16,24},{20,28},{24,16},{28,20},{1,9},{5... | collective-permute-start | bytes 688136 | tf_op jit(solution)/shard_map/ppermute | solution.py:416
  54.4 1.5 %collective-permute-start.20 = (bf16[896,128]{1,0:T(8,128)(2,1)S(1)}, bf16[896,128]{1,0:T(8,128)(2,1)S(1)}, u32[]{:S(2)}, u32[]{:S(2)}) collective-permute-start(bf16[896,128]{1,0:T(8,128)(2,1)S(1)} %shard_map.104.refs_0_), channel_id=1, source_target_pairs={{0,16},{4,20},{8,24},{12,28},{16,0},{20,4},{24,8},{28,12},{1,17},{... | collective-permute-start | bytes 688136 | tf_op jit(solution)/shard_map/ppermute | solution.py:416
  56.3 4.8 %collective-permute-done.22.refs_1_ = bf16[896,128]{1,0:T(8,128)(2,1)S(1)} collective-permute-done((bf16[896,128]{1,0:T(8,128)(2,1)S(1)}, bf16[896,128]{1,0:T(8,128)(2,1)S(1)}, u32[]{:S(2)}, u32[]{:S(2)}) %collective-permute-start.22) | collective-permute-done | bytes 229408 | tf_op jit(solution)/shard_map/ppermute | solution.py:416
  61.1 3.5 %shard_map.100 = (bf16[576,128]{1,0:T(8,128)(2,1)}, f32[8,128]{1,0:T(8,128)S(1)}) custom-call(s32[1,1,16]{2,1,0:T(1,128)S(1)} %copy-done.1, s32[1,1]{1,0:T(1,128)S(6)} %copy.19.counts, bf16[768,256]{1,0:T(8,128)(2,1)S(1)} %get-tuple-element.49.hb, bf16[64,256]{1,0:T(8,128)(2,1)S(1)} %collective-permute-done.7.got_first.after_first, ...), custom_call_target="tpu_custom_call" | custom-call | tf_op jit(solution)/shard_map/pallas_call | solution.py:456
  65.7 1.6 %shard_map.105 = (f32[27,128,128]{2,1,0:T(8,128)}, f32[27,128,128]{2,1,0:T(8,128)}) custom-call(f32[8,128]{1,0:T(8,128)S(1)} %get-tuple-element.54.after, bf16[896,128]{1,0:T(8,128)(2,1)S(1)} %shard_map.104.refs_0_, bf16[896,128]{1,0:T(8,128)(2,1)S(1)} %collective-permute-done.22.refs_1_, bf16[896,128]{1,0:T(8,128)(2,1)S(1)} %collective-permute-done.23.refs_2_, ...), custom_call_target="tpu_custom_call" | custom-call | flops 49999998976 | tf_op jit(solution)/shard_map/pallas_call | solution.py:484
  67.4 1.2 %shard_map.106 = (f32[27,128,128]{2,1,0:T(8,128)}, f32[27,128,128]{2,1,0:T(8,128)}) custom-call(f32[8,128]{1,0:T(8,128)S(1)} %get-tuple-element.54.after, bf16[896,128]{1,0:T(8,128)(2,1)S(1)} %collective-permute-done.20.refs_0_, bf16[896,128]{1,0:T(8,128)(2,1)S(1)} %collective-permute-done.21.refs_1_, ...), custom_call_target="tpu_custom_call", output_to_operand_aliasing={{0}: (3, {}), {1}: (4, {})} | custom-call | flops 49999998976 | tf_op jit(solution)/shard_map/pallas_call | solution.py:484
  68.5 1.1 %shard_map.107 = (f32[27,128,128]{2,1,0:T(8,128)}, f32[27,128,128]{2,1,0:T(8,128)}) custom-call(f32[8,128]{1,0:T(8,128)S(1)} %get-tuple-element.54.after, bf16[896,128]{1,0:T(8,128)(2,1)S(1)} %collective-permute-done.18.refs_0_, bf16[896,128]{1,0:T(8,128)(2,1)S(1)} %collective-permute-done.19.refs_1_, ...), custom_call_target="tpu_custom_call", output_to_operand_aliasing={{0}: (3, {}), {1}: (4, {})} | custom-call | flops 49999998976 | tf_op jit(solution)/shard_map/pallas_call | solution.py:484
  (42 shorter events, 5.2 us)
Async XLA Ops:
  2.3 0.7 copy-start
  3.0 9.4 %copy-start.2 = (bf16[27,128,128]{2,1,0:T(8,128)(2,1)S(1)}, bf16[27,128,128]{2,1,0:T(8,128)(2,1)}, u32[]{:S(2)}) copy-start(bf16[27,128,128]{2,1,0:T(8,128)(2,1)} %param.9) | copy-start | bytes 2654212
  4.1 4.9 %collective-permute-start = (bf16[48,256]{1,0:T(8,128)(2,1)S(1)}, bf16[48,256]{1,0:T(8,128)(2,1)S(1)}, u32[]{:S(2)}, u32[]{:S(2)}) collective-permute-start(bf16[48,256]{1,0:T(8,128)(2,1)S(1)} %get-tuple-element.38), channel_id=1, source_target_pairs={{0,1},{1,0},{2,3},{3,2},{4,5},{5,4},{6,7},{7,6},{8,9},{9,8},{10,11... | collective-permute-start | bytes 73736 | tf_op jit(solution)/shard_map/ppermute | solution.py:394
  7.2 1.8 %collective-permute-start.1 = (bf16[48,256]{1,0:T(8,128)(2,1)S(1)}, bf16[48,256]{1,0:T(8,128)(2,1)S(1)}, u32[]{:S(2)}, u32[]{:S(2)}) collective-permute-start(bf16[48,256]{1,0:T(8,128)(2,1)S(1)} %get-tuple-element.39), channel_id=1, source_target_pairs={{0,4},{1,2},{2,1},{3,7},{4,0},{5,6},{6,5},{7,3},{8,12},{9,10},{10,... | collective-permute-start | bytes 73736 | tf_op jit(solution)/shard_map/ppermute | solution.py:393
  9.3 4.8 %collective-permute-start.2 = (bf16[64,256]{1,0:T(8,128)(2,1)S(1)}, bf16[64,256]{1,0:T(8,128)(2,1)S(1)}, u32[]{:S(2)}, u32[]{:S(2)}) collective-permute-start(bf16[64,256]{1,0:T(8,128)(2,1)S(1)} %get-tuple-element.41), channel_id=1, source_target_pairs={{0,4},{4,0},{8,12},{12,8},{16,20},{20,16},{24,28},{28,24},{1,5},{5... | collective-permute-start | bytes 98312 | tf_op jit(solution)/shard_map/ppermute | solution.py:394
  9.3 4.8 %collective-permute-start.3 = (bf16[64,256]{1,0:T(8,128)(2,1)S(1)}, bf16[64,256]{1,0:T(8,128)(2,1)S(1)}, u32[]{:S(2)}, u32[]{:S(2)}) collective-permute-start(bf16[64,256]{1,0:T(8,128)(2,1)S(1)} %get-tuple-element.42), channel_id=1, source_target_pairs={{0,28},{4,8},{8,4},{12,16},{16,12},{20,24},{24,20},{28,0},{1,29},{... | collective-permute-start | bytes 98312 | tf_op jit(solution)/shard_map/ppermute | solution.py:386
  16.3 1.8 %collective-permute-start.4 = (bf16[1664,128]{1,0:T(8,128)(2,1)S(1)}, bf16[1664,128]{1,0:T(8,128)(2,1)S(1)}, u32[]{:S(2)}, u32[]{:S(2)}) collective-permute-start(bf16[1664,128]{1,0:T(8,128)(2,1)S(1)} %get-tuple-element.46), channel_id=1, source_target_pairs={{0,4},{4,0},{8,12},{12,8},{16,20},{20,16},{24,28},{28,24},{1,5},{5... | collective-permute-start | bytes 1277960 | tf_op jit(solution)/shard_map/ppermute | solution.py:413
  18.1 30.3 %copy-start.1 = (s32[1,1,16]{2,1,0:T(1,128)S(1)}, s32[1,1,16]{2,1,0:T(1,128)}, u32[]{:S(2)}) copy-start(s32[1,1,16]{2,1,0:T(1,128)} %lists.5) | copy-start | bytes 196
  19.3 12.6 %collective-permute-start.10 = (bf16[896,128]{1,0:T(8,128)(2,1)S(1)}, bf16[896,128]{1,0:T(8,128)(2,1)S(1)}, u32[]{:S(2)}, u32[]{:S(2)}) collective-permute-start(bf16[896,128]{1,0:T(8,128)(2,1)S(1)} %get-tuple-element.58), channel_id=1, source_target_pairs={{0,16},{4,20},{8,24},{12,28},{16,0},{20,4},{24,8},{28,12},{1,17},{... | collective-permute-start | bytes 688136 | tf_op jit(solution)/shard_map/ppermute | solution.py:416
  20.9 11.0 %collective-permute-start.11 = (bf16[896,128]{1,0:T(8,128)(2,1)S(1)}, bf16[896,128]{1,0:T(8,128)(2,1)S(1)}, u32[]{:S(2)}, u32[]{:S(2)}) collective-permute-start(bf16[896,128]{1,0:T(8,128)(2,1)S(1)} %get-tuple-element.59), channel_id=1, source_target_pairs={{0,24},{4,28},{8,16},{12,20},{16,8},{20,12},{24,0},{28,4},{1,25},{... | collective-permute-start | bytes 688136 | tf_op jit(solution)/shard_map/ppermute | solution.py:416
  22.4 10.9 %collective-permute-start.9 = (bf16[896,128]{1,0:T(8,128)(2,1)S(1)}, bf16[896,128]{1,0:T(8,128)(2,1)S(1)}, u32[]{:S(2)}, u32[]{:S(2)}) collective-permute-start(bf16[896,128]{1,0:T(8,128)(2,1)S(1)} %get-tuple-element.57), channel_id=1, source_target_pairs={{0,8},{4,12},{8,0},{12,4},{16,24},{20,28},{24,16},{28,20},{1,9},{5... | collective-permute-start | bytes 688136 | tf_op jit(solution)/shard_map/ppermute | solution.py:416
  22.9 4.5 %collective-permute-start.5 = (bf16[48,256]{1,0:T(8,128)(2,1)S(1)}, bf16[48,256]{1,0:T(8,128)(2,1)S(1)}, u32[]{:S(2)}, u32[]{:S(2)}) collective-permute-start(bf16[48,256]{1,0:T(8,128)(2,1)S(1)} %get-tuple-element.47), channel_id=1, source_target_pairs={{0,1},{1,0},{2,3},{3,2},{4,5},{5,4},{6,7},{7,6},{8,9},{9,8},{10,11... | collective-permute-start | bytes 73736 | tf_op jit(solution)/shard_map/ppermute | solution.py:394
  25.6 1.8 %collective-permute-start.6 = (bf16[48,256]{1,0:T(8,128)(2,1)S(1)}, bf16[48,256]{1,0:T(8,128)(2,1)S(1)}, u32[]{:S(2)}, u32[]{:S(2)}) collective-permute-start(bf16[48,256]{1,0:T(8,128)(2,1)S(1)} %get-tuple-element.48), channel_id=1, source_target_pairs={{0,4},{1,2},{2,1},{3,7},{4,0},{5,6},{6,5},{7,3},{8,12},{9,10},{10,... | collective-permute-start | bytes 73736 | tf_op jit(solution)/shard_map/ppermute | solution.py:393
  33.5 10.1 %collective-permute-start.12 = (bf16[224,128]{1,0:T(8,128)(2,1)S(1)}, bf16[224,128]{1,0:T(8,128)(2,1)S(1)}, u32[]{:S(2)}, u32[]{:S(2)}) collective-permute-start(bf16[224,128]{1,0:T(8,128)(2,1)S(1)} %get-tuple-element.61), channel_id=1, source_target_pairs={{0,1},{1,0},{2,3},{3,2},{4,5},{5,4},{6,7},{7,6},{8,9},{9,8},{10,11... | collective-permute-start | bytes 172040 | tf_op jit(solution)/shard_map/ppermute | solution.py:419
  36.2 7.3 %collective-permute-start.13 = (bf16[224,128]{1,0:T(8,128)(2,1)S(1)}, bf16[224,128]{1,0:T(8,128)(2,1)S(1)}, u32[]{:S(2)}, u32[]{:S(2)}) collective-permute-start(bf16[224,128]{1,0:T(8,128)(2,1)S(1)} %get-tuple-element.62), channel_id=1, source_target_pairs={{0,2},{1,3},{2,0},{3,1},{4,6},{5,7},{6,4},{7,5},{8,10},{9,11},{10,... | collective-permute-start | bytes 172040 | tf_op jit(solution)/shard_map/ppermute | solution.py:419
  37.8 6.1 %collective-permute-start.14 = (bf16[224,128]{1,0:T(8,128)(2,1)S(1)}, bf16[224,128]{1,0:T(8,128)(2,1)S(1)}, u32[]{:S(2)}, u32[]{:S(2)}) collective-permute-start(bf16[224,128]{1,0:T(8,128)(2,1)S(1)} %get-tuple-element.63), channel_id=1, source_target_pairs={{0,3},{1,2},{2,1},{3,0},{4,7},{5,6},{6,5},{7,4},{8,11},{9,10},{10,... | collective-permute-start | bytes 172040 | tf_op jit(solution)/shard_map/ppermute | solution.py:419
  39.2 2.8 %collective-permute-start.7 = (bf16[64,256]{1,0:T(8,128)(2,1)S(1)}, bf16[64,256]{1,0:T(8,128)(2,1)S(1)}, u32[]{:S(2)}, u32[]{:S(2)}) collective-permute-start(bf16[64,256]{1,0:T(8,128)(2,1)S(1)} %get-tuple-element.50.after), channel_id=1, source_target_pairs={{0,4},{4,0},{8,12},{12,8},{16,20},{20,16},{24,28},{28,24},{1,5},{5... | collective-permute-start | bytes 98312 | tf_op jit(solution)/shard_map/ppermute | solution.py:394
  39.2 4.3 %collective-permute-start.8 = (bf16[64,256]{1,0:T(8,128)(2,1)S(1)}, bf16[64,256]{1,0:T(8,128)(2,1)S(1)}, u32[]{:S(2)}, u32[]{:S(2)}) collective-permute-start(bf16[64,256]{1,0:T(8,128)(2,1)S(1)} %get-tuple-element.51), channel_id=1, source_target_pairs={{0,28},{4,8},{8,4},{12,16},{16,12},{20,24},{24,20},{28,0},{1,29},{... | collective-permute-start | bytes 98312 | tf_op jit(solution)/shard_map/ppermute | solution.py:386
  43.9 8.1 %collective-permute-start.15 = (bf16[224,128]{1,0:T(8,128)(2,1)S(1)}, bf16[224,128]{1,0:T(8,128)(2,1)S(1)}, u32[]{:S(2)}, u32[]{:S(2)}) collective-permute-start(bf16[224,128]{1,0:T(8,128)(2,1)S(1)} %shard_map.103.refs_0_), channel_id=1, source_target_pairs={{0,1},{1,0},{2,3},{3,2},{4,5},{5,4},{6,7},{7,6},{8,9},{9,8},{10,11... | collective-permute-start | bytes 172040 | tf_op jit(solution)/shard_map/ppermute | solution.py:419
  44.7 7.3 %collective-permute-start.16 = (bf16[224,128]{1,0:T(8,128)(2,1)S(1)}, bf16[224,128]{1,0:T(8,128)(2,1)S(1)}, u32[]{:S(2)}, u32[]{:S(2)}) collective-permute-start(bf16[224,128]{1,0:T(8,128)(2,1)S(1)} %shard_map.103.refs_0_), channel_id=1, source_target_pairs={{0,2},{1,3},{2,0},{3,1},{4,6},{5,7},{6,4},{7,5},{8,10},{9,11},{10,... | collective-permute-start | bytes 172040 | tf_op jit(solution)/shard_map/ppermute | solution.py:419
  46.6 6.1 %collective-permute-start.17 = (bf16[224,128]{1,0:T(8,128)(2,1)S(1)}, bf16[224,128]{1,0:T(8,128)(2,1)S(1)}, u32[]{:S(2)}, u32[]{:S(2)}) collective-permute-start(bf16[224,128]{1,0:T(8,128)(2,1)S(1)} %shard_map.103.refs_0_), channel_id=1, source_target_pairs={{0,3},{1,2},{2,1},{3,0},{4,7},{5,6},{6,5},{7,4},{8,11},{9,10},{10,... | collective-permute-start | bytes 172040 | tf_op jit(solution)/shard_map/ppermute | solution.py:419
  52.7 8.4 %collective-permute-start.22 = (bf16[896,128]{1,0:T(8,128)(2,1)S(1)}, bf16[896,128]{1,0:T(8,128)(2,1)S(1)}, u32[]{:S(2)}, u32[]{:S(2)}) collective-permute-start(bf16[896,128]{1,0:T(8,128)(2,1)S(1)} %shard_map.104.refs_0_), channel_id=1, source_target_pairs={{0,8},{4,12},{8,0},{12,4},{16,24},{20,28},{24,16},{28,20},{1,9},{5... | collective-permute-start | bytes 688136 | tf_op jit(solution)/shard_map/ppermute | solution.py:416
  54.4 10.8 %collective-permute-start.20 = (bf16[896,128]{1,0:T(8,128)(2,1)S(1)}, bf16[896,128]{1,0:T(8,128)(2,1)S(1)}, u32[]{:S(2)}, u32[]{:S(2)}) collective-permute-start(bf16[896,128]{1,0:T(8,128)(2,1)S(1)} %shard_map.104.refs_0_), channel_id=1, source_target_pairs={{0,16},{4,20},{8,24},{12,28},{16,0},{20,4},{24,8},{28,12},{1,17},{... | collective-permute-start | bytes 688136 | tf_op jit(solution)/shard_map/ppermute | solution.py:416
  55.9 9.3 %collective-permute-start.18 = (bf16[896,128]{1,0:T(8,128)(2,1)S(1)}, bf16[896,128]{1,0:T(8,128)(2,1)S(1)}, u32[]{:S(2)}, u32[]{:S(2)}) collective-permute-start(bf16[896,128]{1,0:T(8,128)(2,1)S(1)} %shard_map.104.refs_0_), channel_id=1, source_target_pairs={{0,24},{4,28},{8,16},{12,20},{16,8},{20,12},{24,0},{28,4},{1,25},{... | collective-permute-start | bytes 688136 | tf_op jit(solution)/shard_map/ppermute | solution.py:416
  56.3 9.4 %collective-permute-start.23 = (bf16[896,128]{1,0:T(8,128)(2,1)S(1)}, bf16[896,128]{1,0:T(8,128)(2,1)S(1)}, u32[]{:S(2)}, u32[]{:S(2)}) collective-permute-start(bf16[896,128]{1,0:T(8,128)(2,1)S(1)} %shard_map.104.refs_0_), channel_id=1, source_target_pairs={{0,4},{4,0},{8,12},{12,8},{16,20},{20,16},{24,28},{28,24},{1,5},{5... | collective-permute-start | bytes 688136 | tf_op jit(solution)/shard_map/ppermute | solution.py:413
  61.1 4.6 %collective-permute-start.24 = (bf16[896,128]{1,0:T(8,128)(2,1)S(1)}, bf16[896,128]{1,0:T(8,128)(2,1)S(1)}, u32[]{:S(2)}, u32[]{:S(2)}) collective-permute-start(bf16[896,128]{1,0:T(8,128)(2,1)S(1)} %collective-permute-done.22.refs_1_), channel_id=1, source_target_pairs={{0,4},{4,0},{8,12},{12,8},{16,20},{20,16},{24,28},{28,24},{1,5},{5... | collective-permute-start | bytes 688136 | tf_op jit(solution)/shard_map/ppermute | solution.py:413
  65.2 2.1 %collective-permute-start.21 = (bf16[896,128]{1,0:T(8,128)(2,1)S(1)}, bf16[896,128]{1,0:T(8,128)(2,1)S(1)}, u32[]{:S(2)}, u32[]{:S(2)}) collective-permute-start(bf16[896,128]{1,0:T(8,128)(2,1)S(1)} %collective-permute-done.20.refs_0_), channel_id=1, source_target_pairs={{0,4},{4,0},{8,12},{12,8},{16,20},{20,16},{24,28},{28,24},{1,5},{5... | collective-permute-start | bytes 688136 | tf_op jit(solution)/shard_map/ppermute | solution.py:413
  65.2 3.3 %collective-permute-start.19 = (bf16[896,128]{1,0:T(8,128)(2,1)S(1)}, bf16[896,128]{1,0:T(8,128)(2,1)S(1)}, u32[]{:S(2)}, u32[]{:S(2)}) collective-permute-start(bf16[896,128]{1,0:T(8,128)(2,1)S(1)} %collective-permute-done.18.refs_0_), channel_id=1, source_target_pairs={{0,4},{4,0},{8,12},{12,8},{16,20},{20,16},{24,28},{28,24},{1,5},{5... | collective-permute-start | bytes 688136 | tf_op jit(solution)/shard_map/ppermute | solution.py:413

commit v3 on v2

--- a/solution.py
+++ b/solution.py
@@ -31,7 +31,7 @@
         kernel,
         out_shape=out_shape,
         in_specs=in_specs,
-        out_specs=jax.tree.map(lambda _: out_spec, out_shape),
+        out_specs=out_spec if isinstance(out_spec, tuple) else jax.tree.map(lambda _: out_spec, out_shape),
         scratch_shapes=list(scratch),
         input_output_aliases=aliases,
         compiler_params=pltpu.CompilerParams(vmem_limit_bytes=vmem * 1024 * 1024),
@@ -247,6 +247,13 @@
         write(send, hidden, g_lanes)
 
 
+def chip_mask(kind, core):
+    if isinstance(kind, int):
+        return kind
+    first = 1 + core
+    return {"own": 0, "first": first, "second": 3 - first, "opposite": 3}[kind]
+
+
 def add_terms(part, window, total, fresh):
     build_window(window, 0, lambda z: part[ROWS + z * WIDE : ROWS + (z + 1) * WIDE, :])
     left = part[0:ROWS, :].astype(jnp.float32).T.astype(jnp.bfloat16)
@@ -266,19 +273,26 @@
     add_terms(mine, window, total, True)
 
 
-def terms_kernel(chunk, mine, theirs, hb, *refs):
-    *sends, own, first, second, window, total = refs
+def terms_kernel(chunk, kinds, mine, theirs, hb, *refs):
+    *outs, first, second, window, total = refs
     total[...] = mine[...]
     add_terms(theirs, window, total, False)
-    me = lax.axis_index("drift") // 2
-    own[...] = total[pl.ds(pl.multiple_of(me * chunk, 16), chunk), :]
-    for step, out in enumerate(sends):
-        start = pl.multiple_of((me ^ (step + 1)) * chunk, 16)
-        out[...] = total[pl.ds(start, chunk), :].astype(jnp.bfloat16)
+    me, core = lax.axis_index("drift") // 2, lax.axis_index("drift") % 2
+    for kind, out in zip(kinds, outs):
+        start = pl.multiple_of((me ^ chip_mask(kind, core)) * chunk, 128)
+        out[...] = total[pl.ds(start, chunk), :].astype(out.dtype)
     z, x = face_indices()
     start = z * PLANE + x * J
     low, high = (dot(one_hot(start + j, ROWS), hb[...]).astype(jnp.bfloat16) for j in (1, NY))
     write_by_parity("wire", low, high, first, second)
+
+
+def passed_on_kernel(partial, received, out):
+    out[...] = (partial[...] + received[...].astype(jnp.float32)).astype(jnp.bfloat16)
+
+
+def relay_kernel(after, value, out):
+    out[...] = value[...]
 
 
 def split_kernel(unit, count, after, own, *refs):
@@ -294,7 +308,7 @@
         out[...] = total[pl.ds(start, unit), :].astype(jnp.bfloat16)
 
 
-def sum_kernel(scale, after_first, after_second, own, *refs):
+def sum_kernel(scale, after_inner, after_first, after_second, own, *refs):
     *received, out = refs
     summed = own[...]
     for part in received:
@@ -302,7 +316,7 @@
     out[...] = (summed * scale).astype(jnp.bfloat16)
 
 
-def joined_kernel(unit, after, *refs):
+def joined_kernel(unit, *refs):
     *parts, out = refs
     me = lax.axis_index("wire")
     for step, part in enumerate(parts):
@@ -310,56 +324,64 @@
         out[pl.ds(start, unit), :] = part[...]
 
 
-def final_kernel(steps, blocks, after, *refs):
-    mine, theirs = refs[: len(steps)], refs[len(steps) : 2 * len(steps)]
-    first, second, staged, sems = refs[-4:]
+def final_kernel(items, blocks, want_done, *refs):
+    parts = refs[: len(items)]
+    first, second, *done, staged, sems = refs[len(refs) - 4 - want_done :]
     me = lax.axis_index("drift") // 2
+    for ref in done:
+        ref[...] = jnp.zeros_like(ref)
+
+    def write(core):
+        copies = []
+        for part, (kind, mine) in zip(parts, items):
+            source = core if mine else 1 - core
+            value = part[...].astype(jnp.float32)
+            count, here = part.shape[0] // 128, len(copies)
+            for i in range(count):
+                block = value[128 * i : 128 * (i + 1), :]
+                staged[here + i] = block.T if source else block
+            chunk = me ^ chip_mask(kind, source)
+            for i in range(count):
+                tap = chunk * blocks + i
+                safe = jnp.minimum(tap, TAPS - 1)
+                to = first.at[safe] if source else second.at[TAPS - 1 - safe]
+                copies.append((tap < TAPS, pltpu.make_async_copy(staged.at[here + i], to, sems.at[here + i])))
+                pl.when(copies[-1][0])(copies[-1][1].start)
+        for used, copy in copies:
+            pl.when(used)(copy.wait)
+
     even = lax.axis_index("drift") % 2 == 0
-
-    def copies(n, i):
-        tap = (me ^ steps[n]) * blocks + i
-        here = n * blocks + i
-        safe = jnp.minimum(tap, TAPS - 1)
-        return tap < TAPS, (
-            pltpu.make_async_copy(staged.at[0, here], second.at[TAPS - 1 - safe], sems.at[0, here]),
-            pltpu.make_async_copy(staged.at[1, here], first.at[safe], sems.at[1, here]),
-        )
-
-    for n in range(len(steps)):
-        a, b = mine[n][...], theirs[n][...]
-        for_second = jnp.where(even, a, b).astype(jnp.float32)
-        for_first = jnp.where(even, b, a).astype(jnp.float32)
-        for i in range(blocks):
-            here = n * blocks + i
-            staged[0, here] = for_second[128 * i : 128 * (i + 1), :]
-            staged[1, here] = for_first[128 * i : 128 * (i + 1), :].T
-            used, pair = copies(n, i)
-
-            @pl.when(used)
-            def _():
-                for copy in pair:
-                    copy.start()
-
-    for n in range(len(steps)):
-        for i in range(blocks):
-            used, pair = copies(n, i)
-
-            @pl.when(used)
-            def _():
-                for copy in pair:
-                    copy.wait()
-
-
-def second_kernel(field, flip, lists, counts, hb, got_first, got_second, base, live, weights, output, done, window, *flipped):
+    pl.when(even)(lambda: write(0))
+    pl.when(jnp.logical_not(even))(lambda: write(1))
+
+
+def second_inner_kernel(hb, weights, inner, done, window, flipped):
+    edge = jnp.zeros((SLAB, 256), jnp.bfloat16)
+    flip_blocks(weights, 0, flipped)
+    build_window(window, 0, lambda z: wide_plane(hb, edge, edge, z, slice(0, 128)))
+    inner[0] = conv(window, weights, TAPS)
+    build_window(window, 0, lambda z: wide_plane(hb, edge, edge, z, slice(128, 256)))
+    inner[1] = conv_flipped(window, flipped)
+    done[...] = jnp.zeros_like(done)
+
+
+def second_kernel(
+    lists, counts, inner, got_first, got_second, base, live, weights, held, output, grad, passed, edge_window, pre, taps
+):
     low, high = read_by_parity("drift", got_first, got_second)
-    lanes = slice(128 * field, 128 * (field + 1))
-    build_window(window, 0, lambda z: wide_plane(hb, low, high, z, lanes))
-    if flip:
-        flip_blocks(weights, 0, *flipped)
-        value = conv_flipped(window, *flipped)
-    else:
-        value = conv(window, weights, TAPS)
-    result = (live[...].astype(jnp.float32) * (base[:, lanes].astype(jnp.float32) + value)).astype(jnp.bfloat16)
+    results = []
+    for field in (0, 1):
+        lanes = slice(128 * field, 128 * (field + 1))
+        pre[...] = inner[field]
+        if field:
+            for k in (*range(9), *range(18, 27)):
+                taps[k] = weights[TAPS - 1 - k].astype(jnp.float32).T.astype(jnp.bfloat16)
+            add_edges(pre, low[:, lanes], high[:, lanes], taps, edge_window)
+        else:
+            add_edges(pre, low[:, lanes], high[:, lanes], weights.at[TAPS:], edge_window)
+        value = base[:, lanes].astype(jnp.float32) + pre[...]
+        results.append((live[...].astype(jnp.float32) * value).astype(jnp.bfloat16))
+    both = jnp.concatenate(results, axis=1)
     slots = position_slots(lists, counts)
     count = output.shape[0]
     pieces = []
@@ -372,8 +394,10 @@
         source = slot_rows(slots, z, x, j - 1, (j >= 1) & (j <= NY))
         source = jnp.broadcast_to(source[0:1, :], (count, 128))
         pieces.append(jnp.where(row == source, 1.0, 0.0).astype(jnp.bfloat16))
-    output[...] = dot(jnp.concatenate(pieces, axis=1), result).astype(jnp.bfloat16)
-    done[...] = jnp.zeros_like(done)
+    by_slot = dot(jnp.concatenate(pieces, axis=1), both).astype(jnp.bfloat16)
+    output[...] = by_slot[:, 0:128]
+    grad[...] = by_slot[:, 128:256]
+    passed[...] = held[...]
 
 
 def pairs(value_first, value_second, axis):
@@ -406,14 +430,15 @@
     slots = f.shape[0]
     padded = -(-slots // 128) * 128
     conv_scratch = [pltpu.VMEM((4, WIDE, 1152), jnp.bfloat16), pltpu.VMEM((128, rows), jnp.bfloat16)]
+    edge_window = pltpu.VMEM((4, J, 1152), jnp.bfloat16)
     faces_scratch = pltpu.VMEM((128, 256), jnp.bfloat16)
     face, slab, grid = bf16(FACE, 256), bf16(SLAB, 256), bf16(ROWS, 256)
 
     def swap_core(value):
         return lax.ppermute(value, "drift", [(i, i ^ 1) for i in range(drift)])
 
-    def to_chip(value, step):
-        return lax.ppermute(value, "drift", [(i, i ^ (2 * step)) for i in range(drift)])
+    def to_chip(value, kind):
+        return lax.ppermute(value, "drift", [(i, i ^ (2 * chip_mask(kind, i % 2))) for i in range(drift)])
 
     def to_wire(value, step):
         return lax.ppermute(value, "wire", [(i, i ^ step) for i in range(wire)])
@@ -435,61 +460,89 @@
         first_kernel,
         (grid, message, message),
         [VMEM] * 6,
-        conv_scratch + [pltpu.VMEM((4, J, 1152), jnp.bfloat16), pltpu.VMEM((ROWS, 128), jnp.float32)],
+        conv_scratch + [edge_window, pltpu.VMEM((ROWS, 128), jnp.float32)],
     )(full, *slabs, live, weights, inner)
     got = swap_core(send)
     term_window = pltpu.VMEM((4, WIDE, 1152), jnp.bfloat16)
     terms = f32(chunk * chips, 128)
     own_terms = call(own_terms_kernel, terms, [VMEM], [term_window])(keep)
+    four = chips == 4
+    kinds = ("opposite", "first", "second", "own") if four else (*range(1, chips), 0)
+    shapes = [f32(chunk, 128) if k in ("second", "own", 0) else bf16(chunk, 128) for k in kinds]
     *sends, own, face_first, face_second = call(
-        functools.partial(terms_kernel, chunk),
-        tuple([bf16(chunk, 128)] * (chips - 1) + [f32(chunk, 128), face, face]),
+        functools.partial(terms_kernel, chunk, kinds),
+        (*shapes, face, face),
         [VMEM] * 3,
         [term_window, pltpu.VMEM(terms.shape, jnp.float32)],
     )(own_terms, got, hb)
-    parts = [to_chip(s, k + 1) for k, s in enumerate(sends)]
+    if four:
+        opposite, first, second_part = sends
+        passed = to_chip(opposite, "first")
+        parts = [to_chip(first, "first")]
+        passed = call(passed_on_kernel, bf16(chunk, 128), [VMEM] * 2)(second_part, passed)
+        parts.append(to_chip(passed, "second"))
+    else:
+        parts = [to_chip(value, k) for k, value in zip(kinds, sends)]
     faces = pairs(face_first, face_second, "wire")
     hb_full, *hb_slabs = call(insert_faces, (grid, slab, slab), [VMEM] * 3, [faces_scratch])(hb, *faces)
     inserted = hb_slabs[0]
     hb_slabs = pairs(*hb_slabs, "drift")
-    def second(field, flip):
-        return call(
-            functools.partial(second_kernel, field, flip),
-            (bf16(slots, 128), f32(8, 128)),
-            [SMEM] * 2 + [VMEM] * 6,
-            conv_scratch if flip else conv_scratch[:1],
-        )(send_lists, counts, hb_full, *hb_slabs, full, live, weights)
-
-    grad_features, grad_done = second(1, True)
-    output, output_done = second(0, False)
+    token = f32(8, 128)
+    inner, inner_done = call(second_inner_kernel, (f32(2, ROWS, 128), token), [VMEM] * 2, conv_scratch)(hb_full, weights)
     *sends, own = call(
-        functools.partial(split_kernel, unit, chips - 1),
+        functools.partial(split_kernel, unit, len(parts)),
         tuple([bf16(unit, 128)] * (wire - 1) + [f32(unit, 128)]),
-        [VMEM] * (1 + chips),
+        [VMEM] * (2 + len(parts)),
         [pltpu.VMEM((chunk, 128), jnp.float32)],
     )(inserted, own, *parts)
 
     received = [to_wire(s, k + 1) for k, s in enumerate(sends)]
     scale = 1.0 / math.sqrt(float(drift * wire * slots))
-    summed = call(functools.partial(sum_kernel, scale), bf16(unit, 128), [VMEM] * (2 + wire))(
-        *hb_slabs, own, *received
+    summed = call(functools.partial(sum_kernel, scale), bf16(unit, 128), [VMEM] * (3 + wire))(
+        inner_done, *hb_slabs, own, *received
     )
     pieces = [summed] + [to_wire(summed, k) for k in range(1, wire)]
-    mine = call(functools.partial(joined_kernel, unit), bf16(chunk, 128), [VMEM] * (1 + wire))(grad_done, *pieces)
-    mine = [mine] + [to_chip(mine, k) for k in range(1, chips)]
+    mine = call(functools.partial(joined_kernel, unit), bf16(chunk, 128), [VMEM] * wire)(*pieces)
+    output, grad_features, passed = call(
+        second_kernel,
+        (bf16(slots, 128), bf16(slots, 128), bf16(chunk, 128)),
+        [SMEM] * 2 + [VMEM] * 7,
+        [edge_window, pltpu.VMEM((ROWS, 128), jnp.float32), pltpu.VMEM((TAPS, 128, 128), jnp.bfloat16)],
+    )(send_lists, counts, inner, *hb_slabs, full, live, weights, mine)
+    if four:
+        brought = {"own": mine, "first": to_chip(mine, "first"), "second": to_chip(passed, "second")}
+        brought["opposite"] = to_chip(brought["first"], "second")
+        early = [
+            [("own", True), ("own", False), ("first", True)],
+            [("second", True), ("first", False), ("second", False)],
+        ]
+        last = "opposite"
+    else:
+        brought = {k: to_chip(passed if k > 1 else mine, k) if k else mine for k in range(chips)}
+        last = chips - 1
+        early = [[(k, True) for k in range(last)] + [(k, False) for k in range(last)]]
+    late = [[(last, True)], [(last, False)]]
+    swapped = {kind: swap_core(value) for kind, value in brought.items() if kind != last}
     grads = ()
-    early = max(1, chips - 2)
-    for steps in [tuple(range(early))] + [(k,) for k in range(early, chips)]:
-        staged = blocks * len(steps)
-        grads = call(
-            functools.partial(final_kernel, steps, blocks),
-            (f32(TAPS, 128, 128), f32(TAPS, 128, 128)),
-            [VMEM] * (1 + 2 * len(steps)) + [HBM] * len(grads),
-            [pltpu.VMEM((2, staged, 128, 128), jnp.float32), pltpu.SemaphoreType.DMA((2, staged))],
-            50 * 10**9,
-            HBM,
-            {1 + 2 * len(steps): 0, 2 + 2 * len(steps): 1} if grads else {},
-        )(output_done, *(mine[k] for k in steps), *(swap_core(mine[k]) for k in steps), *grads)
+    for n, items in enumerate(early + late):
+        if n == len(early):
+            held = call(relay_kernel, bf16(*brought[last].shape), [VMEM] * 2)(done, brought[last])
+            swapped[last] = swap_core(held)
+        values = [(brought if own_core else swapped)[kind] for kind, own_core in items]
+        staged = sum(value.shape[0] for value in values) // CHANNELS
+        want_done = n == len(early) - 1
+        *grads, done = (
+            *call(
+                functools.partial(final_kernel, items, blocks, want_done),
+                (f32(TAPS, 128, 128), f32(TAPS, 128, 128)) + (token,) * want_done,
+                [VMEM] * len(items) + [HBM] * len(grads),
+                [pltpu.VMEM((staged, 128, 128), jnp.float32), pltpu.SemaphoreType.DMA((staged,))],
+                50 * 10**9,
+                (HBM, HBM) + (VMEM,) * want_done,
+                {len(items): 0, len(items) + 1: 1} if grads else {},
+            )(*values, *grads),
+            *(() if want_done else (None,)),
+        )
     grad_first, grad_second = grads
     return output[None, None], grad_features[None, None], grad_first, grad_second
 

time: 70 us -> 66.3 us (0.947)
  waiting for transfers between devices: 16.7 us -> 14.2 us
  Pallas kernels: 18.9 us -> 17.7 us
    ppermute x6, waiting for transfers between devices: 11.1 us -> 6.78 us  [to_chip(): lax.ppermute(value, 'drift', [(i, i ^ 2 * chip_mask(kind, i % 2)) for i i...]
    ppermute x6, waiting for transfers between devices: 1.1 us -> 3.93 us  [to_wire(): return lax.ppermute(value, 'wire', [(i, i ^ step) for i in range(wire)])]
    ppermute x2, starting transfers between devices: 5.75 us -> 3.44 us  [pairs(): got_second = lax.ppermute(value_second, axis, sorted(second.items()))]
    ppermute x2, waiting for transfers between devices: 1.6 us -> 0.01 us  [pairs(): got_second = lax.ppermute(value_second, axis, sorted(second.items()))]
    ppermute x6, starting transfers between devices: 7.11 us -> 8.63 us  [to_chip(): lax.ppermute(value, 'drift', [(i, i ^ 2 * chip_mask(kind, i % 2)) for i i...]
    pallas_call x9 -> x12, Pallas kernels: 12.4 us -> 11.2 us  [the longest x4 4.33 us: on_device(): call(functools.partial(final_kernel, items, blocks, want_done), (f32(TAPS...]
    ppermute x4, starting transfers between devices: 5.87 us -> 7.07 us  [pairs(): got_first = lax.ppermute(value_first, axis, first)]
  transfers between devices with their start and end apart: 25 -> 25, of which waited for: 10 -> 11; matrix products, arithmetic and copies ran while one was open for 2% -> 2% of each run, Pallas kernels for 18% -> 18%
where the time goes in v3:
time: 66.3 us; the launch traced here: 66.1 us
  starting transfers between devices  29.5 us (44%)
  Pallas kernels  17.7 us (27%)
  waiting for transfers between devices  14.2 us (21%)
  local copies, waits for them, and re-layouts  2 us (3%)
  between operations  1.68 us (3%)
  other arithmetic  1.02 us (2%)
    ppermute x6, starting transfers between devices, to_wire(): return lax.ppermute(value, 'wire', [(i, i ^ step) for i in range(wire)])  9.84 us
    ppermute x6, starting transfers between devices, to_chip(): lax.ppermute(value, 'drift', [(i, i ^ 2 * chip_mask(kind, i % 2)) for i i...  8.63 us
    ppermute x4, starting transfers between devices, pairs(): got_first = lax.ppermute(value_first, axis, first)  7.07 us
    ppermute x6, waiting for transfers between devices, to_chip(): lax.ppermute(value, 'drift', [(i, i ^ 2 * chip_mask(kind, i % 2)) for i i...  6.78 us
    pallas_call x4, Pallas kernels, on_device(): call(functools.partial(final_kernel, items, blocks, want_done), (f32(TAPS...  4.33 us
    ppermute x6, waiting for transfers between devices, to_wire(): return lax.ppermute(value, 'wire', [(i, i ^ step) for i in range(wire)])  3.93 us
    ppermute x2, starting transfers between devices, pairs(): got_second = lax.ppermute(value_second, axis, sorted(second.items()))  3.44 us
    pallas_call x1, Pallas kernels, on_device(): call(second_inner_kernel, (f32(2, ROWS, 128), token), [VMEM] * 2, conv_sc...  3.25 us
  transfers between devices with their start and end apart: 25, of which 11 were waited for; matrix products, arithmetic and copies ran while one was open for 2% of the time, Pallas kernels for 18%

profile of v3, /device:TPU:0, one launch (start us, length us, event | category | flops | bytes accessed | tf_op | source)
XLA Modules:
  0.0 66.1 jit_solution(4580267537787499876)
XLA Ops:
  1.3 1.0 %pad_maximum_fusion.pair = bf16[576,256]{1,0:T(8,128)(2,1)S(1)} fusion(bf16[576,128]{1,0:T(8,128)(2,1)} %bitcast.4, bf16[576,128]{1,0:T(8,128)(2,1)} %bitcast.5), kind=kLoop, calls=%fused_computation | loop fusion | flops 589824 | bytes 589824 | tf_op jit(solution)/shard_map/concatenate | solution.py:446
  3.0 1.1 %shard_map.93 = (bf16[48,256]{1,0:T(8,128)(2,1)S(1)}, bf16[48,256]{1,0:T(8,128)(2,1)S(1)}, bf16[768,256]{1,0:T(8,128)(2,1)S(1)}, bf16[768,128]{1,0:T(8,128)(2,1)S(1)}) custom-call(s32[1,1]{1,0:T(1,128)S(6)} %copy.23.counts, s32[1,1,16]{2,1,0:T(1,128)S(1)} %copy-done, bf16[576,256]{1,0:T(8,128)(2,1)S(1)} %pad_maximum_fusion.pair), custom_call_target="tpu_custom_call" | custom-call | tf_op jit(solution)/shard_map/pallas_call | solution.py:448
  4.1 3.1 %collective-permute-start = (bf16[48,256]{1,0:T(8,128)(2,1)S(1)}, bf16[48,256]{1,0:T(8,128)(2,1)S(1)}, u32[]{:S(2)}, u32[]{:S(2)}) collective-permute-start(bf16[48,256]{1,0:T(8,128)(2,1)S(1)} %get-tuple-element.42), channel_id=1, source_target_pairs={{0,1},{1,0},{2,3},{3,2},{4,5},{5,4},{6,7},{7,6},{8,9},{9,8},{10,11... | collective-permute-start | bytes 73736 | tf_op jit(solution)/shard_map/ppermute | solution.py:418
  7.2 1.2 %constant_dynamic-update-slice_fusion.1 = bf16[54,128,128]{2,1,0:T(8,128)(2,1)S(1)} fusion(bf16[27,128,128]{2,1,0:T(8,128)(2,1)} %param.8), kind=kLoop, calls=%fused_computation.2 | loop fusion | bytes 1769472
  9.3 3.0 %collective-permute-start.3 = (bf16[64,256]{1,0:T(8,128)(2,1)S(1)}, bf16[64,256]{1,0:T(8,128)(2,1)S(1)}, u32[]{:S(2)}, u32[]{:S(2)}) collective-permute-start(bf16[64,256]{1,0:T(8,128)(2,1)S(1)} %get-tuple-element.46), channel_id=1, source_target_pairs={{0,28},{4,8},{8,4},{12,16},{16,12},{20,24},{24,20},{28,0},{1,29},{... | collective-permute-start | bytes 98312 | tf_op jit(solution)/shard_map/ppermute | solution.py:410
  12.5 1.6 %shard_map.95.inner = f32[768,128]{1,0:T(8,128)S(1)} custom-call(bf16[768,256]{1,0:T(8,128)(2,1)S(1)} %get-tuple-element.44.full.base, bf16[54,128,128]{2,1,0:T(8,128)(2,1)S(1)} %constant_dynamic-update-slice_fusion.weights), custom_call_target="tpu_custom_call" | custom-call | tf_op jit(solution)/shard_map/pallas_call | solution.py:458
  14.1 2.1 %shard_map.96 = (bf16[768,256]{1,0:T(8,128)(2,1)S(1)}, bf16[1664,128]{1,0:T(8,128)(2,1)S(1)}, bf16[1664,128]{1,0:T(8,128)(2,1)S(1)}) custom-call(bf16[768,256]{1,0:T(8,128)(2,1)S(1)} %get-tuple-element.44.full.base, bf16[64,256]{1,0:T(8,128)(2,1)S(1)} %collective-permute-done.2.got_first, bf16[64,256]{1,0:T(8,128)(2,1)S(1)} %collective-permute-done.3.got_second, ...), custom_call_target="tpu_custom_call" | custom-call | tf_op jit(solution)/shard_map/pallas_call | solution.py:459
  16.3 1.1 %shard_map.97.mine = f32[3584,128]{1,0:T(8,128)S(1)} custom-call(bf16[1664,128]{1,0:T(8,128)(2,1)S(1)} %get-tuple-element.49.mine), custom_call_target="tpu_custom_call" | custom-call | tf_op jit(solution)/shard_map/pallas_call | solution.py:468
  18.1 1.3 %shard_map.98 = (bf16[896,128]{1,0:T(8,128)(2,1)S(1)}, bf16[896,128]{1,0:T(8,128)(2,1)S(1)}, f32[896,128]{1,0:T(8,128)S(1)}, f32[896,128]{1,0:T(8,128)S(1)}, bf1...) custom-call(f32[3584,128]{1,0:T(8,128)S(1)} %shard_map.97.mine, ...), custom_call_target="tpu_custom_call" | custom-call | tf_op jit(solution)/shard_map/pallas_call | solution.py:472
  19.3 1.6 %collective-permute-start.10 = (bf16[896,128]{1,0:T(8,128)(2,1)S(1)}, bf16[896,128]{1,0:T(8,128)(2,1)S(1)}, u32[]{:S(2)}, u32[]{:S(2)}) collective-permute-start(bf16[896,128]{1,0:T(8,128)(2,1)S(1)} %get-tuple-element.61), channel_id=1, source_target_pairs={{0,8},{4,20},{8,0},{12,28},{16,24},{20,4},{24,16},{28,12},{1,9},{5... | collective-permute-start | bytes 688136 | tf_op jit(solution)/shard_map/ppermute | solution.py:441
  21.4 4.0 %collective-permute-done.10.received = bf16[896,128]{1,0:T(8,128)(2,1)S(1)} collective-permute-done((bf16[896,128]{1,0:T(8,128)(2,1)S(1)}, bf16[896,128]{1,0:T(8,128)(2,1)S(1)}, u32[]{:S(2)}, u32[]{:S(2)}) %collective-permute-start.10) | collective-permute-done | bytes 229408 | tf_op jit(solution)/shard_map/ppermute | solution.py:441
  25.5 1.6 %collective-permute-start.11 = (bf16[896,128]{1,0:T(8,128)(2,1)S(1)}, bf16[896,128]{1,0:T(8,128)(2,1)S(1)}, u32[]{:S(2)}, u32[]{:S(2)}) collective-permute-start(bf16[896,128]{1,0:T(8,128)(2,1)S(1)} %shard_map.101), channel_id=1, source_target_pairs={{0,16},{4,12},{8,24},{12,4},{16,0},{20,28},{24,8},{28,20},{1,17},{... | collective-permute-start | bytes 688136 | tf_op jit(solution)/shard_map/ppermute | solution.py:441
  27.0 2.7 %collective-permute-start.5 = (bf16[48,256]{1,0:T(8,128)(2,1)S(1)}, bf16[48,256]{1,0:T(8,128)(2,1)S(1)}, u32[]{:S(2)}, u32[]{:S(2)}) collective-permute-start(bf16[48,256]{1,0:T(8,128)(2,1)S(1)} %get-tuple-element.51), channel_id=1, source_target_pairs={{0,1},{1,0},{2,3},{3,2},{4,5},{5,4},{6,7},{7,6},{8,9},{9,8},{10,11... | collective-permute-start | bytes 73736 | tf_op jit(solution)/shard_map/ppermute | solution.py:418
  29.7 1.8 %collective-permute-done.5.got_first = bf16[48,256]{1,0:T(8,128)(2,1)S(1)} collective-permute-done((bf16[48,256]{1,0:T(8,128)(2,1)S(1)}, bf16[48,256]{1,0:T(8,128)(2,1)S(1)}, u32[]{:S(2)}, u32[]{:S(2)}) %collective-permute-start.5) | collective-permute-done | bytes 24608 | tf_op jit(solution)/shard_map/ppermute | solution.py:418
  32.0 2.5 %collective-permute-start.12 = (bf16[224,128]{1,0:T(8,128)(2,1)S(1)}, bf16[224,128]{1,0:T(8,128)(2,1)S(1)}, u32[]{:S(2)}, u32[]{:S(2)}) collective-permute-start(bf16[224,128]{1,0:T(8,128)(2,1)S(1)} %get-tuple-element.63), channel_id=1, source_target_pairs={{0,1},{1,0},{2,3},{3,2},{4,5},{5,4},{6,7},{7,6},{8,9},{9,8},{10,11... | collective-permute-start | bytes 172040 | tf_op jit(solution)/shard_map/ppermute | solution.py:444
  34.4 1.5 %collective-permute-start.13 = (bf16[224,128]{1,0:T(8,128)(2,1)S(1)}, bf16[224,128]{1,0:T(8,128)(2,1)S(1)}, u32[]{:S(2)}, u32[]{:S(2)}) collective-permute-start(bf16[224,128]{1,0:T(8,128)(2,1)S(1)} %get-tuple-element.64), channel_id=1, source_target_pairs={{0,2},{1,3},{2,0},{3,1},{4,6},{5,7},{6,4},{7,5},{8,10},{9,11},{10,... | collective-permute-start | bytes 172040 | tf_op jit(solution)/shard_map/ppermute | solution.py:444
  36.0 1.4 %collective-permute-start.14 = (bf16[224,128]{1,0:T(8,128)(2,1)S(1)}, bf16[224,128]{1,0:T(8,128)(2,1)S(1)}, u32[]{:S(2)}, u32[]{:S(2)}) collective-permute-start(bf16[224,128]{1,0:T(8,128)(2,1)S(1)} %get-tuple-element.65), channel_id=1, source_target_pairs={{0,3},{1,2},{2,1},{3,0},{4,7},{5,6},{6,5},{7,4},{8,11},{9,10},{10,... | collective-permute-start | bytes 172040 | tf_op jit(solution)/shard_map/ppermute | solution.py:444
  37.8 1.2 %collective-permute-start.7 = (bf16[64,256]{1,0:T(8,128)(2,1)S(1)}, bf16[64,256]{1,0:T(8,128)(2,1)S(1)}, u32[]{:S(2)}, u32[]{:S(2)}) collective-permute-start(bf16[64,256]{1,0:T(8,128)(2,1)S(1)} %get-tuple-element.55.after), channel_id=1, source_target_pairs={{0,4},{4,0},{8,12},{12,8},{16,20},{20,16},{24,28},{28,24},{1,5},{5... | collective-permute-start | bytes 98312 | tf_op jit(solution)/shard_map/ppermute | solution.py:418
  39.0 3.3 %shard_map.100 = (f32[2,768,128]{2,1,0:T(8,128)S(1)}, f32[8,128]{1,0:T(8,128)S(1)}) custom-call(bf16[768,256]{1,0:T(8,128)(2,1)S(1)} %get-tuple-element.53.hb, bf16[54,128,128]{2,1,0:T(8,128)(2,1)S(1)} %constant_dynamic-update-slice_fusion.weights), custom_call_target="tpu_custom_call" | custom-call | tf_op jit(solution)/shard_map/pallas_call | solution.py:491
  42.4 2.5 %collective-permute-start.17 = (bf16[224,128]{1,0:T(8,128)(2,1)S(1)}, bf16[224,128]{1,0:T(8,128)(2,1)S(1)}, u32[]{:S(2)}, u32[]{:S(2)}) collective-permute-start(bf16[224,128]{1,0:T(8,128)(2,1)S(1)} %shard_map.103.refs_0_), channel_id=1, source_target_pairs={{0,3},{1,2},{2,1},{3,0},{4,7},{5,6},{6,5},{7,4},{8,11},{9,10},{10,... | collective-permute-start | bytes 172040 | tf_op jit(solution)/shard_map/ppermute | solution.py:444
  44.9 1.9 %collective-permute-start.15 = (bf16[224,128]{1,0:T(8,128)(2,1)S(1)}, bf16[224,128]{1,0:T(8,128)(2,1)S(1)}, u32[]{:S(2)}, u32[]{:S(2)}) collective-permute-start(bf16[224,128]{1,0:T(8,128)(2,1)S(1)} %shard_map.103.refs_0_), channel_id=1, source_target_pairs={{0,1},{1,0},{2,3},{3,2},{4,5},{5,4},{6,7},{7,6},{8,9},{9,8},{10,11... | collective-permute-start | bytes 172040 | tf_op jit(solution)/shard_map/ppermute | solution.py:444
  46.8 2.2 %collective-permute-done.17.refs_3_ = bf16[224,128]{1,0:T(8,128)(2,1)S(1)} collective-permute-done((bf16[224,128]{1,0:T(8,128)(2,1)S(1)}, bf16[224,128]{1,0:T(8,128)(2,1)S(1)}, u32[]{:S(2)}, u32[]{:S(2)}) %collective-permute-start.17) | collective-permute-done | bytes 57376 | tf_op jit(solution)/shard_map/ppermute | solution.py:444
  49.0 1.7 %collective-permute-done.16.refs_2_ = bf16[224,128]{1,0:T(8,128)(2,1)S(1)} collective-permute-done((bf16[224,128]{1,0:T(8,128)(2,1)S(1)}, bf16[224,128]{1,0:T(8,128)(2,1)S(1)}, u32[]{:S(2)}, u32[]{:S(2)}) %collective-permute-start.16) | collective-permute-done | bytes 57376 | tf_op jit(solution)/shard_map/ppermute | solution.py:444
  50.8 1.5 %collective-permute-start.19 = (bf16[896,128]{1,0:T(8,128)(2,1)S(1)}, bf16[896,128]{1,0:T(8,128)(2,1)S(1)}, u32[]{:S(2)}, u32[]{:S(2)}) collective-permute-start(bf16[896,128]{1,0:T(8,128)(2,1)S(1)} %shard_map.104.held.refs_0_), channel_id=1, source_target_pairs={{0,8},{4,20},{8,0},{12,28},{16,24},{20,4},{24,16},{28,12},{1,9},{5... | collective-permute-start | bytes 688136 | tf_op jit(solution)/shard_map/ppermute | solution.py:441
  52.3 2.1 %shard_map.105 = (bf16[576,128]{1,0:T(8,128)(2,1)}, bf16[576,128]{1,0:T(8,128)(2,1)}, bf16[896,128]{1,0:T(8,128)(2,1)S(1)}) custom-call(s32[1,1,16]{2,1,0:T(1,128)S(1)} %copy-done.1, s32[1,1]{1,0:T(1,128)S(6)} %copy.23.counts, f32[2,768,128]{2,1,0:T(8,128)S(1)} %get-tuple-element.54.inner, bf16[64,256]{1,0:T(8,128)(2,1)S(1)} %collective-permute-done.7.after_first.got_first, ...), custom_call_target="tpu_custom_call" | custom-call | tf_op jit(solution)/shard_map/pallas_call | solution.py:506
  54.4 0.9 %collective-permute-start.18 = (bf16[896,128]{1,0:T(8,128)(2,1)S(1)}, bf16[896,128]{1,0:T(8,128)(2,1)S(1)}, u32[]{:S(2)}, u32[]{:S(2)}) collective-permute-start(bf16[896,128]{1,0:T(8,128)(2,1)S(1)} %get-tuple-element.68), channel_id=1, source_target_pairs={{0,16},{4,12},{8,24},{12,4},{16,0},{20,28},{24,8},{28,20},{1,17},{... | collective-permute-start | bytes 688136 | tf_op jit(solution)/shard_map/ppermute | solution.py:441
  55.3 1.6 %collective-permute-done.19.refs_2_ = bf16[896,128]{1,0:T(8,128)(2,1)S(1)} collective-permute-done((bf16[896,128]{1,0:T(8,128)(2,1)S(1)}, bf16[896,128]{1,0:T(8,128)(2,1)S(1)}, u32[]{:S(2)}, u32[]{:S(2)}) %collective-permute-start.19) | collective-permute-done | bytes 229408 | tf_op jit(solution)/shard_map/ppermute | solution.py:441
  56.9 2.6 %collective-permute-start.23 = (bf16[896,128]{1,0:T(8,128)(2,1)S(1)}, bf16[896,128]{1,0:T(8,128)(2,1)S(1)}, u32[]{:S(2)}, u32[]{:S(2)}) collective-permute-start(bf16[896,128]{1,0:T(8,128)(2,1)S(1)} %collective-permute-done.19.refs_2_), channel_id=1, source_target_pairs={{0,16},{4,12},{8,24},{12,4},{16,0},{20,28},{24,8},{28,20},{1,17},{... | collective-permute-start | bytes 688136 | tf_op jit(solution)/shard_map/ppermute | solution.py:441
  59.4 1.0 %collective-permute-done.18.refs_0_ = bf16[896,128]{1,0:T(8,128)(2,1)S(1)} collective-permute-done((bf16[896,128]{1,0:T(8,128)(2,1)S(1)}, bf16[896,128]{1,0:T(8,128)(2,1)S(1)}, u32[]{:S(2)}, u32[]{:S(2)}) %collective-permute-start.18) | collective-permute-done | bytes 229408 | tf_op jit(solution)/shard_map/ppermute | solution.py:441
  60.4 1.3 %shard_map.106 = (f32[27,128,128]{2,1,0:T(8,128)}, f32[27,128,128]{2,1,0:T(8,128)}) custom-call(bf16[896,128]{1,0:T(8,128)(2,1)S(1)} %shard_map.104.held.refs_0_, bf16[896,128]{1,0:T(8,128)(2,1)S(1)} %collective-permute-done.22.refs_1_, bf16[896,128]{1,0:T(8,128)(2,1)S(1)} %collective-permute-done.19.refs_2_), custom_call_target="tpu_custom_call" | custom-call | flops 49999998976 | tf_op jit(solution)/shard_map/pallas_call | solution.py:535
  61.9 1.3 %shard_map.107 = (f32[27,128,128]{2,1,0:T(8,128)}, f32[27,128,128]{2,1,0:T(8,128)}, f32[8,128]{1,0:T(8,128)S(1)}) custom-call(bf16[896,128]{1,0:T(8,128)(2,1)S(1)} %collective-permute-done.18.refs_0_, bf16[896,128]{1,0:T(8,128)(2,1)S(1)} %collective-permute-done.20.refs_1_, ...), custom_call_target="tpu_custom_call", output_to_operand_aliasing={{0}: (3, {}), {1}: (4, {})} | custom-call | flops 49999998976 | tf_op jit(solution)/shard_map/pallas_call | solution.py:535
  65.0 0.9 %shard_map.110 = (f32[27,128,128]{2,1,0:T(8,128)}, f32[27,128,128]{2,1,0:T(8,128)}) custom-call(bf16[896,128]{1,0:T(8,128)(2,1)S(1)} %collective-permute-done.24.refs_0_, f32[27,128,128]{2,1,0:T(8,128)} %get-tuple-element.74.refs_1_, f32[27,128,128]{2,1,0:T(8,128)} %get-tuple-element.75.refs_2_), custom_call_target="tpu_custom_call", output_to_operand_aliasing={{0}: (1, {}), {1}: (2, {})} | custom-call | flops 49999998976 | tf_op jit(solution)/shard_map/pallas_call | solution.py:535
  (45 shorter events, 5.8 us)
Async XLA Ops:
  2.3 0.7 copy-start
  3.0 9.4 %copy-start.2 = (bf16[27,128,128]{2,1,0:T(8,128)(2,1)S(1)}, bf16[27,128,128]{2,1,0:T(8,128)(2,1)}, u32[]{:S(2)}) copy-start(bf16[27,128,128]{2,1,0:T(8,128)(2,1)} %param.9) | copy-start | bytes 2654212
  4.1 4.9 %collective-permute-start = (bf16[48,256]{1,0:T(8,128)(2,1)S(1)}, bf16[48,256]{1,0:T(8,128)(2,1)S(1)}, u32[]{:S(2)}, u32[]{:S(2)}) collective-permute-start(bf16[48,256]{1,0:T(8,128)(2,1)S(1)} %get-tuple-element.42), channel_id=1, source_target_pairs={{0,1},{1,0},{2,3},{3,2},{4,5},{5,4},{6,7},{7,6},{8,9},{9,8},{10,11... | collective-permute-start | bytes 73736 | tf_op jit(solution)/shard_map/ppermute | solution.py:418
  7.2 1.8 %collective-permute-start.1 = (bf16[48,256]{1,0:T(8,128)(2,1)S(1)}, bf16[48,256]{1,0:T(8,128)(2,1)S(1)}, u32[]{:S(2)}, u32[]{:S(2)}) collective-permute-start(bf16[48,256]{1,0:T(8,128)(2,1)S(1)} %get-tuple-element.43), channel_id=1, source_target_pairs={{0,4},{1,2},{2,1},{3,7},{4,0},{5,6},{6,5},{7,3},{8,12},{9,10},{10,... | collective-permute-start | bytes 73736 | tf_op jit(solution)/shard_map/ppermute | solution.py:417
  9.3 4.8 %collective-permute-start.2 = (bf16[64,256]{1,0:T(8,128)(2,1)S(1)}, bf16[64,256]{1,0:T(8,128)(2,1)S(1)}, u32[]{:S(2)}, u32[]{:S(2)}) collective-permute-start(bf16[64,256]{1,0:T(8,128)(2,1)S(1)} %get-tuple-element.45), channel_id=1, source_target_pairs={{0,4},{4,0},{8,12},{12,8},{16,20},{20,16},{24,28},{28,24},{1,5},{5... | collective-permute-start | bytes 98312 | tf_op jit(solution)/shard_map/ppermute | solution.py:418
  9.3 4.8 %collective-permute-start.3 = (bf16[64,256]{1,0:T(8,128)(2,1)S(1)}, bf16[64,256]{1,0:T(8,128)(2,1)S(1)}, u32[]{:S(2)}, u32[]{:S(2)}) collective-permute-start(bf16[64,256]{1,0:T(8,128)(2,1)S(1)} %get-tuple-element.46), channel_id=1, source_target_pairs={{0,28},{4,8},{8,4},{12,16},{16,12},{20,24},{24,20},{28,0},{1,29},{... | collective-permute-start | bytes 98312 | tf_op jit(solution)/shard_map/ppermute | solution.py:410
  16.2 1.8 %collective-permute-start.4 = (bf16[1664,128]{1,0:T(8,128)(2,1)S(1)}, bf16[1664,128]{1,0:T(8,128)(2,1)S(1)}, u32[]{:S(2)}, u32[]{:S(2)}) collective-permute-start(bf16[1664,128]{1,0:T(8,128)(2,1)S(1)} %get-tuple-element.50), channel_id=1, source_target_pairs={{0,4},{4,0},{8,12},{12,8},{16,20},{20,16},{24,28},{28,24},{1,5},{5... | collective-permute-start | bytes 1277960 | tf_op jit(solution)/shard_map/ppermute | solution.py:438
  19.3 6.1 %collective-permute-start.10 = (bf16[896,128]{1,0:T(8,128)(2,1)S(1)}, bf16[896,128]{1,0:T(8,128)(2,1)S(1)}, u32[]{:S(2)}, u32[]{:S(2)}) collective-permute-start(bf16[896,128]{1,0:T(8,128)(2,1)S(1)} %get-tuple-element.61), channel_id=1, source_target_pairs={{0,8},{4,20},{8,0},{12,28},{16,24},{20,4},{24,16},{28,12},{1,9},{5... | collective-permute-start | bytes 688136 | tf_op jit(solution)/shard_map/ppermute | solution.py:441
  20.9 10.9 %collective-permute-start.9 = (bf16[896,128]{1,0:T(8,128)(2,1)S(1)}, bf16[896,128]{1,0:T(8,128)(2,1)S(1)}, u32[]{:S(2)}, u32[]{:S(2)}) collective-permute-start(bf16[896,128]{1,0:T(8,128)(2,1)S(1)} %get-tuple-element.59), channel_id=1, source_target_pairs={{0,8},{4,20},{8,0},{12,28},{16,24},{20,4},{24,16},{28,12},{1,9},{5... | collective-permute-start | bytes 688136 | tf_op jit(solution)/shard_map/ppermute | solution.py:441
  25.5 6.4 %collective-permute-start.11 = (bf16[896,128]{1,0:T(8,128)(2,1)S(1)}, bf16[896,128]{1,0:T(8,128)(2,1)S(1)}, u32[]{:S(2)}, u32[]{:S(2)}) collective-permute-start(bf16[896,128]{1,0:T(8,128)(2,1)S(1)} %shard_map.101), channel_id=1, source_target_pairs={{0,16},{4,12},{8,24},{12,4},{16,0},{20,28},{24,8},{28,20},{1,17},{... | collective-permute-start | bytes 688136 | tf_op jit(solution)/shard_map/ppermute | solution.py:441
  27.0 4.5 %collective-permute-start.5 = (bf16[48,256]{1,0:T(8,128)(2,1)S(1)}, bf16[48,256]{1,0:T(8,128)(2,1)S(1)}, u32[]{:S(2)}, u32[]{:S(2)}) collective-permute-start(bf16[48,256]{1,0:T(8,128)(2,1)S(1)} %get-tuple-element.51), channel_id=1, source_target_pairs={{0,1},{1,0},{2,3},{3,2},{4,5},{5,4},{6,7},{7,6},{8,9},{9,8},{10,11... | collective-permute-start | bytes 73736 | tf_op jit(solution)/shard_map/ppermute | solution.py:418
  29.7 1.8 %collective-permute-start.6 = (bf16[48,256]{1,0:T(8,128)(2,1)S(1)}, bf16[48,256]{1,0:T(8,128)(2,1)S(1)}, u32[]{:S(2)}, u32[]{:S(2)}) collective-permute-start(bf16[48,256]{1,0:T(8,128)(2,1)S(1)} %get-tuple-element.52), channel_id=1, source_target_pairs={{0,4},{1,2},{2,1},{3,7},{4,0},{5,6},{6,5},{7,3},{8,12},{9,10},{10,... | collective-permute-start | bytes 73736 | tf_op jit(solution)/shard_map/ppermute | solution.py:417
  31.8 20.4 %copy-start.1 = (s32[1,1,16]{2,1,0:T(1,128)S(1)}, s32[1,1,16]{2,1,0:T(1,128)}, u32[]{:S(2)}) copy-start(s32[1,1,16]{2,1,0:T(1,128)} %lists.3) | copy-start | bytes 196
  32.0 10.3 %collective-permute-start.12 = (bf16[224,128]{1,0:T(8,128)(2,1)S(1)}, bf16[224,128]{1,0:T(8,128)(2,1)S(1)}, u32[]{:S(2)}, u32[]{:S(2)}) collective-permute-start(bf16[224,128]{1,0:T(8,128)(2,1)S(1)} %get-tuple-element.63), channel_id=1, source_target_pairs={{0,1},{1,0},{2,3},{3,2},{4,5},{5,4},{6,7},{7,6},{8,9},{9,8},{10,11... | collective-permute-start | bytes 172040 | tf_op jit(solution)/shard_map/ppermute | solution.py:444
  34.4 7.9 %collective-permute-start.13 = (bf16[224,128]{1,0:T(8,128)(2,1)S(1)}, bf16[224,128]{1,0:T(8,128)(2,1)S(1)}, u32[]{:S(2)}, u32[]{:S(2)}) collective-permute-start(bf16[224,128]{1,0:T(8,128)(2,1)S(1)} %get-tuple-element.64), channel_id=1, source_target_pairs={{0,2},{1,3},{2,0},{3,1},{4,6},{5,7},{6,4},{7,5},{8,10},{9,11},{10,... | collective-permute-start | bytes 172040 | tf_op jit(solution)/shard_map/ppermute | solution.py:444
  36.0 6.3 %collective-permute-start.14 = (bf16[224,128]{1,0:T(8,128)(2,1)S(1)}, bf16[224,128]{1,0:T(8,128)(2,1)S(1)}, u32[]{:S(2)}, u32[]{:S(2)}) collective-permute-start(bf16[224,128]{1,0:T(8,128)(2,1)S(1)} %get-tuple-element.65), channel_id=1, source_target_pairs={{0,3},{1,2},{2,1},{3,0},{4,7},{5,6},{6,5},{7,4},{8,11},{9,10},{10,... | collective-permute-start | bytes 172040 | tf_op jit(solution)/shard_map/ppermute | solution.py:444
  37.4 4.9 %collective-permute-start.8 = (bf16[64,256]{1,0:T(8,128)(2,1)S(1)}, bf16[64,256]{1,0:T(8,128)(2,1)S(1)}, u32[]{:S(2)}, u32[]{:S(2)}) collective-permute-start(bf16[64,256]{1,0:T(8,128)(2,1)S(1)} %get-tuple-element.56), channel_id=1, source_target_pairs={{0,28},{4,8},{8,4},{12,16},{16,12},{20,24},{24,20},{28,0},{1,29},{... | collective-permute-start | bytes 98312 | tf_op jit(solution)/shard_map/ppermute | solution.py:410
  37.8 4.5 %collective-permute-start.7 = (bf16[64,256]{1,0:T(8,128)(2,1)S(1)}, bf16[64,256]{1,0:T(8,128)(2,1)S(1)}, u32[]{:S(2)}, u32[]{:S(2)}) collective-permute-start(bf16[64,256]{1,0:T(8,128)(2,1)S(1)} %get-tuple-element.55.after), channel_id=1, source_target_pairs={{0,4},{4,0},{8,12},{12,8},{16,20},{20,16},{24,28},{28,24},{1,5},{5... | collective-permute-start | bytes 98312 | tf_op jit(solution)/shard_map/ppermute | solution.py:418
  42.4 6.6 %collective-permute-start.17 = (bf16[224,128]{1,0:T(8,128)(2,1)S(1)}, bf16[224,128]{1,0:T(8,128)(2,1)S(1)}, u32[]{:S(2)}, u32[]{:S(2)}) collective-permute-start(bf16[224,128]{1,0:T(8,128)(2,1)S(1)} %shard_map.103.refs_0_), channel_id=1, source_target_pairs={{0,3},{1,2},{2,1},{3,0},{4,7},{5,6},{6,5},{7,4},{8,11},{9,10},{10,... | collective-permute-start | bytes 172040 | tf_op jit(solution)/shard_map/ppermute | solution.py:444
  44.9 5.9 %collective-permute-start.16 = (bf16[224,128]{1,0:T(8,128)(2,1)S(1)}, bf16[224,128]{1,0:T(8,128)(2,1)S(1)}, u32[]{:S(2)}, u32[]{:S(2)}) collective-permute-start(bf16[224,128]{1,0:T(8,128)(2,1)S(1)} %shard_map.103.refs_0_), channel_id=1, source_target_pairs={{0,2},{1,3},{2,0},{3,1},{4,6},{5,7},{6,4},{7,5},{8,10},{9,11},{10,... | collective-permute-start | bytes 172040 | tf_op jit(solution)/shard_map/ppermute | solution.py:444
  44.9 5.9 %collective-permute-start.15 = (bf16[224,128]{1,0:T(8,128)(2,1)S(1)}, bf16[224,128]{1,0:T(8,128)(2,1)S(1)}, u32[]{:S(2)}, u32[]{:S(2)}) collective-permute-start(bf16[224,128]{1,0:T(8,128)(2,1)S(1)} %shard_map.103.refs_0_), channel_id=1, source_target_pairs={{0,1},{1,0},{2,3},{3,2},{4,5},{5,4},{6,7},{7,6},{8,9},{9,8},{10,11... | collective-permute-start | bytes 172040 | tf_op jit(solution)/shard_map/ppermute | solution.py:444
  50.8 6.1 %collective-permute-start.19 = (bf16[896,128]{1,0:T(8,128)(2,1)S(1)}, bf16[896,128]{1,0:T(8,128)(2,1)S(1)}, u32[]{:S(2)}, u32[]{:S(2)}) collective-permute-start(bf16[896,128]{1,0:T(8,128)(2,1)S(1)} %shard_map.104.held.refs_0_), channel_id=1, source_target_pairs={{0,8},{4,20},{8,0},{12,28},{16,24},{20,4},{24,16},{28,12},{1,9},{5... | collective-permute-start | bytes 688136 | tf_op jit(solution)/shard_map/ppermute | solution.py:441
  54.4 6.0 %collective-permute-start.18 = (bf16[896,128]{1,0:T(8,128)(2,1)S(1)}, bf16[896,128]{1,0:T(8,128)(2,1)S(1)}, u32[]{:S(2)}, u32[]{:S(2)}) collective-permute-start(bf16[896,128]{1,0:T(8,128)(2,1)S(1)} %get-tuple-element.68), channel_id=1, source_target_pairs={{0,16},{4,12},{8,24},{12,4},{16,0},{20,28},{24,8},{28,20},{1,17},{... | collective-permute-start | bytes 688136 | tf_op jit(solution)/shard_map/ppermute | solution.py:441
  55.3 5.1 %collective-permute-start.22 = (bf16[896,128]{1,0:T(8,128)(2,1)S(1)}, bf16[896,128]{1,0:T(8,128)(2,1)S(1)}, u32[]{:S(2)}, u32[]{:S(2)}) collective-permute-start(bf16[896,128]{1,0:T(8,128)(2,1)S(1)} %shard_map.104.held.refs_0_), channel_id=1, source_target_pairs={{0,4},{4,0},{8,12},{12,8},{16,20},{20,16},{24,28},{28,24},{1,5},{5... | collective-permute-start | bytes 688136 | tf_op jit(solution)/shard_map/ppermute | solution.py:438
  56.9 6.6 %collective-permute-start.23 = (bf16[896,128]{1,0:T(8,128)(2,1)S(1)}, bf16[896,128]{1,0:T(8,128)(2,1)S(1)}, u32[]{:S(2)}, u32[]{:S(2)}) collective-permute-start(bf16[896,128]{1,0:T(8,128)(2,1)S(1)} %collective-permute-done.19.refs_2_), channel_id=1, source_target_pairs={{0,16},{4,12},{8,24},{12,4},{16,0},{20,28},{24,8},{28,20},{1,17},{... | collective-permute-start | bytes 688136 | tf_op jit(solution)/shard_map/ppermute | solution.py:441
  59.4 2.5 %collective-permute-start.20 = (bf16[896,128]{1,0:T(8,128)(2,1)S(1)}, bf16[896,128]{1,0:T(8,128)(2,1)S(1)}, u32[]{:S(2)}, u32[]{:S(2)}) collective-permute-start(bf16[896,128]{1,0:T(8,128)(2,1)S(1)} %collective-permute-done.19.refs_2_), channel_id=1, source_target_pairs={{0,4},{4,0},{8,12},{12,8},{16,20},{20,16},{24,28},{28,24},{1,5},{5... | collective-permute-start | bytes 688136 | tf_op jit(solution)/shard_map/ppermute | solution.py:438
  60.4 1.5 %collective-permute-start.21 = (bf16[896,128]{1,0:T(8,128)(2,1)S(1)}, bf16[896,128]{1,0:T(8,128)(2,1)S(1)}, u32[]{:S(2)}, u32[]{:S(2)}) collective-permute-start(bf16[896,128]{1,0:T(8,128)(2,1)S(1)} %collective-permute-done.18.refs_0_), channel_id=1, source_target_pairs={{0,4},{4,0},{8,12},{12,8},{16,20},{20,16},{24,28},{28,24},{1,5},{5... | collective-permute-start | bytes 688136 | tf_op jit(solution)/shard_map/ppermute | solution.py:438
  63.5 1.6 %collective-permute-start.24 = (bf16[896,128]{1,0:T(8,128)(2,1)S(1)}, bf16[896,128]{1,0:T(8,128)(2,1)S(1)}, u32[]{:S(2)}, u32[]{:S(2)}) collective-permute-start(bf16[896,128]{1,0:T(8,128)(2,1)S(1)} %shard_map.108), channel_id=1, source_target_pairs={{0,4},{4,0},{8,12},{12,8},{16,20},{20,16},{24,28},{28,24},{1,5},{5... | collective-permute-start | bytes 688136 | tf_op jit(solution)/shard_map/ppermute | solution.py:438

commit v4 on v3

--- a/solution.py
+++ b/solution.py
@@ -53,12 +53,12 @@
     return lax.broadcasted_iota(jnp.int32, shape, dim)
 
 
-def position_slots(lists, counts):
-    slots = {p: lists[0, 0, i] for p, i in LISTED.items()}
+def position_slots(listed, count):
+    slots = {p: listed(i) for p, i in LISTED.items()}
     present = {p: (s < 9).astype(jnp.int32) for p, s in slots.items()}
     before = present[0] + present[1] + present[2] + present[3]
     others = before + present[5] + present[6] + present[7] + present[8]
-    slots[4] = jnp.where(counts[0, 0] > others, before, 9)
+    slots[4] = jnp.where(count > others, before, 9)
     return slots
 
 
@@ -113,7 +113,12 @@
     count = pair.shape[0]
     both[0:count, :] = pair[...]
     both[count:, :] = jnp.zeros((both.shape[0] - count, 256), jnp.bfloat16)
-    slots = position_slots(lists, counts)
+    entries = lists[0]
+
+    def entry(i):
+        return jnp.sum(jnp.where(iota(entries.shape, 1) == i, entries, 0), axis=1, keepdims=True)
+
+    slots = position_slots(entry, counts[...])
     z, x = face_indices()
     low, high = (
         dot(
@@ -254,29 +259,62 @@
     return {"own": 0, "first": first, "second": 3 - first, "opposite": 3}[kind]
 
 
-def add_terms(part, window, total, fresh):
-    build_window(window, 0, lambda z: part[ROWS + z * WIDE : ROWS + (z + 1) * WIDE, :])
-    left = part[0:ROWS, :].astype(jnp.float32).T.astype(jnp.bfloat16)
+def left_rows(part):
+    return part[0:ROWS, :].astype(jnp.float32).T.astype(jnp.bfloat16)
+
+
+def term_planes(part):
+    return lambda z: part[ROWS + z * WIDE : ROWS + (z + 1) * WIDE, :]
+
+
+def add_terms(left, window, add_block):
     for ox in range(3):
         shifted = window[:, ox * J : ox * J + PLANE, :].reshape(ROWS, 1152)
         product = dot(left, shifted)
         for k in range(9):
-            start = 128 * (9 * ox + k)
-            term = product[:, 128 * k : 128 * (k + 1)]
-            total[start : start + 128, :] = term if fresh else total[start : start + 128, :] + term
+            add_block(128 * (9 * ox + k), product[:, 128 * k : 128 * (k + 1)])
 
 
 def own_terms_kernel(mine, total, window):
     rows = TAPS * CHANNELS
     if total.shape[0] > rows:
         total[rows:, :] = jnp.zeros((total.shape[0] - rows, 128), jnp.float32)
-    add_terms(mine, window, total, True)
-
-
-def terms_kernel(chunk, kinds, mine, theirs, hb, *refs):
-    *outs, first, second, window, total = refs
-    total[...] = mine[...]
-    add_terms(theirs, window, total, False)
+    build_window(window, 0, term_planes(mine))
+
+    def put(start, block):
+        total[start : start + 128, :] = block
+
+    add_terms(left_rows(mine), window, put)
+
+
+def lead_terms_kernel(blocks, kind, mine, theirs, out, left, window):
+    build_window(window, 0, term_planes(theirs))
+    left[...] = left_rows(theirs)
+    me, core = lax.axis_index("drift") // 2, lax.axis_index("drift") % 2
+    lead = (me ^ chip_mask(kind, core)) * blocks
+    columns = []
+    for i in range(blocks):
+        tap = jnp.minimum(lead + i, TAPS - 1)
+        row = pl.multiple_of(tap // 9 * J, J)
+        lane = pl.multiple_of(tap % 9 * 128, 128)
+        columns.append(window[:, pl.ds(row, PLANE), pl.ds(lane, 128)].reshape(ROWS, 128))
+    product = dot(left[...], jnp.concatenate(columns, axis=1))
+    for i in range(blocks):
+        held = mine[pl.ds(pl.multiple_of((lead + i) * 128, 128), 128), :]
+        term = product[:, 128 * i : 128 * (i + 1)]
+        out[128 * i : 128 * (i + 1), :] = (held + jnp.where(lead + i < TAPS, term, 0.0)).astype(out.dtype)
+
+
+def terms_kernel(chunk, kinds, mine, left, window, hb, *refs):
+    *outs, first, second, total = refs
+    rows = TAPS * CHANNELS
+    if total.shape[0] > rows:
+        total[rows:, :] = mine[rows:, :]
+
+    def put(start, block):
+        total[start : start + 128, :] = mine[start : start + 128, :] + block
+
+    add_terms(left[...], window, put)
     me, core = lax.axis_index("drift") // 2, lax.axis_index("drift") % 2
     for kind, out in zip(kinds, outs):
         start = pl.multiple_of((me ^ chip_mask(kind, core)) * chunk, 128)
@@ -316,7 +354,7 @@
     out[...] = (summed * scale).astype(jnp.bfloat16)
 
 
-def joined_kernel(unit, *refs):
+def joined_kernel(unit, after, *refs):
     *parts, out = refs
     me = lax.axis_index("wire")
     for step, part in enumerate(parts):
@@ -355,24 +393,25 @@
     pl.when(jnp.logical_not(even))(lambda: write(1))
 
 
-def second_inner_kernel(hb, weights, inner, done, window, flipped):
+def second_inner_kernel(field, hb, weights, inner, done, window, *flipped):
     edge = jnp.zeros((SLAB, 256), jnp.bfloat16)
-    flip_blocks(weights, 0, flipped)
-    build_window(window, 0, lambda z: wide_plane(hb, edge, edge, z, slice(0, 128)))
-    inner[0] = conv(window, weights, TAPS)
-    build_window(window, 0, lambda z: wide_plane(hb, edge, edge, z, slice(128, 256)))
-    inner[1] = conv_flipped(window, flipped)
+    build_window(window, 0, lambda z: wide_plane(hb, edge, edge, z, slice(128 * field, 128 * (field + 1))))
+    if field:
+        flip_blocks(weights, 0, *flipped)
+        inner[...] = conv_flipped(window, *flipped)
+    else:
+        inner[...] = conv(window, weights, TAPS)
     done[...] = jnp.zeros_like(done)
 
 
 def second_kernel(
-    lists, counts, inner, got_first, got_second, base, live, weights, held, output, grad, passed, edge_window, pre, taps
+    lists, counts, inner_hidden, inner_back, got_first, got_second, base, live, weights, held, output, grad, passed, edge_window, pre, taps
 ):
     low, high = read_by_parity("drift", got_first, got_second)
     results = []
     for field in (0, 1):
         lanes = slice(128 * field, 128 * (field + 1))
-        pre[...] = inner[field]
+        pre[...] = inner_back[...] if field else inner_hidden[...]
         if field:
             for k in (*range(9), *range(18, 27)):
                 taps[k] = weights[TAPS - 1 - k].astype(jnp.float32).T.astype(jnp.bfloat16)
@@ -382,7 +421,7 @@
         value = base[:, lanes].astype(jnp.float32) + pre[...]
         results.append((live[...].astype(jnp.float32) * value).astype(jnp.bfloat16))
     both = jnp.concatenate(results, axis=1)
-    slots = position_slots(lists, counts)
+    slots = position_slots(lambda i: lists[0, 0, i], counts[0, 0])
     count = output.shape[0]
     pieces = []
     row = iota((count, 128), 0)
@@ -448,7 +487,7 @@
     *faces, placed, live = call(
         place_kernel,
         (face, face, grid, bf16(ROWS, 128)),
-        [SMEM] * 2 + [VMEM],
+        [VMEM] * 3,
         [pltpu.VMEM((padded, 256), jnp.bfloat16)],
     )(counts, send_lists, pair)
     faces = pairs(*faces, "wire")
@@ -469,12 +508,18 @@
     four = chips == 4
     kinds = ("opposite", "first", "second", "own") if four else (*range(1, chips), 0)
     shapes = [f32(chunk, 128) if k in ("second", "own", 0) else bf16(chunk, 128) for k in kinds]
+    lead, left, held_window = call(
+        functools.partial(lead_terms_kernel, blocks, kinds[0]),
+        (shapes[0], bf16(128, ROWS), bf16(4, WIDE, 1152)),
+        [VMEM] * 2,
+    )(own_terms, got)
     *sends, own, face_first, face_second = call(
-        functools.partial(terms_kernel, chunk, kinds),
-        (*shapes, face, face),
-        [VMEM] * 3,
-        [term_window, pltpu.VMEM(terms.shape, jnp.float32)],
-    )(own_terms, got, hb)
+        functools.partial(terms_kernel, chunk, kinds[1:]),
+        (*shapes[1:], face, face),
+        [VMEM] * 4,
+        [pltpu.VMEM(terms.shape, jnp.float32)],
+    )(own_terms, left, held_window, hb)
+    sends = [lead] + sends
     if four:
         opposite, first, second_part = sends
         passed = to_chip(opposite, "first")
@@ -488,7 +533,15 @@
     inserted = hb_slabs[0]
     hb_slabs = pairs(*hb_slabs, "drift")
     token = f32(8, 128)
-    inner, inner_done = call(second_inner_kernel, (f32(2, ROWS, 128), token), [VMEM] * 2, conv_scratch)(hb_full, weights)
+    (inner_hidden, hidden_done), (inner_back, back_done) = (
+        call(
+            functools.partial(second_inner_kernel, field),
+            (f32(ROWS, 128), token),
+            [VMEM] * 2,
+            conv_scratch[: 1 + field],
+        )(hb_full, weights)
+        for field in (0, 1)
+    )
     *sends, own = call(
         functools.partial(split_kernel, unit, len(parts)),
         tuple([bf16(unit, 128)] * (wire - 1) + [f32(unit, 128)]),
@@ -499,16 +552,16 @@
     received = [to_wire(s, k + 1) for k, s in enumerate(sends)]
     scale = 1.0 / math.sqrt(float(drift * wire * slots))
     summed = call(functools.partial(sum_kernel, scale), bf16(unit, 128), [VMEM] * (3 + wire))(
-        inner_done, *hb_slabs, own, *received
+        hidden_done, *hb_slabs, own, *received
     )
     pieces = [summed] + [to_wire(summed, k) for k in range(1, wire)]
-    mine = call(functools.partial(joined_kernel, unit), bf16(chunk, 128), [VMEM] * wire)(*pieces)
+    mine = call(functools.partial(joined_kernel, unit), bf16(chunk, 128), [VMEM] * (1 + wire))(back_done, *pieces)
     output, grad_features, passed = call(
         second_kernel,
         (bf16(slots, 128), bf16(slots, 128), bf16(chunk, 128)),
-        [SMEM] * 2 + [VMEM] * 7,
+        [SMEM] * 2 + [VMEM] * 8,
         [edge_window, pltpu.VMEM((ROWS, 128), jnp.float32), pltpu.VMEM((TAPS, 128, 128), jnp.bfloat16)],
-    )(send_lists, counts, inner, *hb_slabs, full, live, weights, mine)
+    )(send_lists, counts, inner_hidden, inner_back, *hb_slabs, full, live, weights, mine)
     if four:
         brought = {"own": mine, "first": to_chip(mine, "first"), "second": to_chip(passed, "second")}
         brought["opposite"] = to_chip(brought["first"], "second")

time: 66.3 us -> 65.3 us (0.985)
  waiting for transfers between devices: 14.2 us -> 11.9 us
  starting transfers between devices: 29.5 us -> 30.4 us
    ppermute x6, waiting for transfers between devices: 3.93 us -> 1.9 us  [to_wire(): return lax.ppermute(value, 'wire', [(i, i ^ step) for i in range(wire)])]
    ppermute x6, waiting for transfers between devices: 6.78 us -> 5.26 us  [to_chip(): lax.ppermute(value, 'drift', [(i, i ^ 2 * chip_mask(kind, i % 2)) for i i...]
    ppermute x2, waiting for transfers between devices: 0.01 us -> 1.14 us  [pairs(): got_second = lax.ppermute(value_second, axis, sorted(second.items()))]
    ppermute x6, starting transfers between devices: 8.63 us -> 9.51 us  [to_chip(): lax.ppermute(value, 'drift', [(i, i ^ 2 * chip_mask(kind, i % 2)) for i i...]
    pallas_call x4 -> x6, Pallas kernels: 5.66 us -> 5.96 us  [the longest x2 3.29 us: on_device(): call(functools.partial(second_inner_kernel, field), (f32(ROWS, 128), toke...]
  transfers between devices with their start and end apart: 25 -> 25, of which waited for: 11 -> 12; matrix products, arithmetic and copies ran while one was open for 2% -> 2% of each run, Pallas kernels for 18% -> 20%
where the time goes in v4:
time: 65.3 us; the launch traced here: 65.1 us
  starting transfers between devices  30.4 us (47%)
  Pallas kernels  18 us (28%)
  waiting for transfers between devices  11.9 us (18%)
  local copies, waits for them, and re-layouts  2 us (3%)
  between operations  1.68 us (3%)
  other arithmetic  1.02 us (2%)
    ppermute x6, starting transfers between devices, to_wire(): return lax.ppermute(value, 'wire', [(i, i ^ step) for i in range(wire)])  9.84 us
    ppermute x6, starting transfers between devices, to_chip(): lax.ppermute(value, 'drift', [(i, i ^ 2 * chip_mask(kind, i % 2)) for i i...  9.51 us
    ppermute x4, starting transfers between devices, pairs(): got_first = lax.ppermute(value_first, axis, first)  7.09 us
    ppermute x6, waiting for transfers between devices, to_chip(): lax.ppermute(value, 'drift', [(i, i ^ 2 * chip_mask(kind, i % 2)) for i i...  5.26 us
    pallas_call x4, Pallas kernels, on_device(): call(functools.partial(final_kernel, items, blocks, want_done), (f32(TAPS...  4.36 us
    ppermute x2, starting transfers between devices, pairs(): got_second = lax.ppermute(value_second, axis, sorted(second.items()))  3.42 us
    pallas_call x2, Pallas kernels, on_device(): call(functools.partial(second_inner_kernel, field), (f32(ROWS, 128), toke...  3.29 us
    ppermute x4, waiting for transfers between devices, pairs(): got_first = lax.ppermute(value_first, axis, first)  2.38 us
  transfers between devices with their start and end apart: 25, of which 12 were waited for; matrix products, arithmetic and copies ran while one was open for 2% of the time, Pallas kernels for 20%

profile of v4, /device:TPU:0, one launch (start us, length us, event | category | flops | bytes accessed | tf_op | source)
XLA Modules:
  0.0 65.1 jit_solution(10485453288521809690)
XLA Ops:
  1.3 1.0 %pad_maximum_fusion.pair = bf16[576,256]{1,0:T(8,128)(2,1)S(1)} fusion(bf16[576,128]{1,0:T(8,128)(2,1)} %bitcast.4, bf16[576,128]{1,0:T(8,128)(2,1)} %bitcast.5), kind=kLoop, calls=%fused_computation | loop fusion | flops 589824 | bytes 589824 | tf_op jit(solution)/shard_map/concatenate | solution.py:485
  3.8 3.1 %collective-permute-start = (bf16[48,256]{1,0:T(8,128)(2,1)S(1)}, bf16[48,256]{1,0:T(8,128)(2,1)S(1)}, u32[]{:S(2)}, u32[]{:S(2)}) collective-permute-start(bf16[48,256]{1,0:T(8,128)(2,1)S(1)} %get-tuple-element.46), channel_id=1, source_target_pairs={{0,1},{1,0},{2,3},{3,2},{4,5},{5,4},{6,7},{7,6},{8,9},{9,8},{10,11... | collective-permute-start | bytes 73736 | tf_op jit(solution)/shard_map/ppermute | solution.py:457
  6.9 1.2 %constant_dynamic-update-slice_fusion.1 = bf16[54,128,128]{2,1,0:T(8,128)(2,1)S(1)} fusion(bf16[27,128,128]{2,1,0:T(8,128)(2,1)} %param.8), kind=kLoop, calls=%fused_computation.2 | loop fusion | bytes 1769472
  9.0 3.0 %collective-permute-start.3 = (bf16[64,256]{1,0:T(8,128)(2,1)S(1)}, bf16[64,256]{1,0:T(8,128)(2,1)S(1)}, u32[]{:S(2)}, u32[]{:S(2)}) collective-permute-start(bf16[64,256]{1,0:T(8,128)(2,1)S(1)} %get-tuple-element.50), channel_id=1, source_target_pairs={{0,28},{4,8},{8,4},{12,16},{16,12},{20,24},{24,20},{28,0},{1,29},{... | collective-permute-start | bytes 98312 | tf_op jit(solution)/shard_map/ppermute | solution.py:449
  12.1 1.6 %shard_map.95.inner = f32[768,128]{1,0:T(8,128)S(1)} custom-call(bf16[768,256]{1,0:T(8,128)(2,1)S(1)} %get-tuple-element.48.full.base, bf16[54,128,128]{2,1,0:T(8,128)(2,1)S(1)} %constant_dynamic-update-slice_fusion.weights), custom_call_target="tpu_custom_call" | custom-call | tf_op jit(solution)/shard_map/pallas_call | solution.py:497
  13.8 2.1 %shard_map.96 = (bf16[768,256]{1,0:T(8,128)(2,1)S(1)}, bf16[1664,128]{1,0:T(8,128)(2,1)S(1)}, bf16[1664,128]{1,0:T(8,128)(2,1)S(1)}) custom-call(bf16[768,256]{1,0:T(8,128)(2,1)S(1)} %get-tuple-element.48.full.base, bf16[64,256]{1,0:T(8,128)(2,1)S(1)} %collective-permute-done.2.got_first, bf16[64,256]{1,0:T(8,128)(2,1)S(1)} %collective-permute-done.3.got_second, ...), custom_call_target="tpu_custom_call" | custom-call | tf_op jit(solution)/shard_map/pallas_call | solution.py:498
  16.0 1.1 %shard_map.97.mine = f32[3584,128]{1,0:T(8,128)S(1)} custom-call(bf16[1664,128]{1,0:T(8,128)(2,1)S(1)} %get-tuple-element.53.mine), custom_call_target="tpu_custom_call" | custom-call | tf_op jit(solution)/shard_map/pallas_call | solution.py:507
  18.5 1.6 %collective-permute-start.10 = (bf16[896,128]{1,0:T(8,128)(2,1)S(1)}, bf16[896,128]{1,0:T(8,128)(2,1)S(1)}, u32[]{:S(2)}, u32[]{:S(2)}) collective-permute-start(bf16[896,128]{1,0:T(8,128)(2,1)S(1)} %get-tuple-element.69), channel_id=1, source_target_pairs={{0,8},{4,20},{8,0},{12,28},{16,24},{20,4},{24,16},{28,12},{1,9},{5... | collective-permute-start | bytes 688136 | tf_op jit(solution)/shard_map/ppermute | solution.py:480
  20.2 1.1 %shard_map.99 = (bf16[896,128]{1,0:T(8,128)(2,1)S(1)}, f32[896,128]{1,0:T(8,128)S(1)}, f32[896,128]{1,0:T(8,128)S(1)}, bf16[48,256]{1,0:T(8,128)(2,1)S(1)}, bf16[48,256]{1,0:T(8,128)(2,1)S(1)}) custom-call(f32[3584,128]{1,0:T(8,128)S(1)} %shard_map.97.mine, bf16[128,768]{1,0:T(8,128)(2,1)S(1)} %get-tuple-element.55.left, ...), custom_call_target="tpu_custom_call" | custom-call | tf_op jit(solution)/shard_map/pallas_call | solution.py:516
  21.8 2.9 %collective-permute-done.10.received = bf16[896,128]{1,0:T(8,128)(2,1)S(1)} collective-permute-done((bf16[896,128]{1,0:T(8,128)(2,1)S(1)}, bf16[896,128]{1,0:T(8,128)(2,1)S(1)}, u32[]{:S(2)}, u32[]{:S(2)}) %collective-permute-start.10) | collective-permute-done | bytes 229408 | tf_op jit(solution)/shard_map/ppermute | solution.py:480
  24.7 1.6 %collective-permute-start.11 = (bf16[896,128]{1,0:T(8,128)(2,1)S(1)}, bf16[896,128]{1,0:T(8,128)(2,1)S(1)}, u32[]{:S(2)}, u32[]{:S(2)}) collective-permute-start(bf16[896,128]{1,0:T(8,128)(2,1)S(1)} %shard_map.103), channel_id=1, source_target_pairs={{0,16},{4,12},{8,24},{12,4},{16,0},{20,28},{24,8},{28,20},{1,17},{... | collective-permute-start | bytes 688136 | tf_op jit(solution)/shard_map/ppermute | solution.py:480
  26.3 2.7 %collective-permute-start.5 = (bf16[48,256]{1,0:T(8,128)(2,1)S(1)}, bf16[48,256]{1,0:T(8,128)(2,1)S(1)}, u32[]{:S(2)}, u32[]{:S(2)}) collective-permute-start(bf16[48,256]{1,0:T(8,128)(2,1)S(1)} %get-tuple-element.57), channel_id=1, source_target_pairs={{0,1},{1,0},{2,3},{3,2},{4,5},{5,4},{6,7},{7,6},{8,9},{9,8},{10,11... | collective-permute-start | bytes 73736 | tf_op jit(solution)/shard_map/ppermute | solution.py:457
  29.0 1.8 %collective-permute-done.5.got_first = bf16[48,256]{1,0:T(8,128)(2,1)S(1)} collective-permute-done((bf16[48,256]{1,0:T(8,128)(2,1)S(1)}, bf16[48,256]{1,0:T(8,128)(2,1)S(1)}, u32[]{:S(2)}, u32[]{:S(2)}) %collective-permute-start.5) | collective-permute-done | bytes 24608 | tf_op jit(solution)/shard_map/ppermute | solution.py:457
  31.2 2.5 %collective-permute-start.12 = (bf16[224,128]{1,0:T(8,128)(2,1)S(1)}, bf16[224,128]{1,0:T(8,128)(2,1)S(1)}, u32[]{:S(2)}, u32[]{:S(2)}) collective-permute-start(bf16[224,128]{1,0:T(8,128)(2,1)S(1)} %get-tuple-element.71), channel_id=1, source_target_pairs={{0,1},{1,0},{2,3},{3,2},{4,5},{5,4},{6,7},{7,6},{8,9},{9,8},{10,11... | collective-permute-start | bytes 172040 | tf_op jit(solution)/shard_map/ppermute | solution.py:483
  33.7 1.5 %collective-permute-start.13 = (bf16[224,128]{1,0:T(8,128)(2,1)S(1)}, bf16[224,128]{1,0:T(8,128)(2,1)S(1)}, u32[]{:S(2)}, u32[]{:S(2)}) collective-permute-start(bf16[224,128]{1,0:T(8,128)(2,1)S(1)} %get-tuple-element.72), channel_id=1, source_target_pairs={{0,2},{1,3},{2,0},{3,1},{4,6},{5,7},{6,4},{7,5},{8,10},{9,11},{10,... | collective-permute-start | bytes 172040 | tf_op jit(solution)/shard_map/ppermute | solution.py:483
  35.2 1.4 %collective-permute-start.14 = (bf16[224,128]{1,0:T(8,128)(2,1)S(1)}, bf16[224,128]{1,0:T(8,128)(2,1)S(1)}, u32[]{:S(2)}, u32[]{:S(2)}) collective-permute-start(bf16[224,128]{1,0:T(8,128)(2,1)S(1)} %get-tuple-element.73), channel_id=1, source_target_pairs={{0,3},{1,2},{2,1},{3,0},{4,7},{5,6},{6,5},{7,4},{8,11},{9,10},{10,... | collective-permute-start | bytes 172040 | tf_op jit(solution)/shard_map/ppermute | solution.py:483
  37.0 1.2 %collective-permute-start.7 = (bf16[64,256]{1,0:T(8,128)(2,1)S(1)}, bf16[64,256]{1,0:T(8,128)(2,1)S(1)}, u32[]{:S(2)}, u32[]{:S(2)}) collective-permute-start(bf16[64,256]{1,0:T(8,128)(2,1)S(1)} %get-tuple-element.62.after), channel_id=1, source_target_pairs={{0,4},{4,0},{8,12},{12,8},{16,20},{20,16},{24,28},{28,24},{1,5},{5... | collective-permute-start | bytes 98312 | tf_op jit(solution)/shard_map/ppermute | solution.py:457
  38.2 1.6 %shard_map.101 = (f32[768,128]{1,0:T(8,128)S(1)}, f32[8,128]{1,0:T(8,128)S(1)}) custom-call(bf16[768,256]{1,0:T(8,128)(2,1)S(1)} %get-tuple-element.59.hb, bf16[54,128,128]{2,1,0:T(8,128)(2,1)S(1)} %constant_dynamic-update-slice_fusion.weights), custom_call_target="tpu_custom_call" | custom-call | tf_op jit(solution)/shard_map/pallas_call | solution.py:537
  39.9 1.1 %collective-permute-done.8.after_second.got_second = bf16[64,256]{1,0:T(8,128)(2,1)S(1)} collective-permute-done((bf16[64,256]{1,0:T(8,128)(2,1)S(1)}, bf16[64,256]{1,0:T(8,128)(2,1)S(1)}, u32[]{:S(2)}, u32[]{:S(2)}) %collective-permute-start.8) | collective-permute-done | bytes 32800 | tf_op jit(solution)/shard_map/ppermute | solution.py:449
  41.3 2.3 %collective-permute-start.17 = (bf16[224,128]{1,0:T(8,128)(2,1)S(1)}, bf16[224,128]{1,0:T(8,128)(2,1)S(1)}, u32[]{:S(2)}, u32[]{:S(2)}) collective-permute-start(bf16[224,128]{1,0:T(8,128)(2,1)S(1)} %shard_map.105.refs_0_), channel_id=1, source_target_pairs={{0,3},{1,2},{2,1},{3,0},{4,7},{5,6},{6,5},{7,4},{8,11},{9,10},{10,... | collective-permute-start | bytes 172040 | tf_op jit(solution)/shard_map/ppermute | solution.py:483
  43.6 2.2 %collective-permute-start.15 = (bf16[224,128]{1,0:T(8,128)(2,1)S(1)}, bf16[224,128]{1,0:T(8,128)(2,1)S(1)}, u32[]{:S(2)}, u32[]{:S(2)}) collective-permute-start(bf16[224,128]{1,0:T(8,128)(2,1)S(1)} %shard_map.105.refs_0_), channel_id=1, source_target_pairs={{0,1},{1,0},{2,3},{3,2},{4,5},{5,4},{6,7},{7,6},{8,9},{9,8},{10,11... | collective-permute-start | bytes 172040 | tf_op jit(solution)/shard_map/ppermute | solution.py:483
  45.8 1.7 %shard_map.102 = (f32[768,128]{1,0:T(8,128)S(1)}, f32[8,128]{1,0:T(8,128)S(1)}) custom-call(bf16[768,256]{1,0:T(8,128)(2,1)S(1)} %get-tuple-element.59.hb, bf16[54,128,128]{2,1,0:T(8,128)(2,1)S(1)} %constant_dynamic-update-slice_fusion.weights), custom_call_target="tpu_custom_call" | custom-call | tf_op jit(solution)/shard_map/pallas_call | solution.py:537
  47.7 1.4 %collective-permute-done.16.refs_2_ = bf16[224,128]{1,0:T(8,128)(2,1)S(1)} collective-permute-done((bf16[224,128]{1,0:T(8,128)(2,1)S(1)}, bf16[224,128]{1,0:T(8,128)(2,1)S(1)}, u32[]{:S(2)}, u32[]{:S(2)}) %collective-permute-start.16) | collective-permute-done | bytes 57376 | tf_op jit(solution)/shard_map/ppermute | solution.py:483
  49.1 1.3 %collective-permute-start.19 = (bf16[896,128]{1,0:T(8,128)(2,1)S(1)}, bf16[896,128]{1,0:T(8,128)(2,1)S(1)}, u32[]{:S(2)}, u32[]{:S(2)}) collective-permute-start(bf16[896,128]{1,0:T(8,128)(2,1)S(1)} %shard_map.106.held.refs_0_), channel_id=1, source_target_pairs={{0,8},{4,20},{8,0},{12,28},{16,24},{20,4},{24,16},{28,12},{1,9},{5... | collective-permute-start | bytes 688136 | tf_op jit(solution)/shard_map/ppermute | solution.py:480
  50.4 2.1 %shard_map.107 = (bf16[576,128]{1,0:T(8,128)(2,1)}, bf16[576,128]{1,0:T(8,128)(2,1)}, bf16[896,128]{1,0:T(8,128)(2,1)S(1)}) custom-call(s32[1,1,16]{2,1,0:T(1,128)S(1)} %copy-done.1, s32[1,1]{1,0:T(1,128)S(6)} %copy.23.counts, f32[768,128]{1,0:T(8,128)S(1)} %get-tuple-element.60.inner_hidden, f32[768,128]{1,0:T(8,128)S(1)} %get-tuple-element.61.inner_back, ...), custom_call_target="tpu_custom_call" | custom-call | tf_op jit(solution)/shard_map/pallas_call | solution.py:559
  52.5 1.6 %collective-permute-start.18 = (bf16[896,128]{1,0:T(8,128)(2,1)S(1)}, bf16[896,128]{1,0:T(8,128)(2,1)S(1)}, u32[]{:S(2)}, u32[]{:S(2)}) collective-permute-start(bf16[896,128]{1,0:T(8,128)(2,1)S(1)} %get-tuple-element.76), channel_id=1, source_target_pairs={{0,16},{4,12},{8,24},{12,4},{16,0},{20,28},{24,8},{28,20},{1,17},{... | collective-permute-start | bytes 688136 | tf_op jit(solution)/shard_map/ppermute | solution.py:480
  54.2 1.4 %collective-permute-done.19.refs_2_ = bf16[896,128]{1,0:T(8,128)(2,1)S(1)} collective-permute-done((bf16[896,128]{1,0:T(8,128)(2,1)S(1)}, bf16[896,128]{1,0:T(8,128)(2,1)S(1)}, u32[]{:S(2)}, u32[]{:S(2)}) %collective-permute-start.19) | collective-permute-done | bytes 229408 | tf_op jit(solution)/shard_map/ppermute | solution.py:480
  55.6 2.9 %collective-permute-start.23 = (bf16[896,128]{1,0:T(8,128)(2,1)S(1)}, bf16[896,128]{1,0:T(8,128)(2,1)S(1)}, u32[]{:S(2)}, u32[]{:S(2)}) collective-permute-start(bf16[896,128]{1,0:T(8,128)(2,1)S(1)} %collective-permute-done.19.refs_2_), channel_id=1, source_target_pairs={{0,16},{4,12},{8,24},{12,4},{16,0},{20,28},{24,8},{28,20},{1,17},{... | collective-permute-start | bytes 688136 | tf_op jit(solution)/shard_map/ppermute | solution.py:480
  59.0 1.3 %shard_map.108 = (f32[27,128,128]{2,1,0:T(8,128)}, f32[27,128,128]{2,1,0:T(8,128)}) custom-call(bf16[896,128]{1,0:T(8,128)(2,1)S(1)} %shard_map.106.held.refs_0_, bf16[896,128]{1,0:T(8,128)(2,1)S(1)} %collective-permute-done.22.refs_1_, bf16[896,128]{1,0:T(8,128)(2,1)S(1)} %collective-permute-done.19.refs_2_), custom_call_target="tpu_custom_call" | custom-call | flops 49999998976 | tf_op jit(solution)/shard_map/pallas_call | solution.py:588
  60.3 1.3 %shard_map.109 = (f32[27,128,128]{2,1,0:T(8,128)}, f32[27,128,128]{2,1,0:T(8,128)}, f32[8,128]{1,0:T(8,128)S(1)}) custom-call(bf16[896,128]{1,0:T(8,128)(2,1)S(1)} %collective-permute-done.18.refs_0_, bf16[896,128]{1,0:T(8,128)(2,1)S(1)} %collective-permute-done.20.refs_1_, ...), custom_call_target="tpu_custom_call", output_to_operand_aliasing={{0}: (3, {}), {1}: (4, {})} | custom-call | flops 49999998976 | tf_op jit(solution)/shard_map/pallas_call | solution.py:588
  61.6 0.9 %collective-permute-done.23.value.refs_0_ = bf16[896,128]{1,0:T(8,128)(2,1)S(1)} collective-permute-done((bf16[896,128]{1,0:T(8,128)(2,1)S(1)}, bf16[896,128]{1,0:T(8,128)(2,1)S(1)}, u32[]{:S(2)}, u32[]{:S(2)}) %collective-permute-start.23) | collective-permute-done | bytes 229408 | tf_op jit(solution)/shard_map/ppermute | solution.py:480
  64.0 0.9 %shard_map.112 = (f32[27,128,128]{2,1,0:T(8,128)}, f32[27,128,128]{2,1,0:T(8,128)}) custom-call(bf16[896,128]{1,0:T(8,128)(2,1)S(1)} %collective-permute-done.24.refs_0_, f32[27,128,128]{2,1,0:T(8,128)} %get-tuple-element.82.refs_1_, f32[27,128,128]{2,1,0:T(8,128)} %get-tuple-element.83.refs_2_), custom_call_target="tpu_custom_call", output_to_operand_aliasing={{0}: (1, {}), {1}: (2, {})} | custom-call | flops 49999998976 | tf_op jit(solution)/shard_map/pallas_call | solution.py:588
  (47 shorter events, 8.1 us)
Async XLA Ops:
  2.3 0.7 %copy-start = (s32[1,1,16]{2,1,0:T(1,128)S(1)}, s32[1,1,16]{2,1,0:T(1,128)}, u32[]{:S(2)}) copy-start(s32[1,1,16]{2,1,0:T(1,128)} %lists.3) | copy-start | bytes 196
  3.0 9.1 %copy-start.2 = (bf16[27,128,128]{2,1,0:T(8,128)(2,1)S(1)}, bf16[27,128,128]{2,1,0:T(8,128)(2,1)}, u32[]{:S(2)}) copy-start(bf16[27,128,128]{2,1,0:T(8,128)(2,1)} %param.9) | copy-start | bytes 2654212
  3.8 4.9 %collective-permute-start = (bf16[48,256]{1,0:T(8,128)(2,1)S(1)}, bf16[48,256]{1,0:T(8,128)(2,1)S(1)}, u32[]{:S(2)}, u32[]{:S(2)}) collective-permute-start(bf16[48,256]{1,0:T(8,128)(2,1)S(1)} %get-tuple-element.46), channel_id=1, source_target_pairs={{0,1},{1,0},{2,3},{3,2},{4,5},{5,4},{6,7},{7,6},{8,9},{9,8},{10,11... | collective-permute-start | bytes 73736 | tf_op jit(solution)/shard_map/ppermute | solution.py:457
  6.9 1.8 %collective-permute-start.1 = (bf16[48,256]{1,0:T(8,128)(2,1)S(1)}, bf16[48,256]{1,0:T(8,128)(2,1)S(1)}, u32[]{:S(2)}, u32[]{:S(2)}) collective-permute-start(bf16[48,256]{1,0:T(8,128)(2,1)S(1)} %get-tuple-element.47), channel_id=1, source_target_pairs={{0,4},{1,2},{2,1},{3,7},{4,0},{5,6},{6,5},{7,3},{8,12},{9,10},{10,... | collective-permute-start | bytes 73736 | tf_op jit(solution)/shard_map/ppermute | solution.py:456
  8.9 4.8 %collective-permute-start.2 = (bf16[64,256]{1,0:T(8,128)(2,1)S(1)}, bf16[64,256]{1,0:T(8,128)(2,1)S(1)}, u32[]{:S(2)}, u32[]{:S(2)}) collective-permute-start(bf16[64,256]{1,0:T(8,128)(2,1)S(1)} %get-tuple-element.49), channel_id=1, source_target_pairs={{0,4},{4,0},{8,12},{12,8},{16,20},{20,16},{24,28},{28,24},{1,5},{5... | collective-permute-start | bytes 98312 | tf_op jit(solution)/shard_map/ppermute | solution.py:457
  9.0 4.7 %collective-permute-start.3 = (bf16[64,256]{1,0:T(8,128)(2,1)S(1)}, bf16[64,256]{1,0:T(8,128)(2,1)S(1)}, u32[]{:S(2)}, u32[]{:S(2)}) collective-permute-start(bf16[64,256]{1,0:T(8,128)(2,1)S(1)} %get-tuple-element.50), channel_id=1, source_target_pairs={{0,28},{4,8},{8,4},{12,16},{16,12},{20,24},{24,20},{28,0},{1,29},{... | collective-permute-start | bytes 98312 | tf_op jit(solution)/shard_map/ppermute | solution.py:449
  15.9 1.8 %collective-permute-start.4 = (bf16[1664,128]{1,0:T(8,128)(2,1)S(1)}, bf16[1664,128]{1,0:T(8,128)(2,1)S(1)}, u32[]{:S(2)}, u32[]{:S(2)}) collective-permute-start(bf16[1664,128]{1,0:T(8,128)(2,1)S(1)} %get-tuple-element.54), channel_id=1, source_target_pairs={{0,4},{4,0},{8,12},{12,8},{16,20},{20,16},{24,28},{28,24},{1,5},{5... | collective-permute-start | bytes 1277960 | tf_op jit(solution)/shard_map/ppermute | solution.py:477
  18.5 6.1 %collective-permute-start.10 = (bf16[896,128]{1,0:T(8,128)(2,1)S(1)}, bf16[896,128]{1,0:T(8,128)(2,1)S(1)}, u32[]{:S(2)}, u32[]{:S(2)}) collective-permute-start(bf16[896,128]{1,0:T(8,128)(2,1)S(1)} %get-tuple-element.69), channel_id=1, source_target_pairs={{0,8},{4,20},{8,0},{12,28},{16,24},{20,4},{24,16},{28,12},{1,9},{5... | collective-permute-start | bytes 688136 | tf_op jit(solution)/shard_map/ppermute | solution.py:480
  21.2 9.8 %collective-permute-start.9 = (bf16[896,128]{1,0:T(8,128)(2,1)S(1)}, bf16[896,128]{1,0:T(8,128)(2,1)S(1)}, u32[]{:S(2)}, u32[]{:S(2)}) collective-permute-start(bf16[896,128]{1,0:T(8,128)(2,1)S(1)} %get-tuple-element.67), channel_id=1, source_target_pairs={{0,8},{4,20},{8,0},{12,28},{16,24},{20,4},{24,16},{28,12},{1,9},{5... | collective-permute-start | bytes 688136 | tf_op jit(solution)/shard_map/ppermute | solution.py:480
  24.7 6.4 %collective-permute-start.11 = (bf16[896,128]{1,0:T(8,128)(2,1)S(1)}, bf16[896,128]{1,0:T(8,128)(2,1)S(1)}, u32[]{:S(2)}, u32[]{:S(2)}) collective-permute-start(bf16[896,128]{1,0:T(8,128)(2,1)S(1)} %shard_map.103), channel_id=1, source_target_pairs={{0,16},{4,12},{8,24},{12,4},{16,0},{20,28},{24,8},{28,20},{1,17},{... | collective-permute-start | bytes 688136 | tf_op jit(solution)/shard_map/ppermute | solution.py:480
  26.3 4.5 %collective-permute-start.5 = (bf16[48,256]{1,0:T(8,128)(2,1)S(1)}, bf16[48,256]{1,0:T(8,128)(2,1)S(1)}, u32[]{:S(2)}, u32[]{:S(2)}) collective-permute-start(bf16[48,256]{1,0:T(8,128)(2,1)S(1)} %get-tuple-element.57), channel_id=1, source_target_pairs={{0,1},{1,0},{2,3},{3,2},{4,5},{5,4},{6,7},{7,6},{8,9},{9,8},{10,11... | collective-permute-start | bytes 73736 | tf_op jit(solution)/shard_map/ppermute | solution.py:457
  29.0 1.8 %collective-permute-start.6 = (bf16[48,256]{1,0:T(8,128)(2,1)S(1)}, bf16[48,256]{1,0:T(8,128)(2,1)S(1)}, u32[]{:S(2)}, u32[]{:S(2)}) collective-permute-start(bf16[48,256]{1,0:T(8,128)(2,1)S(1)} %get-tuple-element.58), channel_id=1, source_target_pairs={{0,4},{1,2},{2,1},{3,7},{4,0},{5,6},{6,5},{7,3},{8,12},{9,10},{10,... | collective-permute-start | bytes 73736 | tf_op jit(solution)/shard_map/ppermute | solution.py:456
  31.2 9.8 %collective-permute-start.12 = (bf16[224,128]{1,0:T(8,128)(2,1)S(1)}, bf16[224,128]{1,0:T(8,128)(2,1)S(1)}, u32[]{:S(2)}, u32[]{:S(2)}) collective-permute-start(bf16[224,128]{1,0:T(8,128)(2,1)S(1)} %get-tuple-element.71), channel_id=1, source_target_pairs={{0,1},{1,0},{2,3},{3,2},{4,5},{5,4},{6,7},{7,6},{8,9},{9,8},{10,11... | collective-permute-start | bytes 172040 | tf_op jit(solution)/shard_map/ppermute | solution.py:483
  33.7 7.4 %collective-permute-start.13 = (bf16[224,128]{1,0:T(8,128)(2,1)S(1)}, bf16[224,128]{1,0:T(8,128)(2,1)S(1)}, u32[]{:S(2)}, u32[]{:S(2)}) collective-permute-start(bf16[224,128]{1,0:T(8,128)(2,1)S(1)} %get-tuple-element.72), channel_id=1, source_target_pairs={{0,2},{1,3},{2,0},{3,1},{4,6},{5,7},{6,4},{7,5},{8,10},{9,11},{10,... | collective-permute-start | bytes 172040 | tf_op jit(solution)/shard_map/ppermute | solution.py:483
  35.2 6.1 %collective-permute-start.14 = (bf16[224,128]{1,0:T(8,128)(2,1)S(1)}, bf16[224,128]{1,0:T(8,128)(2,1)S(1)}, u32[]{:S(2)}, u32[]{:S(2)}) collective-permute-start(bf16[224,128]{1,0:T(8,128)(2,1)S(1)} %get-tuple-element.73), channel_id=1, source_target_pairs={{0,3},{1,2},{2,1},{3,0},{4,7},{5,6},{6,5},{7,4},{8,11},{9,10},{10,... | collective-permute-start | bytes 172040 | tf_op jit(solution)/shard_map/ppermute | solution.py:483
  36.6 4.4 %collective-permute-start.8 = (bf16[64,256]{1,0:T(8,128)(2,1)S(1)}, bf16[64,256]{1,0:T(8,128)(2,1)S(1)}, u32[]{:S(2)}, u32[]{:S(2)}) collective-permute-start(bf16[64,256]{1,0:T(8,128)(2,1)S(1)} %get-tuple-element.63), channel_id=1, source_target_pairs={{0,28},{4,8},{8,4},{12,16},{16,12},{20,24},{24,20},{28,0},{1,29},{... | collective-permute-start | bytes 98312 | tf_op jit(solution)/shard_map/ppermute | solution.py:449
  37.0 4.0 %collective-permute-start.7 = (bf16[64,256]{1,0:T(8,128)(2,1)S(1)}, bf16[64,256]{1,0:T(8,128)(2,1)S(1)}, u32[]{:S(2)}, u32[]{:S(2)}) collective-permute-start(bf16[64,256]{1,0:T(8,128)(2,1)S(1)} %get-tuple-element.62.after), channel_id=1, source_target_pairs={{0,4},{4,0},{8,12},{12,8},{16,20},{20,16},{24,28},{28,24},{1,5},{5... | collective-permute-start | bytes 98312 | tf_op jit(solution)/shard_map/ppermute | solution.py:457
  39.9 10.6 %copy-start.1 = (s32[1,1,16]{2,1,0:T(1,128)S(1)}, s32[1,1,16]{2,1,0:T(1,128)}, u32[]{:S(2)}) copy-start(s32[1,1,16]{2,1,0:T(1,128)} %lists.3) | copy-start | bytes 196
  41.3 6.4 %collective-permute-start.17 = (bf16[224,128]{1,0:T(8,128)(2,1)S(1)}, bf16[224,128]{1,0:T(8,128)(2,1)S(1)}, u32[]{:S(2)}, u32[]{:S(2)}) collective-permute-start(bf16[224,128]{1,0:T(8,128)(2,1)S(1)} %shard_map.105.refs_0_), channel_id=1, source_target_pairs={{0,3},{1,2},{2,1},{3,0},{4,7},{5,6},{6,5},{7,4},{8,11},{9,10},{10,... | collective-permute-start | bytes 172040 | tf_op jit(solution)/shard_map/ppermute | solution.py:483
  43.6 5.5 %collective-permute-start.16 = (bf16[224,128]{1,0:T(8,128)(2,1)S(1)}, bf16[224,128]{1,0:T(8,128)(2,1)S(1)}, u32[]{:S(2)}, u32[]{:S(2)}) collective-permute-start(bf16[224,128]{1,0:T(8,128)(2,1)S(1)} %shard_map.105.refs_0_), channel_id=1, source_target_pairs={{0,2},{1,3},{2,0},{3,1},{4,6},{5,7},{6,4},{7,5},{8,10},{9,11},{10,... | collective-permute-start | bytes 172040 | tf_op jit(solution)/shard_map/ppermute | solution.py:483
  43.6 5.5 %collective-permute-start.15 = (bf16[224,128]{1,0:T(8,128)(2,1)S(1)}, bf16[224,128]{1,0:T(8,128)(2,1)S(1)}, u32[]{:S(2)}, u32[]{:S(2)}) collective-permute-start(bf16[224,128]{1,0:T(8,128)(2,1)S(1)} %shard_map.105.refs_0_), channel_id=1, source_target_pairs={{0,1},{1,0},{2,3},{3,2},{4,5},{5,4},{6,7},{7,6},{8,9},{9,8},{10,11... | collective-permute-start | bytes 172040 | tf_op jit(solution)/shard_map/ppermute | solution.py:483
  49.1 6.4 %collective-permute-start.19 = (bf16[896,128]{1,0:T(8,128)(2,1)S(1)}, bf16[896,128]{1,0:T(8,128)(2,1)S(1)}, u32[]{:S(2)}, u32[]{:S(2)}) collective-permute-start(bf16[896,128]{1,0:T(8,128)(2,1)S(1)} %shard_map.106.held.refs_0_), channel_id=1, source_target_pairs={{0,8},{4,20},{8,0},{12,28},{16,24},{20,4},{24,16},{28,12},{1,9},{5... | collective-permute-start | bytes 688136 | tf_op jit(solution)/shard_map/ppermute | solution.py:480
  52.5 6.0 %collective-permute-start.18 = (bf16[896,128]{1,0:T(8,128)(2,1)S(1)}, bf16[896,128]{1,0:T(8,128)(2,1)S(1)}, u32[]{:S(2)}, u32[]{:S(2)}) collective-permute-start(bf16[896,128]{1,0:T(8,128)(2,1)S(1)} %get-tuple-element.76), channel_id=1, source_target_pairs={{0,16},{4,12},{8,24},{12,4},{16,0},{20,28},{24,8},{28,20},{1,17},{... | collective-permute-start | bytes 688136 | tf_op jit(solution)/shard_map/ppermute | solution.py:480
  54.1 4.8 %collective-permute-start.22 = (bf16[896,128]{1,0:T(8,128)(2,1)S(1)}, bf16[896,128]{1,0:T(8,128)(2,1)S(1)}, u32[]{:S(2)}, u32[]{:S(2)}) collective-permute-start(bf16[896,128]{1,0:T(8,128)(2,1)S(1)} %shard_map.106.held.refs_0_), channel_id=1, source_target_pairs={{0,4},{4,0},{8,12},{12,8},{16,20},{20,16},{24,28},{28,24},{1,5},{5... | collective-permute-start | bytes 688136 | tf_op jit(solution)/shard_map/ppermute | solution.py:477
  55.6 6.9 %collective-permute-start.23 = (bf16[896,128]{1,0:T(8,128)(2,1)S(1)}, bf16[896,128]{1,0:T(8,128)(2,1)S(1)}, u32[]{:S(2)}, u32[]{:S(2)}) collective-permute-start(bf16[896,128]{1,0:T(8,128)(2,1)S(1)} %collective-permute-done.19.refs_2_), channel_id=1, source_target_pairs={{0,16},{4,12},{8,24},{12,4},{16,0},{20,28},{24,8},{28,20},{1,17},{... | collective-permute-start | bytes 688136 | tf_op jit(solution)/shard_map/ppermute | solution.py:480
  58.4 1.8 %collective-permute-start.20 = (bf16[896,128]{1,0:T(8,128)(2,1)S(1)}, bf16[896,128]{1,0:T(8,128)(2,1)S(1)}, u32[]{:S(2)}, u32[]{:S(2)}) collective-permute-start(bf16[896,128]{1,0:T(8,128)(2,1)S(1)} %collective-permute-done.19.refs_2_), channel_id=1, source_target_pairs={{0,4},{4,0},{8,12},{12,8},{16,20},{20,16},{24,28},{28,24},{1,5},{5... | collective-permute-start | bytes 688136 | tf_op jit(solution)/shard_map/ppermute | solution.py:477
  58.5 1.7 %collective-permute-start.21 = (bf16[896,128]{1,0:T(8,128)(2,1)S(1)}, bf16[896,128]{1,0:T(8,128)(2,1)S(1)}, u32[]{:S(2)}, u32[]{:S(2)}) collective-permute-start(bf16[896,128]{1,0:T(8,128)(2,1)S(1)} %collective-permute-done.18.refs_0_), channel_id=1, source_target_pairs={{0,4},{4,0},{8,12},{12,8},{16,20},{20,16},{24,28},{28,24},{1,5},{5... | collective-permute-start | bytes 688136 | tf_op jit(solution)/shard_map/ppermute | solution.py:477
  62.5 1.6 %collective-permute-start.24 = (bf16[896,128]{1,0:T(8,128)(2,1)S(1)}, bf16[896,128]{1,0:T(8,128)(2,1)S(1)}, u32[]{:S(2)}, u32[]{:S(2)}) collective-permute-start(bf16[896,128]{1,0:T(8,128)(2,1)S(1)} %shard_map.110), channel_id=1, source_target_pairs={{0,4},{4,0},{8,12},{12,8},{16,20},{20,16},{24,28},{28,24},{1,5},{5... | collective-permute-start | bytes 688136 | tf_op jit(solution)/shard_map/ppermute | solution.py:477

commit v5 on v4

--- a/solution.py
+++ b/solution.py
@@ -346,7 +346,7 @@
         out[...] = total[pl.ds(start, unit), :].astype(jnp.bfloat16)
 
 
-def sum_kernel(scale, after_inner, after_first, after_second, own, *refs):
+def sum_kernel(scale, after, own, *refs):
     *received, out = refs
     summed = own[...]
     for part in received:
@@ -549,10 +549,10 @@
         [pltpu.VMEM((chunk, 128), jnp.float32)],
     )(inserted, own, *parts)
 
-    received = [to_wire(s, k + 1) for k, s in enumerate(sends)]
+    received = [to_wire(sends[k - 1], k) for k in reversed(range(1, wire))]
     scale = 1.0 / math.sqrt(float(drift * wire * slots))
-    summed = call(functools.partial(sum_kernel, scale), bf16(unit, 128), [VMEM] * (3 + wire))(
-        hidden_done, *hb_slabs, own, *received
+    summed = call(functools.partial(sum_kernel, scale), bf16(unit, 128), [VMEM] * (1 + wire))(
+        hidden_done, own, *received
     )
     pieces = [summed] + [to_wire(summed, k) for k in range(1, wire)]
     mine = call(functools.partial(joined_kernel, unit), bf16(chunk, 128), [VMEM] * (1 + wire))(back_done, *pieces)

time: 65.3 us -> 63.9 us (0.979)
  starting transfers between devices: 30.4 us -> 28.6 us
    ppermute x6, waiting for transfers between devices: 1.9 us -> 3.22 us  [to_wire(): return lax.ppermute(value, 'wire', [(i, i ^ step) for i in range(wire)])]
    ppermute x2, waiting for transfers between devices: 1.14 us -> 0.01 us  [pairs(): got_second = lax.ppermute(value_second, axis, sorted(second.items()))]
    ppermute x6, starting transfers between devices: 9.84 us -> 8.94 us  [to_wire(): return lax.ppermute(value, 'wire', [(i, i ^ step) for i in range(wire)])]
  transfers between devices with their start and end apart: 25 -> 25, of which waited for: 12 -> 11; matrix products, arithmetic and copies ran while one was open for 2% -> 2% of each run, Pallas kernels for 20% -> 20%
where the time goes in v5:
time: 63.9 us; the launch traced here: 63.7 us
  starting transfers between devices  28.6 us (45%)
  Pallas kernels  18 us (28%)
  waiting for transfers between devices  12.4 us (19%)
  local copies, waits for them, and re-layouts  2 us (3%)
  between operations  1.67 us (3%)
  other arithmetic  1.02 us (2%)
    ppermute x6, starting transfers between devices, to_chip(): lax.ppermute(value, 'drift', [(i, i ^ 2 * chip_mask(kind, i % 2)) for i i...  8.95 us
    ppermute x6, starting transfers between devices, to_wire(): return lax.ppermute(value, 'wire', [(i, i ^ step) for i in range(wire)])  8.94 us
    ppermute x4, starting transfers between devices, pairs(): got_first = lax.ppermute(value_first, axis, first)  7.38 us
    ppermute x6, waiting for transfers between devices, to_chip(): lax.ppermute(value, 'drift', [(i, i ^ 2 * chip_mask(kind, i % 2)) for i i...  5.48 us
    pallas_call x4, Pallas kernels, on_device(): call(functools.partial(final_kernel, items, blocks, want_done), (f32(TAPS...  4.33 us
    pallas_call x2, Pallas kernels, on_device(): call(functools.partial(second_inner_kernel, field), (f32(ROWS, 128), toke...  3.29 us
    ppermute x6, waiting for transfers between devices, to_wire(): return lax.ppermute(value, 'wire', [(i, i ^ step) for i in range(wire)])  3.22 us
    ppermute x2, starting transfers between devices, pairs(): got_second = lax.ppermute(value_second, axis, sorted(second.items()))  2.98 us
  transfers between devices with their start and end apart: 25, of which 11 were waited for; matrix products, arithmetic and copies ran while one was open for 2% of the time, Pallas kernels for 20%

profile of v5, /device:TPU:0, one launch (start us, length us, event | category | flops | bytes accessed | tf_op | source)
XLA Modules:
  0.0 63.7 jit_solution(7407386724732219479)
XLA Ops:
  1.3 1.0 %pad_maximum_fusion.pair = bf16[576,256]{1,0:T(8,128)(2,1)S(1)} fusion(bf16[576,128]{1,0:T(8,128)(2,1)} %bitcast.4, bf16[576,128]{1,0:T(8,128)(2,1)} %bitcast.5), kind=kLoop, calls=%fused_computation | loop fusion | flops 589824 | bytes 589824 | tf_op jit(solution)/shard_map/concatenate | solution.py:485
  3.0 0.8 %shard_map.93 = (bf16[48,256]{1,0:T(8,128)(2,1)S(1)}, bf16[48,256]{1,0:T(8,128)(2,1)S(1)}, bf16[768,256]{1,0:T(8,128)(2,1)S(1)}, bf16[768,128]{1,0:T(8,128)(2,1)S(1)}) custom-call(s32[1,1]{1,0:T(1,128)S(6)} %copy.23.counts, s32[1,1,16]{2,1,0:T(1,128)S(1)} %copy-done, bf16[576,256]{1,0:T(8,128)(2,1)S(1)} %pad_maximum_fusion.pair), custom_call_target="tpu_custom_call" | custom-call | tf_op jit(solution)/shard_map/pallas_call | solution.py:487
  3.8 3.1 %collective-permute-start = (bf16[48,256]{1,0:T(8,128)(2,1)S(1)}, bf16[48,256]{1,0:T(8,128)(2,1)S(1)}, u32[]{:S(2)}, u32[]{:S(2)}) collective-permute-start(bf16[48,256]{1,0:T(8,128)(2,1)S(1)} %get-tuple-element.46), channel_id=1, source_target_pairs={{0,1},{1,0},{2,3},{3,2},{4,5},{5,4},{6,7},{7,6},{8,9},{9,8},{10,11... | collective-permute-start | bytes 73736 | tf_op jit(solution)/shard_map/ppermute | solution.py:457
  6.9 1.2 %constant_dynamic-update-slice_fusion.1 = bf16[54,128,128]{2,1,0:T(8,128)(2,1)S(1)} fusion(bf16[27,128,128]{2,1,0:T(8,128)(2,1)} %param.8), kind=kLoop, calls=%fused_computation.2 | loop fusion | bytes 1769472
  9.0 3.0 %collective-permute-start.3 = (bf16[64,256]{1,0:T(8,128)(2,1)S(1)}, bf16[64,256]{1,0:T(8,128)(2,1)S(1)}, u32[]{:S(2)}, u32[]{:S(2)}) collective-permute-start(bf16[64,256]{1,0:T(8,128)(2,1)S(1)} %get-tuple-element.50), channel_id=1, source_target_pairs={{0,28},{4,8},{8,4},{12,16},{16,12},{20,24},{24,20},{28,0},{1,29},{... | collective-permute-start | bytes 98312 | tf_op jit(solution)/shard_map/ppermute | solution.py:449
  12.1 1.6 %shard_map.95.inner = f32[768,128]{1,0:T(8,128)S(1)} custom-call(bf16[768,256]{1,0:T(8,128)(2,1)S(1)} %get-tuple-element.48.full.base, bf16[54,128,128]{2,1,0:T(8,128)(2,1)S(1)} %constant_dynamic-update-slice_fusion.weights), custom_call_target="tpu_custom_call" | custom-call | tf_op jit(solution)/shard_map/pallas_call | solution.py:497
  13.8 2.1 %shard_map.96 = (bf16[768,256]{1,0:T(8,128)(2,1)S(1)}, bf16[1664,128]{1,0:T(8,128)(2,1)S(1)}, bf16[1664,128]{1,0:T(8,128)(2,1)S(1)}) custom-call(bf16[768,256]{1,0:T(8,128)(2,1)S(1)} %get-tuple-element.48.full.base, bf16[64,256]{1,0:T(8,128)(2,1)S(1)} %collective-permute-done.2.got_first, bf16[64,256]{1,0:T(8,128)(2,1)S(1)} %collective-permute-done.3.got_second, ...), custom_call_target="tpu_custom_call" | custom-call | tf_op jit(solution)/shard_map/pallas_call | solution.py:498
  16.0 1.1 %shard_map.97.mine = f32[3584,128]{1,0:T(8,128)S(1)} custom-call(bf16[1664,128]{1,0:T(8,128)(2,1)S(1)} %get-tuple-element.53.mine), custom_call_target="tpu_custom_call" | custom-call | tf_op jit(solution)/shard_map/pallas_call | solution.py:507
  17.8 0.8 %shard_map.98 = (bf16[896,128]{1,0:T(8,128)(2,1)S(1)}, bf16[128,768]{1,0:T(8,128)(2,1)S(1)}, bf16[4,224,1152]{2,1,0:T(8,128)(2,1)S(1)}) custom-call(f32[3584,128]{1,0:T(8,128)S(1)} %shard_map.97.mine, bf16[1664,128]{1,0:T(8,128)(2,1)S(1)} %collective-permute-done.4.theirs), custom_call_target="tpu_custom_call" | custom-call | tf_op jit(solution)/shard_map/pallas_call | solution.py:511
  18.5 1.6 %collective-permute-start.10 = (bf16[896,128]{1,0:T(8,128)(2,1)S(1)}, bf16[896,128]{1,0:T(8,128)(2,1)S(1)}, u32[]{:S(2)}, u32[]{:S(2)}) collective-permute-start(bf16[896,128]{1,0:T(8,128)(2,1)S(1)} %get-tuple-element.69), channel_id=1, source_target_pairs={{0,8},{4,20},{8,0},{12,28},{16,24},{20,4},{24,16},{28,12},{1,9},{5... | collective-permute-start | bytes 688136 | tf_op jit(solution)/shard_map/ppermute | solution.py:480
  20.2 1.1 %shard_map.99 = (bf16[896,128]{1,0:T(8,128)(2,1)S(1)}, f32[896,128]{1,0:T(8,128)S(1)}, f32[896,128]{1,0:T(8,128)S(1)}, bf16[48,256]{1,0:T(8,128)(2,1)S(1)}, bf16[48,256]{1,0:T(8,128)(2,1)S(1)}) custom-call(f32[3584,128]{1,0:T(8,128)S(1)} %shard_map.97.mine, bf16[128,768]{1,0:T(8,128)(2,1)S(1)} %get-tuple-element.55.left, ...), custom_call_target="tpu_custom_call" | custom-call | tf_op jit(solution)/shard_map/pallas_call | solution.py:516
  21.8 2.9 %collective-permute-done.10.received = bf16[896,128]{1,0:T(8,128)(2,1)S(1)} collective-permute-done((bf16[896,128]{1,0:T(8,128)(2,1)S(1)}, bf16[896,128]{1,0:T(8,128)(2,1)S(1)}, u32[]{:S(2)}, u32[]{:S(2)}) %collective-permute-start.10) | collective-permute-done | bytes 229408 | tf_op jit(solution)/shard_map/ppermute | solution.py:480
  24.7 1.6 %collective-permute-start.11 = (bf16[896,128]{1,0:T(8,128)(2,1)S(1)}, bf16[896,128]{1,0:T(8,128)(2,1)S(1)}, u32[]{:S(2)}, u32[]{:S(2)}) collective-permute-start(bf16[896,128]{1,0:T(8,128)(2,1)S(1)} %shard_map.103), channel_id=1, source_target_pairs={{0,16},{4,12},{8,24},{12,4},{16,0},{20,28},{24,8},{28,20},{1,17},{... | collective-permute-start | bytes 688136 | tf_op jit(solution)/shard_map/ppermute | solution.py:480
  26.3 2.7 %collective-permute-start.5 = (bf16[48,256]{1,0:T(8,128)(2,1)S(1)}, bf16[48,256]{1,0:T(8,128)(2,1)S(1)}, u32[]{:S(2)}, u32[]{:S(2)}) collective-permute-start(bf16[48,256]{1,0:T(8,128)(2,1)S(1)} %get-tuple-element.57), channel_id=1, source_target_pairs={{0,1},{1,0},{2,3},{3,2},{4,5},{5,4},{6,7},{7,6},{8,9},{9,8},{10,11... | collective-permute-start | bytes 73736 | tf_op jit(solution)/shard_map/ppermute | solution.py:457
  29.0 1.8 %collective-permute-done.5.got_first = bf16[48,256]{1,0:T(8,128)(2,1)S(1)} collective-permute-done((bf16[48,256]{1,0:T(8,128)(2,1)S(1)}, bf16[48,256]{1,0:T(8,128)(2,1)S(1)}, u32[]{:S(2)}, u32[]{:S(2)}) %collective-permute-start.5) | collective-permute-done | bytes 24608 | tf_op jit(solution)/shard_map/ppermute | solution.py:457
  31.2 3.4 %collective-permute-start.12 = (bf16[224,128]{1,0:T(8,128)(2,1)S(1)}, bf16[224,128]{1,0:T(8,128)(2,1)S(1)}, u32[]{:S(2)}, u32[]{:S(2)}) collective-permute-start(bf16[224,128]{1,0:T(8,128)(2,1)S(1)} %get-tuple-element.71), channel_id=1, source_target_pairs={{0,3},{1,2},{2,1},{3,0},{4,7},{5,6},{6,5},{7,4},{8,11},{9,10},{10,... | collective-permute-start | bytes 172040 | tf_op jit(solution)/shard_map/ppermute | solution.py:483
  35.7 1.6 %shard_map.101 = (f32[768,128]{1,0:T(8,128)S(1)}, f32[8,128]{1,0:T(8,128)S(1)}) custom-call(bf16[768,256]{1,0:T(8,128)(2,1)S(1)} %get-tuple-element.59.hb, bf16[54,128,128]{2,1,0:T(8,128)(2,1)S(1)} %constant_dynamic-update-slice_fusion.weights), custom_call_target="tpu_custom_call" | custom-call | tf_op jit(solution)/shard_map/pallas_call | solution.py:537
  37.3 3.0 %collective-permute-done.13.refs_1_ = bf16[224,128]{1,0:T(8,128)(2,1)S(1)} collective-permute-done((bf16[224,128]{1,0:T(8,128)(2,1)S(1)}, bf16[224,128]{1,0:T(8,128)(2,1)S(1)}, u32[]{:S(2)}, u32[]{:S(2)}) %collective-permute-start.13) | collective-permute-done | bytes 57376 | tf_op jit(solution)/shard_map/ppermute | solution.py:483
  40.4 2.8 %collective-permute-start.17 = (bf16[224,128]{1,0:T(8,128)(2,1)S(1)}, bf16[224,128]{1,0:T(8,128)(2,1)S(1)}, u32[]{:S(2)}, u32[]{:S(2)}) collective-permute-start(bf16[224,128]{1,0:T(8,128)(2,1)S(1)} %shard_map.105.refs_0_), channel_id=1, source_target_pairs={{0,3},{1,2},{2,1},{3,0},{4,7},{5,6},{6,5},{7,4},{8,11},{9,10},{10,... | collective-permute-start | bytes 172040 | tf_op jit(solution)/shard_map/ppermute | solution.py:483
  43.1 1.7 %collective-permute-start.15 = (bf16[224,128]{1,0:T(8,128)(2,1)S(1)}, bf16[224,128]{1,0:T(8,128)(2,1)S(1)}, u32[]{:S(2)}, u32[]{:S(2)}) collective-permute-start(bf16[224,128]{1,0:T(8,128)(2,1)S(1)} %shard_map.105.refs_0_), channel_id=1, source_target_pairs={{0,1},{1,0},{2,3},{3,2},{4,5},{5,4},{6,7},{7,6},{8,9},{9,8},{10,11... | collective-permute-start | bytes 172040 | tf_op jit(solution)/shard_map/ppermute | solution.py:483
  44.8 1.5 %collective-permute-start.7 = (bf16[64,256]{1,0:T(8,128)(2,1)S(1)}, bf16[64,256]{1,0:T(8,128)(2,1)S(1)}, u32[]{:S(2)}, u32[]{:S(2)}) collective-permute-start(bf16[64,256]{1,0:T(8,128)(2,1)S(1)} %get-tuple-element.62.after), channel_id=1, source_target_pairs={{0,4},{4,0},{8,12},{12,8},{16,20},{20,16},{24,28},{28,24},{1,5},{5... | collective-permute-start | bytes 98312 | tf_op jit(solution)/shard_map/ppermute | solution.py:457
  46.3 1.7 %shard_map.102 = (f32[768,128]{1,0:T(8,128)S(1)}, f32[8,128]{1,0:T(8,128)S(1)}) custom-call(bf16[768,256]{1,0:T(8,128)(2,1)S(1)} %get-tuple-element.59.hb, bf16[54,128,128]{2,1,0:T(8,128)(2,1)S(1)} %constant_dynamic-update-slice_fusion.weights), custom_call_target="tpu_custom_call" | custom-call | tf_op jit(solution)/shard_map/pallas_call | solution.py:537
  48.3 1.5 %collective-permute-start.19 = (bf16[896,128]{1,0:T(8,128)(2,1)S(1)}, bf16[896,128]{1,0:T(8,128)(2,1)S(1)}, u32[]{:S(2)}, u32[]{:S(2)}) collective-permute-start(bf16[896,128]{1,0:T(8,128)(2,1)S(1)} %shard_map.106.held.refs_0_), channel_id=1, source_target_pairs={{0,8},{4,20},{8,0},{12,28},{16,24},{20,4},{24,16},{28,12},{1,9},{5... | collective-permute-start | bytes 688136 | tf_op jit(solution)/shard_map/ppermute | solution.py:480
  49.7 2.1 %shard_map.107 = (bf16[576,128]{1,0:T(8,128)(2,1)}, bf16[576,128]{1,0:T(8,128)(2,1)}, bf16[896,128]{1,0:T(8,128)(2,1)S(1)}) custom-call(s32[1,1,16]{2,1,0:T(1,128)S(1)} %copy-done.1, s32[1,1]{1,0:T(1,128)S(6)} %copy.23.counts, f32[768,128]{1,0:T(8,128)S(1)} %get-tuple-element.60.inner_hidden, f32[768,128]{1,0:T(8,128)S(1)} %get-tuple-element.61.inner_back, ...), custom_call_target="tpu_custom_call" | custom-call | tf_op jit(solution)/shard_map/pallas_call | solution.py:559
  51.8 1.5 %collective-permute-start.18 = (bf16[896,128]{1,0:T(8,128)(2,1)S(1)}, bf16[896,128]{1,0:T(8,128)(2,1)S(1)}, u32[]{:S(2)}, u32[]{:S(2)}) collective-permute-start(bf16[896,128]{1,0:T(8,128)(2,1)S(1)} %get-tuple-element.76), channel_id=1, source_target_pairs={{0,16},{4,12},{8,24},{12,4},{16,0},{20,28},{24,8},{28,20},{1,17},{... | collective-permute-start | bytes 688136 | tf_op jit(solution)/shard_map/ppermute | solution.py:480
  53.3 1.4 %collective-permute-done.19.refs_2_ = bf16[896,128]{1,0:T(8,128)(2,1)S(1)} collective-permute-done((bf16[896,128]{1,0:T(8,128)(2,1)S(1)}, bf16[896,128]{1,0:T(8,128)(2,1)S(1)}, u32[]{:S(2)}, u32[]{:S(2)}) %collective-permute-start.19) | collective-permute-done | bytes 229408 | tf_op jit(solution)/shard_map/ppermute | solution.py:480
  54.7 2.3 %collective-permute-start.23 = (bf16[896,128]{1,0:T(8,128)(2,1)S(1)}, bf16[896,128]{1,0:T(8,128)(2,1)S(1)}, u32[]{:S(2)}, u32[]{:S(2)}) collective-permute-start(bf16[896,128]{1,0:T(8,128)(2,1)S(1)} %collective-permute-done.19.refs_2_), channel_id=1, source_target_pairs={{0,16},{4,12},{8,24},{12,4},{16,0},{20,28},{24,8},{28,20},{1,17},{... | collective-permute-start | bytes 688136 | tf_op jit(solution)/shard_map/ppermute | solution.py:480
  57.0 0.9 %collective-permute-done.18.refs_0_ = bf16[896,128]{1,0:T(8,128)(2,1)S(1)} collective-permute-done((bf16[896,128]{1,0:T(8,128)(2,1)S(1)}, bf16[896,128]{1,0:T(8,128)(2,1)S(1)}, u32[]{:S(2)}, u32[]{:S(2)}) %collective-permute-start.18) | collective-permute-done | bytes 229408 | tf_op jit(solution)/shard_map/ppermute | solution.py:480
  57.9 1.3 %shard_map.108 = (f32[27,128,128]{2,1,0:T(8,128)}, f32[27,128,128]{2,1,0:T(8,128)}) custom-call(bf16[896,128]{1,0:T(8,128)(2,1)S(1)} %shard_map.106.held.refs_0_, bf16[896,128]{1,0:T(8,128)(2,1)S(1)} %collective-permute-done.22.refs_1_, bf16[896,128]{1,0:T(8,128)(2,1)S(1)} %collective-permute-done.19.refs_2_), custom_call_target="tpu_custom_call" | custom-call | flops 49999998976 | tf_op jit(solution)/shard_map/pallas_call | solution.py:588
  59.4 1.3 %shard_map.109 = (f32[27,128,128]{2,1,0:T(8,128)}, f32[27,128,128]{2,1,0:T(8,128)}, f32[8,128]{1,0:T(8,128)S(1)}) custom-call(bf16[896,128]{1,0:T(8,128)(2,1)S(1)} %collective-permute-done.18.refs_0_, bf16[896,128]{1,0:T(8,128)(2,1)S(1)} %collective-permute-done.20.refs_1_, ...), custom_call_target="tpu_custom_call", output_to_operand_aliasing={{0}: (3, {}), {1}: (4, {})} | custom-call | flops 49999998976 | tf_op jit(solution)/shard_map/pallas_call | solution.py:588
  61.3 0.8 %shard_map.111 = (f32[27,128,128]{2,1,0:T(8,128)}, f32[27,128,128]{2,1,0:T(8,128)}) custom-call(bf16[896,128]{1,0:T(8,128)(2,1)S(1)} %collective-permute-done.23.value.refs_0_, f32[27,128,128]{2,1,0:T(8,128)} %get-tuple-element.80.refs_1_, f32[27,128,128]{2,1,0:T(8,128)} %get-tuple-element.81.refs_2_), custom_call_target="tpu_custom_call", output_to_operand_aliasing={{0}: (1, {}), {1}: (2, {})} | custom-call | flops 49999998976 | tf_op jit(solution)/shard_map/pallas_call | solution.py:588
  62.6 0.9 %shard_map.112 = (f32[27,128,128]{2,1,0:T(8,128)}, f32[27,128,128]{2,1,0:T(8,128)}) custom-call(bf16[896,128]{1,0:T(8,128)(2,1)S(1)} %collective-permute-done.24.refs_0_, f32[27,128,128]{2,1,0:T(8,128)} %get-tuple-element.82.refs_1_, f32[27,128,128]{2,1,0:T(8,128)} %get-tuple-element.83.refs_2_), custom_call_target="tpu_custom_call", output_to_operand_aliasing={{0}: (1, {}), {1}: (2, {})} | custom-call | flops 49999998976 | tf_op jit(solution)/shard_map/pallas_call | solution.py:588
  (47 shorter events, 6.1 us)
Async XLA Ops:
  2.3 0.7 %copy-start = (s32[1,1,16]{2,1,0:T(1,128)S(1)}, s32[1,1,16]{2,1,0:T(1,128)}, u32[]{:S(2)}) copy-start(s32[1,1,16]{2,1,0:T(1,128)} %lists.3) | copy-start | bytes 196
  3.0 9.1 %copy-start.2 = (bf16[27,128,128]{2,1,0:T(8,128)(2,1)S(1)}, bf16[27,128,128]{2,1,0:T(8,128)(2,1)}, u32[]{:S(2)}) copy-start(bf16[27,128,128]{2,1,0:T(8,128)(2,1)} %param.9) | copy-start | bytes 2654212
  3.8 4.9 %collective-permute-start = (bf16[48,256]{1,0:T(8,128)(2,1)S(1)}, bf16[48,256]{1,0:T(8,128)(2,1)S(1)}, u32[]{:S(2)}, u32[]{:S(2)}) collective-permute-start(bf16[48,256]{1,0:T(8,128)(2,1)S(1)} %get-tuple-element.46), channel_id=1, source_target_pairs={{0,1},{1,0},{2,3},{3,2},{4,5},{5,4},{6,7},{7,6},{8,9},{9,8},{10,11... | collective-permute-start | bytes 73736 | tf_op jit(solution)/shard_map/ppermute | solution.py:457
  6.9 1.8 %collective-permute-start.1 = (bf16[48,256]{1,0:T(8,128)(2,1)S(1)}, bf16[48,256]{1,0:T(8,128)(2,1)S(1)}, u32[]{:S(2)}, u32[]{:S(2)}) collective-permute-start(bf16[48,256]{1,0:T(8,128)(2,1)S(1)} %get-tuple-element.47), channel_id=1, source_target_pairs={{0,4},{1,2},{2,1},{3,7},{4,0},{5,6},{6,5},{7,3},{8,12},{9,10},{10,... | collective-permute-start | bytes 73736 | tf_op jit(solution)/shard_map/ppermute | solution.py:456
  8.9 4.8 %collective-permute-start.2 = (bf16[64,256]{1,0:T(8,128)(2,1)S(1)}, bf16[64,256]{1,0:T(8,128)(2,1)S(1)}, u32[]{:S(2)}, u32[]{:S(2)}) collective-permute-start(bf16[64,256]{1,0:T(8,128)(2,1)S(1)} %get-tuple-element.49), channel_id=1, source_target_pairs={{0,4},{4,0},{8,12},{12,8},{16,20},{20,16},{24,28},{28,24},{1,5},{5... | collective-permute-start | bytes 98312 | tf_op jit(solution)/shard_map/ppermute | solution.py:457
  9.0 4.7 %collective-permute-start.3 = (bf16[64,256]{1,0:T(8,128)(2,1)S(1)}, bf16[64,256]{1,0:T(8,128)(2,1)S(1)}, u32[]{:S(2)}, u32[]{:S(2)}) collective-permute-start(bf16[64,256]{1,0:T(8,128)(2,1)S(1)} %get-tuple-element.50), channel_id=1, source_target_pairs={{0,28},{4,8},{8,4},{12,16},{16,12},{20,24},{24,20},{28,0},{1,29},{... | collective-permute-start | bytes 98312 | tf_op jit(solution)/shard_map/ppermute | solution.py:449
  15.9 1.8 %collective-permute-start.4 = (bf16[1664,128]{1,0:T(8,128)(2,1)S(1)}, bf16[1664,128]{1,0:T(8,128)(2,1)S(1)}, u32[]{:S(2)}, u32[]{:S(2)}) collective-permute-start(bf16[1664,128]{1,0:T(8,128)(2,1)S(1)} %get-tuple-element.54), channel_id=1, source_target_pairs={{0,4},{4,0},{8,12},{12,8},{16,20},{20,16},{24,28},{28,24},{1,5},{5... | collective-permute-start | bytes 1277960 | tf_op jit(solution)/shard_map/ppermute | solution.py:477
  18.5 6.1 %collective-permute-start.10 = (bf16[896,128]{1,0:T(8,128)(2,1)S(1)}, bf16[896,128]{1,0:T(8,128)(2,1)S(1)}, u32[]{:S(2)}, u32[]{:S(2)}) collective-permute-start(bf16[896,128]{1,0:T(8,128)(2,1)S(1)} %get-tuple-element.69), channel_id=1, source_target_pairs={{0,8},{4,20},{8,0},{12,28},{16,24},{20,4},{24,16},{28,12},{1,9},{5... | collective-permute-start | bytes 688136 | tf_op jit(solution)/shard_map/ppermute | solution.py:480
  21.2 9.8 %collective-permute-start.9 = (bf16[896,128]{1,0:T(8,128)(2,1)S(1)}, bf16[896,128]{1,0:T(8,128)(2,1)S(1)}, u32[]{:S(2)}, u32[]{:S(2)}) collective-permute-start(bf16[896,128]{1,0:T(8,128)(2,1)S(1)} %get-tuple-element.67), channel_id=1, source_target_pairs={{0,8},{4,20},{8,0},{12,28},{16,24},{20,4},{24,16},{28,12},{1,9},{5... | collective-permute-start | bytes 688136 | tf_op jit(solution)/shard_map/ppermute | solution.py:480
  24.7 6.4 %collective-permute-start.11 = (bf16[896,128]{1,0:T(8,128)(2,1)S(1)}, bf16[896,128]{1,0:T(8,128)(2,1)S(1)}, u32[]{:S(2)}, u32[]{:S(2)}) collective-permute-start(bf16[896,128]{1,0:T(8,128)(2,1)S(1)} %shard_map.103), channel_id=1, source_target_pairs={{0,16},{4,12},{8,24},{12,4},{16,0},{20,28},{24,8},{28,20},{1,17},{... | collective-permute-start | bytes 688136 | tf_op jit(solution)/shard_map/ppermute | solution.py:480
  26.3 4.5 %collective-permute-start.5 = (bf16[48,256]{1,0:T(8,128)(2,1)S(1)}, bf16[48,256]{1,0:T(8,128)(2,1)S(1)}, u32[]{:S(2)}, u32[]{:S(2)}) collective-permute-start(bf16[48,256]{1,0:T(8,128)(2,1)S(1)} %get-tuple-element.57), channel_id=1, source_target_pairs={{0,1},{1,0},{2,3},{3,2},{4,5},{5,4},{6,7},{7,6},{8,9},{9,8},{10,11... | collective-permute-start | bytes 73736 | tf_op jit(solution)/shard_map/ppermute | solution.py:457
  29.0 1.8 %collective-permute-start.6 = (bf16[48,256]{1,0:T(8,128)(2,1)S(1)}, bf16[48,256]{1,0:T(8,128)(2,1)S(1)}, u32[]{:S(2)}, u32[]{:S(2)}) collective-permute-start(bf16[48,256]{1,0:T(8,128)(2,1)S(1)} %get-tuple-element.58), channel_id=1, source_target_pairs={{0,4},{1,2},{2,1},{3,7},{4,0},{5,6},{6,5},{7,3},{8,12},{9,10},{10,... | collective-permute-start | bytes 73736 | tf_op jit(solution)/shard_map/ppermute | solution.py:456
  31.2 6.1 %collective-permute-start.12 = (bf16[224,128]{1,0:T(8,128)(2,1)S(1)}, bf16[224,128]{1,0:T(8,128)(2,1)S(1)}, u32[]{:S(2)}, u32[]{:S(2)}) collective-permute-start(bf16[224,128]{1,0:T(8,128)(2,1)S(1)} %get-tuple-element.71), channel_id=1, source_target_pairs={{0,3},{1,2},{2,1},{3,0},{4,7},{5,6},{6,5},{7,4},{8,11},{9,10},{10,... | collective-permute-start | bytes 172040 | tf_op jit(solution)/shard_map/ppermute | solution.py:483
  34.6 5.8 %collective-permute-start.13 = (bf16[224,128]{1,0:T(8,128)(2,1)S(1)}, bf16[224,128]{1,0:T(8,128)(2,1)S(1)}, u32[]{:S(2)}, u32[]{:S(2)}) collective-permute-start(bf16[224,128]{1,0:T(8,128)(2,1)S(1)} %get-tuple-element.72), channel_id=1, source_target_pairs={{0,2},{1,3},{2,0},{3,1},{4,6},{5,7},{6,4},{7,5},{8,10},{9,11},{10,... | collective-permute-start | bytes 172040 | tf_op jit(solution)/shard_map/ppermute | solution.py:483
  35.2 5.1 %collective-permute-start.14 = (bf16[224,128]{1,0:T(8,128)(2,1)S(1)}, bf16[224,128]{1,0:T(8,128)(2,1)S(1)}, u32[]{:S(2)}, u32[]{:S(2)}) collective-permute-start(bf16[224,128]{1,0:T(8,128)(2,1)S(1)} %get-tuple-element.73), channel_id=1, source_target_pairs={{0,1},{1,0},{2,3},{3,2},{4,5},{5,4},{6,7},{7,6},{8,9},{9,8},{10,11... | collective-permute-start | bytes 172040 | tf_op jit(solution)/shard_map/ppermute | solution.py:483
  37.3 12.4 %copy-start.1 = (s32[1,1,16]{2,1,0:T(1,128)S(1)}, s32[1,1,16]{2,1,0:T(1,128)}, u32[]{:S(2)}) copy-start(s32[1,1,16]{2,1,0:T(1,128)} %lists.3) | copy-start | bytes 196
  40.4 7.7 %collective-permute-start.17 = (bf16[224,128]{1,0:T(8,128)(2,1)S(1)}, bf16[224,128]{1,0:T(8,128)(2,1)S(1)}, u32[]{:S(2)}, u32[]{:S(2)}) collective-permute-start(bf16[224,128]{1,0:T(8,128)(2,1)S(1)} %shard_map.105.refs_0_), channel_id=1, source_target_pairs={{0,3},{1,2},{2,1},{3,0},{4,7},{5,6},{6,5},{7,4},{8,11},{9,10},{10,... | collective-permute-start | bytes 172040 | tf_op jit(solution)/shard_map/ppermute | solution.py:483
  43.1 5.1 %collective-permute-start.16 = (bf16[224,128]{1,0:T(8,128)(2,1)S(1)}, bf16[224,128]{1,0:T(8,128)(2,1)S(1)}, u32[]{:S(2)}, u32[]{:S(2)}) collective-permute-start(bf16[224,128]{1,0:T(8,128)(2,1)S(1)} %shard_map.105.refs_0_), channel_id=1, source_target_pairs={{0,2},{1,3},{2,0},{3,1},{4,6},{5,7},{6,4},{7,5},{8,10},{9,11},{10,... | collective-permute-start | bytes 172040 | tf_op jit(solution)/shard_map/ppermute | solution.py:483
  43.1 5.1 %collective-permute-start.15 = (bf16[224,128]{1,0:T(8,128)(2,1)S(1)}, bf16[224,128]{1,0:T(8,128)(2,1)S(1)}, u32[]{:S(2)}, u32[]{:S(2)}) collective-permute-start(bf16[224,128]{1,0:T(8,128)(2,1)S(1)} %shard_map.105.refs_0_), channel_id=1, source_target_pairs={{0,1},{1,0},{2,3},{3,2},{4,5},{5,4},{6,7},{7,6},{8,9},{9,8},{10,11... | collective-permute-start | bytes 172040 | tf_op jit(solution)/shard_map/ppermute | solution.py:483
  44.8 4.9 %collective-permute-start.8 = (bf16[64,256]{1,0:T(8,128)(2,1)S(1)}, bf16[64,256]{1,0:T(8,128)(2,1)S(1)}, u32[]{:S(2)}, u32[]{:S(2)}) collective-permute-start(bf16[64,256]{1,0:T(8,128)(2,1)S(1)} %get-tuple-element.63), channel_id=1, source_target_pairs={{0,28},{4,8},{8,4},{12,16},{16,12},{20,24},{24,20},{28,0},{1,29},{... | collective-permute-start | bytes 98312 | tf_op jit(solution)/shard_map/ppermute | solution.py:449
  44.8 4.9 %collective-permute-start.7 = (bf16[64,256]{1,0:T(8,128)(2,1)S(1)}, bf16[64,256]{1,0:T(8,128)(2,1)S(1)}, u32[]{:S(2)}, u32[]{:S(2)}) collective-permute-start(bf16[64,256]{1,0:T(8,128)(2,1)S(1)} %get-tuple-element.62.after), channel_id=1, source_target_pairs={{0,4},{4,0},{8,12},{12,8},{16,20},{20,16},{24,28},{28,24},{1,5},{5... | collective-permute-start | bytes 98312 | tf_op jit(solution)/shard_map/ppermute | solution.py:457
  48.3 6.4 %collective-permute-start.19 = (bf16[896,128]{1,0:T(8,128)(2,1)S(1)}, bf16[896,128]{1,0:T(8,128)(2,1)S(1)}, u32[]{:S(2)}, u32[]{:S(2)}) collective-permute-start(bf16[896,128]{1,0:T(8,128)(2,1)S(1)} %shard_map.106.held.refs_0_), channel_id=1, source_target_pairs={{0,8},{4,20},{8,0},{12,28},{16,24},{20,4},{24,16},{28,12},{1,9},{5... | collective-permute-start | bytes 688136 | tf_op jit(solution)/shard_map/ppermute | solution.py:480
  51.8 6.0 %collective-permute-start.18 = (bf16[896,128]{1,0:T(8,128)(2,1)S(1)}, bf16[896,128]{1,0:T(8,128)(2,1)S(1)}, u32[]{:S(2)}, u32[]{:S(2)}) collective-permute-start(bf16[896,128]{1,0:T(8,128)(2,1)S(1)} %get-tuple-element.76), channel_id=1, source_target_pairs={{0,16},{4,12},{8,24},{12,4},{16,0},{20,28},{24,8},{28,20},{1,17},{... | collective-permute-start | bytes 688136 | tf_op jit(solution)/shard_map/ppermute | solution.py:480
  53.3 4.6 %collective-permute-start.22 = (bf16[896,128]{1,0:T(8,128)(2,1)S(1)}, bf16[896,128]{1,0:T(8,128)(2,1)S(1)}, u32[]{:S(2)}, u32[]{:S(2)}) collective-permute-start(bf16[896,128]{1,0:T(8,128)(2,1)S(1)} %shard_map.106.held.refs_0_), channel_id=1, source_target_pairs={{0,4},{4,0},{8,12},{12,8},{16,20},{20,16},{24,28},{28,24},{1,5},{5... | collective-permute-start | bytes 688136 | tf_op jit(solution)/shard_map/ppermute | solution.py:477
  54.7 6.3 %collective-permute-start.23 = (bf16[896,128]{1,0:T(8,128)(2,1)S(1)}, bf16[896,128]{1,0:T(8,128)(2,1)S(1)}, u32[]{:S(2)}, u32[]{:S(2)}) collective-permute-start(bf16[896,128]{1,0:T(8,128)(2,1)S(1)} %collective-permute-done.19.refs_2_), channel_id=1, source_target_pairs={{0,16},{4,12},{8,24},{12,4},{16,0},{20,28},{24,8},{28,20},{1,17},{... | collective-permute-start | bytes 688136 | tf_op jit(solution)/shard_map/ppermute | solution.py:480
  57.0 2.4 %collective-permute-start.20 = (bf16[896,128]{1,0:T(8,128)(2,1)S(1)}, bf16[896,128]{1,0:T(8,128)(2,1)S(1)}, u32[]{:S(2)}, u32[]{:S(2)}) collective-permute-start(bf16[896,128]{1,0:T(8,128)(2,1)S(1)} %collective-permute-done.19.refs_2_), channel_id=1, source_target_pairs={{0,4},{4,0},{8,12},{12,8},{16,20},{20,16},{24,28},{28,24},{1,5},{5... | collective-permute-start | bytes 688136 | tf_op jit(solution)/shard_map/ppermute | solution.py:477
  57.9 1.5 %collective-permute-start.21 = (bf16[896,128]{1,0:T(8,128)(2,1)S(1)}, bf16[896,128]{1,0:T(8,128)(2,1)S(1)}, u32[]{:S(2)}, u32[]{:S(2)}) collective-permute-start(bf16[896,128]{1,0:T(8,128)(2,1)S(1)} %collective-permute-done.18.refs_0_), channel_id=1, source_target_pairs={{0,4},{4,0},{8,12},{12,8},{16,20},{20,16},{24,28},{28,24},{1,5},{5... | collective-permute-start | bytes 688136 | tf_op jit(solution)/shard_map/ppermute | solution.py:477
  61.0 1.6 %collective-permute-start.24 = (bf16[896,128]{1,0:T(8,128)(2,1)S(1)}, bf16[896,128]{1,0:T(8,128)(2,1)S(1)}, u32[]{:S(2)}, u32[]{:S(2)}) collective-permute-start(bf16[896,128]{1,0:T(8,128)(2,1)S(1)} %shard_map.110), channel_id=1, source_target_pairs={{0,4},{4,0},{8,12},{12,8},{16,20},{20,16},{24,28},{28,24},{1,5},{5... | collective-permute-start | bytes 688136 | tf_op jit(solution)/shard_map/ppermute | solution.py:477

commit v6 on v5

--- a/solution.py
+++ b/solution.py
@@ -109,7 +109,7 @@
     return low, high
 
 
-def place_kernel(counts, lists, pair, first, second, out, live, both):
+def load_slots(counts, lists, pair, both):
     count = pair.shape[0]
     both[0:count, :] = pair[...]
     both[count:, :] = jnp.zeros((both.shape[0] - count, 256), jnp.bfloat16)
@@ -118,7 +118,11 @@
     def entry(i):
         return jnp.sum(jnp.where(iota(entries.shape, 1) == i, entries, 0), axis=1, keepdims=True)
 
-    slots = position_slots(entry, counts[...])
+    return position_slots(entry, counts[...])
+
+
+def faces_kernel(counts, lists, pair, first, second, both):
+    slots = load_slots(counts, lists, pair, both)
     z, x = face_indices()
     low, high = (
         dot(
@@ -127,13 +131,17 @@
         for y in (0, NY - 1)
     )
     write_by_parity("wire", low, high, first, second)
+
+
+def place_kernel(counts, lists, pair, out, live, both):
+    slots = load_slots(counts, lists, pair, both)
     z, x, j = grid_indices()
     rows = slot_rows(slots, z, x, j - 1, (j >= 1) & (j <= NY))
     live[...] = (rows >= 0).astype(jnp.bfloat16)
     out[...] = dot(one_hot(rows, both.shape[0]), both[...]).astype(jnp.bfloat16)
 
 
-def insert_faces(placed, got_first, got_second, out, slab_first, slab_second, faces):
+def insert_faces(placed, got_second, got_first, out, slab_first, slab_second, faces):
     low, high = read_by_parity("wire", got_first, got_second)
     faces[0:FACE, :] = low
     faces[FACE : 2 * FACE, :] = high
@@ -373,13 +381,11 @@
         copies = []
         for part, (kind, mine) in zip(parts, items):
             source = core if mine else 1 - core
-            value = part[...].astype(jnp.float32)
             count, here = part.shape[0] // 128, len(copies)
-            for i in range(count):
-                block = value[128 * i : 128 * (i + 1), :]
-                staged[here + i] = block.T if source else block
             chunk = me ^ chip_mask(kind, source)
             for i in range(count):
+                block = part[128 * i : 128 * (i + 1), :].astype(jnp.float32)
+                staged[here + i] = block.T if source else block
                 tap = chunk * blocks + i
                 safe = jnp.minimum(tap, TAPS - 1)
                 to = first.at[safe] if source else second.at[TAPS - 1 - safe]
@@ -484,14 +490,11 @@
 
     pair = jnp.concatenate([f, g], axis=1)
     weights = jnp.concatenate([first_weight, second_weight], axis=0)
-    *faces, placed, live = call(
-        place_kernel,
-        (face, face, grid, bf16(ROWS, 128)),
-        [VMEM] * 3,
-        [pltpu.VMEM((padded, 256), jnp.bfloat16)],
-    )(counts, send_lists, pair)
+    pair_scratch = [pltpu.VMEM((padded, 256), jnp.bfloat16)]
+    faces = call(faces_kernel, (face, face), [VMEM] * 3, pair_scratch)(counts, send_lists, pair)
+    placed, live = call(place_kernel, (grid, bf16(ROWS, 128)), [VMEM] * 3, pair_scratch)(counts, send_lists, pair)
     faces = pairs(*faces, "wire")
-    full, *slabs = call(insert_faces, (grid, slab, slab), [VMEM] * 3, [faces_scratch])(placed, *faces)
+    full, *slabs = call(insert_faces, (grid, slab, slab), [VMEM] * 3, [faces_scratch])(placed, *faces[::-1])
     slabs = pairs(*slabs, "drift")
     message = bf16(ROWS + 4 * WIDE, 128)
     inner = call(inner_kernel, f32(ROWS, 128), [VMEM] * 2, conv_scratch[:1])(full, weights)
@@ -529,7 +532,7 @@
     else:
         parts = [to_chip(value, k) for k, value in zip(kinds, sends)]
     faces = pairs(face_first, face_second, "wire")
-    hb_full, *hb_slabs = call(insert_faces, (grid, slab, slab), [VMEM] * 3, [faces_scratch])(hb, *faces)
+    hb_full, *hb_slabs = call(insert_faces, (grid, slab, slab), [VMEM] * 3, [faces_scratch])(hb, *faces[::-1])
     inserted = hb_slabs[0]
     hb_slabs = pairs(*hb_slabs, "drift")
     token = f32(8, 128)

time: 63.9 us -> 63.4 us (level)
  waiting for transfers between devices: 12.4 us -> 10.5 us
  starting transfers between devices: 28.6 us -> 29.8 us
    ppermute x6, waiting for transfers between devices: 3.22 us -> 2.15 us  [to_wire(): return lax.ppermute(value, 'wire', [(i, i ^ step) for i in range(wire)])]
    ppermute x4, starting transfers between devices: 7.38 us -> 8.18 us  [pairs(): got_first = lax.ppermute(value_first, axis, first)]
  transfers between devices with their start and end apart: 25 -> 25, of which waited for: 11 -> 13; matrix products, arithmetic and copies ran while one was open for 2% -> 2% of each run, Pallas kernels for 20% -> 21%
where the time goes in v6:
time: 63.4 us; the launch traced here: 63.2 us
  starting transfers between devices  29.8 us (47%)
  Pallas kernels  18.2 us (29%)
  waiting for transfers between devices  10.5 us (17%)
  local copies, waits for them, and re-layouts  2 us (3%)
  between operations  1.68 us (3%)
  other arithmetic  1.02 us (2%)
    ppermute x6, starting transfers between devices, to_chip(): lax.ppermute(value, 'drift', [(i, i ^ 2 * chip_mask(kind, i % 2)) for i i...  9.08 us
    ppermute x6, starting transfers between devices, to_wire(): return lax.ppermute(value, 'wire', [(i, i ^ step) for i in range(wire)])  8.91 us
    ppermute x4, starting transfers between devices, pairs(): got_first = lax.ppermute(value_first, axis, first)  8.18 us
    ppermute x6, waiting for transfers between devices, to_chip(): lax.ppermute(value, 'drift', [(i, i ^ 2 * chip_mask(kind, i % 2)) for i i...  5.41 us
    pallas_call x4, Pallas kernels, on_device(): call(functools.partial(final_kernel, items, blocks, want_done), (f32(TAPS...  4.22 us
    pallas_call x2, Pallas kernels, on_device(): call(functools.partial(second_inner_kernel, field), (f32(ROWS, 128), toke...  3.29 us
    ppermute x2, starting transfers between devices, pairs(): got_second = lax.ppermute(value_second, axis, sorted(second.items()))  2.55 us
    ppermute x6, waiting for transfers between devices, to_wire(): return lax.ppermute(value, 'wire', [(i, i ^ step) for i in range(wire)])  2.15 us
  transfers between devices with their start and end apart: 25, of which 13 were waited for; matrix products, arithmetic and copies ran while one was open for 2% of the time, Pallas kernels for 21%

profile of v6, /device:TPU:0, one launch (start us, length us, event | category | flops | bytes accessed | tf_op | source)
XLA Modules:
  0.0 63.2 jit_solution(119675668869314064)
XLA Ops:
  1.3 1.0 %pad_maximum_fusion.pair = bf16[576,256]{1,0:T(8,128)(2,1)S(1)} fusion(bf16[576,128]{1,0:T(8,128)(2,1)} %bitcast.4, bf16[576,128]{1,0:T(8,128)(2,1)} %bitcast.5), kind=kLoop, calls=%fused_computation | loop fusion | flops 589824 | bytes 589824 | tf_op jit(solution)/shard_map/concatenate | solution.py:491
  3.9 4.1 %collective-permute-start.1 = (bf16[48,256]{1,0:T(8,128)(2,1)S(1)}, bf16[48,256]{1,0:T(8,128)(2,1)S(1)}, u32[]{:S(2)}, u32[]{:S(2)}) collective-permute-start(bf16[48,256]{1,0:T(8,128)(2,1)S(1)} %get-tuple-element.47), channel_id=1, source_target_pairs={{0,1},{1,0},{2,3},{3,2},{4,5},{5,4},{6,7},{7,6},{8,9},{9,8},{10,11... | collective-permute-start | bytes 73736 | tf_op jit(solution)/shard_map/ppermute | solution.py:463
  8.0 1.2 %constant_dynamic-update-slice_fusion.1 = bf16[54,128,128]{2,1,0:T(8,128)(2,1)S(1)} fusion(bf16[27,128,128]{2,1,0:T(8,128)(2,1)} %param.8), kind=kLoop, calls=%fused_computation.2 | loop fusion | bytes 1769472
  10.3 2.5 %collective-permute-start.3 = (bf16[64,256]{1,0:T(8,128)(2,1)S(1)}, bf16[64,256]{1,0:T(8,128)(2,1)S(1)}, u32[]{:S(2)}, u32[]{:S(2)}) collective-permute-start(bf16[64,256]{1,0:T(8,128)(2,1)S(1)} %get-tuple-element.50), channel_id=1, source_target_pairs={{0,28},{4,8},{8,4},{12,16},{16,12},{20,24},{24,20},{28,0},{1,29},{... | collective-permute-start | bytes 98312 | tf_op jit(solution)/shard_map/ppermute | solution.py:455
  13.0 1.6 %shard_map.96.inner = f32[768,128]{1,0:T(8,128)S(1)} custom-call(bf16[768,256]{1,0:T(8,128)(2,1)S(1)} %get-tuple-element.48.full.base, bf16[54,128,128]{2,1,0:T(8,128)(2,1)S(1)} %constant_dynamic-update-slice_fusion.weights), custom_call_target="tpu_custom_call" | custom-call | tf_op jit(solution)/shard_map/pallas_call | solution.py:500
  14.6 2.1 %shard_map.97 = (bf16[768,256]{1,0:T(8,128)(2,1)S(1)}, bf16[1664,128]{1,0:T(8,128)(2,1)S(1)}, bf16[1664,128]{1,0:T(8,128)(2,1)S(1)}) custom-call(bf16[768,256]{1,0:T(8,128)(2,1)S(1)} %get-tuple-element.48.full.base, bf16[64,256]{1,0:T(8,128)(2,1)S(1)} %collective-permute-done.2.got_first, bf16[64,256]{1,0:T(8,128)(2,1)S(1)} %collective-permute-done.3.got_second, ...), custom_call_target="tpu_custom_call" | custom-call | tf_op jit(solution)/shard_map/pallas_call | solution.py:501
  16.9 1.1 %shard_map.98.mine = f32[3584,128]{1,0:T(8,128)S(1)} custom-call(bf16[1664,128]{1,0:T(8,128)(2,1)S(1)} %get-tuple-element.53.mine), custom_call_target="tpu_custom_call" | custom-call | tf_op jit(solution)/shard_map/pallas_call | solution.py:510
  19.4 1.6 %collective-permute-start.10 = (bf16[896,128]{1,0:T(8,128)(2,1)S(1)}, bf16[896,128]{1,0:T(8,128)(2,1)S(1)}, u32[]{:S(2)}, u32[]{:S(2)}) collective-permute-start(bf16[896,128]{1,0:T(8,128)(2,1)S(1)} %get-tuple-element.69), channel_id=1, source_target_pairs={{0,8},{4,20},{8,0},{12,28},{16,24},{20,4},{24,16},{28,12},{1,9},{5... | collective-permute-start | bytes 688136 | tf_op jit(solution)/shard_map/ppermute | solution.py:486
  21.0 1.1 %shard_map.100 = (bf16[896,128]{1,0:T(8,128)(2,1)S(1)}, f32[896,128]{1,0:T(8,128)S(1)}, f32[896,128]{1,0:T(8,128)S(1)}, bf16[48,256]{1,0:T(8,128)(2,1)S(1)}, bf16[48,256]{1,0:T(8,128)(2,1)S(1)}) custom-call(f32[3584,128]{1,0:T(8,128)S(1)} %shard_map.98.mine, bf16[128,768]{1,0:T(8,128)(2,1)S(1)} %get-tuple-element.55.left, ...), custom_call_target="tpu_custom_call" | custom-call | tf_op jit(solution)/shard_map/pallas_call | solution.py:519
  22.6 2.9 %collective-permute-done.10.received = bf16[896,128]{1,0:T(8,128)(2,1)S(1)} collective-permute-done((bf16[896,128]{1,0:T(8,128)(2,1)S(1)}, bf16[896,128]{1,0:T(8,128)(2,1)S(1)}, u32[]{:S(2)}, u32[]{:S(2)}) %collective-permute-start.10) | collective-permute-done | bytes 229408 | tf_op jit(solution)/shard_map/ppermute | solution.py:486
  25.5 1.6 %collective-permute-start.11 = (bf16[896,128]{1,0:T(8,128)(2,1)S(1)}, bf16[896,128]{1,0:T(8,128)(2,1)S(1)}, u32[]{:S(2)}, u32[]{:S(2)}) collective-permute-start(bf16[896,128]{1,0:T(8,128)(2,1)S(1)} %shard_map.104), channel_id=1, source_target_pairs={{0,16},{4,12},{8,24},{12,4},{16,0},{20,28},{24,8},{28,20},{1,17},{... | collective-permute-start | bytes 688136 | tf_op jit(solution)/shard_map/ppermute | solution.py:486
  27.1 2.3 %collective-permute-start.6 = (bf16[48,256]{1,0:T(8,128)(2,1)S(1)}, bf16[48,256]{1,0:T(8,128)(2,1)S(1)}, u32[]{:S(2)}, u32[]{:S(2)}) collective-permute-start(bf16[48,256]{1,0:T(8,128)(2,1)S(1)} %get-tuple-element.58), channel_id=1, source_target_pairs={{0,1},{1,0},{2,3},{3,2},{4,5},{5,4},{6,7},{7,6},{8,9},{9,8},{10,11... | collective-permute-start | bytes 73736 | tf_op jit(solution)/shard_map/ppermute | solution.py:463
  29.4 1.8 %collective-permute-done.6.got_first = bf16[48,256]{1,0:T(8,128)(2,1)S(1)} collective-permute-done((bf16[48,256]{1,0:T(8,128)(2,1)S(1)}, bf16[48,256]{1,0:T(8,128)(2,1)S(1)}, u32[]{:S(2)}, u32[]{:S(2)}) %collective-permute-start.6) | collective-permute-done | bytes 24608 | tf_op jit(solution)/shard_map/ppermute | solution.py:463
  31.8 2.5 %collective-permute-start.12 = (bf16[224,128]{1,0:T(8,128)(2,1)S(1)}, bf16[224,128]{1,0:T(8,128)(2,1)S(1)}, u32[]{:S(2)}, u32[]{:S(2)}) collective-permute-start(bf16[224,128]{1,0:T(8,128)(2,1)S(1)} %get-tuple-element.71), channel_id=1, source_target_pairs={{0,3},{1,2},{2,1},{3,0},{4,7},{5,6},{6,5},{7,4},{8,11},{9,10},{10,... | collective-permute-start | bytes 172040 | tf_op jit(solution)/shard_map/ppermute | solution.py:489
  34.2 1.0 %collective-permute-start.13 = (bf16[224,128]{1,0:T(8,128)(2,1)S(1)}, bf16[224,128]{1,0:T(8,128)(2,1)S(1)}, u32[]{:S(2)}, u32[]{:S(2)}) collective-permute-start(bf16[224,128]{1,0:T(8,128)(2,1)S(1)} %get-tuple-element.72), channel_id=1, source_target_pairs={{0,2},{1,3},{2,0},{3,1},{4,6},{5,7},{6,4},{7,5},{8,10},{9,11},{10,... | collective-permute-start | bytes 172040 | tf_op jit(solution)/shard_map/ppermute | solution.py:489
  35.2 1.0 %collective-permute-start.14 = (bf16[224,128]{1,0:T(8,128)(2,1)S(1)}, bf16[224,128]{1,0:T(8,128)(2,1)S(1)}, u32[]{:S(2)}, u32[]{:S(2)}) collective-permute-start(bf16[224,128]{1,0:T(8,128)(2,1)S(1)} %get-tuple-element.73), channel_id=1, source_target_pairs={{0,1},{1,0},{2,3},{3,2},{4,5},{5,4},{6,7},{7,6},{8,9},{9,8},{10,11... | collective-permute-start | bytes 172040 | tf_op jit(solution)/shard_map/ppermute | solution.py:489
  36.2 1.6 %shard_map.102 = (f32[768,128]{1,0:T(8,128)S(1)}, f32[8,128]{1,0:T(8,128)S(1)}) custom-call(bf16[768,256]{1,0:T(8,128)(2,1)S(1)} %get-tuple-element.59.hb, bf16[54,128,128]{2,1,0:T(8,128)(2,1)S(1)} %constant_dynamic-update-slice_fusion.weights), custom_call_target="tpu_custom_call" | custom-call | tf_op jit(solution)/shard_map/pallas_call | solution.py:540
  37.9 1.5 %collective-permute-done.13.refs_1_ = bf16[224,128]{1,0:T(8,128)(2,1)S(1)} collective-permute-done((bf16[224,128]{1,0:T(8,128)(2,1)S(1)}, bf16[224,128]{1,0:T(8,128)(2,1)S(1)}, u32[]{:S(2)}, u32[]{:S(2)}) %collective-permute-start.13) | collective-permute-done | bytes 57376 | tf_op jit(solution)/shard_map/ppermute | solution.py:489
  40.0 2.7 %collective-permute-start.17 = (bf16[224,128]{1,0:T(8,128)(2,1)S(1)}, bf16[224,128]{1,0:T(8,128)(2,1)S(1)}, u32[]{:S(2)}, u32[]{:S(2)}) collective-permute-start(bf16[224,128]{1,0:T(8,128)(2,1)S(1)} %shard_map.106.refs_0_), channel_id=1, source_target_pairs={{0,3},{1,2},{2,1},{3,0},{4,7},{5,6},{6,5},{7,4},{8,11},{9,10},{10,... | collective-permute-start | bytes 172040 | tf_op jit(solution)/shard_map/ppermute | solution.py:489
  42.7 1.7 %collective-permute-start.15 = (bf16[224,128]{1,0:T(8,128)(2,1)S(1)}, bf16[224,128]{1,0:T(8,128)(2,1)S(1)}, u32[]{:S(2)}, u32[]{:S(2)}) collective-permute-start(bf16[224,128]{1,0:T(8,128)(2,1)S(1)} %shard_map.106.refs_0_), channel_id=1, source_target_pairs={{0,1},{1,0},{2,3},{3,2},{4,5},{5,4},{6,7},{7,6},{8,9},{9,8},{10,11... | collective-permute-start | bytes 172040 | tf_op jit(solution)/shard_map/ppermute | solution.py:489
  44.4 1.7 %collective-permute-start.7 = (bf16[64,256]{1,0:T(8,128)(2,1)S(1)}, bf16[64,256]{1,0:T(8,128)(2,1)S(1)}, u32[]{:S(2)}, u32[]{:S(2)}) collective-permute-start(bf16[64,256]{1,0:T(8,128)(2,1)S(1)} %get-tuple-element.62.after), channel_id=1, source_target_pairs={{0,4},{4,0},{8,12},{12,8},{16,20},{20,16},{24,28},{28,24},{1,5},{5... | collective-permute-start | bytes 98312 | tf_op jit(solution)/shard_map/ppermute | solution.py:463
  46.1 1.7 %shard_map.103 = (f32[768,128]{1,0:T(8,128)S(1)}, f32[8,128]{1,0:T(8,128)S(1)}) custom-call(bf16[768,256]{1,0:T(8,128)(2,1)S(1)} %get-tuple-element.59.hb, bf16[54,128,128]{2,1,0:T(8,128)(2,1)S(1)} %constant_dynamic-update-slice_fusion.weights), custom_call_target="tpu_custom_call" | custom-call | tf_op jit(solution)/shard_map/pallas_call | solution.py:540
  47.9 1.6 %collective-permute-start.19 = (bf16[896,128]{1,0:T(8,128)(2,1)S(1)}, bf16[896,128]{1,0:T(8,128)(2,1)S(1)}, u32[]{:S(2)}, u32[]{:S(2)}) collective-permute-start(bf16[896,128]{1,0:T(8,128)(2,1)S(1)} %shard_map.107.held.refs_0_), channel_id=1, source_target_pairs={{0,8},{4,20},{8,0},{12,28},{16,24},{20,4},{24,16},{28,12},{1,9},{5... | collective-permute-start | bytes 688136 | tf_op jit(solution)/shard_map/ppermute | solution.py:486
  49.5 2.1 %shard_map.108 = (bf16[576,128]{1,0:T(8,128)(2,1)}, bf16[576,128]{1,0:T(8,128)(2,1)}, bf16[896,128]{1,0:T(8,128)(2,1)S(1)}) custom-call(s32[1,1,16]{2,1,0:T(1,128)S(1)} %copy-done.1, s32[1,1]{1,0:T(1,128)S(6)} %copy.23.counts, f32[768,128]{1,0:T(8,128)S(1)} %get-tuple-element.60.inner_hidden, f32[768,128]{1,0:T(8,128)S(1)} %get-tuple-element.61.inner_back, ...), custom_call_target="tpu_custom_call" | custom-call | tf_op jit(solution)/shard_map/pallas_call | solution.py:562
  51.6 1.4 %collective-permute-start.18 = (bf16[896,128]{1,0:T(8,128)(2,1)S(1)}, bf16[896,128]{1,0:T(8,128)(2,1)S(1)}, u32[]{:S(2)}, u32[]{:S(2)}) collective-permute-start(bf16[896,128]{1,0:T(8,128)(2,1)S(1)} %get-tuple-element.76), channel_id=1, source_target_pairs={{0,16},{4,12},{8,24},{12,4},{16,0},{20,28},{24,8},{28,20},{1,17},{... | collective-permute-start | bytes 688136 | tf_op jit(solution)/shard_map/ppermute | solution.py:486
  53.0 1.2 %collective-permute-done.19.refs_2_ = bf16[896,128]{1,0:T(8,128)(2,1)S(1)} collective-permute-done((bf16[896,128]{1,0:T(8,128)(2,1)S(1)}, bf16[896,128]{1,0:T(8,128)(2,1)S(1)}, u32[]{:S(2)}, u32[]{:S(2)}) %collective-permute-start.19) | collective-permute-done | bytes 229408 | tf_op jit(solution)/shard_map/ppermute | solution.py:486
  54.2 2.3 %collective-permute-start.23 = (bf16[896,128]{1,0:T(8,128)(2,1)S(1)}, bf16[896,128]{1,0:T(8,128)(2,1)S(1)}, u32[]{:S(2)}, u32[]{:S(2)}) collective-permute-start(bf16[896,128]{1,0:T(8,128)(2,1)S(1)} %collective-permute-done.19.refs_2_), channel_id=1, source_target_pairs={{0,16},{4,12},{8,24},{12,4},{16,0},{20,28},{24,8},{28,20},{1,17},{... | collective-permute-start | bytes 688136 | tf_op jit(solution)/shard_map/ppermute | solution.py:486
  56.5 1.1 %collective-permute-done.18.refs_0_ = bf16[896,128]{1,0:T(8,128)(2,1)S(1)} collective-permute-done((bf16[896,128]{1,0:T(8,128)(2,1)S(1)}, bf16[896,128]{1,0:T(8,128)(2,1)S(1)}, u32[]{:S(2)}, u32[]{:S(2)}) %collective-permute-start.18) | collective-permute-done | bytes 229408 | tf_op jit(solution)/shard_map/ppermute | solution.py:486
  57.6 1.3 %shard_map.109 = (f32[27,128,128]{2,1,0:T(8,128)}, f32[27,128,128]{2,1,0:T(8,128)}) custom-call(bf16[896,128]{1,0:T(8,128)(2,1)S(1)} %shard_map.107.held.refs_0_, bf16[896,128]{1,0:T(8,128)(2,1)S(1)} %collective-permute-done.22.refs_1_, bf16[896,128]{1,0:T(8,128)(2,1)S(1)} %collective-permute-done.19.refs_2_), custom_call_target="tpu_custom_call" | custom-call | flops 49999998976 | tf_op jit(solution)/shard_map/pallas_call | solution.py:591
  59.1 1.3 %shard_map.110 = (f32[27,128,128]{2,1,0:T(8,128)}, f32[27,128,128]{2,1,0:T(8,128)}, f32[8,128]{1,0:T(8,128)S(1)}) custom-call(bf16[896,128]{1,0:T(8,128)(2,1)S(1)} %collective-permute-done.18.refs_0_, bf16[896,128]{1,0:T(8,128)(2,1)S(1)} %collective-permute-done.20.refs_1_, ...), custom_call_target="tpu_custom_call", output_to_operand_aliasing={{0}: (3, {}), {1}: (4, {})} | custom-call | flops 49999998976 | tf_op jit(solution)/shard_map/pallas_call | solution.py:591
  61.0 0.8 %shard_map.112 = (f32[27,128,128]{2,1,0:T(8,128)}, f32[27,128,128]{2,1,0:T(8,128)}) custom-call(bf16[896,128]{1,0:T(8,128)(2,1)S(1)} %collective-permute-done.23.value.refs_0_, f32[27,128,128]{2,1,0:T(8,128)} %get-tuple-element.80.refs_1_, f32[27,128,128]{2,1,0:T(8,128)} %get-tuple-element.81.refs_2_), custom_call_target="tpu_custom_call", output_to_operand_aliasing={{0}: (1, {}), {1}: (2, {})} | custom-call | flops 49999998976 | tf_op jit(solution)/shard_map/pallas_call | solution.py:591
  62.1 0.9 %shard_map.113 = (f32[27,128,128]{2,1,0:T(8,128)}, f32[27,128,128]{2,1,0:T(8,128)}) custom-call(bf16[896,128]{1,0:T(8,128)(2,1)S(1)} %collective-permute-done.24.refs_0_, f32[27,128,128]{2,1,0:T(8,128)} %get-tuple-element.82.refs_1_, f32[27,128,128]{2,1,0:T(8,128)} %get-tuple-element.83.refs_2_), custom_call_target="tpu_custom_call", output_to_operand_aliasing={{0}: (1, {}), {1}: (2, {})} | custom-call | flops 49999998976 | tf_op jit(solution)/shard_map/pallas_call | solution.py:591
  (48 shorter events, 7.2 us)
Async XLA Ops:
  2.3 0.7 %copy-start = (s32[1,1,16]{2,1,0:T(1,128)S(1)}, s32[1,1,16]{2,1,0:T(1,128)}, u32[]{:S(2)}) copy-start(s32[1,1,16]{2,1,0:T(1,128)} %lists.5) | copy-start | bytes 196
  3.0 9.9 %copy-start.2 = (bf16[27,128,128]{2,1,0:T(8,128)(2,1)S(1)}, bf16[27,128,128]{2,1,0:T(8,128)(2,1)}, u32[]{:S(2)}) copy-start(bf16[27,128,128]{2,1,0:T(8,128)(2,1)} %param.9) | copy-start | bytes 2654212
  3.4 6.6 %collective-permute-start = (bf16[48,256]{1,0:T(8,128)(2,1)S(1)}, bf16[48,256]{1,0:T(8,128)(2,1)S(1)}, u32[]{:S(2)}, u32[]{:S(2)}) collective-permute-start(bf16[48,256]{1,0:T(8,128)(2,1)S(1)} %get-tuple-element.46), channel_id=1, source_target_pairs={{0,4},{1,2},{2,1},{3,7},{4,0},{5,6},{6,5},{7,3},{8,12},{9,10},{10,... | collective-permute-start | bytes 73736 | tf_op jit(solution)/shard_map/ppermute | solution.py:462
  3.9 6.1 %collective-permute-start.1 = (bf16[48,256]{1,0:T(8,128)(2,1)S(1)}, bf16[48,256]{1,0:T(8,128)(2,1)S(1)}, u32[]{:S(2)}, u32[]{:S(2)}) collective-permute-start(bf16[48,256]{1,0:T(8,128)(2,1)S(1)} %get-tuple-element.47), channel_id=1, source_target_pairs={{0,1},{1,0},{2,3},{3,2},{4,5},{5,4},{6,7},{7,6},{8,9},{9,8},{10,11... | collective-permute-start | bytes 73736 | tf_op jit(solution)/shard_map/ppermute | solution.py:463
  10.2 4.4 %collective-permute-start.2 = (bf16[64,256]{1,0:T(8,128)(2,1)S(1)}, bf16[64,256]{1,0:T(8,128)(2,1)S(1)}, u32[]{:S(2)}, u32[]{:S(2)}) collective-permute-start(bf16[64,256]{1,0:T(8,128)(2,1)S(1)} %get-tuple-element.49), channel_id=1, source_target_pairs={{0,4},{4,0},{8,12},{12,8},{16,20},{20,16},{24,28},{28,24},{1,5},{5... | collective-permute-start | bytes 98312 | tf_op jit(solution)/shard_map/ppermute | solution.py:463
  10.3 4.3 %collective-permute-start.3 = (bf16[64,256]{1,0:T(8,128)(2,1)S(1)}, bf16[64,256]{1,0:T(8,128)(2,1)S(1)}, u32[]{:S(2)}, u32[]{:S(2)}) collective-permute-start(bf16[64,256]{1,0:T(8,128)(2,1)S(1)} %get-tuple-element.50), channel_id=1, source_target_pairs={{0,28},{4,8},{8,4},{12,16},{16,12},{20,24},{24,20},{28,0},{1,29},{... | collective-permute-start | bytes 98312 | tf_op jit(solution)/shard_map/ppermute | solution.py:455
  16.8 1.8 %collective-permute-start.4 = (bf16[1664,128]{1,0:T(8,128)(2,1)S(1)}, bf16[1664,128]{1,0:T(8,128)(2,1)S(1)}, u32[]{:S(2)}, u32[]{:S(2)}) collective-permute-start(bf16[1664,128]{1,0:T(8,128)(2,1)S(1)} %get-tuple-element.54), channel_id=1, source_target_pairs={{0,4},{4,0},{8,12},{12,8},{16,20},{20,16},{24,28},{28,24},{1,5},{5... | collective-permute-start | bytes 1277960 | tf_op jit(solution)/shard_map/ppermute | solution.py:483
  19.4 6.1 %collective-permute-start.10 = (bf16[896,128]{1,0:T(8,128)(2,1)S(1)}, bf16[896,128]{1,0:T(8,128)(2,1)S(1)}, u32[]{:S(2)}, u32[]{:S(2)}) collective-permute-start(bf16[896,128]{1,0:T(8,128)(2,1)S(1)} %get-tuple-element.69), channel_id=1, source_target_pairs={{0,8},{4,20},{8,0},{12,28},{16,24},{20,4},{24,16},{28,12},{1,9},{5... | collective-permute-start | bytes 688136 | tf_op jit(solution)/shard_map/ppermute | solution.py:486
  22.1 9.4 %collective-permute-start.9 = (bf16[896,128]{1,0:T(8,128)(2,1)S(1)}, bf16[896,128]{1,0:T(8,128)(2,1)S(1)}, u32[]{:S(2)}, u32[]{:S(2)}) collective-permute-start(bf16[896,128]{1,0:T(8,128)(2,1)S(1)} %get-tuple-element.67), channel_id=1, source_target_pairs={{0,8},{4,20},{8,0},{12,28},{16,24},{20,4},{24,16},{28,12},{1,9},{5... | collective-permute-start | bytes 688136 | tf_op jit(solution)/shard_map/ppermute | solution.py:486
  25.5 6.1 %collective-permute-start.11 = (bf16[896,128]{1,0:T(8,128)(2,1)S(1)}, bf16[896,128]{1,0:T(8,128)(2,1)S(1)}, u32[]{:S(2)}, u32[]{:S(2)}) collective-permute-start(bf16[896,128]{1,0:T(8,128)(2,1)S(1)} %shard_map.104), channel_id=1, source_target_pairs={{0,16},{4,12},{8,24},{12,4},{16,0},{20,28},{24,8},{28,20},{1,17},{... | collective-permute-start | bytes 688136 | tf_op jit(solution)/shard_map/ppermute | solution.py:486
  27.1 2.3 %collective-permute-start.5 = (bf16[48,256]{1,0:T(8,128)(2,1)S(1)}, bf16[48,256]{1,0:T(8,128)(2,1)S(1)}, u32[]{:S(2)}, u32[]{:S(2)}) collective-permute-start(bf16[48,256]{1,0:T(8,128)(2,1)S(1)} %get-tuple-element.57), channel_id=1, source_target_pairs={{0,4},{1,2},{2,1},{3,7},{4,0},{5,6},{6,5},{7,3},{8,12},{9,10},{10,... | collective-permute-start | bytes 73736 | tf_op jit(solution)/shard_map/ppermute | solution.py:462
  27.1 4.1 %collective-permute-start.6 = (bf16[48,256]{1,0:T(8,128)(2,1)S(1)}, bf16[48,256]{1,0:T(8,128)(2,1)S(1)}, u32[]{:S(2)}, u32[]{:S(2)}) collective-permute-start(bf16[48,256]{1,0:T(8,128)(2,1)S(1)} %get-tuple-element.58), channel_id=1, source_target_pairs={{0,1},{1,0},{2,3},{3,2},{4,5},{5,4},{6,7},{7,6},{8,9},{9,8},{10,11... | collective-permute-start | bytes 73736 | tf_op jit(solution)/shard_map/ppermute | solution.py:463
  31.8 6.1 %collective-permute-start.12 = (bf16[224,128]{1,0:T(8,128)(2,1)S(1)}, bf16[224,128]{1,0:T(8,128)(2,1)S(1)}, u32[]{:S(2)}, u32[]{:S(2)}) collective-permute-start(bf16[224,128]{1,0:T(8,128)(2,1)S(1)} %get-tuple-element.71), channel_id=1, source_target_pairs={{0,3},{1,2},{2,1},{3,0},{4,7},{5,6},{6,5},{7,4},{8,11},{9,10},{10,... | collective-permute-start | bytes 172040 | tf_op jit(solution)/shard_map/ppermute | solution.py:489
  34.2 5.1 %collective-permute-start.13 = (bf16[224,128]{1,0:T(8,128)(2,1)S(1)}, bf16[224,128]{1,0:T(8,128)(2,1)S(1)}, u32[]{:S(2)}, u32[]{:S(2)}) collective-permute-start(bf16[224,128]{1,0:T(8,128)(2,1)S(1)} %get-tuple-element.72), channel_id=1, source_target_pairs={{0,2},{1,3},{2,0},{3,1},{4,6},{5,7},{6,4},{7,5},{8,10},{9,11},{10,... | collective-permute-start | bytes 172040 | tf_op jit(solution)/shard_map/ppermute | solution.py:489
  35.2 4.7 %collective-permute-start.14 = (bf16[224,128]{1,0:T(8,128)(2,1)S(1)}, bf16[224,128]{1,0:T(8,128)(2,1)S(1)}, u32[]{:S(2)}, u32[]{:S(2)}) collective-permute-start(bf16[224,128]{1,0:T(8,128)(2,1)S(1)} %get-tuple-element.73), channel_id=1, source_target_pairs={{0,1},{1,0},{2,3},{3,2},{4,5},{5,4},{6,7},{7,6},{8,9},{9,8},{10,11... | collective-permute-start | bytes 172040 | tf_op jit(solution)/shard_map/ppermute | solution.py:489
  37.8 11.7 %copy-start.1 = (s32[1,1,16]{2,1,0:T(1,128)S(1)}, s32[1,1,16]{2,1,0:T(1,128)}, u32[]{:S(2)}) copy-start(s32[1,1,16]{2,1,0:T(1,128)} %lists.5) | copy-start | bytes 196
  40.0 7.8 %collective-permute-start.17 = (bf16[224,128]{1,0:T(8,128)(2,1)S(1)}, bf16[224,128]{1,0:T(8,128)(2,1)S(1)}, u32[]{:S(2)}, u32[]{:S(2)}) collective-permute-start(bf16[224,128]{1,0:T(8,128)(2,1)S(1)} %shard_map.106.refs_0_), channel_id=1, source_target_pairs={{0,3},{1,2},{2,1},{3,0},{4,7},{5,6},{6,5},{7,4},{8,11},{9,10},{10,... | collective-permute-start | bytes 172040 | tf_op jit(solution)/shard_map/ppermute | solution.py:489
  42.7 5.2 %collective-permute-start.16 = (bf16[224,128]{1,0:T(8,128)(2,1)S(1)}, bf16[224,128]{1,0:T(8,128)(2,1)S(1)}, u32[]{:S(2)}, u32[]{:S(2)}) collective-permute-start(bf16[224,128]{1,0:T(8,128)(2,1)S(1)} %shard_map.106.refs_0_), channel_id=1, source_target_pairs={{0,2},{1,3},{2,0},{3,1},{4,6},{5,7},{6,4},{7,5},{8,10},{9,11},{10,... | collective-permute-start | bytes 172040 | tf_op jit(solution)/shard_map/ppermute | solution.py:489
  42.7 5.2 %collective-permute-start.15 = (bf16[224,128]{1,0:T(8,128)(2,1)S(1)}, bf16[224,128]{1,0:T(8,128)(2,1)S(1)}, u32[]{:S(2)}, u32[]{:S(2)}) collective-permute-start(bf16[224,128]{1,0:T(8,128)(2,1)S(1)} %shard_map.106.refs_0_), channel_id=1, source_target_pairs={{0,1},{1,0},{2,3},{3,2},{4,5},{5,4},{6,7},{7,6},{8,9},{9,8},{10,11... | collective-permute-start | bytes 172040 | tf_op jit(solution)/shard_map/ppermute | solution.py:489
  44.4 5.1 %collective-permute-start.8 = (bf16[64,256]{1,0:T(8,128)(2,1)S(1)}, bf16[64,256]{1,0:T(8,128)(2,1)S(1)}, u32[]{:S(2)}, u32[]{:S(2)}) collective-permute-start(bf16[64,256]{1,0:T(8,128)(2,1)S(1)} %get-tuple-element.63), channel_id=1, source_target_pairs={{0,28},{4,8},{8,4},{12,16},{16,12},{20,24},{24,20},{28,0},{1,29},{... | collective-permute-start | bytes 98312 | tf_op jit(solution)/shard_map/ppermute | solution.py:455
  44.4 5.1 %collective-permute-start.7 = (bf16[64,256]{1,0:T(8,128)(2,1)S(1)}, bf16[64,256]{1,0:T(8,128)(2,1)S(1)}, u32[]{:S(2)}, u32[]{:S(2)}) collective-permute-start(bf16[64,256]{1,0:T(8,128)(2,1)S(1)} %get-tuple-element.62.after), channel_id=1, source_target_pairs={{0,4},{4,0},{8,12},{12,8},{16,20},{20,16},{24,28},{28,24},{1,5},{5... | collective-permute-start | bytes 98312 | tf_op jit(solution)/shard_map/ppermute | solution.py:463
  47.9 6.3 %collective-permute-start.19 = (bf16[896,128]{1,0:T(8,128)(2,1)S(1)}, bf16[896,128]{1,0:T(8,128)(2,1)S(1)}, u32[]{:S(2)}, u32[]{:S(2)}) collective-permute-start(bf16[896,128]{1,0:T(8,128)(2,1)S(1)} %shard_map.107.held.refs_0_), channel_id=1, source_target_pairs={{0,8},{4,20},{8,0},{12,28},{16,24},{20,4},{24,16},{28,12},{1,9},{5... | collective-permute-start | bytes 688136 | tf_op jit(solution)/shard_map/ppermute | solution.py:486
  51.6 6.0 %collective-permute-start.18 = (bf16[896,128]{1,0:T(8,128)(2,1)S(1)}, bf16[896,128]{1,0:T(8,128)(2,1)S(1)}, u32[]{:S(2)}, u32[]{:S(2)}) collective-permute-start(bf16[896,128]{1,0:T(8,128)(2,1)S(1)} %get-tuple-element.76), channel_id=1, source_target_pairs={{0,16},{4,12},{8,24},{12,4},{16,0},{20,28},{24,8},{28,20},{1,17},{... | collective-permute-start | bytes 688136 | tf_op jit(solution)/shard_map/ppermute | solution.py:486
  53.0 4.6 %collective-permute-start.22 = (bf16[896,128]{1,0:T(8,128)(2,1)S(1)}, bf16[896,128]{1,0:T(8,128)(2,1)S(1)}, u32[]{:S(2)}, u32[]{:S(2)}) collective-permute-start(bf16[896,128]{1,0:T(8,128)(2,1)S(1)} %shard_map.107.held.refs_0_), channel_id=1, source_target_pairs={{0,4},{4,0},{8,12},{12,8},{16,20},{20,16},{24,28},{28,24},{1,5},{5... | collective-permute-start | bytes 688136 | tf_op jit(solution)/shard_map/ppermute | solution.py:483
  54.2 6.3 %collective-permute-start.23 = (bf16[896,128]{1,0:T(8,128)(2,1)S(1)}, bf16[896,128]{1,0:T(8,128)(2,1)S(1)}, u32[]{:S(2)}, u32[]{:S(2)}) collective-permute-start(bf16[896,128]{1,0:T(8,128)(2,1)S(1)} %collective-permute-done.19.refs_2_), channel_id=1, source_target_pairs={{0,16},{4,12},{8,24},{12,4},{16,0},{20,28},{24,8},{28,20},{1,17},{... | collective-permute-start | bytes 688136 | tf_op jit(solution)/shard_map/ppermute | solution.py:486
  56.5 2.6 %collective-permute-start.20 = (bf16[896,128]{1,0:T(8,128)(2,1)S(1)}, bf16[896,128]{1,0:T(8,128)(2,1)S(1)}, u32[]{:S(2)}, u32[]{:S(2)}) collective-permute-start(bf16[896,128]{1,0:T(8,128)(2,1)S(1)} %collective-permute-done.19.refs_2_), channel_id=1, source_target_pairs={{0,4},{4,0},{8,12},{12,8},{16,20},{20,16},{24,28},{28,24},{1,5},{5... | collective-permute-start | bytes 688136 | tf_op jit(solution)/shard_map/ppermute | solution.py:483
  57.6 1.5 %collective-permute-start.21 = (bf16[896,128]{1,0:T(8,128)(2,1)S(1)}, bf16[896,128]{1,0:T(8,128)(2,1)S(1)}, u32[]{:S(2)}, u32[]{:S(2)}) collective-permute-start(bf16[896,128]{1,0:T(8,128)(2,1)S(1)} %collective-permute-done.18.refs_0_), channel_id=1, source_target_pairs={{0,4},{4,0},{8,12},{12,8},{16,20},{20,16},{24,28},{28,24},{1,5},{5... | collective-permute-start | bytes 688136 | tf_op jit(solution)/shard_map/ppermute | solution.py:483
  60.5 1.6 %collective-permute-start.24 = (bf16[896,128]{1,0:T(8,128)(2,1)S(1)}, bf16[896,128]{1,0:T(8,128)(2,1)S(1)}, u32[]{:S(2)}, u32[]{:S(2)}) collective-permute-start(bf16[896,128]{1,0:T(8,128)(2,1)S(1)} %shard_map.111), channel_id=1, source_target_pairs={{0,4},{4,0},{8,12},{12,8},{16,20},{20,16},{24,28},{28,24},{1,5},{5... | collective-permute-start | bytes 688136 | tf_op jit(solution)/shard_map/ppermute | solution.py:483

commit v7 on v6

--- a/solution.py
+++ b/solution.py
@@ -154,6 +154,10 @@
     low = jnp.concatenate([full[z * PLANE : z * PLANE + J, :] for z in range(4)], axis=0)
     high = jnp.concatenate([full[(z + 1) * PLANE - J : (z + 1) * PLANE, :] for z in range(4)], axis=0)
     write_by_parity("drift", low, high, slab_first, slab_second)
+
+
+def insert_hidden_faces(placed, got_first, got_second, *refs):
+    insert_faces(placed, got_second, got_first, *refs)
 
 
 def build_window(window, base, plane_of):
@@ -532,7 +536,7 @@
     else:
         parts = [to_chip(value, k) for k, value in zip(kinds, sends)]
     faces = pairs(face_first, face_second, "wire")
-    hb_full, *hb_slabs = call(insert_faces, (grid, slab, slab), [VMEM] * 3, [faces_scratch])(hb, *faces[::-1])
+    hb_full, *hb_slabs = call(insert_hidden_faces, (grid, slab, slab), [VMEM] * 3, [faces_scratch])(hb, *faces)
     inserted = hb_slabs[0]
     hb_slabs = pairs(*hb_slabs, "drift")
     token = f32(8, 128)

time: 63.4 us -> 63.3 us (level)
  transfers between devices with their start and end apart: 25 -> 25, of which waited for: 13 -> 11; matrix products, arithmetic and copies ran while one was open for 2% -> 2% of each run, Pallas kernels for 21% -> 21%
where the time goes in v7:
time: 63.3 us; the launch traced here: 63.1 us
  starting transfers between devices  29.4 us (46%)
  Pallas kernels  18.2 us (29%)
  waiting for transfers between devices  10.8 us (17%)
  local copies, waits for them, and re-layouts  2 us (3%)
  between operations  1.69 us (3%)
  other arithmetic  1.02 us (2%)
    ppermute x6, starting transfers between devices, to_chip(): lax.ppermute(value, 'drift', [(i, i ^ 2 * chip_mask(kind, i % 2)) for i i...  9.22 us
    ppermute x6, starting transfers between devices, to_wire(): return lax.ppermute(value, 'wire', [(i, i ^ step) for i in range(wire)])  8.91 us
    ppermute x4, starting transfers between devices, pairs(): got_first = lax.ppermute(value_first, axis, first)  7.74 us
    ppermute x6, waiting for transfers between devices, to_chip(): lax.ppermute(value, 'drift', [(i, i ^ 2 * chip_mask(kind, i % 2)) for i i...  5.56 us
    pallas_call x4, Pallas kernels, on_device(): call(functools.partial(final_kernel, items, blocks, want_done), (f32(TAPS...  4.22 us
    pallas_call x2, Pallas kernels, on_device(): call(functools.partial(second_inner_kernel, field), (f32(ROWS, 128), toke...  3.3 us
    ppermute x2, starting transfers between devices, pairs(): got_second = lax.ppermute(value_second, axis, sorted(second.items()))  2.55 us
    pallas_call x1, Pallas kernels, on_device(): call(first_kernel, (grid, message, message), [VMEM] * 6, conv_scratch + [...  2.14 us
  transfers between devices with their start and end apart: 25, of which 11 were waited for; matrix products, arithmetic and copies ran while one was open for 2% of the time, Pallas kernels for 21%

profile of v7, /device:TPU:0, one launch (start us, length us, event | category | flops | bytes accessed | tf_op | source)
XLA Modules:
  0.0 63.1 jit_solution(7707461891366278802)
XLA Ops:
  1.3 1.0 %pad_maximum_fusion.pair = bf16[576,256]{1,0:T(8,128)(2,1)S(1)} fusion(bf16[576,128]{1,0:T(8,128)(2,1)} %bitcast.4, bf16[576,128]{1,0:T(8,128)(2,1)} %bitcast.5), kind=kLoop, calls=%fused_computation | loop fusion | flops 589824 | bytes 589824 | tf_op jit(solution)/shard_map/concatenate | solution.py:495
  3.9 4.1 %collective-permute-start.1 = (bf16[48,256]{1,0:T(8,128)(2,1)S(1)}, bf16[48,256]{1,0:T(8,128)(2,1)S(1)}, u32[]{:S(2)}, u32[]{:S(2)}) collective-permute-start(bf16[48,256]{1,0:T(8,128)(2,1)S(1)} %get-tuple-element.47), channel_id=1, source_target_pairs={{0,1},{1,0},{2,3},{3,2},{4,5},{5,4},{6,7},{7,6},{8,9},{9,8},{10,11... | collective-permute-start | bytes 73736 | tf_op jit(solution)/shard_map/ppermute | solution.py:467
  8.0 1.2 %constant_dynamic-update-slice_fusion.1 = bf16[54,128,128]{2,1,0:T(8,128)(2,1)S(1)} fusion(bf16[27,128,128]{2,1,0:T(8,128)(2,1)} %param.8), kind=kLoop, calls=%fused_computation.2 | loop fusion | bytes 1769472
  10.3 2.5 %collective-permute-start.3 = (bf16[64,256]{1,0:T(8,128)(2,1)S(1)}, bf16[64,256]{1,0:T(8,128)(2,1)S(1)}, u32[]{:S(2)}, u32[]{:S(2)}) collective-permute-start(bf16[64,256]{1,0:T(8,128)(2,1)S(1)} %get-tuple-element.50), channel_id=1, source_target_pairs={{0,28},{4,8},{8,4},{12,16},{16,12},{20,24},{24,20},{28,0},{1,29},{... | collective-permute-start | bytes 98312 | tf_op jit(solution)/shard_map/ppermute | solution.py:459
  13.0 1.6 %shard_map.96.inner = f32[768,128]{1,0:T(8,128)S(1)} custom-call(bf16[768,256]{1,0:T(8,128)(2,1)S(1)} %get-tuple-element.48.full.base, bf16[54,128,128]{2,1,0:T(8,128)(2,1)S(1)} %constant_dynamic-update-slice_fusion.weights), custom_call_target="tpu_custom_call" | custom-call | tf_op jit(solution)/shard_map/pallas_call | solution.py:504
  14.6 2.1 %shard_map.97 = (bf16[768,256]{1,0:T(8,128)(2,1)S(1)}, bf16[1664,128]{1,0:T(8,128)(2,1)S(1)}, bf16[1664,128]{1,0:T(8,128)(2,1)S(1)}) custom-call(bf16[768,256]{1,0:T(8,128)(2,1)S(1)} %get-tuple-element.48.full.base, bf16[64,256]{1,0:T(8,128)(2,1)S(1)} %collective-permute-done.2.got_first, bf16[64,256]{1,0:T(8,128)(2,1)S(1)} %collective-permute-done.3.got_second, ...), custom_call_target="tpu_custom_call" | custom-call | tf_op jit(solution)/shard_map/pallas_call | solution.py:505
  16.9 1.1 %shard_map.98.mine = f32[3584,128]{1,0:T(8,128)S(1)} custom-call(bf16[1664,128]{1,0:T(8,128)(2,1)S(1)} %get-tuple-element.53.mine), custom_call_target="tpu_custom_call" | custom-call | tf_op jit(solution)/shard_map/pallas_call | solution.py:514
  19.4 1.6 %collective-permute-start.10 = (bf16[896,128]{1,0:T(8,128)(2,1)S(1)}, bf16[896,128]{1,0:T(8,128)(2,1)S(1)}, u32[]{:S(2)}, u32[]{:S(2)}) collective-permute-start(bf16[896,128]{1,0:T(8,128)(2,1)S(1)} %get-tuple-element.69), channel_id=1, source_target_pairs={{0,8},{4,20},{8,0},{12,28},{16,24},{20,4},{24,16},{28,12},{1,9},{5... | collective-permute-start | bytes 688136 | tf_op jit(solution)/shard_map/ppermute | solution.py:490
  21.0 1.1 %shard_map.100 = (bf16[896,128]{1,0:T(8,128)(2,1)S(1)}, f32[896,128]{1,0:T(8,128)S(1)}, f32[896,128]{1,0:T(8,128)S(1)}, bf16[48,256]{1,0:T(8,128)(2,1)S(1)}, bf16[48,256]{1,0:T(8,128)(2,1)S(1)}) custom-call(f32[3584,128]{1,0:T(8,128)S(1)} %shard_map.98.mine, bf16[128,768]{1,0:T(8,128)(2,1)S(1)} %get-tuple-element.55.left, ...), custom_call_target="tpu_custom_call" | custom-call | tf_op jit(solution)/shard_map/pallas_call | solution.py:523
  22.6 2.9 %collective-permute-done.10.received = bf16[896,128]{1,0:T(8,128)(2,1)S(1)} collective-permute-done((bf16[896,128]{1,0:T(8,128)(2,1)S(1)}, bf16[896,128]{1,0:T(8,128)(2,1)S(1)}, u32[]{:S(2)}, u32[]{:S(2)}) %collective-permute-start.10) | collective-permute-done | bytes 229408 | tf_op jit(solution)/shard_map/ppermute | solution.py:490
  25.5 1.6 %collective-permute-start.11 = (bf16[896,128]{1,0:T(8,128)(2,1)S(1)}, bf16[896,128]{1,0:T(8,128)(2,1)S(1)}, u32[]{:S(2)}, u32[]{:S(2)}) collective-permute-start(bf16[896,128]{1,0:T(8,128)(2,1)S(1)} %shard_map.104), channel_id=1, source_target_pairs={{0,16},{4,12},{8,24},{12,4},{16,0},{20,28},{24,8},{28,20},{1,17},{... | collective-permute-start | bytes 688136 | tf_op jit(solution)/shard_map/ppermute | solution.py:490
  27.1 1.9 %collective-permute-start.5 = (bf16[48,256]{1,0:T(8,128)(2,1)S(1)}, bf16[48,256]{1,0:T(8,128)(2,1)S(1)}, u32[]{:S(2)}, u32[]{:S(2)}) collective-permute-start(bf16[48,256]{1,0:T(8,128)(2,1)S(1)} %get-tuple-element.57), channel_id=1, source_target_pairs={{0,1},{1,0},{2,3},{3,2},{4,5},{5,4},{6,7},{7,6},{8,9},{9,8},{10,11... | collective-permute-start | bytes 73736 | tf_op jit(solution)/shard_map/ppermute | solution.py:467
  29.0 2.0 %collective-permute-done.5.got_first = bf16[48,256]{1,0:T(8,128)(2,1)S(1)} collective-permute-done((bf16[48,256]{1,0:T(8,128)(2,1)S(1)}, bf16[48,256]{1,0:T(8,128)(2,1)S(1)}, u32[]{:S(2)}, u32[]{:S(2)}) %collective-permute-start.5) | collective-permute-done | bytes 24608 | tf_op jit(solution)/shard_map/ppermute | solution.py:467
  31.8 2.5 %collective-permute-start.12 = (bf16[224,128]{1,0:T(8,128)(2,1)S(1)}, bf16[224,128]{1,0:T(8,128)(2,1)S(1)}, u32[]{:S(2)}, u32[]{:S(2)}) collective-permute-start(bf16[224,128]{1,0:T(8,128)(2,1)S(1)} %get-tuple-element.71), channel_id=1, source_target_pairs={{0,3},{1,2},{2,1},{3,0},{4,7},{5,6},{6,5},{7,4},{8,11},{9,10},{10,... | collective-permute-start | bytes 172040 | tf_op jit(solution)/shard_map/ppermute | solution.py:493
  34.2 0.9 %collective-permute-start.13 = (bf16[224,128]{1,0:T(8,128)(2,1)S(1)}, bf16[224,128]{1,0:T(8,128)(2,1)S(1)}, u32[]{:S(2)}, u32[]{:S(2)}) collective-permute-start(bf16[224,128]{1,0:T(8,128)(2,1)S(1)} %get-tuple-element.72), channel_id=1, source_target_pairs={{0,2},{1,3},{2,0},{3,1},{4,6},{5,7},{6,4},{7,5},{8,10},{9,11},{10,... | collective-permute-start | bytes 172040 | tf_op jit(solution)/shard_map/ppermute | solution.py:493
  35.2 1.0 %collective-permute-start.14 = (bf16[224,128]{1,0:T(8,128)(2,1)S(1)}, bf16[224,128]{1,0:T(8,128)(2,1)S(1)}, u32[]{:S(2)}, u32[]{:S(2)}) collective-permute-start(bf16[224,128]{1,0:T(8,128)(2,1)S(1)} %get-tuple-element.73), channel_id=1, source_target_pairs={{0,1},{1,0},{2,3},{3,2},{4,5},{5,4},{6,7},{7,6},{8,9},{9,8},{10,11... | collective-permute-start | bytes 172040 | tf_op jit(solution)/shard_map/ppermute | solution.py:493
  36.2 1.6 %shard_map.102 = (f32[768,128]{1,0:T(8,128)S(1)}, f32[8,128]{1,0:T(8,128)S(1)}) custom-call(bf16[768,256]{1,0:T(8,128)(2,1)S(1)} %get-tuple-element.59.hb, bf16[54,128,128]{2,1,0:T(8,128)(2,1)S(1)} %constant_dynamic-update-slice_fusion.weights), custom_call_target="tpu_custom_call" | custom-call | tf_op jit(solution)/shard_map/pallas_call | solution.py:544
  37.9 2.0 %collective-permute-done.13.refs_1_ = bf16[224,128]{1,0:T(8,128)(2,1)S(1)} collective-permute-done((bf16[224,128]{1,0:T(8,128)(2,1)S(1)}, bf16[224,128]{1,0:T(8,128)(2,1)S(1)}, u32[]{:S(2)}, u32[]{:S(2)}) %collective-permute-start.13) | collective-permute-done | bytes 57376 | tf_op jit(solution)/shard_map/ppermute | solution.py:493
  40.0 2.3 %collective-permute-start.17 = (bf16[224,128]{1,0:T(8,128)(2,1)S(1)}, bf16[224,128]{1,0:T(8,128)(2,1)S(1)}, u32[]{:S(2)}, u32[]{:S(2)}) collective-permute-start(bf16[224,128]{1,0:T(8,128)(2,1)S(1)} %shard_map.106.refs_0_), channel_id=1, source_target_pairs={{0,3},{1,2},{2,1},{3,0},{4,7},{5,6},{6,5},{7,4},{8,11},{9,10},{10,... | collective-permute-start | bytes 172040 | tf_op jit(solution)/shard_map/ppermute | solution.py:493
  42.3 2.1 %collective-permute-start.15 = (bf16[224,128]{1,0:T(8,128)(2,1)S(1)}, bf16[224,128]{1,0:T(8,128)(2,1)S(1)}, u32[]{:S(2)}, u32[]{:S(2)}) collective-permute-start(bf16[224,128]{1,0:T(8,128)(2,1)S(1)} %shard_map.106.refs_0_), channel_id=1, source_target_pairs={{0,1},{1,0},{2,3},{3,2},{4,5},{5,4},{6,7},{7,6},{8,9},{9,8},{10,11... | collective-permute-start | bytes 172040 | tf_op jit(solution)/shard_map/ppermute | solution.py:493
  44.4 1.7 %collective-permute-start.7 = (bf16[64,256]{1,0:T(8,128)(2,1)S(1)}, bf16[64,256]{1,0:T(8,128)(2,1)S(1)}, u32[]{:S(2)}, u32[]{:S(2)}) collective-permute-start(bf16[64,256]{1,0:T(8,128)(2,1)S(1)} %get-tuple-element.62.after), channel_id=1, source_target_pairs={{0,4},{4,0},{8,12},{12,8},{16,20},{20,16},{24,28},{28,24},{1,5},{5... | collective-permute-start | bytes 98312 | tf_op jit(solution)/shard_map/ppermute | solution.py:467
  46.1 1.7 %shard_map.103 = (f32[768,128]{1,0:T(8,128)S(1)}, f32[8,128]{1,0:T(8,128)S(1)}) custom-call(bf16[768,256]{1,0:T(8,128)(2,1)S(1)} %get-tuple-element.59.hb, bf16[54,128,128]{2,1,0:T(8,128)(2,1)S(1)} %constant_dynamic-update-slice_fusion.weights), custom_call_target="tpu_custom_call" | custom-call | tf_op jit(solution)/shard_map/pallas_call | solution.py:544
  47.8 1.6 %collective-permute-start.19 = (bf16[896,128]{1,0:T(8,128)(2,1)S(1)}, bf16[896,128]{1,0:T(8,128)(2,1)S(1)}, u32[]{:S(2)}, u32[]{:S(2)}) collective-permute-start(bf16[896,128]{1,0:T(8,128)(2,1)S(1)} %shard_map.107.held.refs_0_), channel_id=1, source_target_pairs={{0,8},{4,20},{8,0},{12,28},{16,24},{20,4},{24,16},{28,12},{1,9},{5... | collective-permute-start | bytes 688136 | tf_op jit(solution)/shard_map/ppermute | solution.py:490
  49.4 2.1 %shard_map.108 = (bf16[576,128]{1,0:T(8,128)(2,1)}, bf16[576,128]{1,0:T(8,128)(2,1)}, bf16[896,128]{1,0:T(8,128)(2,1)S(1)}) custom-call(s32[1,1,16]{2,1,0:T(1,128)S(1)} %copy-done.1, s32[1,1]{1,0:T(1,128)S(6)} %copy.23.counts, f32[768,128]{1,0:T(8,128)S(1)} %get-tuple-element.60.inner_hidden, f32[768,128]{1,0:T(8,128)S(1)} %get-tuple-element.61.inner_back, ...), custom_call_target="tpu_custom_call" | custom-call | tf_op jit(solution)/shard_map/pallas_call | solution.py:566
  51.5 1.5 %collective-permute-start.18 = (bf16[896,128]{1,0:T(8,128)(2,1)S(1)}, bf16[896,128]{1,0:T(8,128)(2,1)S(1)}, u32[]{:S(2)}, u32[]{:S(2)}) collective-permute-start(bf16[896,128]{1,0:T(8,128)(2,1)S(1)} %get-tuple-element.76), channel_id=1, source_target_pairs={{0,16},{4,12},{8,24},{12,4},{16,0},{20,28},{24,8},{28,20},{1,17},{... | collective-permute-start | bytes 688136 | tf_op jit(solution)/shard_map/ppermute | solution.py:490
  53.0 1.1 %collective-permute-done.19.refs_2_ = bf16[896,128]{1,0:T(8,128)(2,1)S(1)} collective-permute-done((bf16[896,128]{1,0:T(8,128)(2,1)S(1)}, bf16[896,128]{1,0:T(8,128)(2,1)S(1)}, u32[]{:S(2)}, u32[]{:S(2)}) %collective-permute-start.19) | collective-permute-done | bytes 229408 | tf_op jit(solution)/shard_map/ppermute | solution.py:490
  54.0 2.5 %collective-permute-start.23 = (bf16[896,128]{1,0:T(8,128)(2,1)S(1)}, bf16[896,128]{1,0:T(8,128)(2,1)S(1)}, u32[]{:S(2)}, u32[]{:S(2)}) collective-permute-start(bf16[896,128]{1,0:T(8,128)(2,1)S(1)} %collective-permute-done.19.refs_2_), channel_id=1, source_target_pairs={{0,16},{4,12},{8,24},{12,4},{16,0},{20,28},{24,8},{28,20},{1,17},{... | collective-permute-start | bytes 688136 | tf_op jit(solution)/shard_map/ppermute | solution.py:490
  56.5 1.1 %collective-permute-done.18.refs_0_ = bf16[896,128]{1,0:T(8,128)(2,1)S(1)} collective-permute-done((bf16[896,128]{1,0:T(8,128)(2,1)S(1)}, bf16[896,128]{1,0:T(8,128)(2,1)S(1)}, u32[]{:S(2)}, u32[]{:S(2)}) %collective-permute-start.18) | collective-permute-done | bytes 229408 | tf_op jit(solution)/shard_map/ppermute | solution.py:490
  57.5 1.3 %shard_map.109 = (f32[27,128,128]{2,1,0:T(8,128)}, f32[27,128,128]{2,1,0:T(8,128)}) custom-call(bf16[896,128]{1,0:T(8,128)(2,1)S(1)} %shard_map.107.held.refs_0_, bf16[896,128]{1,0:T(8,128)(2,1)S(1)} %collective-permute-done.22.refs_1_, bf16[896,128]{1,0:T(8,128)(2,1)S(1)} %collective-permute-done.19.refs_2_), custom_call_target="tpu_custom_call" | custom-call | flops 49999998976 | tf_op jit(solution)/shard_map/pallas_call | solution.py:595
  59.0 1.3 %shard_map.110 = (f32[27,128,128]{2,1,0:T(8,128)}, f32[27,128,128]{2,1,0:T(8,128)}, f32[8,128]{1,0:T(8,128)S(1)}) custom-call(bf16[896,128]{1,0:T(8,128)(2,1)S(1)} %collective-permute-done.18.refs_0_, bf16[896,128]{1,0:T(8,128)(2,1)S(1)} %collective-permute-done.20.refs_1_, ...), custom_call_target="tpu_custom_call", output_to_operand_aliasing={{0}: (3, {}), {1}: (4, {})} | custom-call | flops 49999998976 | tf_op jit(solution)/shard_map/pallas_call | solution.py:595
  60.9 0.8 %shard_map.112 = (f32[27,128,128]{2,1,0:T(8,128)}, f32[27,128,128]{2,1,0:T(8,128)}) custom-call(bf16[896,128]{1,0:T(8,128)(2,1)S(1)} %collective-permute-done.23.value.refs_0_, f32[27,128,128]{2,1,0:T(8,128)} %get-tuple-element.80.refs_1_, f32[27,128,128]{2,1,0:T(8,128)} %get-tuple-element.81.refs_2_), custom_call_target="tpu_custom_call", output_to_operand_aliasing={{0}: (1, {}), {1}: (2, {})} | custom-call | flops 49999998976 | tf_op jit(solution)/shard_map/pallas_call | solution.py:595
  62.1 0.9 %shard_map.113 = (f32[27,128,128]{2,1,0:T(8,128)}, f32[27,128,128]{2,1,0:T(8,128)}) custom-call(bf16[896,128]{1,0:T(8,128)(2,1)S(1)} %collective-permute-done.24.refs_0_, f32[27,128,128]{2,1,0:T(8,128)} %get-tuple-element.82.refs_1_, f32[27,128,128]{2,1,0:T(8,128)} %get-tuple-element.83.refs_2_), custom_call_target="tpu_custom_call", output_to_operand_aliasing={{0}: (1, {}), {1}: (2, {})} | custom-call | flops 49999998976 | tf_op jit(solution)/shard_map/pallas_call | solution.py:595
  (48 shorter events, 6.9 us)
Async XLA Ops:
  2.3 0.7 %copy-start = (s32[1,1,16]{2,1,0:T(1,128)S(1)}, s32[1,1,16]{2,1,0:T(1,128)}, u32[]{:S(2)}) copy-start(s32[1,1,16]{2,1,0:T(1,128)} %lists.5) | copy-start | bytes 196
  3.0 9.9 %copy-start.2 = (bf16[27,128,128]{2,1,0:T(8,128)(2,1)S(1)}, bf16[27,128,128]{2,1,0:T(8,128)(2,1)}, u32[]{:S(2)}) copy-start(bf16[27,128,128]{2,1,0:T(8,128)(2,1)} %param.9) | copy-start | bytes 2654212
  3.4 6.6 %collective-permute-start = (bf16[48,256]{1,0:T(8,128)(2,1)S(1)}, bf16[48,256]{1,0:T(8,128)(2,1)S(1)}, u32[]{:S(2)}, u32[]{:S(2)}) collective-permute-start(bf16[48,256]{1,0:T(8,128)(2,1)S(1)} %get-tuple-element.46), channel_id=1, source_target_pairs={{0,4},{1,2},{2,1},{3,7},{4,0},{5,6},{6,5},{7,3},{8,12},{9,10},{10,... | collective-permute-start | bytes 73736 | tf_op jit(solution)/shard_map/ppermute | solution.py:466
  3.9 6.1 %collective-permute-start.1 = (bf16[48,256]{1,0:T(8,128)(2,1)S(1)}, bf16[48,256]{1,0:T(8,128)(2,1)S(1)}, u32[]{:S(2)}, u32[]{:S(2)}) collective-permute-start(bf16[48,256]{1,0:T(8,128)(2,1)S(1)} %get-tuple-element.47), channel_id=1, source_target_pairs={{0,1},{1,0},{2,3},{3,2},{4,5},{5,4},{6,7},{7,6},{8,9},{9,8},{10,11... | collective-permute-start | bytes 73736 | tf_op jit(solution)/shard_map/ppermute | solution.py:467
  10.2 4.4 %collective-permute-start.2 = (bf16[64,256]{1,0:T(8,128)(2,1)S(1)}, bf16[64,256]{1,0:T(8,128)(2,1)S(1)}, u32[]{:S(2)}, u32[]{:S(2)}) collective-permute-start(bf16[64,256]{1,0:T(8,128)(2,1)S(1)} %get-tuple-element.49), channel_id=1, source_target_pairs={{0,4},{4,0},{8,12},{12,8},{16,20},{20,16},{24,28},{28,24},{1,5},{5... | collective-permute-start | bytes 98312 | tf_op jit(solution)/shard_map/ppermute | solution.py:467
  10.3 4.3 %collective-permute-start.3 = (bf16[64,256]{1,0:T(8,128)(2,1)S(1)}, bf16[64,256]{1,0:T(8,128)(2,1)S(1)}, u32[]{:S(2)}, u32[]{:S(2)}) collective-permute-start(bf16[64,256]{1,0:T(8,128)(2,1)S(1)} %get-tuple-element.50), channel_id=1, source_target_pairs={{0,28},{4,8},{8,4},{12,16},{16,12},{20,24},{24,20},{28,0},{1,29},{... | collective-permute-start | bytes 98312 | tf_op jit(solution)/shard_map/ppermute | solution.py:459
  16.8 1.8 %collective-permute-start.4 = (bf16[1664,128]{1,0:T(8,128)(2,1)S(1)}, bf16[1664,128]{1,0:T(8,128)(2,1)S(1)}, u32[]{:S(2)}, u32[]{:S(2)}) collective-permute-start(bf16[1664,128]{1,0:T(8,128)(2,1)S(1)} %get-tuple-element.54), channel_id=1, source_target_pairs={{0,4},{4,0},{8,12},{12,8},{16,20},{20,16},{24,28},{28,24},{1,5},{5... | collective-permute-start | bytes 1277960 | tf_op jit(solution)/shard_map/ppermute | solution.py:487
  19.4 6.1 %collective-permute-start.10 = (bf16[896,128]{1,0:T(8,128)(2,1)S(1)}, bf16[896,128]{1,0:T(8,128)(2,1)S(1)}, u32[]{:S(2)}, u32[]{:S(2)}) collective-permute-start(bf16[896,128]{1,0:T(8,128)(2,1)S(1)} %get-tuple-element.69), channel_id=1, source_target_pairs={{0,8},{4,20},{8,0},{12,28},{16,24},{20,4},{24,16},{28,12},{1,9},{5... | collective-permute-start | bytes 688136 | tf_op jit(solution)/shard_map/ppermute | solution.py:490
  22.1 9.1 %collective-permute-start.9 = (bf16[896,128]{1,0:T(8,128)(2,1)S(1)}, bf16[896,128]{1,0:T(8,128)(2,1)S(1)}, u32[]{:S(2)}, u32[]{:S(2)}) collective-permute-start(bf16[896,128]{1,0:T(8,128)(2,1)S(1)} %get-tuple-element.67), channel_id=1, source_target_pairs={{0,8},{4,20},{8,0},{12,28},{16,24},{20,4},{24,16},{28,12},{1,9},{5... | collective-permute-start | bytes 688136 | tf_op jit(solution)/shard_map/ppermute | solution.py:490
  25.5 6.1 %collective-permute-start.11 = (bf16[896,128]{1,0:T(8,128)(2,1)S(1)}, bf16[896,128]{1,0:T(8,128)(2,1)S(1)}, u32[]{:S(2)}, u32[]{:S(2)}) collective-permute-start(bf16[896,128]{1,0:T(8,128)(2,1)S(1)} %shard_map.104), channel_id=1, source_target_pairs={{0,16},{4,12},{8,24},{12,4},{16,0},{20,28},{24,8},{28,20},{1,17},{... | collective-permute-start | bytes 688136 | tf_op jit(solution)/shard_map/ppermute | solution.py:490
  27.1 3.8 %collective-permute-start.5 = (bf16[48,256]{1,0:T(8,128)(2,1)S(1)}, bf16[48,256]{1,0:T(8,128)(2,1)S(1)}, u32[]{:S(2)}, u32[]{:S(2)}) collective-permute-start(bf16[48,256]{1,0:T(8,128)(2,1)S(1)} %get-tuple-element.57), channel_id=1, source_target_pairs={{0,1},{1,0},{2,3},{3,2},{4,5},{5,4},{6,7},{7,6},{8,9},{9,8},{10,11... | collective-permute-start | bytes 73736 | tf_op jit(solution)/shard_map/ppermute | solution.py:467
  29.0 2.0 %collective-permute-start.6 = (bf16[48,256]{1,0:T(8,128)(2,1)S(1)}, bf16[48,256]{1,0:T(8,128)(2,1)S(1)}, u32[]{:S(2)}, u32[]{:S(2)}) collective-permute-start(bf16[48,256]{1,0:T(8,128)(2,1)S(1)} %get-tuple-element.58), channel_id=1, source_target_pairs={{0,4},{1,2},{2,1},{3,7},{4,0},{5,6},{6,5},{7,3},{8,12},{9,10},{10,... | collective-permute-start | bytes 73736 | tf_op jit(solution)/shard_map/ppermute | solution.py:466
  31.8 6.2 %collective-permute-start.12 = (bf16[224,128]{1,0:T(8,128)(2,1)S(1)}, bf16[224,128]{1,0:T(8,128)(2,1)S(1)}, u32[]{:S(2)}, u32[]{:S(2)}) collective-permute-start(bf16[224,128]{1,0:T(8,128)(2,1)S(1)} %get-tuple-element.71), channel_id=1, source_target_pairs={{0,3},{1,2},{2,1},{3,0},{4,7},{5,6},{6,5},{7,4},{8,11},{9,10},{10,... | collective-permute-start | bytes 172040 | tf_op jit(solution)/shard_map/ppermute | solution.py:493
  34.2 5.7 %collective-permute-start.13 = (bf16[224,128]{1,0:T(8,128)(2,1)S(1)}, bf16[224,128]{1,0:T(8,128)(2,1)S(1)}, u32[]{:S(2)}, u32[]{:S(2)}) collective-permute-start(bf16[224,128]{1,0:T(8,128)(2,1)S(1)} %get-tuple-element.72), channel_id=1, source_target_pairs={{0,2},{1,3},{2,0},{3,1},{4,6},{5,7},{6,4},{7,5},{8,10},{9,11},{10,... | collective-permute-start | bytes 172040 | tf_op jit(solution)/shard_map/ppermute | solution.py:493
  35.2 4.8 %collective-permute-start.14 = (bf16[224,128]{1,0:T(8,128)(2,1)S(1)}, bf16[224,128]{1,0:T(8,128)(2,1)S(1)}, u32[]{:S(2)}, u32[]{:S(2)}) collective-permute-start(bf16[224,128]{1,0:T(8,128)(2,1)S(1)} %get-tuple-element.73), channel_id=1, source_target_pairs={{0,1},{1,0},{2,3},{3,2},{4,5},{5,4},{6,7},{7,6},{8,9},{9,8},{10,11... | collective-permute-start | bytes 172040 | tf_op jit(solution)/shard_map/ppermute | solution.py:493
  37.8 11.6 %copy-start.1 = (s32[1,1,16]{2,1,0:T(1,128)S(1)}, s32[1,1,16]{2,1,0:T(1,128)}, u32[]{:S(2)}) copy-start(s32[1,1,16]{2,1,0:T(1,128)} %lists.5) | copy-start | bytes 196
  40.0 7.8 %collective-permute-start.17 = (bf16[224,128]{1,0:T(8,128)(2,1)S(1)}, bf16[224,128]{1,0:T(8,128)(2,1)S(1)}, u32[]{:S(2)}, u32[]{:S(2)}) collective-permute-start(bf16[224,128]{1,0:T(8,128)(2,1)S(1)} %shard_map.106.refs_0_), channel_id=1, source_target_pairs={{0,3},{1,2},{2,1},{3,0},{4,7},{5,6},{6,5},{7,4},{8,11},{9,10},{10,... | collective-permute-start | bytes 172040 | tf_op jit(solution)/shard_map/ppermute | solution.py:493
  42.3 5.5 %collective-permute-start.16 = (bf16[224,128]{1,0:T(8,128)(2,1)S(1)}, bf16[224,128]{1,0:T(8,128)(2,1)S(1)}, u32[]{:S(2)}, u32[]{:S(2)}) collective-permute-start(bf16[224,128]{1,0:T(8,128)(2,1)S(1)} %shard_map.106.refs_0_), channel_id=1, source_target_pairs={{0,2},{1,3},{2,0},{3,1},{4,6},{5,7},{6,4},{7,5},{8,10},{9,11},{10,... | collective-permute-start | bytes 172040 | tf_op jit(solution)/shard_map/ppermute | solution.py:493
  42.3 5.5 %collective-permute-start.15 = (bf16[224,128]{1,0:T(8,128)(2,1)S(1)}, bf16[224,128]{1,0:T(8,128)(2,1)S(1)}, u32[]{:S(2)}, u32[]{:S(2)}) collective-permute-start(bf16[224,128]{1,0:T(8,128)(2,1)S(1)} %shard_map.106.refs_0_), channel_id=1, source_target_pairs={{0,1},{1,0},{2,3},{3,2},{4,5},{5,4},{6,7},{7,6},{8,9},{9,8},{10,11... | collective-permute-start | bytes 172040 | tf_op jit(solution)/shard_map/ppermute | solution.py:493
  44.4 5.0 %collective-permute-start.8 = (bf16[64,256]{1,0:T(8,128)(2,1)S(1)}, bf16[64,256]{1,0:T(8,128)(2,1)S(1)}, u32[]{:S(2)}, u32[]{:S(2)}) collective-permute-start(bf16[64,256]{1,0:T(8,128)(2,1)S(1)} %get-tuple-element.63), channel_id=1, source_target_pairs={{0,28},{4,8},{8,4},{12,16},{16,12},{20,24},{24,20},{28,0},{1,29},{... | collective-permute-start | bytes 98312 | tf_op jit(solution)/shard_map/ppermute | solution.py:459
  44.4 5.0 %collective-permute-start.7 = (bf16[64,256]{1,0:T(8,128)(2,1)S(1)}, bf16[64,256]{1,0:T(8,128)(2,1)S(1)}, u32[]{:S(2)}, u32[]{:S(2)}) collective-permute-start(bf16[64,256]{1,0:T(8,128)(2,1)S(1)} %get-tuple-element.62.after), channel_id=1, source_target_pairs={{0,4},{4,0},{8,12},{12,8},{16,20},{20,16},{24,28},{28,24},{1,5},{5... | collective-permute-start | bytes 98312 | tf_op jit(solution)/shard_map/ppermute | solution.py:467
  47.8 6.2 %collective-permute-start.19 = (bf16[896,128]{1,0:T(8,128)(2,1)S(1)}, bf16[896,128]{1,0:T(8,128)(2,1)S(1)}, u32[]{:S(2)}, u32[]{:S(2)}) collective-permute-start(bf16[896,128]{1,0:T(8,128)(2,1)S(1)} %shard_map.107.held.refs_0_), channel_id=1, source_target_pairs={{0,8},{4,20},{8,0},{12,28},{16,24},{20,4},{24,16},{28,12},{1,9},{5... | collective-permute-start | bytes 688136 | tf_op jit(solution)/shard_map/ppermute | solution.py:490
  51.5 6.0 %collective-permute-start.18 = (bf16[896,128]{1,0:T(8,128)(2,1)S(1)}, bf16[896,128]{1,0:T(8,128)(2,1)S(1)}, u32[]{:S(2)}, u32[]{:S(2)}) collective-permute-start(bf16[896,128]{1,0:T(8,128)(2,1)S(1)} %get-tuple-element.76), channel_id=1, source_target_pairs={{0,16},{4,12},{8,24},{12,4},{16,0},{20,28},{24,8},{28,20},{1,17},{... | collective-permute-start | bytes 688136 | tf_op jit(solution)/shard_map/ppermute | solution.py:490
  53.0 4.6 %collective-permute-start.22 = (bf16[896,128]{1,0:T(8,128)(2,1)S(1)}, bf16[896,128]{1,0:T(8,128)(2,1)S(1)}, u32[]{:S(2)}, u32[]{:S(2)}) collective-permute-start(bf16[896,128]{1,0:T(8,128)(2,1)S(1)} %shard_map.107.held.refs_0_), channel_id=1, source_target_pairs={{0,4},{4,0},{8,12},{12,8},{16,20},{20,16},{24,28},{28,24},{1,5},{5... | collective-permute-start | bytes 688136 | tf_op jit(solution)/shard_map/ppermute | solution.py:487
  54.0 6.5 %collective-permute-start.23 = (bf16[896,128]{1,0:T(8,128)(2,1)S(1)}, bf16[896,128]{1,0:T(8,128)(2,1)S(1)}, u32[]{:S(2)}, u32[]{:S(2)}) collective-permute-start(bf16[896,128]{1,0:T(8,128)(2,1)S(1)} %collective-permute-done.19.refs_2_), channel_id=1, source_target_pairs={{0,16},{4,12},{8,24},{12,4},{16,0},{20,28},{24,8},{28,20},{1,17},{... | collective-permute-start | bytes 688136 | tf_op jit(solution)/shard_map/ppermute | solution.py:490
  56.5 2.5 %collective-permute-start.20 = (bf16[896,128]{1,0:T(8,128)(2,1)S(1)}, bf16[896,128]{1,0:T(8,128)(2,1)S(1)}, u32[]{:S(2)}, u32[]{:S(2)}) collective-permute-start(bf16[896,128]{1,0:T(8,128)(2,1)S(1)} %collective-permute-done.19.refs_2_), channel_id=1, source_target_pairs={{0,4},{4,0},{8,12},{12,8},{16,20},{20,16},{24,28},{28,24},{1,5},{5... | collective-permute-start | bytes 688136 | tf_op jit(solution)/shard_map/ppermute | solution.py:487
  57.5 1.5 %collective-permute-start.21 = (bf16[896,128]{1,0:T(8,128)(2,1)S(1)}, bf16[896,128]{1,0:T(8,128)(2,1)S(1)}, u32[]{:S(2)}, u32[]{:S(2)}) collective-permute-start(bf16[896,128]{1,0:T(8,128)(2,1)S(1)} %collective-permute-done.18.refs_0_), channel_id=1, source_target_pairs={{0,4},{4,0},{8,12},{12,8},{16,20},{20,16},{24,28},{28,24},{1,5},{5... | collective-permute-start | bytes 688136 | tf_op jit(solution)/shard_map/ppermute | solution.py:487
  60.5 1.6 %collective-permute-start.24 = (bf16[896,128]{1,0:T(8,128)(2,1)S(1)}, bf16[896,128]{1,0:T(8,128)(2,1)S(1)}, u32[]{:S(2)}, u32[]{:S(2)}) collective-permute-start(bf16[896,128]{1,0:T(8,128)(2,1)S(1)} %shard_map.111), channel_id=1, source_target_pairs={{0,4},{4,0},{8,12},{12,8},{16,20},{20,16},{24,28},{28,24},{1,5},{5... | collective-permute-start | bytes 688136 | tf_op jit(solution)/shard_map/ppermute | solution.py:487

commit v8 on v7

--- a/solution.py
+++ b/solution.py
@@ -109,32 +109,42 @@
     return low, high
 
 
-def load_slots(counts, lists, pair, both):
+def entry_of(lists):
+    entries = lists[0]
+
+    def entry(i):
+        return jnp.sum(jnp.where(iota(entries.shape, 1) == i, entries, 0), axis=1, keepdims=True)
+
+    return entry
+
+
+def faces_kernel(lists, f, g, first, second, held, both, sems):
+    count = f.shape[0]
+    copies = [
+        pltpu.make_async_copy(lists, held, sems.at[0]),
+        pltpu.make_async_copy(f, both.at[pl.ds(0, count), pl.ds(0, 128)], sems.at[1]),
+        pltpu.make_async_copy(g, both.at[pl.ds(0, count), pl.ds(128, 128)], sems.at[2]),
+    ]
+    for copy in copies:
+        copy.start()
+    both[count:, :] = jnp.zeros((both.shape[0] - count, 256), jnp.bfloat16)
+    z, x = face_indices()
+    copies[0].wait()
+    slots = position_slots(entry_of(held), 0)
+    picks = [
+        one_hot(slot_rows(slots, z, x, jnp.full_like(x, y), x >= 0), both.shape[0]) for y in (0, NY - 1)
+    ]
+    for copy in copies[1:]:
+        copy.wait()
+    low, high = (dot(pick, both[...]).astype(jnp.bfloat16) for pick in picks)
+    write_by_parity("wire", low, high, first, second)
+
+
+def place_kernel(counts, lists, pair, out, live, both):
     count = pair.shape[0]
     both[0:count, :] = pair[...]
     both[count:, :] = jnp.zeros((both.shape[0] - count, 256), jnp.bfloat16)
-    entries = lists[0]
-
-    def entry(i):
-        return jnp.sum(jnp.where(iota(entries.shape, 1) == i, entries, 0), axis=1, keepdims=True)
-
-    return position_slots(entry, counts[...])
-
-
-def faces_kernel(counts, lists, pair, first, second, both):
-    slots = load_slots(counts, lists, pair, both)
-    z, x = face_indices()
-    low, high = (
-        dot(
-            one_hot(slot_rows(slots, z, x, jnp.full_like(x, y), x >= 0), both.shape[0]), both[...]
-        ).astype(jnp.bfloat16)
-        for y in (0, NY - 1)
-    )
-    write_by_parity("wire", low, high, first, second)
-
-
-def place_kernel(counts, lists, pair, out, live, both):
-    slots = load_slots(counts, lists, pair, both)
+    slots = position_slots(entry_of(lists), counts[...])
     z, x, j = grid_indices()
     rows = slot_rows(slots, z, x, j - 1, (j >= 1) & (j <= NY))
     live[...] = (rows >= 0).astype(jnp.bfloat16)
@@ -495,7 +505,13 @@
     pair = jnp.concatenate([f, g], axis=1)
     weights = jnp.concatenate([first_weight, second_weight], axis=0)
     pair_scratch = [pltpu.VMEM((padded, 256), jnp.bfloat16)]
-    faces = call(faces_kernel, (face, face), [VMEM] * 3, pair_scratch)(counts, send_lists, pair)
+    faces = call(
+        faces_kernel,
+        (face, face),
+        [HBM] * 3,
+        [pltpu.VMEM(send_lists.shape, jnp.int32)] + pair_scratch + [pltpu.SemaphoreType.DMA((3,))],
+        vmem=60,
+    )(send_lists, f, g)
     placed, live = call(place_kernel, (grid, bf16(ROWS, 128)), [VMEM] * 3, pair_scratch)(counts, send_lists, pair)
     faces = pairs(*faces, "wire")
     full, *slabs = call(insert_faces, (grid, slab, slab), [VMEM] * 3, [faces_scratch])(placed, *faces[::-1])

time: 63.3 us -> 62.9 us (level)
  Pallas kernels: 18.2 us -> 19.7 us
  starting transfers between devices: 29.4 us -> 28.2 us
  other arithmetic: 1.02 us -> 0.04 us
  waiting for transfers between devices: 10.8 us -> 11.6 us
    pallas_call x1, Pallas kernels: 0.4 us -> 1.97 us  [on_device(): call(faces_kernel, (face, face), [HBM] * 3, [pltpu.VMEM(send_lists.shape,...]
    concatenate x1, other arithmetic: 1.02 us -> 0.04 us  [on_device(): pair = jnp.concatenate([f, g], axis=1)]
    ppermute x6, starting transfers between devices: 9.22 us -> 8.38 us  [to_chip(): lax.ppermute(value, 'drift', [(i, i ^ 2 * chip_mask(kind, i % 2)) for i i...]
    unnamed x7 -> x9, local copies, waits for them, and re-layouts: 1.88 us -> 1.24 us
  transfers between devices with their start and end apart: 25 -> 25, of which waited for: 11 -> 10; matrix products, arithmetic and copies ran while one was open for 2% -> 2% of each run, Pallas kernels for 21% -> 22%
where the time goes in v8:
time: 62.9 us; the launch traced here: 62.7 us
  starting transfers between devices  28.2 us (45%)
  Pallas kernels  19.7 us (31%)
  waiting for transfers between devices  11.6 us (18%)
  between operations  1.75 us (3%)
  local copies, waits for them, and re-layouts  1.38 us (2%)
    ppermute x6, starting transfers between devices, to_wire(): return lax.ppermute(value, 'wire', [(i, i ^ step) for i in range(wire)])  8.91 us
    ppermute x6, starting transfers between devices, to_chip(): lax.ppermute(value, 'drift', [(i, i ^ 2 * chip_mask(kind, i % 2)) for i i...  8.38 us
    ppermute x4, starting transfers between devices, pairs(): got_first = lax.ppermute(value_first, axis, first)  7.21 us
    ppermute x6, waiting for transfers between devices, to_chip(): lax.ppermute(value, 'drift', [(i, i ^ 2 * chip_mask(kind, i % 2)) for i i...  6.18 us
    pallas_call x4, Pallas kernels, on_device(): call(functools.partial(final_kernel, items, blocks, want_done), (f32(TAPS...  4.22 us
    pallas_call x2, Pallas kernels, on_device(): call(functools.partial(second_inner_kernel, field), (f32(ROWS, 128), toke...  3.29 us
    ppermute x2, starting transfers between devices, pairs(): got_second = lax.ppermute(value_second, axis, sorted(second.items()))  2.56 us
    ppermute x4, waiting for transfers between devices, pairs(): got_first = lax.ppermute(value_first, axis, first)  2.46 us
  transfers between devices with their start and end apart: 25, of which 10 were waited for; matrix products, arithmetic and copies ran while one was open for 2% of the time, Pallas kernels for 22%

profile of v8, /device:TPU:0, one launch (start us, length us, event | category | flops | bytes accessed | tf_op | source)
XLA Modules:
  0.0 62.7 jit_solution(13927322898459699461)
XLA Ops:
  0.7 2.0 %shard_map.94 = (bf16[48,256]{1,0:T(8,128)(2,1)}, bf16[48,256]{1,0:T(8,128)(2,1)}) custom-call(s32[1,1,16]{2,1,0:T(1,128)} %lists.5, bf16[576,128]{1,0:T(8,128)(2,1)} %bitcast.6, bf16[576,128]{1,0:T(8,128)(2,1)} %bitcast.4), custom_call_target="tpu_custom_call" | custom-call | tf_op jit(solution)/shard_map/pallas_call | solution.py:508
  3.2 4.1 %collective-permute-start.1 = (bf16[48,256]{1,0:T(8,128)(2,1)}, bf16[48,256]{1,0:T(8,128)(2,1)S(1)}, u32[]{:S(2)}, u32[]{:S(2)}) collective-permute-start(bf16[48,256]{1,0:T(8,128)(2,1)} %get-tuple-element.47), channel_id=1, source_target_pairs={{0,1},{1,0},{2,3},{3,2},{4,5},{5,4},{6,7},{7,6},{8,9},{9,8},{10,11... | collective-permute-start | bytes 73736 | tf_op jit(solution)/shard_map/ppermute | solution.py:477
  7.3 1.2 %constant_dynamic-update-slice_fusion.1 = bf16[54,128,128]{2,1,0:T(8,128)(2,1)S(1)} fusion(bf16[27,128,128]{2,1,0:T(8,128)(2,1)} %param.8), kind=kLoop, calls=%fused_computation.2 | loop fusion | bytes 1769472
  10.3 2.6 %collective-permute-start.3 = (bf16[64,256]{1,0:T(8,128)(2,1)S(1)}, bf16[64,256]{1,0:T(8,128)(2,1)S(1)}, u32[]{:S(2)}, u32[]{:S(2)}) collective-permute-start(bf16[64,256]{1,0:T(8,128)(2,1)S(1)} %get-tuple-element.50), channel_id=1, source_target_pairs={{0,28},{4,8},{8,4},{12,16},{16,12},{20,24},{24,20},{28,0},{1,29},{... | collective-permute-start | bytes 98312 | tf_op jit(solution)/shard_map/ppermute | solution.py:469
  13.0 1.6 %shard_map.96.inner = f32[768,128]{1,0:T(8,128)S(1)} custom-call(bf16[768,256]{1,0:T(8,128)(2,1)S(1)} %get-tuple-element.48.full.base, bf16[54,128,128]{2,1,0:T(8,128)(2,1)S(1)} %constant_dynamic-update-slice_fusion.weights), custom_call_target="tpu_custom_call" | custom-call | tf_op jit(solution)/shard_map/pallas_call | solution.py:520
  14.7 2.1 %shard_map.97 = (bf16[768,256]{1,0:T(8,128)(2,1)S(1)}, bf16[1664,128]{1,0:T(8,128)(2,1)S(1)}, bf16[1664,128]{1,0:T(8,128)(2,1)S(1)}) custom-call(bf16[768,256]{1,0:T(8,128)(2,1)S(1)} %get-tuple-element.48.full.base, bf16[64,256]{1,0:T(8,128)(2,1)S(1)} %collective-permute-done.2.got_first, bf16[64,256]{1,0:T(8,128)(2,1)S(1)} %collective-permute-done.3.got_second, ...), custom_call_target="tpu_custom_call" | custom-call | tf_op jit(solution)/shard_map/pallas_call | solution.py:521
  16.9 1.1 %shard_map.98.mine = f32[3584,128]{1,0:T(8,128)S(1)} custom-call(bf16[1664,128]{1,0:T(8,128)(2,1)S(1)} %get-tuple-element.53.mine), custom_call_target="tpu_custom_call" | custom-call | tf_op jit(solution)/shard_map/pallas_call | solution.py:530
  19.4 1.6 %collective-permute-start.10 = (bf16[896,128]{1,0:T(8,128)(2,1)S(1)}, bf16[896,128]{1,0:T(8,128)(2,1)S(1)}, u32[]{:S(2)}, u32[]{:S(2)}) collective-permute-start(bf16[896,128]{1,0:T(8,128)(2,1)S(1)} %get-tuple-element.69), channel_id=1, source_target_pairs={{0,8},{4,20},{8,0},{12,28},{16,24},{20,4},{24,16},{28,12},{1,9},{5... | collective-permute-start | bytes 688136 | tf_op jit(solution)/shard_map/ppermute | solution.py:500
  21.0 1.1 %shard_map.100 = (bf16[896,128]{1,0:T(8,128)(2,1)S(1)}, f32[896,128]{1,0:T(8,128)S(1)}, f32[896,128]{1,0:T(8,128)S(1)}, bf16[48,256]{1,0:T(8,128)(2,1)S(1)}, bf16[48,256]{1,0:T(8,128)(2,1)S(1)}) custom-call(f32[3584,128]{1,0:T(8,128)S(1)} %shard_map.98.mine, bf16[128,768]{1,0:T(8,128)(2,1)S(1)} %get-tuple-element.55.left, ...), custom_call_target="tpu_custom_call" | custom-call | tf_op jit(solution)/shard_map/pallas_call | solution.py:539
  22.7 2.9 %collective-permute-done.10.received = bf16[896,128]{1,0:T(8,128)(2,1)S(1)} collective-permute-done((bf16[896,128]{1,0:T(8,128)(2,1)S(1)}, bf16[896,128]{1,0:T(8,128)(2,1)S(1)}, u32[]{:S(2)}, u32[]{:S(2)}) %collective-permute-start.10) | collective-permute-done | bytes 229408 | tf_op jit(solution)/shard_map/ppermute | solution.py:500
  25.6 1.5 %collective-permute-start.11 = (bf16[896,128]{1,0:T(8,128)(2,1)S(1)}, bf16[896,128]{1,0:T(8,128)(2,1)S(1)}, u32[]{:S(2)}, u32[]{:S(2)}) collective-permute-start(bf16[896,128]{1,0:T(8,128)(2,1)S(1)} %shard_map.104), channel_id=1, source_target_pairs={{0,16},{4,12},{8,24},{12,4},{16,0},{20,28},{24,8},{28,20},{1,17},{... | collective-permute-start | bytes 688136 | tf_op jit(solution)/shard_map/ppermute | solution.py:500
  27.1 1.4 %collective-permute-start.5 = (bf16[48,256]{1,0:T(8,128)(2,1)S(1)}, bf16[48,256]{1,0:T(8,128)(2,1)S(1)}, u32[]{:S(2)}, u32[]{:S(2)}) collective-permute-start(bf16[48,256]{1,0:T(8,128)(2,1)S(1)} %get-tuple-element.57), channel_id=1, source_target_pairs={{0,1},{1,0},{2,3},{3,2},{4,5},{5,4},{6,7},{7,6},{8,9},{9,8},{10,11... | collective-permute-start | bytes 73736 | tf_op jit(solution)/shard_map/ppermute | solution.py:477
  28.5 2.5 %collective-permute-done.5.got_first = bf16[48,256]{1,0:T(8,128)(2,1)S(1)} collective-permute-done((bf16[48,256]{1,0:T(8,128)(2,1)S(1)}, bf16[48,256]{1,0:T(8,128)(2,1)S(1)}, u32[]{:S(2)}, u32[]{:S(2)}) %collective-permute-start.5) | collective-permute-done | bytes 24608 | tf_op jit(solution)/shard_map/ppermute | solution.py:477
  31.8 2.0 %collective-permute-start.12 = (bf16[224,128]{1,0:T(8,128)(2,1)S(1)}, bf16[224,128]{1,0:T(8,128)(2,1)S(1)}, u32[]{:S(2)}, u32[]{:S(2)}) collective-permute-start(bf16[224,128]{1,0:T(8,128)(2,1)S(1)} %get-tuple-element.71), channel_id=1, source_target_pairs={{0,3},{1,2},{2,1},{3,0},{4,7},{5,6},{6,5},{7,4},{8,11},{9,10},{10,... | collective-permute-start | bytes 172040 | tf_op jit(solution)/shard_map/ppermute | solution.py:503
  33.7 1.2 %collective-permute-start.13 = (bf16[224,128]{1,0:T(8,128)(2,1)S(1)}, bf16[224,128]{1,0:T(8,128)(2,1)S(1)}, u32[]{:S(2)}, u32[]{:S(2)}) collective-permute-start(bf16[224,128]{1,0:T(8,128)(2,1)S(1)} %get-tuple-element.72), channel_id=1, source_target_pairs={{0,2},{1,3},{2,0},{3,1},{4,6},{5,7},{6,4},{7,5},{8,10},{9,11},{10,... | collective-permute-start | bytes 172040 | tf_op jit(solution)/shard_map/ppermute | solution.py:503
  34.9 1.3 %collective-permute-start.14 = (bf16[224,128]{1,0:T(8,128)(2,1)S(1)}, bf16[224,128]{1,0:T(8,128)(2,1)S(1)}, u32[]{:S(2)}, u32[]{:S(2)}) collective-permute-start(bf16[224,128]{1,0:T(8,128)(2,1)S(1)} %get-tuple-element.73), channel_id=1, source_target_pairs={{0,1},{1,0},{2,3},{3,2},{4,5},{5,4},{6,7},{7,6},{8,9},{9,8},{10,11... | collective-permute-start | bytes 172040 | tf_op jit(solution)/shard_map/ppermute | solution.py:503
  36.2 1.6 %shard_map.102 = (f32[768,128]{1,0:T(8,128)S(1)}, f32[8,128]{1,0:T(8,128)S(1)}) custom-call(bf16[768,256]{1,0:T(8,128)(2,1)S(1)} %get-tuple-element.59.hb, bf16[54,128,128]{2,1,0:T(8,128)(2,1)S(1)} %constant_dynamic-update-slice_fusion.weights), custom_call_target="tpu_custom_call" | custom-call | tf_op jit(solution)/shard_map/pallas_call | solution.py:560
  38.4 1.2 %collective-permute-done.13.refs_1_ = bf16[224,128]{1,0:T(8,128)(2,1)S(1)} collective-permute-done((bf16[224,128]{1,0:T(8,128)(2,1)S(1)}, bf16[224,128]{1,0:T(8,128)(2,1)S(1)}, u32[]{:S(2)}, u32[]{:S(2)}) %collective-permute-start.13) | collective-permute-done | bytes 57376 | tf_op jit(solution)/shard_map/ppermute | solution.py:503
  39.7 2.0 %collective-permute-start.17 = (bf16[224,128]{1,0:T(8,128)(2,1)S(1)}, bf16[224,128]{1,0:T(8,128)(2,1)S(1)}, u32[]{:S(2)}, u32[]{:S(2)}) collective-permute-start(bf16[224,128]{1,0:T(8,128)(2,1)S(1)} %shard_map.106.refs_0_), channel_id=1, source_target_pairs={{0,3},{1,2},{2,1},{3,0},{4,7},{5,6},{6,5},{7,4},{8,11},{9,10},{10,... | collective-permute-start | bytes 172040 | tf_op jit(solution)/shard_map/ppermute | solution.py:503
  42.0 2.1 %collective-permute-start.15 = (bf16[224,128]{1,0:T(8,128)(2,1)S(1)}, bf16[224,128]{1,0:T(8,128)(2,1)S(1)}, u32[]{:S(2)}, u32[]{:S(2)}) collective-permute-start(bf16[224,128]{1,0:T(8,128)(2,1)S(1)} %shard_map.106.refs_0_), channel_id=1, source_target_pairs={{0,1},{1,0},{2,3},{3,2},{4,5},{5,4},{6,7},{7,6},{8,9},{9,8},{10,11... | collective-permute-start | bytes 172040 | tf_op jit(solution)/shard_map/ppermute | solution.py:503
  44.1 1.6 %collective-permute-start.7 = (bf16[64,256]{1,0:T(8,128)(2,1)S(1)}, bf16[64,256]{1,0:T(8,128)(2,1)S(1)}, u32[]{:S(2)}, u32[]{:S(2)}) collective-permute-start(bf16[64,256]{1,0:T(8,128)(2,1)S(1)} %get-tuple-element.62.after), channel_id=1, source_target_pairs={{0,4},{4,0},{8,12},{12,8},{16,20},{20,16},{24,28},{28,24},{1,5},{5... | collective-permute-start | bytes 98312 | tf_op jit(solution)/shard_map/ppermute | solution.py:477
  45.8 1.7 %shard_map.103 = (f32[768,128]{1,0:T(8,128)S(1)}, f32[8,128]{1,0:T(8,128)S(1)}) custom-call(bf16[768,256]{1,0:T(8,128)(2,1)S(1)} %get-tuple-element.59.hb, bf16[54,128,128]{2,1,0:T(8,128)(2,1)S(1)} %constant_dynamic-update-slice_fusion.weights), custom_call_target="tpu_custom_call" | custom-call | tf_op jit(solution)/shard_map/pallas_call | solution.py:560
  47.5 1.5 %collective-permute-start.19 = (bf16[896,128]{1,0:T(8,128)(2,1)S(1)}, bf16[896,128]{1,0:T(8,128)(2,1)S(1)}, u32[]{:S(2)}, u32[]{:S(2)}) collective-permute-start(bf16[896,128]{1,0:T(8,128)(2,1)S(1)} %shard_map.107.held.refs_0_), channel_id=1, source_target_pairs={{0,8},{4,20},{8,0},{12,28},{16,24},{20,4},{24,16},{28,12},{1,9},{5... | collective-permute-start | bytes 688136 | tf_op jit(solution)/shard_map/ppermute | solution.py:500
  49.1 2.1 %shard_map.108 = (bf16[576,128]{1,0:T(8,128)(2,1)}, bf16[576,128]{1,0:T(8,128)(2,1)}, bf16[896,128]{1,0:T(8,128)(2,1)S(1)}) custom-call(s32[1,1,16]{2,1,0:T(1,128)S(1)} %copy-done, s32[1,1]{1,0:T(1,128)S(6)} %copy.23.counts, f32[768,128]{1,0:T(8,128)S(1)} %get-tuple-element.60.inner_hidden, f32[768,128]{1,0:T(8,128)S(1)} %get-tuple-element.61.inner_back, ...), custom_call_target="tpu_custom_call" | custom-call | tf_op jit(solution)/shard_map/pallas_call | solution.py:582
  51.2 1.0 %collective-permute-start.18 = (bf16[896,128]{1,0:T(8,128)(2,1)S(1)}, bf16[896,128]{1,0:T(8,128)(2,1)S(1)}, u32[]{:S(2)}, u32[]{:S(2)}) collective-permute-start(bf16[896,128]{1,0:T(8,128)(2,1)S(1)} %get-tuple-element.76), channel_id=1, source_target_pairs={{0,16},{4,12},{8,24},{12,4},{16,0},{20,28},{24,8},{28,20},{1,17},{... | collective-permute-start | bytes 688136 | tf_op jit(solution)/shard_map/ppermute | solution.py:500
  52.2 1.5 %collective-permute-done.19.refs_2_ = bf16[896,128]{1,0:T(8,128)(2,1)S(1)} collective-permute-done((bf16[896,128]{1,0:T(8,128)(2,1)S(1)}, bf16[896,128]{1,0:T(8,128)(2,1)S(1)}, u32[]{:S(2)}, u32[]{:S(2)}) %collective-permute-start.19) | collective-permute-done | bytes 229408 | tf_op jit(solution)/shard_map/ppermute | solution.py:500
  53.7 2.1 %collective-permute-start.23 = (bf16[896,128]{1,0:T(8,128)(2,1)S(1)}, bf16[896,128]{1,0:T(8,128)(2,1)S(1)}, u32[]{:S(2)}, u32[]{:S(2)}) collective-permute-start(bf16[896,128]{1,0:T(8,128)(2,1)S(1)} %collective-permute-done.19.refs_2_), channel_id=1, source_target_pairs={{0,16},{4,12},{8,24},{12,4},{16,0},{20,28},{24,8},{28,20},{1,17},{... | collective-permute-start | bytes 688136 | tf_op jit(solution)/shard_map/ppermute | solution.py:500
  55.9 1.3 %collective-permute-done.18.refs_0_ = bf16[896,128]{1,0:T(8,128)(2,1)S(1)} collective-permute-done((bf16[896,128]{1,0:T(8,128)(2,1)S(1)}, bf16[896,128]{1,0:T(8,128)(2,1)S(1)}, u32[]{:S(2)}, u32[]{:S(2)}) %collective-permute-start.18) | collective-permute-done | bytes 229408 | tf_op jit(solution)/shard_map/ppermute | solution.py:500
  57.2 1.3 %shard_map.109 = (f32[27,128,128]{2,1,0:T(8,128)}, f32[27,128,128]{2,1,0:T(8,128)}) custom-call(bf16[896,128]{1,0:T(8,128)(2,1)S(1)} %shard_map.107.held.refs_0_, bf16[896,128]{1,0:T(8,128)(2,1)S(1)} %collective-permute-done.22.refs_1_, bf16[896,128]{1,0:T(8,128)(2,1)S(1)} %collective-permute-done.19.refs_2_), custom_call_target="tpu_custom_call" | custom-call | flops 49999998976 | tf_op jit(solution)/shard_map/pallas_call | solution.py:611
  58.7 1.3 %shard_map.110 = (f32[27,128,128]{2,1,0:T(8,128)}, f32[27,128,128]{2,1,0:T(8,128)}, f32[8,128]{1,0:T(8,128)S(1)}) custom-call(bf16[896,128]{1,0:T(8,128)(2,1)S(1)} %collective-permute-done.18.refs_0_, bf16[896,128]{1,0:T(8,128)(2,1)S(1)} %collective-permute-done.20.refs_1_, ...), custom_call_target="tpu_custom_call", output_to_operand_aliasing={{0}: (3, {}), {1}: (4, {})} | custom-call | flops 49999998976 | tf_op jit(solution)/shard_map/pallas_call | solution.py:611
  60.5 0.8 %shard_map.112 = (f32[27,128,128]{2,1,0:T(8,128)}, f32[27,128,128]{2,1,0:T(8,128)}) custom-call(bf16[896,128]{1,0:T(8,128)(2,1)S(1)} %collective-permute-done.23.value.refs_0_, f32[27,128,128]{2,1,0:T(8,128)} %get-tuple-element.80.refs_1_, f32[27,128,128]{2,1,0:T(8,128)} %get-tuple-element.81.refs_2_), custom_call_target="tpu_custom_call", output_to_operand_aliasing={{0}: (1, {}), {1}: (2, {})} | custom-call | flops 49999998976 | tf_op jit(solution)/shard_map/pallas_call | solution.py:611
  61.7 0.9 %shard_map.113 = (f32[27,128,128]{2,1,0:T(8,128)}, f32[27,128,128]{2,1,0:T(8,128)}) custom-call(bf16[896,128]{1,0:T(8,128)(2,1)S(1)} %collective-permute-done.24.refs_0_, f32[27,128,128]{2,1,0:T(8,128)} %get-tuple-element.82.refs_1_, f32[27,128,128]{2,1,0:T(8,128)} %get-tuple-element.83.refs_2_), custom_call_target="tpu_custom_call", output_to_operand_aliasing={{0}: (1, {}), {1}: (2, {})} | custom-call | flops 49999998976 | tf_op jit(solution)/shard_map/pallas_call | solution.py:611
  (50 shorter events, 6.7 us)
Async XLA Ops:
  0.6 8.6 %copy-start = (s32[1,1,16]{2,1,0:T(1,128)S(1)}, s32[1,1,16]{2,1,0:T(1,128)}, u32[]{:S(2)}) copy-start(s32[1,1,16]{2,1,0:T(1,128)} %lists.5) | copy-start | bytes 196
  0.6 7.9 %copy-start.2 = (bf16[1,1,576,128]{3,2,1,0:T(8,128)(2,1)S(1)}, bf16[1,1,576,128]{3,2,1,0:T(8,128)(2,1)}, u32[]{:S(2)}) copy-start(bf16[1,1,576,128]{3,2,1,0:T(8,128)(2,1)} %param.10) | copy-start | bytes 442372
  0.7 7.9 %copy-start.3 = (bf16[1,1,576,128]{3,2,1,0:T(8,128)(2,1)S(1)}, bf16[1,1,576,128]{3,2,1,0:T(8,128)(2,1)}, u32[]{:S(2)}) copy-start(bf16[1,1,576,128]{3,2,1,0:T(8,128)(2,1)} %param.7) | copy-start | bytes 442372
  0.7 12.2 %copy-start.1 = (bf16[27,128,128]{2,1,0:T(8,128)(2,1)S(1)}, bf16[27,128,128]{2,1,0:T(8,128)(2,1)}, u32[]{:S(2)}) copy-start(bf16[27,128,128]{2,1,0:T(8,128)(2,1)} %param.9) | copy-start | bytes 2654212
  2.6 7.3 %collective-permute-start = (bf16[48,256]{1,0:T(8,128)(2,1)}, bf16[48,256]{1,0:T(8,128)(2,1)S(1)}, u32[]{:S(2)}, u32[]{:S(2)}) collective-permute-start(bf16[48,256]{1,0:T(8,128)(2,1)} %get-tuple-element.46), channel_id=1, source_target_pairs={{0,4},{1,2},{2,1},{3,7},{4,0},{5,6},{6,5},{7,3},{8,12},{9,10},{10,... | collective-permute-start | bytes 73736 | tf_op jit(solution)/shard_map/ppermute | solution.py:476
  3.2 6.8 %collective-permute-start.1 = (bf16[48,256]{1,0:T(8,128)(2,1)}, bf16[48,256]{1,0:T(8,128)(2,1)S(1)}, u32[]{:S(2)}, u32[]{:S(2)}) collective-permute-start(bf16[48,256]{1,0:T(8,128)(2,1)} %get-tuple-element.47), channel_id=1, source_target_pairs={{0,1},{1,0},{2,3},{3,2},{4,5},{5,4},{6,7},{7,6},{8,9},{9,8},{10,11... | collective-permute-start | bytes 73736 | tf_op jit(solution)/shard_map/ppermute | solution.py:477
  10.2 4.4 %collective-permute-start.2 = (bf16[64,256]{1,0:T(8,128)(2,1)S(1)}, bf16[64,256]{1,0:T(8,128)(2,1)S(1)}, u32[]{:S(2)}, u32[]{:S(2)}) collective-permute-start(bf16[64,256]{1,0:T(8,128)(2,1)S(1)} %get-tuple-element.49), channel_id=1, source_target_pairs={{0,4},{4,0},{8,12},{12,8},{16,20},{20,16},{24,28},{28,24},{1,5},{5... | collective-permute-start | bytes 98312 | tf_op jit(solution)/shard_map/ppermute | solution.py:477
  10.3 4.3 %collective-permute-start.3 = (bf16[64,256]{1,0:T(8,128)(2,1)S(1)}, bf16[64,256]{1,0:T(8,128)(2,1)S(1)}, u32[]{:S(2)}, u32[]{:S(2)}) collective-permute-start(bf16[64,256]{1,0:T(8,128)(2,1)S(1)} %get-tuple-element.50), channel_id=1, source_target_pairs={{0,28},{4,8},{8,4},{12,16},{16,12},{20,24},{24,20},{28,0},{1,29},{... | collective-permute-start | bytes 98312 | tf_op jit(solution)/shard_map/ppermute | solution.py:469
  16.8 1.8 %collective-permute-start.4 = (bf16[1664,128]{1,0:T(8,128)(2,1)S(1)}, bf16[1664,128]{1,0:T(8,128)(2,1)S(1)}, u32[]{:S(2)}, u32[]{:S(2)}) collective-permute-start(bf16[1664,128]{1,0:T(8,128)(2,1)S(1)} %get-tuple-element.54), channel_id=1, source_target_pairs={{0,4},{4,0},{8,12},{12,8},{16,20},{20,16},{24,28},{28,24},{1,5},{5... | collective-permute-start | bytes 1277960 | tf_op jit(solution)/shard_map/ppermute | solution.py:497
  19.4 6.1 %collective-permute-start.10 = (bf16[896,128]{1,0:T(8,128)(2,1)S(1)}, bf16[896,128]{1,0:T(8,128)(2,1)S(1)}, u32[]{:S(2)}, u32[]{:S(2)}) collective-permute-start(bf16[896,128]{1,0:T(8,128)(2,1)S(1)} %get-tuple-element.69), channel_id=1, source_target_pairs={{0,8},{4,20},{8,0},{12,28},{16,24},{20,4},{24,16},{28,12},{1,9},{5... | collective-permute-start | bytes 688136 | tf_op jit(solution)/shard_map/ppermute | solution.py:500
  22.1 9.1 %collective-permute-start.9 = (bf16[896,128]{1,0:T(8,128)(2,1)S(1)}, bf16[896,128]{1,0:T(8,128)(2,1)S(1)}, u32[]{:S(2)}, u32[]{:S(2)}) collective-permute-start(bf16[896,128]{1,0:T(8,128)(2,1)S(1)} %get-tuple-element.67), channel_id=1, source_target_pairs={{0,8},{4,20},{8,0},{12,28},{16,24},{20,4},{24,16},{28,12},{1,9},{5... | collective-permute-start | bytes 688136 | tf_op jit(solution)/shard_map/ppermute | solution.py:500
  25.6 6.1 %collective-permute-start.11 = (bf16[896,128]{1,0:T(8,128)(2,1)S(1)}, bf16[896,128]{1,0:T(8,128)(2,1)S(1)}, u32[]{:S(2)}, u32[]{:S(2)}) collective-permute-start(bf16[896,128]{1,0:T(8,128)(2,1)S(1)} %shard_map.104), channel_id=1, source_target_pairs={{0,16},{4,12},{8,24},{12,4},{16,0},{20,28},{24,8},{28,20},{1,17},{... | collective-permute-start | bytes 688136 | tf_op jit(solution)/shard_map/ppermute | solution.py:500
  27.1 3.8 %collective-permute-start.5 = (bf16[48,256]{1,0:T(8,128)(2,1)S(1)}, bf16[48,256]{1,0:T(8,128)(2,1)S(1)}, u32[]{:S(2)}, u32[]{:S(2)}) collective-permute-start(bf16[48,256]{1,0:T(8,128)(2,1)S(1)} %get-tuple-element.57), channel_id=1, source_target_pairs={{0,1},{1,0},{2,3},{3,2},{4,5},{5,4},{6,7},{7,6},{8,9},{9,8},{10,11... | collective-permute-start | bytes 73736 | tf_op jit(solution)/shard_map/ppermute | solution.py:477
  28.5 2.5 %collective-permute-start.6 = (bf16[48,256]{1,0:T(8,128)(2,1)S(1)}, bf16[48,256]{1,0:T(8,128)(2,1)S(1)}, u32[]{:S(2)}, u32[]{:S(2)}) collective-permute-start(bf16[48,256]{1,0:T(8,128)(2,1)S(1)} %get-tuple-element.58), channel_id=1, source_target_pairs={{0,4},{1,2},{2,1},{3,7},{4,0},{5,6},{6,5},{7,3},{8,12},{9,10},{10,... | collective-permute-start | bytes 73736 | tf_op jit(solution)/shard_map/ppermute | solution.py:476
  31.8 6.7 %collective-permute-start.12 = (bf16[224,128]{1,0:T(8,128)(2,1)S(1)}, bf16[224,128]{1,0:T(8,128)(2,1)S(1)}, u32[]{:S(2)}, u32[]{:S(2)}) collective-permute-start(bf16[224,128]{1,0:T(8,128)(2,1)S(1)} %get-tuple-element.71), channel_id=1, source_target_pairs={{0,3},{1,2},{2,1},{3,0},{4,7},{5,6},{6,5},{7,4},{8,11},{9,10},{10,... | collective-permute-start | bytes 172040 | tf_op jit(solution)/shard_map/ppermute | solution.py:503
  33.7 5.9 %collective-permute-start.13 = (bf16[224,128]{1,0:T(8,128)(2,1)S(1)}, bf16[224,128]{1,0:T(8,128)(2,1)S(1)}, u32[]{:S(2)}, u32[]{:S(2)}) collective-permute-start(bf16[224,128]{1,0:T(8,128)(2,1)S(1)} %get-tuple-element.72), channel_id=1, source_target_pairs={{0,2},{1,3},{2,0},{3,1},{4,6},{5,7},{6,4},{7,5},{8,10},{9,11},{10,... | collective-permute-start | bytes 172040 | tf_op jit(solution)/shard_map/ppermute | solution.py:503
  34.9 4.7 %collective-permute-start.14 = (bf16[224,128]{1,0:T(8,128)(2,1)S(1)}, bf16[224,128]{1,0:T(8,128)(2,1)S(1)}, u32[]{:S(2)}, u32[]{:S(2)}) collective-permute-start(bf16[224,128]{1,0:T(8,128)(2,1)S(1)} %get-tuple-element.73), channel_id=1, source_target_pairs={{0,1},{1,0},{2,3},{3,2},{4,5},{5,4},{6,7},{7,6},{8,9},{9,8},{10,11... | collective-permute-start | bytes 172040 | tf_op jit(solution)/shard_map/ppermute | solution.py:503
  39.7 7.8 %collective-permute-start.17 = (bf16[224,128]{1,0:T(8,128)(2,1)S(1)}, bf16[224,128]{1,0:T(8,128)(2,1)S(1)}, u32[]{:S(2)}, u32[]{:S(2)}) collective-permute-start(bf16[224,128]{1,0:T(8,128)(2,1)S(1)} %shard_map.106.refs_0_), channel_id=1, source_target_pairs={{0,3},{1,2},{2,1},{3,0},{4,7},{5,6},{6,5},{7,4},{8,11},{9,10},{10,... | collective-permute-start | bytes 172040 | tf_op jit(solution)/shard_map/ppermute | solution.py:503
  41.7 5.7 %collective-permute-start.16 = (bf16[224,128]{1,0:T(8,128)(2,1)S(1)}, bf16[224,128]{1,0:T(8,128)(2,1)S(1)}, u32[]{:S(2)}, u32[]{:S(2)}) collective-permute-start(bf16[224,128]{1,0:T(8,128)(2,1)S(1)} %shard_map.106.refs_0_), channel_id=1, source_target_pairs={{0,2},{1,3},{2,0},{3,1},{4,6},{5,7},{6,4},{7,5},{8,10},{9,11},{10,... | collective-permute-start | bytes 172040 | tf_op jit(solution)/shard_map/ppermute | solution.py:503
  42.0 5.5 %collective-permute-start.15 = (bf16[224,128]{1,0:T(8,128)(2,1)S(1)}, bf16[224,128]{1,0:T(8,128)(2,1)S(1)}, u32[]{:S(2)}, u32[]{:S(2)}) collective-permute-start(bf16[224,128]{1,0:T(8,128)(2,1)S(1)} %shard_map.106.refs_0_), channel_id=1, source_target_pairs={{0,1},{1,0},{2,3},{3,2},{4,5},{5,4},{6,7},{7,6},{8,9},{9,8},{10,11... | collective-permute-start | bytes 172040 | tf_op jit(solution)/shard_map/ppermute | solution.py:503
  44.1 4.9 %collective-permute-start.8 = (bf16[64,256]{1,0:T(8,128)(2,1)S(1)}, bf16[64,256]{1,0:T(8,128)(2,1)S(1)}, u32[]{:S(2)}, u32[]{:S(2)}) collective-permute-start(bf16[64,256]{1,0:T(8,128)(2,1)S(1)} %get-tuple-element.63), channel_id=1, source_target_pairs={{0,28},{4,8},{8,4},{12,16},{16,12},{20,24},{24,20},{28,0},{1,29},{... | collective-permute-start | bytes 98312 | tf_op jit(solution)/shard_map/ppermute | solution.py:469
  44.1 4.9 %collective-permute-start.7 = (bf16[64,256]{1,0:T(8,128)(2,1)S(1)}, bf16[64,256]{1,0:T(8,128)(2,1)S(1)}, u32[]{:S(2)}, u32[]{:S(2)}) collective-permute-start(bf16[64,256]{1,0:T(8,128)(2,1)S(1)} %get-tuple-element.62.after), channel_id=1, source_target_pairs={{0,4},{4,0},{8,12},{12,8},{16,20},{20,16},{24,28},{28,24},{1,5},{5... | collective-permute-start | bytes 98312 | tf_op jit(solution)/shard_map/ppermute | solution.py:477
  47.5 6.2 %collective-permute-start.19 = (bf16[896,128]{1,0:T(8,128)(2,1)S(1)}, bf16[896,128]{1,0:T(8,128)(2,1)S(1)}, u32[]{:S(2)}, u32[]{:S(2)}) collective-permute-start(bf16[896,128]{1,0:T(8,128)(2,1)S(1)} %shard_map.107.held.refs_0_), channel_id=1, source_target_pairs={{0,8},{4,20},{8,0},{12,28},{16,24},{20,4},{24,16},{28,12},{1,9},{5... | collective-permute-start | bytes 688136 | tf_op jit(solution)/shard_map/ppermute | solution.py:500
  51.2 6.0 %collective-permute-start.18 = (bf16[896,128]{1,0:T(8,128)(2,1)S(1)}, bf16[896,128]{1,0:T(8,128)(2,1)S(1)}, u32[]{:S(2)}, u32[]{:S(2)}) collective-permute-start(bf16[896,128]{1,0:T(8,128)(2,1)S(1)} %get-tuple-element.76), channel_id=1, source_target_pairs={{0,16},{4,12},{8,24},{12,4},{16,0},{20,28},{24,8},{28,20},{1,17},{... | collective-permute-start | bytes 688136 | tf_op jit(solution)/shard_map/ppermute | solution.py:500
  52.2 5.0 %collective-permute-start.22 = (bf16[896,128]{1,0:T(8,128)(2,1)S(1)}, bf16[896,128]{1,0:T(8,128)(2,1)S(1)}, u32[]{:S(2)}, u32[]{:S(2)}) collective-permute-start(bf16[896,128]{1,0:T(8,128)(2,1)S(1)} %shard_map.107.held.refs_0_), channel_id=1, source_target_pairs={{0,4},{4,0},{8,12},{12,8},{16,20},{20,16},{24,28},{28,24},{1,5},{5... | collective-permute-start | bytes 688136 | tf_op jit(solution)/shard_map/ppermute | solution.py:497
  53.7 6.2 %collective-permute-start.23 = (bf16[896,128]{1,0:T(8,128)(2,1)S(1)}, bf16[896,128]{1,0:T(8,128)(2,1)S(1)}, u32[]{:S(2)}, u32[]{:S(2)}) collective-permute-start(bf16[896,128]{1,0:T(8,128)(2,1)S(1)} %collective-permute-done.19.refs_2_), channel_id=1, source_target_pairs={{0,16},{4,12},{8,24},{12,4},{16,0},{20,28},{24,8},{28,20},{1,17},{... | collective-permute-start | bytes 688136 | tf_op jit(solution)/shard_map/ppermute | solution.py:500
  55.9 2.8 %collective-permute-start.20 = (bf16[896,128]{1,0:T(8,128)(2,1)S(1)}, bf16[896,128]{1,0:T(8,128)(2,1)S(1)}, u32[]{:S(2)}, u32[]{:S(2)}) collective-permute-start(bf16[896,128]{1,0:T(8,128)(2,1)S(1)} %collective-permute-done.19.refs_2_), channel_id=1, source_target_pairs={{0,4},{4,0},{8,12},{12,8},{16,20},{20,16},{24,28},{28,24},{1,5},{5... | collective-permute-start | bytes 688136 | tf_op jit(solution)/shard_map/ppermute | solution.py:497
  57.2 1.5 %collective-permute-start.21 = (bf16[896,128]{1,0:T(8,128)(2,1)S(1)}, bf16[896,128]{1,0:T(8,128)(2,1)S(1)}, u32[]{:S(2)}, u32[]{:S(2)}) collective-permute-start(bf16[896,128]{1,0:T(8,128)(2,1)S(1)} %collective-permute-done.18.refs_0_), channel_id=1, source_target_pairs={{0,4},{4,0},{8,12},{12,8},{16,20},{20,16},{24,28},{28,24},{1,5},{5... | collective-permute-start | bytes 688136 | tf_op jit(solution)/shard_map/ppermute | solution.py:497
  60.0 1.7 %collective-permute-start.24 = (bf16[896,128]{1,0:T(8,128)(2,1)S(1)}, bf16[896,128]{1,0:T(8,128)(2,1)S(1)}, u32[]{:S(2)}, u32[]{:S(2)}) collective-permute-start(bf16[896,128]{1,0:T(8,128)(2,1)S(1)} %shard_map.111), channel_id=1, source_target_pairs={{0,4},{4,0},{8,12},{12,8},{16,20},{20,16},{24,28},{28,24},{1,5},{5... | collective-permute-start | bytes 688136 | tf_op jit(solution)/shard_map/ppermute | solution.py:497

commit v9 on v8

--- a/solution.py
+++ b/solution.py
@@ -225,35 +225,50 @@
     return total
 
 
-def inner_kernel(full, weights, pre, window):
-    edge = jnp.zeros((SLAB, 128), jnp.bfloat16)
+def inner_kernel(full, weights, pre, back, flipped, window):
+    edge = jnp.zeros((SLAB, 256), jnp.bfloat16)
+    flip_blocks(weights, TAPS, flipped)
     build_window(window, 0, lambda z: wide_plane(full, edge, edge, z, slice(0, 128)))
     pre[...] = conv(window, weights, 0)
-
-
-def add_edges(pre, low, high, weights, edge_window):
+    build_window(window, 0, lambda z: wide_plane(full, edge, edge, z, slice(128, 256)))
+    back[...] = conv_flipped(window, flipped)
+
+
+def add_edges(pre, low, high, edge_window, taps_dot):
     for ox, x, slab in ((0, 0, low), (2, NX - 1, high)):
         build_window(edge_window, 0, lambda z: slab[z * J : (z + 1) * J, :])
-        taps = weights[9 * ox : 9 * (ox + 1)].reshape(1152, 128)
-        term = dot(edge_window[...].reshape(SLAB, 1152), taps)
+        term = taps_dot(edge_window[...].reshape(SLAB, 1152), ox)
         for z in range(4):
             start = z * PLANE + x * J
             pre[start : start + J, :] += term[z * J : (z + 1) * J, :]
 
 
-def first_kernel(full, got_first, got_second, live, weights, inner, hb, keep, send, window, flipped, edge_window, pre):
+def taps_of(weights):
+    return lambda rows, ox: dot(rows, weights[9 * ox : 9 * (ox + 1)].reshape(1152, 128))
+
+
+def flipped_taps_of(flipped):
+    return lambda rows, ox: lax.dot_general(
+        rows,
+        flipped[:, 1152 * ox : 1152 * (ox + 1)],
+        (((1,), (1,)), ((), ())),
+        preferred_element_type=jnp.float32,
+    )
+
+
+def first_kernel(full, got_second, got_first, live, weights, inner, inner_back, flipped, hb, keep, send, edge_window, pre):
     f_lanes, g_lanes = slice(0, 128), slice(128, 256)
     low, high = read_by_parity("drift", got_first, got_second)
     alive = live[...].astype(jnp.float32)
-    flip_blocks(weights, TAPS, flipped)
     pre[...] = inner[...]
-    add_edges(pre, low[:, f_lanes], high[:, f_lanes], weights, edge_window)
+    add_edges(pre, low[:, f_lanes], high[:, f_lanes], edge_window, taps_of(weights))
     first_pre = pre[...]
     gate = jax.nn.sigmoid(first_pre)
     hidden = (alive * (first_pre * gate)).astype(jnp.bfloat16)
     slope = alive * (gate * (1.0 + first_pre * (1.0 - gate)))
-    build_window(window, 0, lambda z: wide_plane(full, low, high, z, g_lanes))
-    back = (conv_flipped(window, flipped) * slope).astype(jnp.bfloat16)
+    pre[...] = inner_back[...]
+    add_edges(pre, low[:, g_lanes], high[:, g_lanes], edge_window, flipped_taps_of(flipped))
+    back = (pre[...] * slope).astype(jnp.bfloat16)
     hb[...] = jnp.concatenate([hidden, back], axis=1)
     core = lax.axis_index("drift") % 2
 
@@ -435,9 +450,9 @@
         if field:
             for k in (*range(9), *range(18, 27)):
                 taps[k] = weights[TAPS - 1 - k].astype(jnp.float32).T.astype(jnp.bfloat16)
-            add_edges(pre, low[:, lanes], high[:, lanes], taps, edge_window)
+            add_edges(pre, low[:, lanes], high[:, lanes], edge_window, taps_of(taps))
         else:
-            add_edges(pre, low[:, lanes], high[:, lanes], weights.at[TAPS:], edge_window)
+            add_edges(pre, low[:, lanes], high[:, lanes], edge_window, taps_of(weights.at[TAPS:]))
         value = base[:, lanes].astype(jnp.float32) + pre[...]
         results.append((live[...].astype(jnp.float32) * value).astype(jnp.bfloat16))
     both = jnp.concatenate(results, axis=1)
@@ -517,13 +532,15 @@
     full, *slabs = call(insert_faces, (grid, slab, slab), [VMEM] * 3, [faces_scratch])(placed, *faces[::-1])
     slabs = pairs(*slabs, "drift")
     message = bf16(ROWS + 4 * WIDE, 128)
-    inner = call(inner_kernel, f32(ROWS, 128), [VMEM] * 2, conv_scratch[:1])(full, weights)
+    inner = call(
+        inner_kernel, (f32(ROWS, 128), f32(ROWS, 128), bf16(128, rows)), [VMEM] * 2, conv_scratch[:1]
+    )(full, weights)
     hb, keep, send = call(
         first_kernel,
         (grid, message, message),
-        [VMEM] * 6,
-        conv_scratch + [edge_window, pltpu.VMEM((ROWS, 128), jnp.float32)],
-    )(full, *slabs, live, weights, inner)
+        [VMEM] * 8,
+        [edge_window, pltpu.VMEM((ROWS, 128), jnp.float32)],
+    )(full, *slabs[::-1], live, weights, *inner)
     got = swap_core(send)
     term_window = pltpu.VMEM((4, WIDE, 1152), jnp.bfloat16)
     terms = f32(chunk * chips, 128)

time: 62.9 us -> 62.8 us (level)
  starting transfers between devices: 28.2 us -> 25 us
  waiting for transfers between devices: 11.6 us -> 14.2 us
    ppermute x6, waiting for transfers between devices: 6.18 us -> 8.39 us  [to_chip(): lax.ppermute(value, 'drift', [(i, i ^ 2 * chip_mask(kind, i % 2)) for i i...]
    ppermute x6, starting transfers between devices: 8.38 us -> 6.68 us  [to_chip(): lax.ppermute(value, 'drift', [(i, i ^ 2 * chip_mask(kind, i % 2)) for i i...]
    ppermute x2, starting transfers between devices: 2.56 us -> 1.4 us  [pairs(): got_second = lax.ppermute(value_second, axis, sorted(second.items()))]
  transfers between devices with their start and end apart: 25 -> 25, of which waited for: 10 -> 12; matrix products, arithmetic and copies ran while one was open for 2% -> 2% of each run, Pallas kernels for 22% -> 24%
where the time goes in v9:
time: 62.8 us; the launch traced here: 62.7 us
  starting transfers between devices  25 us (40%)
  Pallas kernels  20.2 us (32%)
  waiting for transfers between devices  14.2 us (23%)
  between operations  1.71 us (3%)
  local copies, waits for them, and re-layouts  1.38 us (2%)
    ppermute x6, starting transfers between devices, to_wire(): return lax.ppermute(value, 'wire', [(i, i ^ step) for i in range(wire)])  8.91 us
    ppermute x6, waiting for transfers between devices, to_chip(): lax.ppermute(value, 'drift', [(i, i ^ 2 * chip_mask(kind, i % 2)) for i i...  8.39 us
    ppermute x4, starting transfers between devices, pairs(): got_first = lax.ppermute(value_first, axis, first)  7.15 us
    ppermute x6, starting transfers between devices, to_chip(): lax.ppermute(value, 'drift', [(i, i ^ 2 * chip_mask(kind, i % 2)) for i i...  6.68 us
    pallas_call x4, Pallas kernels, on_device(): call(functools.partial(final_kernel, items, blocks, want_done), (f32(TAPS...  4.24 us
    pallas_call x2, Pallas kernels, on_device(): call(functools.partial(second_inner_kernel, field), (f32(ROWS, 128), toke...  3.3 us
    pallas_call x1, Pallas kernels, on_device(): call(inner_kernel, (f32(ROWS, 128), f32(ROWS, 128), bf16(128, rows)), [VM...  3.25 us
    ppermute x4, waiting for transfers between devices, pairs(): got_first = lax.ppermute(value_first, axis, first)  2.46 us
  transfers between devices with their start and end apart: 25, of which 12 were waited for; matrix products, arithmetic and copies ran while one was open for 2% of the time, Pallas kernels for 24%

profile of v9, /device:TPU:0, one launch (start us, length us, event | category | flops | bytes accessed | tf_op | source)
XLA Modules:
  0.0 62.7 jit_solution(6310491949594728069)
XLA Ops:
  0.7 2.0 %shard_map.94 = (bf16[48,256]{1,0:T(8,128)(2,1)}, bf16[48,256]{1,0:T(8,128)(2,1)}) custom-call(s32[1,1,16]{2,1,0:T(1,128)} %lists.5, bf16[576,128]{1,0:T(8,128)(2,1)} %bitcast.6, bf16[576,128]{1,0:T(8,128)(2,1)} %bitcast.4), custom_call_target="tpu_custom_call" | custom-call | tf_op jit(solution)/shard_map/pallas_call | solution.py:523
  3.2 4.1 %collective-permute-start.1 = (bf16[48,256]{1,0:T(8,128)(2,1)}, bf16[48,256]{1,0:T(8,128)(2,1)S(1)}, u32[]{:S(2)}, u32[]{:S(2)}) collective-permute-start(bf16[48,256]{1,0:T(8,128)(2,1)} %get-tuple-element.50), channel_id=1, source_target_pairs={{0,1},{1,0},{2,3},{3,2},{4,5},{5,4},{6,7},{7,6},{8,9},{9,8},{10,11... | collective-permute-start | bytes 73736 | tf_op jit(solution)/shard_map/ppermute | solution.py:492
  7.3 1.2 %constant_dynamic-update-slice_fusion.1 = bf16[54,128,128]{2,1,0:T(8,128)(2,1)S(1)} fusion(bf16[27,128,128]{2,1,0:T(8,128)(2,1)} %param.8), kind=kLoop, calls=%fused_computation.2 | loop fusion | bytes 1769472
  10.2 1.4 %collective-permute-start.2 = (bf16[64,256]{1,0:T(8,128)(2,1)S(1)}, bf16[64,256]{1,0:T(8,128)(2,1)S(1)}, u32[]{:S(2)}, u32[]{:S(2)}) collective-permute-start(bf16[64,256]{1,0:T(8,128)(2,1)S(1)} %get-tuple-element.52), channel_id=1, source_target_pairs={{0,28},{4,8},{8,4},{12,16},{16,12},{20,24},{24,20},{28,0},{1,29},{... | collective-permute-start | bytes 98312 | tf_op jit(solution)/shard_map/ppermute | solution.py:484
  12.1 3.3 %shard_map.96 = (f32[768,128]{1,0:T(8,128)S(1)}, f32[768,128]{1,0:T(8,128)S(1)}, bf16[128,3456]{1,0:T(8,128)(2,1)S(1)}) custom-call(bf16[768,256]{1,0:T(8,128)(2,1)S(1)} %get-tuple-element.51.full.base, bf16[54,128,128]{2,1,0:T(8,128)(2,1)S(1)} %constant_dynamic-update-slice_fusion.weights), custom_call_target="tpu_custom_call" | custom-call | tf_op jit(solution)/shard_map/pallas_call | solution.py:535
  15.3 0.9 %shard_map.97 = (bf16[768,256]{1,0:T(8,128)(2,1)S(1)}, bf16[1664,128]{1,0:T(8,128)(2,1)S(1)}, bf16[1664,128]{1,0:T(8,128)(2,1)S(1)}) custom-call(bf16[768,256]{1,0:T(8,128)(2,1)S(1)} %get-tuple-element.51.full.base, bf16[64,256]{1,0:T(8,128)(2,1)S(1)} %collective-permute-done.2.got_second, bf16[64,256]{1,0:T(8,128)(2,1)S(1)} %collective-permute-done.3.got_first, ...), custom_call_target="tpu_custom_call" | custom-call | tf_op jit(solution)/shard_map/pallas_call | solution.py:538
  16.5 1.1 %shard_map.98.mine = f32[3584,128]{1,0:T(8,128)S(1)} custom-call(bf16[1664,128]{1,0:T(8,128)(2,1)S(1)} %get-tuple-element.59.mine), custom_call_target="tpu_custom_call" | custom-call | tf_op jit(solution)/shard_map/pallas_call | solution.py:547
  18.1 0.8 %shard_map.99 = (bf16[896,128]{1,0:T(8,128)(2,1)S(1)}, bf16[128,768]{1,0:T(8,128)(2,1)S(1)}, bf16[4,224,1152]{2,1,0:T(8,128)(2,1)S(1)}) custom-call(f32[3584,128]{1,0:T(8,128)S(1)} %shard_map.98.mine, bf16[1664,128]{1,0:T(8,128)(2,1)S(1)} %collective-permute-done.4.theirs), custom_call_target="tpu_custom_call" | custom-call | tf_op jit(solution)/shard_map/pallas_call | solution.py:551
  18.9 1.6 %collective-permute-start.10 = (bf16[896,128]{1,0:T(8,128)(2,1)S(1)}, bf16[896,128]{1,0:T(8,128)(2,1)S(1)}, u32[]{:S(2)}, u32[]{:S(2)}) collective-permute-start(bf16[896,128]{1,0:T(8,128)(2,1)S(1)} %get-tuple-element.75), channel_id=1, source_target_pairs={{0,8},{4,20},{8,0},{12,28},{16,24},{20,4},{24,16},{28,12},{1,9},{5... | collective-permute-start | bytes 688136 | tf_op jit(solution)/shard_map/ppermute | solution.py:515
  20.4 1.1 %shard_map.100 = (bf16[896,128]{1,0:T(8,128)(2,1)S(1)}, f32[896,128]{1,0:T(8,128)S(1)}, f32[896,128]{1,0:T(8,128)S(1)}, bf16[48,256]{1,0:T(8,128)(2,1)S(1)}, bf16[48,256]{1,0:T(8,128)(2,1)S(1)}) custom-call(f32[3584,128]{1,0:T(8,128)S(1)} %shard_map.98.mine, bf16[128,768]{1,0:T(8,128)(2,1)S(1)} %get-tuple-element.61.left, ...), custom_call_target="tpu_custom_call" | custom-call | tf_op jit(solution)/shard_map/pallas_call | solution.py:556
  22.2 2.8 %collective-permute-done.10.received = bf16[896,128]{1,0:T(8,128)(2,1)S(1)} collective-permute-done((bf16[896,128]{1,0:T(8,128)(2,1)S(1)}, bf16[896,128]{1,0:T(8,128)(2,1)S(1)}, u32[]{:S(2)}, u32[]{:S(2)}) %collective-permute-start.10) | collective-permute-done | bytes 229408 | tf_op jit(solution)/shard_map/ppermute | solution.py:515
  25.0 1.6 %collective-permute-start.11 = (bf16[896,128]{1,0:T(8,128)(2,1)S(1)}, bf16[896,128]{1,0:T(8,128)(2,1)S(1)}, u32[]{:S(2)}, u32[]{:S(2)}) collective-permute-start(bf16[896,128]{1,0:T(8,128)(2,1)S(1)} %shard_map.104), channel_id=1, source_target_pairs={{0,16},{4,12},{8,24},{12,4},{16,0},{20,28},{24,8},{28,20},{1,17},{... | collective-permute-start | bytes 688136 | tf_op jit(solution)/shard_map/ppermute | solution.py:515
  26.6 1.4 %collective-permute-start.5 = (bf16[48,256]{1,0:T(8,128)(2,1)S(1)}, bf16[48,256]{1,0:T(8,128)(2,1)S(1)}, u32[]{:S(2)}, u32[]{:S(2)}) collective-permute-start(bf16[48,256]{1,0:T(8,128)(2,1)S(1)} %get-tuple-element.63), channel_id=1, source_target_pairs={{0,1},{1,0},{2,3},{3,2},{4,5},{5,4},{6,7},{7,6},{8,9},{9,8},{10,11... | collective-permute-start | bytes 73736 | tf_op jit(solution)/shard_map/ppermute | solution.py:492
  28.0 2.4 %collective-permute-done.5.got_first = bf16[48,256]{1,0:T(8,128)(2,1)S(1)} collective-permute-done((bf16[48,256]{1,0:T(8,128)(2,1)S(1)}, bf16[48,256]{1,0:T(8,128)(2,1)S(1)}, u32[]{:S(2)}, u32[]{:S(2)}) %collective-permute-start.5) | collective-permute-done | bytes 24608 | tf_op jit(solution)/shard_map/ppermute | solution.py:492
  31.2 2.0 %collective-permute-start.12 = (bf16[224,128]{1,0:T(8,128)(2,1)S(1)}, bf16[224,128]{1,0:T(8,128)(2,1)S(1)}, u32[]{:S(2)}, u32[]{:S(2)}) collective-permute-start(bf16[224,128]{1,0:T(8,128)(2,1)S(1)} %get-tuple-element.77), channel_id=1, source_target_pairs={{0,3},{1,2},{2,1},{3,0},{4,7},{5,6},{6,5},{7,4},{8,11},{9,10},{10,... | collective-permute-start | bytes 172040 | tf_op jit(solution)/shard_map/ppermute | solution.py:518
  33.2 1.2 %collective-permute-start.13 = (bf16[224,128]{1,0:T(8,128)(2,1)S(1)}, bf16[224,128]{1,0:T(8,128)(2,1)S(1)}, u32[]{:S(2)}, u32[]{:S(2)}) collective-permute-start(bf16[224,128]{1,0:T(8,128)(2,1)S(1)} %get-tuple-element.78), channel_id=1, source_target_pairs={{0,2},{1,3},{2,0},{3,1},{4,6},{5,7},{6,4},{7,5},{8,10},{9,11},{10,... | collective-permute-start | bytes 172040 | tf_op jit(solution)/shard_map/ppermute | solution.py:518
  34.4 1.3 %collective-permute-start.14 = (bf16[224,128]{1,0:T(8,128)(2,1)S(1)}, bf16[224,128]{1,0:T(8,128)(2,1)S(1)}, u32[]{:S(2)}, u32[]{:S(2)}) collective-permute-start(bf16[224,128]{1,0:T(8,128)(2,1)S(1)} %get-tuple-element.79), channel_id=1, source_target_pairs={{0,1},{1,0},{2,3},{3,2},{4,5},{5,4},{6,7},{7,6},{8,9},{9,8},{10,11... | collective-permute-start | bytes 172040 | tf_op jit(solution)/shard_map/ppermute | solution.py:518
  35.7 1.6 %shard_map.102 = (f32[768,128]{1,0:T(8,128)S(1)}, f32[8,128]{1,0:T(8,128)S(1)}) custom-call(bf16[768,256]{1,0:T(8,128)(2,1)S(1)} %get-tuple-element.65.hb, bf16[54,128,128]{2,1,0:T(8,128)(2,1)S(1)} %constant_dynamic-update-slice_fusion.weights), custom_call_target="tpu_custom_call" | custom-call | tf_op jit(solution)/shard_map/pallas_call | solution.py:577
  37.8 1.4 %collective-permute-done.13.refs_1_ = bf16[224,128]{1,0:T(8,128)(2,1)S(1)} collective-permute-done((bf16[224,128]{1,0:T(8,128)(2,1)S(1)}, bf16[224,128]{1,0:T(8,128)(2,1)S(1)}, u32[]{:S(2)}, u32[]{:S(2)}) %collective-permute-start.13) | collective-permute-done | bytes 57376 | tf_op jit(solution)/shard_map/ppermute | solution.py:518
  39.2 2.0 %collective-permute-start.17 = (bf16[224,128]{1,0:T(8,128)(2,1)S(1)}, bf16[224,128]{1,0:T(8,128)(2,1)S(1)}, u32[]{:S(2)}, u32[]{:S(2)}) collective-permute-start(bf16[224,128]{1,0:T(8,128)(2,1)S(1)} %shard_map.106.refs_0_), channel_id=1, source_target_pairs={{0,3},{1,2},{2,1},{3,0},{4,7},{5,6},{6,5},{7,4},{8,11},{9,10},{10,... | collective-permute-start | bytes 172040 | tf_op jit(solution)/shard_map/ppermute | solution.py:518
  41.4 2.3 %collective-permute-start.15 = (bf16[224,128]{1,0:T(8,128)(2,1)S(1)}, bf16[224,128]{1,0:T(8,128)(2,1)S(1)}, u32[]{:S(2)}, u32[]{:S(2)}) collective-permute-start(bf16[224,128]{1,0:T(8,128)(2,1)S(1)} %shard_map.106.refs_0_), channel_id=1, source_target_pairs={{0,1},{1,0},{2,3},{3,2},{4,5},{5,4},{6,7},{7,6},{8,9},{9,8},{10,11... | collective-permute-start | bytes 172040 | tf_op jit(solution)/shard_map/ppermute | solution.py:518
  43.7 1.4 %collective-permute-start.7 = (bf16[64,256]{1,0:T(8,128)(2,1)S(1)}, bf16[64,256]{1,0:T(8,128)(2,1)S(1)}, u32[]{:S(2)}, u32[]{:S(2)}) collective-permute-start(bf16[64,256]{1,0:T(8,128)(2,1)S(1)} %get-tuple-element.68.after), channel_id=1, source_target_pairs={{0,4},{4,0},{8,12},{12,8},{16,20},{20,16},{24,28},{28,24},{1,5},{5... | collective-permute-start | bytes 98312 | tf_op jit(solution)/shard_map/ppermute | solution.py:492
  45.0 1.7 %shard_map.103 = (f32[768,128]{1,0:T(8,128)S(1)}, f32[8,128]{1,0:T(8,128)S(1)}) custom-call(bf16[768,256]{1,0:T(8,128)(2,1)S(1)} %get-tuple-element.65.hb, bf16[54,128,128]{2,1,0:T(8,128)(2,1)S(1)} %constant_dynamic-update-slice_fusion.weights), custom_call_target="tpu_custom_call" | custom-call | tf_op jit(solution)/shard_map/pallas_call | solution.py:577
  47.0 1.4 %collective-permute-start.19 = (bf16[896,128]{1,0:T(8,128)(2,1)S(1)}, bf16[896,128]{1,0:T(8,128)(2,1)S(1)}, u32[]{:S(2)}, u32[]{:S(2)}) collective-permute-start(bf16[896,128]{1,0:T(8,128)(2,1)S(1)} %shard_map.107.held.refs_0_), channel_id=1, source_target_pairs={{0,8},{4,20},{8,0},{12,28},{16,24},{20,4},{24,16},{28,12},{1,9},{5... | collective-permute-start | bytes 688136 | tf_op jit(solution)/shard_map/ppermute | solution.py:515
  48.4 2.1 %shard_map.108 = (bf16[576,128]{1,0:T(8,128)(2,1)}, bf16[576,128]{1,0:T(8,128)(2,1)}, bf16[896,128]{1,0:T(8,128)(2,1)S(1)}) custom-call(s32[1,1,16]{2,1,0:T(1,128)S(1)} %copy-done, s32[1,1]{1,0:T(1,128)S(6)} %copy.23.counts, f32[768,128]{1,0:T(8,128)S(1)} %get-tuple-element.66.inner_hidden, f32[768,128]{1,0:T(8,128)S(1)} %get-tuple-element.67.inner_back, ...), custom_call_target="tpu_custom_call" | custom-call | tf_op jit(solution)/shard_map/pallas_call | solution.py:599
  50.5 0.9 %collective-permute-start.18 = (bf16[896,128]{1,0:T(8,128)(2,1)S(1)}, bf16[896,128]{1,0:T(8,128)(2,1)S(1)}, u32[]{:S(2)}, u32[]{:S(2)}) collective-permute-start(bf16[896,128]{1,0:T(8,128)(2,1)S(1)} %get-tuple-element.82), channel_id=1, source_target_pairs={{0,16},{4,12},{8,24},{12,4},{16,0},{20,28},{24,8},{28,20},{1,17},{... | collective-permute-start | bytes 688136 | tf_op jit(solution)/shard_map/ppermute | solution.py:515
  51.4 2.6 %collective-permute-done.19.refs_2_ = bf16[896,128]{1,0:T(8,128)(2,1)S(1)} collective-permute-done((bf16[896,128]{1,0:T(8,128)(2,1)S(1)}, bf16[896,128]{1,0:T(8,128)(2,1)S(1)}, u32[]{:S(2)}, u32[]{:S(2)}) %collective-permute-start.19) | collective-permute-done | bytes 229408 | tf_op jit(solution)/shard_map/ppermute | solution.py:515
  54.7 1.8 %collective-permute-done.18.refs_0_ = bf16[896,128]{1,0:T(8,128)(2,1)S(1)} collective-permute-done((bf16[896,128]{1,0:T(8,128)(2,1)S(1)}, bf16[896,128]{1,0:T(8,128)(2,1)S(1)}, u32[]{:S(2)}, u32[]{:S(2)}) %collective-permute-start.18) | collective-permute-done | bytes 229408 | tf_op jit(solution)/shard_map/ppermute | solution.py:515
  56.5 1.3 %shard_map.109 = (f32[27,128,128]{2,1,0:T(8,128)}, f32[27,128,128]{2,1,0:T(8,128)}) custom-call(bf16[896,128]{1,0:T(8,128)(2,1)S(1)} %shard_map.107.held.refs_0_, bf16[896,128]{1,0:T(8,128)(2,1)S(1)} %collective-permute-done.22.refs_1_, bf16[896,128]{1,0:T(8,128)(2,1)S(1)} %collective-permute-done.19.refs_2_), custom_call_target="tpu_custom_call" | custom-call | flops 49999998976 | tf_op jit(solution)/shard_map/pallas_call | solution.py:628
  58.0 1.3 %shard_map.110 = (f32[27,128,128]{2,1,0:T(8,128)}, f32[27,128,128]{2,1,0:T(8,128)}, f32[8,128]{1,0:T(8,128)S(1)}) custom-call(bf16[896,128]{1,0:T(8,128)(2,1)S(1)} %collective-permute-done.18.refs_0_, bf16[896,128]{1,0:T(8,128)(2,1)S(1)} %collective-permute-done.20.refs_1_, ...), custom_call_target="tpu_custom_call", output_to_operand_aliasing={{0}: (3, {}), {1}: (4, {})} | custom-call | flops 49999998976 | tf_op jit(solution)/shard_map/pallas_call | solution.py:628
  60.1 0.8 %shard_map.112 = (f32[27,128,128]{2,1,0:T(8,128)}, f32[27,128,128]{2,1,0:T(8,128)}) custom-call(bf16[896,128]{1,0:T(8,128)(2,1)S(1)} %collective-permute-done.23.value.refs_0_, f32[27,128,128]{2,1,0:T(8,128)} %get-tuple-element.86.refs_1_, f32[27,128,128]{2,1,0:T(8,128)} %get-tuple-element.87.refs_2_), custom_call_target="tpu_custom_call", output_to_operand_aliasing={{0}: (1, {}), {1}: (2, {})} | custom-call | flops 49999998976 | tf_op jit(solution)/shard_map/pallas_call | solution.py:628
  61.6 0.9 %shard_map.113 = (f32[27,128,128]{2,1,0:T(8,128)}, f32[27,128,128]{2,1,0:T(8,128)}) custom-call(bf16[896,128]{1,0:T(8,128)(2,1)S(1)} %collective-permute-done.24.refs_0_, f32[27,128,128]{2,1,0:T(8,128)} %get-tuple-element.88.refs_1_, f32[27,128,128]{2,1,0:T(8,128)} %get-tuple-element.89.refs_2_), custom_call_target="tpu_custom_call", output_to_operand_aliasing={{0}: (1, {}), {1}: (2, {})} | custom-call | flops 49999998976 | tf_op jit(solution)/shard_map/pallas_call | solution.py:628
  (50 shorter events, 7.4 us)
Async XLA Ops:
  0.6 8.6 %copy-start = (s32[1,1,16]{2,1,0:T(1,128)S(1)}, s32[1,1,16]{2,1,0:T(1,128)}, u32[]{:S(2)}) copy-start(s32[1,1,16]{2,1,0:T(1,128)} %lists.5) | copy-start | bytes 196
  0.6 7.9 %copy-start.2 = (bf16[1,1,576,128]{3,2,1,0:T(8,128)(2,1)S(1)}, bf16[1,1,576,128]{3,2,1,0:T(8,128)(2,1)}, u32[]{:S(2)}) copy-start(bf16[1,1,576,128]{3,2,1,0:T(8,128)(2,1)} %param.10) | copy-start | bytes 442372
  0.7 7.9 %copy-start.3 = (bf16[1,1,576,128]{3,2,1,0:T(8,128)(2,1)S(1)}, bf16[1,1,576,128]{3,2,1,0:T(8,128)(2,1)}, u32[]{:S(2)}) copy-start(bf16[1,1,576,128]{3,2,1,0:T(8,128)(2,1)} %param.7) | copy-start | bytes 442372
  0.7 11.3 %copy-start.1 = (bf16[27,128,128]{2,1,0:T(8,128)(2,1)S(1)}, bf16[27,128,128]{2,1,0:T(8,128)(2,1)}, u32[]{:S(2)}) copy-start(bf16[27,128,128]{2,1,0:T(8,128)(2,1)} %param.9) | copy-start | bytes 2654212
  2.6 7.3 %collective-permute-start = (bf16[48,256]{1,0:T(8,128)(2,1)}, bf16[48,256]{1,0:T(8,128)(2,1)S(1)}, u32[]{:S(2)}, u32[]{:S(2)}) collective-permute-start(bf16[48,256]{1,0:T(8,128)(2,1)} %get-tuple-element.49), channel_id=1, source_target_pairs={{0,4},{1,2},{2,1},{3,7},{4,0},{5,6},{6,5},{7,3},{8,12},{9,10},{10,... | collective-permute-start | bytes 73736 | tf_op jit(solution)/shard_map/ppermute | solution.py:491
  3.2 6.8 %collective-permute-start.1 = (bf16[48,256]{1,0:T(8,128)(2,1)}, bf16[48,256]{1,0:T(8,128)(2,1)S(1)}, u32[]{:S(2)}, u32[]{:S(2)}) collective-permute-start(bf16[48,256]{1,0:T(8,128)(2,1)} %get-tuple-element.50), channel_id=1, source_target_pairs={{0,1},{1,0},{2,3},{3,2},{4,5},{5,4},{6,7},{7,6},{8,9},{9,8},{10,11... | collective-permute-start | bytes 73736 | tf_op jit(solution)/shard_map/ppermute | solution.py:492
  10.2 5.1 %collective-permute-start.2 = (bf16[64,256]{1,0:T(8,128)(2,1)S(1)}, bf16[64,256]{1,0:T(8,128)(2,1)S(1)}, u32[]{:S(2)}, u32[]{:S(2)}) collective-permute-start(bf16[64,256]{1,0:T(8,128)(2,1)S(1)} %get-tuple-element.52), channel_id=1, source_target_pairs={{0,28},{4,8},{8,4},{12,16},{16,12},{20,24},{24,20},{28,0},{1,29},{... | collective-permute-start | bytes 98312 | tf_op jit(solution)/shard_map/ppermute | solution.py:484
  11.6 3.7 %collective-permute-start.3 = (bf16[64,256]{1,0:T(8,128)(2,1)S(1)}, bf16[64,256]{1,0:T(8,128)(2,1)S(1)}, u32[]{:S(2)}, u32[]{:S(2)}) collective-permute-start(bf16[64,256]{1,0:T(8,128)(2,1)S(1)} %get-tuple-element.53), channel_id=1, source_target_pairs={{0,4},{4,0},{8,12},{12,8},{16,20},{20,16},{24,28},{28,24},{1,5},{5... | collective-permute-start | bytes 98312 | tf_op jit(solution)/shard_map/ppermute | solution.py:492
  16.2 1.8 %collective-permute-start.4 = (bf16[1664,128]{1,0:T(8,128)(2,1)S(1)}, bf16[1664,128]{1,0:T(8,128)(2,1)S(1)}, u32[]{:S(2)}, u32[]{:S(2)}) collective-permute-start(bf16[1664,128]{1,0:T(8,128)(2,1)S(1)} %get-tuple-element.60), channel_id=1, source_target_pairs={{0,4},{4,0},{8,12},{12,8},{16,20},{20,16},{24,28},{28,24},{1,5},{5... | collective-permute-start | bytes 1277960 | tf_op jit(solution)/shard_map/ppermute | solution.py:512
  18.9 6.1 %collective-permute-start.10 = (bf16[896,128]{1,0:T(8,128)(2,1)S(1)}, bf16[896,128]{1,0:T(8,128)(2,1)S(1)}, u32[]{:S(2)}, u32[]{:S(2)}) collective-permute-start(bf16[896,128]{1,0:T(8,128)(2,1)S(1)} %get-tuple-element.75), channel_id=1, source_target_pairs={{0,8},{4,20},{8,0},{12,28},{16,24},{20,4},{24,16},{28,12},{1,9},{5... | collective-permute-start | bytes 688136 | tf_op jit(solution)/shard_map/ppermute | solution.py:515
  21.6 9.1 %collective-permute-start.9 = (bf16[896,128]{1,0:T(8,128)(2,1)S(1)}, bf16[896,128]{1,0:T(8,128)(2,1)S(1)}, u32[]{:S(2)}, u32[]{:S(2)}) collective-permute-start(bf16[896,128]{1,0:T(8,128)(2,1)S(1)} %get-tuple-element.73), channel_id=1, source_target_pairs={{0,8},{4,20},{8,0},{12,28},{16,24},{20,4},{24,16},{28,12},{1,9},{5... | collective-permute-start | bytes 688136 | tf_op jit(solution)/shard_map/ppermute | solution.py:515
  25.0 6.1 %collective-permute-start.11 = (bf16[896,128]{1,0:T(8,128)(2,1)S(1)}, bf16[896,128]{1,0:T(8,128)(2,1)S(1)}, u32[]{:S(2)}, u32[]{:S(2)}) collective-permute-start(bf16[896,128]{1,0:T(8,128)(2,1)S(1)} %shard_map.104), channel_id=1, source_target_pairs={{0,16},{4,12},{8,24},{12,4},{16,0},{20,28},{24,8},{28,20},{1,17},{... | collective-permute-start | bytes 688136 | tf_op jit(solution)/shard_map/ppermute | solution.py:515
  26.6 3.8 %collective-permute-start.5 = (bf16[48,256]{1,0:T(8,128)(2,1)S(1)}, bf16[48,256]{1,0:T(8,128)(2,1)S(1)}, u32[]{:S(2)}, u32[]{:S(2)}) collective-permute-start(bf16[48,256]{1,0:T(8,128)(2,1)S(1)} %get-tuple-element.63), channel_id=1, source_target_pairs={{0,1},{1,0},{2,3},{3,2},{4,5},{5,4},{6,7},{7,6},{8,9},{9,8},{10,11... | collective-permute-start | bytes 73736 | tf_op jit(solution)/shard_map/ppermute | solution.py:492
  28.0 2.5 %collective-permute-start.6 = (bf16[48,256]{1,0:T(8,128)(2,1)S(1)}, bf16[48,256]{1,0:T(8,128)(2,1)S(1)}, u32[]{:S(2)}, u32[]{:S(2)}) collective-permute-start(bf16[48,256]{1,0:T(8,128)(2,1)S(1)} %get-tuple-element.64), channel_id=1, source_target_pairs={{0,4},{1,2},{2,1},{3,7},{4,0},{5,6},{6,5},{7,3},{8,12},{9,10},{10,... | collective-permute-start | bytes 73736 | tf_op jit(solution)/shard_map/ppermute | solution.py:491
  31.2 6.6 %collective-permute-start.12 = (bf16[224,128]{1,0:T(8,128)(2,1)S(1)}, bf16[224,128]{1,0:T(8,128)(2,1)S(1)}, u32[]{:S(2)}, u32[]{:S(2)}) collective-permute-start(bf16[224,128]{1,0:T(8,128)(2,1)S(1)} %get-tuple-element.77), channel_id=1, source_target_pairs={{0,3},{1,2},{2,1},{3,0},{4,7},{5,6},{6,5},{7,4},{8,11},{9,10},{10,... | collective-permute-start | bytes 172040 | tf_op jit(solution)/shard_map/ppermute | solution.py:518
  33.2 6.0 %collective-permute-start.13 = (bf16[224,128]{1,0:T(8,128)(2,1)S(1)}, bf16[224,128]{1,0:T(8,128)(2,1)S(1)}, u32[]{:S(2)}, u32[]{:S(2)}) collective-permute-start(bf16[224,128]{1,0:T(8,128)(2,1)S(1)} %get-tuple-element.78), channel_id=1, source_target_pairs={{0,2},{1,3},{2,0},{3,1},{4,6},{5,7},{6,4},{7,5},{8,10},{9,11},{10,... | collective-permute-start | bytes 172040 | tf_op jit(solution)/shard_map/ppermute | solution.py:518
  34.4 4.8 %collective-permute-start.14 = (bf16[224,128]{1,0:T(8,128)(2,1)S(1)}, bf16[224,128]{1,0:T(8,128)(2,1)S(1)}, u32[]{:S(2)}, u32[]{:S(2)}) collective-permute-start(bf16[224,128]{1,0:T(8,128)(2,1)S(1)} %get-tuple-element.79), channel_id=1, source_target_pairs={{0,1},{1,0},{2,3},{3,2},{4,5},{5,4},{6,7},{7,6},{8,9},{9,8},{10,11... | collective-permute-start | bytes 172040 | tf_op jit(solution)/shard_map/ppermute | solution.py:518
  39.2 7.5 %collective-permute-start.17 = (bf16[224,128]{1,0:T(8,128)(2,1)S(1)}, bf16[224,128]{1,0:T(8,128)(2,1)S(1)}, u32[]{:S(2)}, u32[]{:S(2)}) collective-permute-start(bf16[224,128]{1,0:T(8,128)(2,1)S(1)} %shard_map.106.refs_0_), channel_id=1, source_target_pairs={{0,3},{1,2},{2,1},{3,0},{4,7},{5,6},{6,5},{7,4},{8,11},{9,10},{10,... | collective-permute-start | bytes 172040 | tf_op jit(solution)/shard_map/ppermute | solution.py:518
  41.2 5.7 %collective-permute-start.16 = (bf16[224,128]{1,0:T(8,128)(2,1)S(1)}, bf16[224,128]{1,0:T(8,128)(2,1)S(1)}, u32[]{:S(2)}, u32[]{:S(2)}) collective-permute-start(bf16[224,128]{1,0:T(8,128)(2,1)S(1)} %shard_map.106.refs_0_), channel_id=1, source_target_pairs={{0,2},{1,3},{2,0},{3,1},{4,6},{5,7},{6,4},{7,5},{8,10},{9,11},{10,... | collective-permute-start | bytes 172040 | tf_op jit(solution)/shard_map/ppermute | solution.py:518
  41.4 5.5 %collective-permute-start.15 = (bf16[224,128]{1,0:T(8,128)(2,1)S(1)}, bf16[224,128]{1,0:T(8,128)(2,1)S(1)}, u32[]{:S(2)}, u32[]{:S(2)}) collective-permute-start(bf16[224,128]{1,0:T(8,128)(2,1)S(1)} %shard_map.106.refs_0_), channel_id=1, source_target_pairs={{0,1},{1,0},{2,3},{3,2},{4,5},{5,4},{6,7},{7,6},{8,9},{9,8},{10,11... | collective-permute-start | bytes 172040 | tf_op jit(solution)/shard_map/ppermute | solution.py:518
  43.7 4.7 %collective-permute-start.8 = (bf16[64,256]{1,0:T(8,128)(2,1)S(1)}, bf16[64,256]{1,0:T(8,128)(2,1)S(1)}, u32[]{:S(2)}, u32[]{:S(2)}) collective-permute-start(bf16[64,256]{1,0:T(8,128)(2,1)S(1)} %get-tuple-element.69), channel_id=1, source_target_pairs={{0,28},{4,8},{8,4},{12,16},{16,12},{20,24},{24,20},{28,0},{1,29},{... | collective-permute-start | bytes 98312 | tf_op jit(solution)/shard_map/ppermute | solution.py:484
  43.7 4.7 %collective-permute-start.7 = (bf16[64,256]{1,0:T(8,128)(2,1)S(1)}, bf16[64,256]{1,0:T(8,128)(2,1)S(1)}, u32[]{:S(2)}, u32[]{:S(2)}) collective-permute-start(bf16[64,256]{1,0:T(8,128)(2,1)S(1)} %get-tuple-element.68.after), channel_id=1, source_target_pairs={{0,4},{4,0},{8,12},{12,8},{16,20},{20,16},{24,28},{28,24},{1,5},{5... | collective-permute-start | bytes 98312 | tf_op jit(solution)/shard_map/ppermute | solution.py:492
  47.0 7.0 %collective-permute-start.19 = (bf16[896,128]{1,0:T(8,128)(2,1)S(1)}, bf16[896,128]{1,0:T(8,128)(2,1)S(1)}, u32[]{:S(2)}, u32[]{:S(2)}) collective-permute-start(bf16[896,128]{1,0:T(8,128)(2,1)S(1)} %shard_map.107.held.refs_0_), channel_id=1, source_target_pairs={{0,8},{4,20},{8,0},{12,28},{16,24},{20,4},{24,16},{28,12},{1,9},{5... | collective-permute-start | bytes 688136 | tf_op jit(solution)/shard_map/ppermute | solution.py:515
  50.5 6.0 %collective-permute-start.18 = (bf16[896,128]{1,0:T(8,128)(2,1)S(1)}, bf16[896,128]{1,0:T(8,128)(2,1)S(1)}, u32[]{:S(2)}, u32[]{:S(2)}) collective-permute-start(bf16[896,128]{1,0:T(8,128)(2,1)S(1)} %get-tuple-element.82), channel_id=1, source_target_pairs={{0,16},{4,12},{8,24},{12,4},{16,0},{20,28},{24,8},{28,20},{1,17},{... | collective-permute-start | bytes 688136 | tf_op jit(solution)/shard_map/ppermute | solution.py:515
  51.4 5.1 %collective-permute-start.22 = (bf16[896,128]{1,0:T(8,128)(2,1)S(1)}, bf16[896,128]{1,0:T(8,128)(2,1)S(1)}, u32[]{:S(2)}, u32[]{:S(2)}) collective-permute-start(bf16[896,128]{1,0:T(8,128)(2,1)S(1)} %shard_map.107.held.refs_0_), channel_id=1, source_target_pairs={{0,4},{4,0},{8,12},{12,8},{16,20},{20,16},{24,28},{28,24},{1,5},{5... | collective-permute-start | bytes 688136 | tf_op jit(solution)/shard_map/ppermute | solution.py:512
  54.0 6.0 %collective-permute-start.23 = (bf16[896,128]{1,0:T(8,128)(2,1)S(1)}, bf16[896,128]{1,0:T(8,128)(2,1)S(1)}, u32[]{:S(2)}, u32[]{:S(2)}) collective-permute-start(bf16[896,128]{1,0:T(8,128)(2,1)S(1)} %collective-permute-done.19.refs_2_), channel_id=1, source_target_pairs={{0,16},{4,12},{8,24},{12,4},{16,0},{20,28},{24,8},{28,20},{1,17},{... | collective-permute-start | bytes 688136 | tf_op jit(solution)/shard_map/ppermute | solution.py:515
  54.6 3.3 %collective-permute-start.20 = (bf16[896,128]{1,0:T(8,128)(2,1)S(1)}, bf16[896,128]{1,0:T(8,128)(2,1)S(1)}, u32[]{:S(2)}, u32[]{:S(2)}) collective-permute-start(bf16[896,128]{1,0:T(8,128)(2,1)S(1)} %collective-permute-done.19.refs_2_), channel_id=1, source_target_pairs={{0,4},{4,0},{8,12},{12,8},{16,20},{20,16},{24,28},{28,24},{1,5},{5... | collective-permute-start | bytes 688136 | tf_op jit(solution)/shard_map/ppermute | solution.py:512
  56.5 1.5 %collective-permute-start.21 = (bf16[896,128]{1,0:T(8,128)(2,1)S(1)}, bf16[896,128]{1,0:T(8,128)(2,1)S(1)}, u32[]{:S(2)}, u32[]{:S(2)}) collective-permute-start(bf16[896,128]{1,0:T(8,128)(2,1)S(1)} %collective-permute-done.18.refs_0_), channel_id=1, source_target_pairs={{0,4},{4,0},{8,12},{12,8},{16,20},{20,16},{24,28},{28,24},{1,5},{5... | collective-permute-start | bytes 688136 | tf_op jit(solution)/shard_map/ppermute | solution.py:512
  60.0 1.6 %collective-permute-start.24 = (bf16[896,128]{1,0:T(8,128)(2,1)S(1)}, bf16[896,128]{1,0:T(8,128)(2,1)S(1)}, u32[]{:S(2)}, u32[]{:S(2)}) collective-permute-start(bf16[896,128]{1,0:T(8,128)(2,1)S(1)} %shard_map.111), channel_id=1, source_target_pairs={{0,4},{4,0},{8,12},{12,8},{16,20},{20,16},{24,28},{28,24},{1,5},{5... | collective-permute-start | bytes 688136 | tf_op jit(solution)/shard_map/ppermute | solution.py:512
